TPU v7x, 32 devices: a whole 2x2x4 slice. The times are simulated.
32 devices in a mesh: gx: 8 (over y, x, core), gy: 4 (over z).
Axes of the slice: x: 2, y: 2, z: 4, core: 2. Of those that a mesh axis runs over, the one named last changes fastest.
Arguments:
- state: bfloat16 [64, 32, 32, 128], P(None, 'gx', 'gy'), may hold values from -6 to 6
- cotangent: bfloat16 [64, 32, 32, 128], P(None, 'gx', 'gy'), may hold values from -6 to 6
- spectral_weight: bfloat16 [2, 16, 32, 32, 4096], P(None, 'gx', 'gy'), may hold values from -0.5 to 0.5
- stencil_weight: bfloat16 [64, 1728], replicated, may hold values from -0.15625 to 0.15625
- pointwise_weight: bfloat16 [64, 64], replicated, may hold values from -0.75 to 0.75
Outputs:
- output: bfloat16 [64, 32, 32, 128], P(None, 'gx', 'gy')
- grad_state: float32 [64, 32, 32, 128], P(None, 'gx', 'gy')
- grad_modes: float32 [2, 16, 32, 32, 4096], P(None, 'gx', 'gy')
- grad_stencil: float32 [64, 1728], replicated
- grad_point: float32 [64, 64], replicated
All inputs are finite; a program needn't handle non-finite values.
Results may differ from a plain program's by a relative error of at most 0.0029.
Values may be sent and summed in bfloat16 or wider, within the bound.
No kernel may reach another device: no remote copies, remote signals or barrier semaphores. Data moves between devices by JAX's collectives and lax.ppermute only.
A program may use at most 192 MiB of HBM per device.

v0:
```python
import math

import jax
import jax.numpy as jnp
from jax import lax
from jax.sharding import PartitionSpec as P

C = 64
MX = 32
MY = 32
MZ = 16
CX = 4
CY = 8
Z = 128


HIGH = lax.Precision.HIGHEST


def with_halo(block, sides, width):
    for axis, dim in sides:
        count = lax.axis_size(axis)
        forward = [(i, i + 1) for i in range(count - 1)]
        backward = [(target, source) for source, target in forward]
        low = lax.ppermute(
            lax.slice_in_dim(block, block.shape[dim] - width, None, axis=dim), axis, forward
        )
        high = lax.ppermute(lax.slice_in_dim(block, 0, width, axis=dim), axis, backward)
        block = jnp.concatenate([low, block, high], axis=dim)
    return block


def phase_pair(count, offset, freqs, length):
    places = offset + jnp.arange(count, dtype=jnp.int32)
    turns = places[:, None] * freqs[None, :] % length
    angle = turns.astype(jnp.float32) * (2.0 * math.pi / length)
    return (jnp.cos(angle), jnp.sin(angle))


def centred(count):
    steps = jnp.arange(count, dtype=jnp.int32)
    return jnp.where(steps < count // 2, steps, steps - count)


def along(values, table, position):
    return jnp.moveaxis(
        jnp.tensordot(values, table, axes=((position,), (0,)), precision=HIGH), -1, position
    )


def forward_pair(pair, cosine, sine, position):
    real_part, imag_part = (pair[0], pair[1])
    where = position - 1
    out_real = along(real_part, cosine, where) + along(imag_part, sine, where)
    out_imag = along(imag_part, cosine, where) - along(real_part, sine, where)
    return jnp.stack([out_real, out_imag])


def inverse_pair(pair, cosine, sine, position):
    real_part, imag_part = (pair[0], pair[1])
    where = position - 1
    out_real = along(real_part, cosine.T, where) - along(imag_part, sine.T, where)
    out_imag = along(imag_part, cosine.T, where) + along(real_part, sine.T, where)
    return jnp.stack([out_real, out_imag])


def body(state, cotangent, spectral_weight, stencil_weight, pointwise_weight):
    wide_x = CX * lax.axis_size("gx")
    wide_y = CY * lax.axis_size("gy")
    alpha = 1.0 / math.sqrt(wide_x * wide_y * Z)
    beta = 1.0 / math.sqrt(2 * MX * MY * MZ)
    mz_dev = spectral_weight.shape[1]
    mx_dev = spectral_weight.shape[2]
    kz_global = lax.axis_index("gx") * mz_dev + jnp.arange(mz_dev, dtype=jnp.int32)
    doubling = jnp.where(kz_global == 0, 1.0, 2.0).astype(jnp.float32)[None, None, :, None, None]
    z_cos, z_sin = phase_pair(Z, 0, jnp.arange(MZ, dtype=jnp.int32), Z)
    x_freq = centred(MX)
    x_cos, x_sin = phase_pair(wide_x, 0, x_freq, wide_x)
    local_cos, local_sin = phase_pair(CX, lax.axis_index("gx") * CX, x_freq, wide_x)
    y_cos, y_sin = phase_pair(wide_y, 0, centred(MY), wide_y)

    def y_forward(block):
        return forward_pair(block, y_cos, y_sin, 4)

    def x_forward(block):
        return forward_pair(block, x_cos, x_sin, 3)

    def x_local_rows(piece):
        return inverse_pair(piece, local_cos, local_sin, 3)

    def to_modes(field):
        real_part = jnp.tensordot(field, z_cos, axes=((3,), (0,)), precision=HIGH)
        imag_part = -jnp.tensordot(field, z_sin, axes=((3,), (0,)), precision=HIGH)
        slab = jnp.moveaxis(jnp.stack([real_part, imag_part]), 4, 2)
        pencil = x_forward(lax.all_to_all(slab, "gx", split_axis=2, concat_axis=3, tiled=True))
        return y_forward(lax.all_to_all(pencil, "gy", split_axis=3, concat_axis=4, tiled=True))

    def to_field(modes):
        spread_y = inverse_pair(modes, y_cos, y_sin, 4)
        pencil = lax.all_to_all(spread_y, "gy", split_axis=4, concat_axis=3, tiled=True)
        slab = x_local_rows(lax.all_gather(pencil, "gx", axis=2, tiled=True))
        return jnp.tensordot(slab[0], z_cos, axes=((1,), (1,)), precision=HIGH) - jnp.tensordot(
            slab[1], z_sin, axes=((1,), (1,)), precision=HIGH
        )

    weights = spectral_weight.astype(jnp.float32).reshape(2, mz_dev, mx_dev, MY, C, C)

    def mix(pair):
        fwd = lambda a, b: jnp.einsum("czxy,zxyco->ozxy", a, b, precision=HIGH)
        return jnp.stack(
            [
                fwd(pair[0], weights[0]) - fwd(pair[1], weights[1]),
                fwd(pair[0], weights[1]) + fwd(pair[1], weights[0]),
            ]
        )

    def mix_back(pair):
        bwd = lambda a, b: jnp.einsum("ozxy,zxyco->czxy", a, b, precision=HIGH)
        return jnp.stack(
            [
                bwd(pair[0], weights[0]) + bwd(pair[1], weights[1]),
                bwd(pair[1], weights[0]) - bwd(pair[0], weights[1]),
            ]
        )

    modes_in = alpha * to_modes(state.astype(jnp.float32))
    mixed_modes = mix(modes_in)
    spectral = to_field(beta * doubling * mixed_modes)
    kernel = stencil_weight.reshape(C, C, 3, 3, 3)
    numbers = ("NCDHW", "OIDHW", "NCDHW")
    padded = with_halo(state, (("gx", 1), ("gy", 2)), 1)
    padded = jnp.pad(padded, ((0, 0), (0, 0), (0, 0), (1, 1)))
    stencil = lax.conv_general_dilated(
        padded[None],
        kernel,
        (1, 1, 1),
        "VALID",
        dimension_numbers=numbers,
        preferred_element_type=jnp.float32,
    )[0]
    flat_state = state.reshape(C, -1)
    point = jnp.dot(pointwise_weight, flat_state, preferred_element_type=jnp.float32).reshape(
        state.shape
    )
    pre = spectral + stencil + point
    activated, pull = jax.vjp(jax.nn.gelu, pre)
    output = activated.astype(jnp.bfloat16)
    grad_pre = pull(cotangent.astype(jnp.float32))[0].astype(jnp.bfloat16)
    back_modes = doubling * to_modes(grad_pre.astype(jnp.float32))
    outer = lambda a, b: jnp.einsum("czxy,ozxy->zxyco", a, b, precision=HIGH)
    grad_real = outer(modes_in[0], back_modes[0]) + outer(modes_in[1], back_modes[1])
    grad_imag = outer(modes_in[0], back_modes[1]) - outer(modes_in[1], back_modes[0])
    grad_modes = alpha * jnp.stack([grad_real, grad_imag]).reshape(2, mz_dev, mx_dev, MY, C * C)
    back_in = mix_back(beta * back_modes)
    flipped = jnp.transpose(kernel, (1, 0, 2, 3, 4))[:, :, ::-1, ::-1, ::-1]
    grad_rim = with_halo(grad_pre, (("gx", 1), ("gy", 2)), 1)
    grad_rim = jnp.pad(grad_rim, ((0, 0), (0, 0), (0, 0), (1, 1)))
    stencil_back = lax.conv_general_dilated(
        grad_rim[None],
        flipped,
        (1, 1, 1),
        "VALID",
        dimension_numbers=numbers,
        preferred_element_type=jnp.float32,
    )[0]
    flat_grad = grad_pre.reshape(C, -1)
    point_back = jnp.dot(pointwise_weight.T, flat_grad, preferred_element_type=jnp.float32).reshape(
        state.shape
    )
    grad_state = alpha * to_field(back_in) + stencil_back + point_back
    terms = []
    for shift_a in range(3):
        for shift_b in range(3):
            for shift_e in range(3):
                window = padded[
                    :, shift_a : shift_a + CX, shift_b : shift_b + CY, shift_e : shift_e + Z
                ].reshape(C, -1)
                terms.append(
                    lax.dot_general(
                        flat_grad,
                        window,
                        (((1,), (1,)), ((), ())),
                        preferred_element_type=jnp.float32,
                    )
                )
    stencil_local = jnp.stack(terms, axis=2).reshape(C, C * 27)
    point_local = lax.dot_general(
        flat_grad, flat_state, (((1,), (1,)), ((), ())), preferred_element_type=jnp.float32
    )
    stencil_total, point_total = lax.psum((stencil_local, point_local), ("gx", "gy"))
    return (output, grad_state, grad_modes, alpha * stencil_total, alpha * point_total)


def solution(mesh):
    in_specs = (
        P(None, "gx", "gy", None),
        P(None, "gx", "gy", None),
        P(None, "gx", "gy", None, None),
        P(),
        P(),
    )
    out_specs = (
        P(None, "gx", "gy", None),
        P(None, "gx", "gy", None),
        P(None, "gx", "gy", None, None),
        P(),
        P(),
    )
    return jax.shard_map(body, mesh=mesh, in_specs=in_specs, out_specs=out_specs, check_vma=False)
```

profile of v0, /device:TPU:0, one launch (start us, length us, event | category | flops | bytes accessed | tf_op | source)
XLA Modules:
  0.0 473.6 jit_solution(8404138764792168874)
XLA Ops:
  13.2 5.2 %all-to-all-start = ((f32[8,1,8192]{2,1,0:T(1,128)}), f32[8,1,8192]{2,1,0:T(1,128)S(1)}, u32[]{:S(2)}, u32[]{:S(2)}) async-start(f32[8,1,8192]{2,1,0:T(1,128)} %reshape.193), calls=%async_computation | async-start | bytes 524288 | tf_op jit(solution)/shard_map/all_to_all | solution.py:95
  18.4 6.9 %all-to-all-done = f32[8,1,8192]{2,1,0:T(1,128)S(1)} async-done(((f32[8,1,8192]{2,1,0:T(1,128)}), f32[8,1,8192]{2,1,0:T(1,128)S(1)}, u32[]{:S(2)}, u32[]{:S(2)}) %all-to-all-start) | async-done | bytes 262176 | tf_op jit(solution)/shard_map/all_to_all | solution.py:95
  30.9 4.9 %all-to-all-start.1 = ((f32[4,1,16384]{2,1,0:T(1,128)}), f32[4,1,16384]{2,1,0:T(1,128)S(1)}, u32[]{:S(2)}, u32[]{:S(2)}) async-start(f32[4,1,16384]{2,1,0:T(1,128)} %reshape.195), calls=%async_computation.1 | async-start | bytes 524288 | tf_op jit(solution)/shard_map/all_to_all | solution.py:96
  36.0 6.2 %fusion.471 = (bf16[1,2,8,32,4096]{4,3,2,1,0:T(8,128)(2,1)}, bf16[1,2,8,32,4096]{4,3,2,1,0:T(8,128)(2,1)}) fusion(bf16[2,2,8,32,4096]{4,3,2,1,0:T(8,128)(2,1)} %param.7), kind=kLoop, calls=%fused_computation.547 | loop fusion | bytes 16777216 | tf_op jit(solution)/shard_map/slice | solution.py:112
  42.1 12.6 %squeeze.101 = bf16[2,8,32,64,64]{4,3,2,1,0:T(8,128)(2,1)} reshape(bf16[1,2,8,32,4096]{4,3,2,1,0:T(8,128)(2,1)} %get-tuple-element.27) | data formatting | bytes 8388608 | tf_op jit(solution)/shard_map/squeeze | solution.py:112
  54.7 12.5 %squeeze.103 = bf16[2,8,32,64,64]{4,3,2,1,0:T(8,128)(2,1)} reshape(bf16[1,2,8,32,4096]{4,3,2,1,0:T(8,128)(2,1)} %get-tuple-element.28) | data formatting | bytes 8388608 | tf_op jit(solution)/shard_map/squeeze | solution.py:112
  72.5 10.1 %fusion.481 = f32[2,8,32,1,64]{4,3,2,1,0:T(1,128)S(1)} fusion(f32[64,2,8,32,1]{0,4,3,2,1:T(1,128)S(1)} %bitcast.714, bf16[2,8,32,64,64]{4,3,2,1,0:T(8,128)(2,1)} %squeeze.101), kind=kOutput, calls=%fused_computation.562 | convolution fusion | flops 25165824 | bytes 4456448 | tf_op jit(solution)/shard_map/czxy,zxyco->ozxy/dot_general | solution.py:109
  82.6 6.7 %fusion.478 = f32[2,8,32,1,64]{4,3,2,1,0:T(1,128)S(1)} fusion(f32[64,2,8,32,1]{0,4,3,2,1:T(1,128)S(1)} %bitcast.718, bf16[2,8,32,64,64]{4,3,2,1,0:T(8,128)(2,1)S(1)} %bitcast.665), kind=kOutput, calls=%fused_computation.559 | convolution fusion | flops 25165824 | bytes 4456448 | tf_op jit(solution)/shard_map/czxy,zxyco->ozxy/dot_general | solution.py:109
  89.3 7.2 %fusion.480 = f32[2,8,32,1,64]{4,3,2,1,0:T(1,128)S(1)} fusion(f32[64,2,8,32,1]{0,4,3,2,1:T(1,128)S(1)} %bitcast.719, bf16[2,8,32,64,64]{4,3,2,1,0:T(8,128)(2,1)S(1)} %bitcast.669), kind=kOutput, calls=%fused_computation.561 | convolution fusion | flops 25165824 | bytes 4456448 | tf_op jit(solution)/shard_map/czxy,zxyco->ozxy/dot_general | solution.py:109
  96.5 6.7 %fusion.479 = f32[2,8,32,1,64]{4,3,2,1,0:T(1,128)S(1)} fusion(f32[64,2,8,32,1]{0,4,3,2,1:T(1,128)S(1)} %bitcast.715, bf16[2,8,32,64,64]{4,3,2,1,0:T(8,128)(2,1)S(1)} %bitcast.669), kind=kOutput, calls=%fused_computation.560 | convolution fusion | flops 25165824 | bytes 4456448 | tf_op jit(solution)/shard_map/czxy,zxyco->ozxy/dot_general | solution.py:109
  105.9 12.7 %all_to_all.96 = f32[4,1,16384]{2,1,0:T(1,128)S(1)} all-to-all(f32[4,1,16384]{2,1,0:T(1,128)S(1)} %reshape.197), channel_id=1, replica_groups=mesh['gx'=8,'gy'=4] {'gy'}, dimensions={0} | all-to-all | bytes 524288 | tf_op jit(solution)/shard_map/all_to_all | solution.py:100
  135.0 4.3 collective-permute-done.3
  149.7 8.6 %fusion.40 = f32[4,8,8,17,64]{4,2,3,1,0:T(8,128)S(1)} fusion(bf16[64,64,3,3,3]{1,0,4,3,2:T(8,128)(2,1)S(1)} %copy.361, bf16[64,6,10,1,7,2]{0,4,5,2,1,3:T(8,128)(2,1)S(1)} %slice.289, bf16[64,6,10,1,8,17]{0,4,5,2,1,3:T(8,128)(2,1)S(1)} %copy.359, pred[8,17]{0,1:T(8,128)(4,1)S(1)} %copy-done.31), kind=kOutput, calls=%fused_computation.51 | convolution fusion | flops 966373376 | bytes 2487432 | tf_op jit(solution)/shard_map/conv_general_dilated | solution.py:133
  161.0 3.5 fusion.36
  178.5 4.6 fusion.100
  217.1 6.0 %all-to-all-start.3 = ((f32[8,1,8192]{2,1,0:T(1,128)}), f32[8,1,8192]{2,1,0:T(1,128)S(1)}, u32[]{:S(2)}, u32[]{:S(2)}) async-start(f32[8,1,8192]{2,1,0:T(1,128)} %reshape.199), calls=%async_computation.3 | async-start | bytes 524288 | tf_op jit(solution)/shard_map/all_to_all | solution.py:95
  235.5 3.9 all-to-all-start.4
  240.9 41.4 %psum.15 = f32[64,64]{1,0:T(8,128)S(1)} all-reduce(f32[64,64]{1,0:T(8,128)S(1)} %bitcast.726), channel_id=1, replica_groups=mesh['gx'=8,'gy'=4] {'gx','gy'}, use_global_device_ids=true, to_apply=%region_1.2 | all-reduce | flops 4096 | bytes 32768 | tf_op jit(solution)/shard_map/psum | solution.py:190
  293.8 16.3 %fusion.482 = f32[2,8,32,1,64]{4,3,2,1,0:T(1,128)S(1)} fusion(f32[64,2,8,32,1]{0,4,3,2,1:T(1,128)S(1)} %bitcast.724, bf16[2,8,32,64,64]{4,3,2,1,0:T(8,128)(2,1)} %squeeze.101), kind=kOutput, calls=%fused_computation.563 | convolution fusion | flops 25165824 | bytes 4456448 | tf_op jit(solution)/shard_map/ozxy,zxyco->czxy/dot_general | solution.py:118
  310.1 16.0 %fusion.485 = f32[2,8,32,1,64]{4,3,2,1,0:T(1,128)S(1)} fusion(f32[64,2,8,32,1]{0,4,3,2,1:T(1,128)S(1)} %bitcast.725, bf16[2,8,32,64,64]{4,3,2,1,0:T(8,128)(2,1)} %squeeze.103), kind=kOutput, calls=%fused_computation.566 | convolution fusion | flops 25165824 | bytes 4456448 | tf_op jit(solution)/shard_map/ozxy,zxyco->czxy/dot_general | solution.py:118
  326.2 13.1 %fusion.484 = f32[2,8,32,1,64]{4,3,2,1,0:T(1,128)S(1)} fusion(f32[64,2,8,32,1]{0,4,3,2,1:T(1,128)S(1)} %bitcast.716, bf16[2,8,32,64,64]{4,3,2,1,0:T(8,128)(2,1)S(1)} %bitcast.667), kind=kOutput, calls=%fused_computation.565 | convolution fusion | flops 25165824 | bytes 4456448 | tf_op jit(solution)/shard_map/ozxy,zxyco->czxy/dot_general | solution.py:118
  339.3 13.3 %fusion.483 = f32[2,8,32,1,64]{4,3,2,1,0:T(1,128)S(1)} fusion(f32[64,2,8,32,1]{0,4,3,2,1:T(1,128)S(1)} %bitcast.717, bf16[2,8,32,64,64]{4,3,2,1,0:T(8,128)(2,1)S(1)} %bitcast.671), kind=kOutput, calls=%fused_computation.564 | convolution fusion | flops 25165824 | bytes 4456448 | tf_op jit(solution)/shard_map/ozxy,zxyco->czxy/dot_general | solution.py:118
  355.8 4.7 all-to-all-start.5
  363.6 4.0 all-to-all-done.5
  370.5 6.1 %fusion.4 = bf16[64,6,10,1,130]{4,2,1,0,3:T(8,128)(2,1)} fusion(bf16[64,6,1,128]{3,2,1,0:T(2,128)(2,1)S(1)} %collective-permute-done.7, bf16[64,6,1,128]{3,2,1,0:T(2,128)(2,1)S(1)} %collective-permute-done.6, bf16[64,1,8,128]{3,2,1,0:T(8,128)(2,1)} %collective-permute-done.5, bf16[64,4,8,128]{3,2,1,0:T(8,128)(2,1)S(1)} %get-tuple-element.31, ...), kind=kLoop, calls=%fused_computation.13 | loop fusion | flops 8985600 | bytes 1981440 | tf_op jit(solution)/shard_map/broadcast_in_dim | solution.py:159
  376.6 5.1 %copy.507 = bf16[64,6,10,1,130]{0,4,2,1,3:T(8,128)(2,1)S(1)} copy(bf16[64,6,10,1,130]{4,2,1,0,3:T(8,128)(2,1)} %fusion.4) | data formatting | bytes 1996800
  383.4 3.6 reshape.116
  388.1 4.5 fusion.37
  395.4 12.6 %multiply_add_fusion = (f32[2,8,32,64,64]{4,3,2,1,0:T(8,128)}, f32[2,8,32,64,64]{4,3,2,1,0:T(8,128)}) fusion(f32[2,8,32,64]{3,2,1,0:T(8,128)S(1)} %get-tuple-element.42, f32[2,8,32,64]{3,2,1,0:T(8,128)} %get-tuple-element.38, f32[2,8,32,64]{3,2,1,0:T(8,128)S(1)} %get-tuple-element.41, f32[2,8,32,64]{3,2,1,0:T(8,128)S(1)} %copy-done.11), kind=kLoop, calls=%fused_computation.2 | loop fusion | flops 12582912 | bytes 17301504 | tf_op jit(solution)/shard_map/add | solution.py:151
  408.1 14.7 %stack.201 = f32[1,2,8,32,4096]{4,3,2,1,0:T(8,128)} reshape(f32[2,8,32,64,64]{4,3,2,1,0:T(8,128)} %get-tuple-element.29) | data formatting | bytes 16777216 | tf_op jit(solution)/shard_map/stack | solution.py:153
  422.8 15.0 %stack.202 = f32[1,2,8,32,4096]{4,3,2,1,0:T(8,128)} reshape(f32[2,8,32,64,64]{4,3,2,1,0:T(8,128)} %get-tuple-element.30) | data formatting | bytes 16777216 | tf_op jit(solution)/shard_map/stack | solution.py:153
  437.8 12.0 %maximum_multiply_fusion = f32[2,2,8,32,4096]{4,3,2,1,0:T(8,128)} fusion(f32[1,2,8,32,4096]{4,3,2,1,0:T(8,128)} %stack.202, f32[1,2,8,32,4096]{4,3,2,1,0:T(8,128)} %stack.201), kind=kLoop, calls=%fused_computation | loop fusion | flops 8388608 | bytes 33554432 | tf_op jit(solution)/shard_map/mul | solution.py:153
  (272 shorter events, 153.5 us)
Async XLA Ops:
  7.2 119.3 %copy-start = (bf16[64,64]{1,0:T(8,128)(2,1)S(1)}, bf16[64,64]{1,0:T(8,128)(2,1)}, u32[]{:S(2)}) copy-start(bf16[64,64]{1,0:T(8,128)(2,1)} %param.9) | copy-start | bytes 24580
  13.2 12.1 %all-to-all-start = ((f32[8,1,8192]{2,1,0:T(1,128)}), f32[8,1,8192]{2,1,0:T(1,128)S(1)}, u32[]{:S(2)}, u32[]{:S(2)}) async-start(f32[8,1,8192]{2,1,0:T(1,128)} %reshape.193), calls=%async_computation | async-start | bytes 524288 | tf_op jit(solution)/shard_map/all_to_all | solution.py:95
  18.4 157.8 %copy-start.13 = (s32[32]{0:T(128)}, s32[32]{0:T(128)S(1)}, u32[]{:S(2)}) copy-start(s32[32]{0:T(128)S(1)} %compare_select_fusion) | copy-start | bytes 388
  30.9 36.9 %all-to-all-start.1 = ((f32[4,1,16384]{2,1,0:T(1,128)}), f32[4,1,16384]{2,1,0:T(1,128)S(1)}, u32[]{:S(2)}, u32[]{:S(2)}) async-start(f32[4,1,16384]{2,1,0:T(1,128)} %reshape.195), calls=%async_computation.1 | async-start | bytes 524288 | tf_op jit(solution)/shard_map/all_to_all | solution.py:96
  35.8 128.6 %all-gather.3.cloned.1.call-start = ((), (), s32[]{:S(2)}) async-start(), calls=%async_computation.6 | async-start | bytes 4718592 | tf_op jit(solution)/shard_map/all_gather | solution.py:101
  71.5 11.1 %slice-start = ((s8[8388608]{0:T(1024)(128)(4,1)}), s8[4194304]{0:T(1024)(128)(4,1)S(1)}, s32[]{:S(2)}) async-start(s8[8388608]{0:T(1024)(128)(4,1)} %bitcast.664), calls=%async_computation.9 | async-start | bytes 8388608
  72.5 16.8 %slice-start.4 = ((s8[8388608]{0:T(1024)(128)(4,1)}), s8[4194304]{0:T(1024)(128)(4,1)S(1)}, s32[]{:S(2)}) async-start(s8[8388608]{0:T(1024)(128)(4,1)} %bitcast.668), calls=%async_computation.13 | async-start | bytes 8388608
  105.3 16.2 %copy-start.4 = (bf16[64,4,8,128]{3,2,1,0:T(8,128)(2,1)S(1)}, bf16[64,4,8,128]{3,2,1,0:T(8,128)(2,1)}, u32[]{:S(2)}) copy-start(bf16[64,4,8,128]{3,2,1,0:T(8,128)(2,1)} %param.5) | copy-start | bytes 1572868
  121.8 7.7 %collective-permute-start.1 = (bf16[64,1,8,128]{3,0,2,1:T(8,128)(2,1)S(1)}, bf16[64,1,8,128]{3,0,2,1:T(8,128)(2,1)S(1)}, u32[]{:S(2)}, u32[]{:S(2)}) collective-permute-start(bf16[64,1,8,128]{3,0,2,1:T(8,128)(2,1)S(1)} %get-tuple-element.49), channel_id=1, source_target_pairs={{4,0},{8,4},{12,8},{16,12},{20,16},{24,20},{28,24},{5,1},{9,5},{13... | collective-permute-start | bytes 393224 | tf_op jit(solution)/shard_map/ppermute | solution.py:28
  123.1 6.1 %collective-permute-start = (bf16[64,1,8,128]{3,0,2,1:T(8,128)(2,1)S(1)}, bf16[64,1,8,128]{3,0,2,1:T(8,128)(2,1)S(1)}, u32[]{:S(2)}, u32[]{:S(2)}) collective-permute-start(bf16[64,1,8,128]{3,0,2,1:T(8,128)(2,1)S(1)} %get-tuple-element.50), channel_id=1, source_target_pairs={{0,4},{4,8},{8,12},{12,16},{16,20},{20,24},{24,28},{1,5},{5,9},{9,... | collective-permute-start | bytes 393224 | tf_op jit(solution)/shard_map/ppermute | solution.py:25
  129.2 20.5 %copy-start.16 = (bf16[64,64,3,3,3]{1,0,4,3,2:T(8,128)(2,1)}, bf16[64,64,3,3,3]{1,0,4,3,2:T(8,128)(2,1)S(1)}, u32[]{:S(2)}) copy-start(bf16[64,64,3,3,3]{1,0,4,3,2:T(8,128)(2,1)S(1)} %copy.361) | copy-start | bytes 663556
  129.6 5.4 %collective-permute-start.2 = (bf16[64,6,1,128]{3,0,2,1:T(8,128)(2,1)S(1)}, bf16[64,6,1,128]{3,0,2,1:T(8,128)(2,1)S(1)}, u32[]{:S(2)}, u32[]{:S(2)}) collective-permute-start(bf16[64,6,1,128]{3,0,2,1:T(8,128)(2,1)S(1)} %get-tuple-element.35), channel_id=1, source_target_pairs={{0,1},{1,2},{2,3},{4,5},{5,6},{6,7},{8,9},{9,10},{10,11},{12,13},{... | collective-permute-start | bytes 294920 | tf_op jit(solution)/shard_map/ppermute | solution.py:25
  131.9 7.4 %collective-permute-start.3 = (bf16[64,6,1,128]{3,0,2,1:T(8,128)(2,1)S(1)}, bf16[64,6,1,128]{3,0,2,1:T(8,128)(2,1)S(1)}, u32[]{:S(2)}, u32[]{:S(2)}) collective-permute-start(bf16[64,6,1,128]{3,0,2,1:T(8,128)(2,1)S(1)} %get-tuple-element.36), channel_id=1, source_target_pairs={{1,0},{2,1},{3,2},{5,4},{6,5},{7,6},{9,8},{10,9},{11,10},{13,12},{... | collective-permute-start | bytes 294920 | tf_op jit(solution)/shard_map/ppermute | solution.py:28
  133.2 43.0 %copy-start.28 = (s32[4]{0:T(128)}, s32[4]{0:T(128)S(1)}, u32[]{:S(2)}) copy-start(s32[4]{0:T(128)S(1)} %iota_add_fusion) | copy-start | bytes 52
  135.0 26.0 %copy-start.20 = (bf16[64,6,1,128]{3,0,2,1:T(8,128)(2,1)}, bf16[64,6,1,128]{3,0,2,1:T(8,128)(2,1)S(1)}, u32[]{:S(2)}) copy-start(bf16[64,6,1,128]{3,0,2,1:T(8,128)(2,1)S(1)} %collective-permute-done.2) | copy-start | bytes 294916
  139.3 21.7 %copy-start.18 = (bf16[64,6,1,128]{3,0,2,1:T(8,128)(2,1)}, bf16[64,6,1,128]{3,0,2,1:T(8,128)(2,1)S(1)}, u32[]{:S(2)}) copy-start(bf16[64,6,1,128]{3,0,2,1:T(8,128)(2,1)S(1)} %collective-permute-done.3) | copy-start | bytes 294916
  185.1 97.9 %collective-permute-start.4 = (bf16[64,1,8,128]{3,2,1,0:T(8,128)(2,1)}, bf16[64,1,8,128]{3,2,1,0:T(8,128)(2,1)S(1)}, u32[]{:S(2)}, u32[]{:S(2)}) collective-permute-start(bf16[64,1,8,128]{3,2,1,0:T(8,128)(2,1)} %get-tuple-element.43), channel_id=1, source_target_pairs={{0,4},{4,8},{8,12},{12,16},{16,20},{20,24},{24,28},{1,5},{5,9},{9,... | collective-permute-start | bytes 393224 | tf_op jit(solution)/shard_map/ppermute | solution.py:25
  187.0 95.9 %collective-permute-start.5 = (bf16[64,1,8,128]{3,2,1,0:T(8,128)(2,1)}, bf16[64,1,8,128]{3,2,1,0:T(8,128)(2,1)}, u32[]{:S(2)}, u32[]{:S(2)}) collective-permute-start(bf16[64,1,8,128]{3,2,1,0:T(8,128)(2,1)} %get-tuple-element.44), channel_id=1, source_target_pairs={{4,0},{8,4},{12,8},{16,12},{20,16},{24,20},{28,24},{5,1},{9,5},{13... | collective-permute-start | bytes 393224 | tf_op jit(solution)/shard_map/ppermute | solution.py:28
  217.1 13.3 %all-to-all-start.3 = ((f32[8,1,8192]{2,1,0:T(1,128)}), f32[8,1,8192]{2,1,0:T(1,128)S(1)}, u32[]{:S(2)}, u32[]{:S(2)}) async-start(f32[8,1,8192]{2,1,0:T(1,128)} %reshape.199), calls=%async_computation.3 | async-start | bytes 524288 | tf_op jit(solution)/shard_map/all_to_all | solution.py:95
  223.1 138.3 %all-reduce.4.cloned.1.call-start = ((), (), s32[]{:S(2)}) async-start(), calls=%async_computation.8 | async-start | bytes 1769472 | tf_op jit(solution)/shard_map/psum | solution.py:190
  235.5 53.5 %all-to-all-start.4 = ((f32[4,1,16384]{2,1,0:T(1,128)}), f32[4,1,16384]{2,1,0:T(1,128)S(1)}, u32[]{:S(2)}, u32[]{:S(2)}) async-start(f32[4,1,16384]{2,1,0:T(1,128)} %reshape.201), calls=%async_computation.4 | async-start | bytes 524288 | tf_op jit(solution)/shard_map/all_to_all | solution.py:96
  240.9 51.9 %copy-start.30 = (f32[2]{0:T(128)S(1)}, f32[2]{0:T(128)}, u32[]{:S(2)}) copy-start(f32[2]{0:T(128)} %get-tuple-element.55) | copy-start | bytes 28
  284.2 86.3 %collective-permute-start.6 = (bf16[64,6,1,128]{3,2,1,0:T(2,128)(2,1)S(1)}, bf16[64,6,1,128]{3,2,1,0:T(2,128)(2,1)S(1)}, u32[]{:S(2)}, u32[]{:S(2)}) collective-permute-start(bf16[64,6,1,128]{3,2,1,0:T(2,128)(2,1)S(1)} %get-tuple-element.33), channel_id=1, source_target_pairs={{0,1},{1,2},{2,3},{4,5},{5,6},{6,7},{8,9},{9,10},{10,11},{12,13},{... | collective-permute-start | bytes 294920 | tf_op jit(solution)/shard_map/ppermute | solution.py:25
  287.6 82.9 %collective-permute-start.7 = (bf16[64,6,1,128]{3,2,1,0:T(2,128)(2,1)S(1)}, bf16[64,6,1,128]{3,2,1,0:T(2,128)(2,1)S(1)}, u32[]{:S(2)}, u32[]{:S(2)}) collective-permute-start(bf16[64,6,1,128]{3,2,1,0:T(2,128)(2,1)S(1)} %get-tuple-element.34), channel_id=1, source_target_pairs={{1,0},{2,1},{3,2},{5,4},{6,5},{7,6},{9,8},{10,9},{11,10},{13,12},{... | collective-permute-start | bytes 294920 | tf_op jit(solution)/shard_map/ppermute | solution.py:28
  293.8 32.4 %slice-start.2 = ((s8[8388608]{0:T(1024)(128)(4,1)}), s8[4194304]{0:T(1024)(128)(4,1)S(1)}, s32[]{:S(2)}) async-start(s8[8388608]{0:T(1024)(128)(4,1)} %bitcast.666), calls=%async_computation.11 | async-start | bytes 8388608
  293.8 45.5 %slice-start.6 = ((s8[8388608]{0:T(1024)(128)(4,1)}), s8[4194304]{0:T(1024)(128)(4,1)S(1)}, s32[]{:S(2)}) async-start(s8[8388608]{0:T(1024)(128)(4,1)} %bitcast.670), calls=%async_computation.15 | async-start | bytes 8388608
  310.1 16.0 %slice-start.3 = ((s8[8388608]{0:T(1024)(128)(4,1)}), s8[4194304]{0:T(1024)(128)(4,1)S(1)}, s32[]{:S(2)}) async-start(s8[8388608]{0:T(1024)(128)(4,1)} %bitcast.666), calls=%async_computation.12 | async-start | bytes 8388608
  310.1 29.1 %slice-start.7 = ((s8[8388608]{0:T(1024)(128)(4,1)}), s8[4194304]{0:T(1024)(128)(4,1)S(1)}, s32[]{:S(2)}) async-start(s8[8388608]{0:T(1024)(128)(4,1)} %bitcast.670), calls=%async_computation.16 | async-start | bytes 8388608
  355.8 11.8 %all-to-all-start.5 = ((f32[4,1,16384]{2,1,0:T(1,128)}), f32[4,1,16384]{2,1,0:T(1,128)S(1)}, u32[]{:S(2)}, u32[]{:S(2)}) async-start(f32[4,1,16384]{2,1,0:T(1,128)} %reshape.203), calls=%async_computation.5 | async-start | bytes 524288 | tf_op jit(solution)/shard_map/all_to_all | solution.py:100
  360.5 89.2 %all-gather.5.cloned.1.call-start = ((), (), s32[]{:S(2)}) async-start(), calls=%async_computation.7 | async-start | bytes 4718592 | tf_op jit(solution)/shard_map/all_gather | solution.py:101
  437.8 12.0 %copy-start.15 = (s32[32]{0:T(128)S(1)}, s32[32]{0:T(128)}, u32[]{:S(2)}) copy-start(s32[32]{0:T(128)} %copy-done.13) | copy-start | bytes 388
  437.8 12.0 %copy-start.29 = (s32[4]{0:T(128)S(1)}, s32[4]{0:T(128)}, u32[]{:S(2)}) copy-start(s32[4]{0:T(128)} %copy-done.28) | copy-start | bytes 52
  (25 other events, 131.9 us)
Sparse Core Ops, SparseCore 0:
  121.6 34.5 all-gather.2
  230.5 130.7 all-reduce.3
  370.6 36.2 all-gather.4
where the time goes:
time: 481 us; the launch traced here: 474 us
  matrix products  181 us (38%)
  local copies, waits for them, and re-layouts  115 us (24%)
  blocking collectives  54.1 us (11%)
  other arithmetic  48.4 us (10%)
  starting transfers between devices  41.5 us (9%)
  waiting for transfers between devices  17.8 us (4%)
  between operations  15.3 us (3%)
    dot_general x4, matrix products, mix_back(): bwd = lambda a, b: jnp.einsum('ozxy,zxyco->czxy', a, b, precision=HIGH)  58.7 us
    psum x1, blocking collectives, body(): lax.psum((stencil_local, point_local), ('gx', 'gy'))  41.4 us
    dot_general x32, matrix products, along(): jnp.tensordot(values, table, axes=((position,), (0,)), precision=HIGH)  31.4 us
    dot_general x4, matrix products, mix(): fwd = lambda a, b: jnp.einsum('czxy,zxyco->ozxy', a, b, precision=HIGH)  30.6 us
    another operation x2, local copies, waits for them, and re-layouts, body(): jnp.stack([grad_real, grad_imag]).reshape(2, mz_dev, mx_dev, MY, C * C)  29.7 us
    dot_general x27, matrix products, body(): lax.dot_general(flat_grad, window, (((1,), (1,)), ((), ())), preferred_el...  28 us
    unnamed x106, local copies, waits for them, and re-layouts  23 us
    all_to_all x1, blocking collectives, to_field(): lax.all_to_all(spread_y, 'gy', split_axis=4, concat_axis=3, tiled=True)  12.7 us
  transfers between devices with their start and end apart: 16, of which 5 were waited for; matrix products, arithmetic and copies ran while one was open for 54% of the time, Pallas kernels for 0%

commit v1 on v0

v1 whole, which is shorter than its diff:
```python
import functools
import math

import jax
import jax.numpy as jnp
import numpy as np
from jax import lax
from jax.experimental import pallas as pl
from jax.experimental.pallas import tpu as pltpu
from jax.sharding import PartitionSpec as P

C = 64
MX = 32
MY = 32
MZ = 16
Z = 128
MIB = 1 << 20

F32 = jnp.float32
BF16 = jnp.bfloat16


def angles(places, freqs, length):
    turns = np.outer(np.asarray(places), np.asarray(freqs)) % length
    return turns * (2.0 * np.pi / length)


def centred(count):
    steps = np.arange(count)
    return np.where(steps < count // 2, steps, steps - count)


def split(table, parts):
    rest = np.asarray(table, np.float64)
    out = []
    for _ in range(parts):
        piece = rest.astype(jnp.bfloat16)
        out.append(piece)
        rest = rest - piece.astype(np.float64)
    return out


def z_forward_table(scale):
    def build(nx, mz):
        theta = angles(np.arange(MZ), np.arange(Z), Z)
        pair = np.stack([np.cos(theta), -np.sin(theta)]) * scale[None, :, None]
        rows = pair.reshape(2, nx, mz, Z).transpose(1, 0, 2, 3).reshape(2 * MZ, Z)
        return np.concatenate(split(rows, 3), axis=0)

    return build


def z_inverse_table(nx, mz, scale):
    theta = angles(np.arange(MZ), np.arange(Z), Z)
    pair = np.stack([np.cos(theta), -np.sin(theta)]) * scale[None, :, None]
    rows = pair.reshape(2, nx, mz, Z).transpose(1, 0, 2, 3).reshape(2 * MZ, Z)
    high, low = split(rows, 2)
    return np.concatenate([high, high, low], axis=0)


def rotation(theta, sign):
    cosine, sine = np.cos(theta), sign * np.sin(theta)
    return np.stack([np.stack([cosine, -sine], 1), np.stack([sine, cosine], 1)])


def x_tables(wide, mz):
    theta = angles(centred(MX), np.arange(wide), wide)
    eye = np.eye(mz)
    forward = np.einsum("rkRx,zZ->krzxRZ", rotation(theta, -1.0), eye)
    inverse = np.einsum("rxRk,zZ->xrzkRZ", rotation(theta.T, 1.0), eye)
    size_k, size_x = MX * 2 * mz, wide * 2 * mz
    return (
        forward.reshape(size_k, size_x).astype(np.float32),
        inverse.reshape(size_x, size_k).astype(np.float32),
    )


def y_tables(wide):
    theta = angles(centred(MY), np.arange(wide), wide)
    forward = rotation(theta, -1.0).reshape(2 * MY, 2 * wide)
    inverse = rotation(theta.T, 1.0).reshape(2 * wide, 2 * MY)
    out = []
    for table in (forward, inverse):
        high, low = split(table, 2)
        out.append(np.concatenate([high, high, low], axis=1))
    return out


def pieces(values):
    high = values.astype(BF16)
    low = (values - high.astype(F32)).astype(BF16)
    return jnp.concatenate([high, low, high], axis=0)


def z_forward(rows, table, out_ref, x, nx):
    got = lax.dot_general(table, rows, (((1,), (1,)), ((), ())), preferred_element_type=F32)
    size = 2 * MZ
    total = got[:size] + (got[size : 2 * size] + got[2 * size :])
    per = size // nx
    for owner in range(nx):
        out_ref[owner, x * per : (x + 1) * per, :] = total[owner * per : (owner + 1) * per]


def z_inverse(in_ref, table, x, nx):
    per = 2 * MZ // nx
    rows = jnp.concatenate(
        [in_ref[owner, x * per : (x + 1) * per, :] for owner in range(nx)], axis=0
    )
    return lax.dot_general(
        pieces(rows), table, (((0,), (0,)), ((), ())), preferred_element_type=F32
    )


def prep_kernel(nx, field_ref, table_ref, turned_ref, slab_ref):
    c, cx, cy, z = field_ref.shape
    for x in range(cx):
        block = jnp.swapaxes(field_ref[:, x].astype(F32), 0, 1)
        turned = block.astype(BF16)
        turned_ref[x] = turned
        z_forward(turned.reshape(cy * c, z), table_ref[...], slab_ref, x, nx)


def plane_rows(p, cx, body_ref, xlo_ref, xhi_ref, ylo_ref, yhi_ref):
    cy = body_ref.shape[1]
    if p == 0:
        middle = [xlo_ref[y] for y in range(cy)]
    elif p == cx + 1:
        middle = [xhi_ref[y] for y in range(cy)]
    else:
        middle = [body_ref[p - 1, y] for y in range(cy)]
    return [ylo_ref[p]] + middle + [yhi_ref[p]]


def fill_shifts(blocks, rim_ref):
    c, z = blocks[0].shape
    lane = lax.broadcasted_iota(jnp.int32, (c, z), 1)
    for y, block in enumerate(blocks):
        wide = block.astype(F32)
        before = jnp.where(lane == 0, 0.0, pltpu.roll(wide, 1, 1))
        after = jnp.where(lane == z - 1, 0.0, pltpu.roll(wide, z - 1, 1))
        columns = slice(y * z, (y + 1) * z)
        rim_ref[0:c, columns] = before.astype(BF16)
        rim_ref[c : 2 * c, columns] = block
        rim_ref[2 * c : 3 * c, columns] = after.astype(BF16)
        rim_ref[3 * c : 4 * c, columns] = block


def conv_kernel(body_ref, xlo_ref, xhi_ref, ylo_ref, yhi_ref, weight_ref, out_ref, rim_ref):
    cx, cy, c, z = body_ref.shape
    for p in range(cx + 2):
        fill_shifts(plane_rows(p, cx, body_ref, xlo_ref, xhi_ref, ylo_ref, yhi_ref), rim_ref)
        first, last = max(0, p - cx + 1), min(2, p)
        got = jnp.dot(
            weight_ref[first * 3 * c : (last + 1) * 3 * c, :],
            rim_ref[...],
            preferred_element_type=F32,
        )
        for a in range(first, last + 1):
            total = None
            for b in range(3):
                row = ((a - first) * 3 + b) * c
                term = got[row : row + c, b * z : (b + cy) * z]
                total = term if total is None else total + term
            if a == 0:
                out_ref[p - a] = total
            else:
                out_ref[p - a] += total


def weight_grad_kernel(
    grad_ref, body_ref, xlo_ref, xhi_ref, ylo_ref, yhi_ref, out_ref, rim_ref, wide_ref
):
    cx, cy, c, z = body_ref.shape
    group = 3 * c
    wide_ref[...] = jnp.zeros_like(wide_ref)
    for x in range(cx):
        for b in range(3):
            for y in range(cy):
                row = x * group + b * c
                wide_ref[row : row + c, (y + b) * z : (y + b + 1) * z] = grad_ref[x, y]
    out_ref[...] = jnp.zeros_like(out_ref)
    for p in range(cx + 2):
        fill_shifts(plane_rows(p, cx, body_ref, xlo_ref, xhi_ref, ylo_ref, yhi_ref), rim_ref)
        first, last = max(0, p - 2), min(cx - 1, p)
        got = lax.dot_general(
            wide_ref[first * group : (last + 1) * group, :],
            rim_ref[...],
            (((1,), (1,)), ((), ())),
            preferred_element_type=F32,
        )
        for x in range(first, last + 1):
            a = p - x
            out_ref[a * group : (a + 1) * group, :] += got[
                (x - first) * group : (x - first + 1) * group, : 3 * c
            ]


def gelu_kernel(
    nx, stencil_ref, slab_ref, cot_ref, inverse_ref, forward_ref, out_ref, turned_ref, back_ref
):
    c, cx, cy, z = cot_ref.shape
    root = math.sqrt(2.0 / math.pi)
    for x in range(cx):
        spectral = z_inverse(slab_ref, inverse_ref[...], x, nx).reshape(cy, c, z)
        stencil = jnp.stack([stencil_ref[x, :, y * z : (y + 1) * z] for y in range(cy)])
        pre = spectral + stencil
        cot = jnp.swapaxes(cot_ref[:, x].astype(F32), 0, 1)
        square = pre * pre
        bent = jnp.tanh(root * (pre * (1.0 + 0.044715 * square)))
        half = 0.5 + 0.5 * bent
        slope = half + (0.5 * pre) * (1.0 - bent * bent) * (root * (1.0 + 0.134145 * square))
        out_ref[:, x] = jnp.swapaxes(pre * half, 0, 1).astype(BF16)
        grad = (cot * slope).astype(BF16)
        turned_ref[x] = grad
        z_forward(grad.reshape(cy * c, z), forward_ref[...], back_ref, x, nx)


def finish_kernel(nx, stencil_ref, slab_ref, inverse_ref, out_ref):
    c, cx, cy, z = out_ref.shape
    for x in range(cx):
        spectral = z_inverse(slab_ref, inverse_ref[...], x, nx).reshape(cy, c, z)
        stencil = jnp.stack([stencil_ref[x, :, y * z : (y + 1) * z] for y in range(cy)])
        out_ref[:, x] = jnp.swapaxes(spectral + stencil, 0, 1)


def y_forward(data_ref, table_ref, modes_ref):
    got = jnp.dot(table_ref[...], pieces(data_ref[...]), preferred_element_type=F32)
    for q in range(modes_ref.shape[0]):
        block = got[:, q * C : (q + 1) * C]
        modes_ref[q] = jnp.concatenate([block[:MY], block[MY:]], axis=1)


def y_inverse(modes_ref, table_ref, out_ref):
    count = modes_ref.shape[0]
    real = jnp.concatenate([modes_ref[q, :, :C] for q in range(count)], axis=1)
    imag = jnp.concatenate([modes_ref[q, :, C:] for q in range(count)], axis=1)
    out_ref[...] = jnp.dot(
        table_ref[...], pieces(jnp.concatenate([real, imag], axis=0)), preferred_element_type=F32
    )


def pick(values, lanes):
    return jnp.take_along_axis(values, lanes, axis=1)


def mix_kernel(data_ref, weight_ref, forward_ref, inverse_ref, modes_ref, out_ref, mixed_ref):
    q = pl.program_id(0)

    @pl.when(q == 0)
    def _():
        y_forward(data_ref, forward_ref, modes_ref)

    rows = 16
    lane = lax.broadcasted_iota(jnp.int32, (rows, 2 * C), 1)
    pair = jnp.where(lane < C, 0, 1)
    for start in range(0, MY, rows):
        here = slice(start, start + rows)
        modes = modes_ref[q, here, :]
        real = jnp.zeros((rows, 2 * C), F32)
        imag = jnp.zeros((rows, 2 * C), F32)
        for t in range(C // 2):
            mode_re = pick(modes, pair + 2 * t)
            mode_im = pick(modes, pair + (2 * t + C))
            columns = slice(t * 2 * C, (t + 1) * 2 * C)
            weight_re = weight_ref[0, 0, 0, here, columns].astype(F32)
            weight_im = weight_ref[1, 0, 0, here, columns].astype(F32)
            real += mode_re * weight_re - mode_im * weight_im
            imag += mode_re * weight_im + mode_im * weight_re
        mixed_ref[q, here, :] = jnp.concatenate(
            [real[:, :C] + real[:, C:], imag[:, :C] + imag[:, C:]], axis=1
        )

    @pl.when(q == pl.num_programs(0) - 1)
    def _():
        y_inverse(mixed_ref, inverse_ref, out_ref)


def twice(half):
    return jnp.concatenate([half, half], axis=1)


def mix_back_kernel(data_ref, weight_ref, forward_ref, inverse_ref, modes_ref, out_ref, mixed_ref):
    q = pl.program_id(0)

    @pl.when(q == 0)
    def _():
        y_forward(data_ref, forward_ref, modes_ref)

    rows = 16
    lane = lax.broadcasted_iota(jnp.int32, (rows, 2 * C), 1)
    channel = lane % C
    order = C * (channel % 2) + 2 * (channel // 2) + jnp.where(lane < C, 0, 1)

    def merge(shift, low, high):
        return jnp.where(
            lane & shift == 0,
            low + pltpu.roll(low, 2 * C - shift, 1),
            high + pltpu.roll(high, shift, 1),
        )

    for start in range(0, MY, rows):
        here = slice(start, start + rows)
        modes = modes_ref[q, here, :]
        mode_re = twice(modes[:, :C])
        mode_im = twice(modes[:, C:])

        def products(t):
            columns = slice(t * 2 * C, (t + 1) * 2 * C)
            weight_re = weight_ref[0, 0, 0, here, columns].astype(F32)
            weight_im = weight_ref[1, 0, 0, here, columns].astype(F32)
            return merge(
                1,
                weight_re * mode_re + weight_im * mode_im,
                weight_re * mode_im - weight_im * mode_re,
            )

        def summed(first, count):
            if count == 1:
                return products(first)
            half = count // 2
            return merge(count, summed(first, half), summed(first + half, half))

        mixed_ref[q, here, :] = pick(summed(0, C // 2), order)

    @pl.when(q == pl.num_programs(0) - 1)
    def _():
        y_inverse(mixed_ref, inverse_ref, out_ref)


def outer_kernel(alpha, modes_ref, back_ref, out_ref):
    rows = 8
    lane = lax.broadcasted_iota(jnp.int32, (rows, 2 * C), 1)
    pair = jnp.where(lane < C, 0, 1)
    for start in range(0, MY, rows):
        here = slice(start, start + rows)
        modes = modes_ref[0, here, :] * alpha
        back = back_ref[0, here, :]
        back_re = twice(back[:, :C])
        back_im = twice(back[:, C:])
        for t in range(C // 2):
            mode_re = pick(modes, pair + 2 * t)
            mode_im = pick(modes, pair + (2 * t + C))
            columns = slice(t * 2 * C, (t + 1) * 2 * C)
            out_ref[0, 0, 0, here, columns] = mode_re * back_re + mode_im * back_im
            out_ref[1, 0, 0, here, columns] = mode_re * back_im - mode_im * back_re


def whole():
    return pl.BlockSpec(memory_space=pltpu.VMEM)


def params(mib):
    return pltpu.CompilerParams(vmem_limit_bytes=mib * MIB)


def cost(flops, moved):
    return pl.CostEstimate(flops=int(flops), bytes_accessed=int(moved), transcendentals=0)


def call(kernel, outs, args, scratch=(), mib=24, flops=0, moved=0):
    return pl.pallas_call(
        kernel,
        out_shape=[jax.ShapeDtypeStruct(*out) for out in outs],
        in_specs=[whole() for _ in args],
        out_specs=[whole() for _ in outs],
        scratch_shapes=list(scratch),
        compiler_params=params(mib),
        cost_estimate=cost(flops, moved),
    )(*args)


def per_mode(kernel, data, weight, forward, inverse):
    _, mz, mx, my, wide = weight.shape
    full = lambda shape: pl.BlockSpec(shape, lambda q: (0,) * len(shape))
    modes_shape = (mz * mx, MY, 2 * C)
    out_shape = (inverse.shape[0], mz * mx * C)
    return pl.pallas_call(
        kernel,
        grid=(mz * mx,),
        in_specs=[
            full(data.shape),
            pl.BlockSpec((2, 1, 1, my, wide), lambda q: (0, q // mx, q % mx, 0, 0)),
            full(forward.shape),
            full(inverse.shape),
        ],
        out_specs=[full(modes_shape), full(out_shape)],
        out_shape=[
            jax.ShapeDtypeStruct(modes_shape, F32),
            jax.ShapeDtypeStruct(out_shape, F32),
        ],
        scratch_shapes=[pltpu.VMEM(modes_shape, F32)],
        compiler_params=params(24),
        cost_estimate=cost(weight.size * 8, weight.size * 2),
    )(data, weight, forward, inverse)


def outer(modes, back, shape, alpha):
    _, mz, mx, my, wide = shape
    small = pl.BlockSpec((1, MY, 2 * C), lambda q: (q, 0, 0))
    return pl.pallas_call(
        functools.partial(outer_kernel, alpha),
        grid=(mz * mx,),
        in_specs=[small, small],
        out_specs=pl.BlockSpec((2, 1, 1, my, wide), lambda q: (0, q // mx, q % mx, 0, 0)),
        out_shape=jax.ShapeDtypeStruct(shape, F32),
        compiler_params=params(16),
        cost_estimate=cost(math.prod(shape) * 4, math.prod(shape) * 4),
    )(modes, back)


def halos(turned):
    def shift(block, axis, step):
        count = lax.axis_size(axis)
        pairs = [(i, i + step) for i in range(count) if 0 <= i + step < count]
        return lax.ppermute(block, axis, pairs)

    xlo = shift(turned[-1], "gx", 1)
    xhi = shift(turned[0], "gx", -1)
    edge = lambda y: jnp.concatenate([xlo[None, y], turned[:, y], xhi[None, y]], axis=0)
    ylo = shift(edge(-1), "gy", 1)
    yhi = shift(edge(0), "gy", -1)
    return xlo, xhi, ylo, yhi


def conv(turned, rim, weight):
    cx, cy, c, z = turned.shape
    return call(
        conv_kernel,
        [((cx, c, cy * z), F32)],
        (turned, *rim, weight),
        [pltpu.VMEM((4 * c, (cy + 2) * z), BF16)],
        mib=32,
        flops=2 * 27 * c * c * cx * cy * z,
        moved=turned.size * 8,
    )[0]


def weight_grad(grad, turned, rim):
    cx, cy, c, z = turned.shape
    return call(
        weight_grad_kernel,
        [((9 * c, 3 * c), F32)],
        (grad, turned, *rim),
        [
            pltpu.VMEM((4 * c, (cy + 2) * z), BF16),
            pltpu.VMEM((cx * 3 * c, (cy + 2) * z), BF16),
        ],
        mib=32,
        flops=2 * 27 * c * c * cx * cy * z,
        moved=turned.size * 8,
    )[0]


def sum_everywhere(part, scale):
    nx, ny = lax.axis_size("gx"), lax.axis_size("gy")
    size = part.size
    rows = -(-size // (128 * nx * ny))
    flat = jnp.pad(part.reshape(-1), (0, rows * 128 * nx * ny - size))
    mine = flat.reshape(nx, ny * rows, 128)
    mine = lax.all_to_all(mine, "gx", split_axis=0, concat_axis=0, tiled=True).sum(0)
    mine = mine.reshape(ny, rows, 128)
    mine = lax.all_to_all(mine, "gy", split_axis=0, concat_axis=0, tiled=True).sum(0)
    full = lax.all_gather(mine * scale, ("gx", "gy"), axis=0, tiled=False)
    return full.reshape(-1)[:size].reshape(part.shape)


def body(state, cotangent, spectral_weight, stencil_weight, pointwise_weight):
    nx, ny = lax.axis_size("gx"), lax.axis_size("gy")
    c, cx, cy, z = state.shape
    _, mz, mx, _, _ = spectral_weight.shape
    wide_x, wide_y = cx * nx, cy * ny
    alpha = 1.0 / math.sqrt(wide_x * wide_y * z)
    beta = 1.0 / math.sqrt(2 * MX * MY * MZ)
    double = np.where(np.arange(MZ) == 0, 1.0, 2.0)
    ones = np.ones(MZ)
    z_state = jnp.asarray(z_forward_table(alpha * ones)(nx, mz))
    z_grad = jnp.asarray(z_forward_table(double)(nx, mz))
    z_spectral = jnp.asarray(z_inverse_table(nx, mz, beta * double))
    z_back = jnp.asarray(z_inverse_table(nx, mz, alpha * beta * ones))
    x_fwd, x_inv = (jnp.asarray(t) for t in x_tables(wide_x, mz))
    y_fwd, y_inv = (jnp.asarray(t) for t in y_tables(wide_y))
    lanes = cy * c
    x_rows = cx * 2 * mz

    def swap(block, axis):
        return lax.all_to_all(block, axis, split_axis=0, concat_axis=0, tiled=True)

    def x_stage(table, block, lead):
        flat = block.reshape(-1, lanes)
        got = jnp.dot(table, flat, precision=lax.Precision.HIGHEST)
        return got.reshape(lead, -1, lanes)

    def to_pencil(slab):
        block = swap(x_stage(x_fwd, swap(slab, "gx"), ny), "gy")
        block = block.reshape(ny, mx, 2, mz, cy, c).transpose(2, 0, 4, 3, 1, 5)
        return block.reshape(2 * wide_y, mz * mx * c)

    def to_slab(pencil):
        block = pencil.reshape(2, ny, cy, mz, mx, c).transpose(1, 4, 0, 3, 2, 5)
        block = swap(block.reshape(ny, mx * 2 * mz, lanes), "gy")
        return swap(x_stage(x_inv, block, nx), "gx")

    slab_shape = ((nx, x_rows, lanes), F32)
    turned_shape = ((cx, cy, c, z), BF16)

    taps = stencil_weight.reshape(c, c, 3, 3, 3)
    none = jnp.zeros((3, 3, c, c), BF16)

    def table_of(tap, point):
        own = none.at[1, 1].set(point).reshape(9 * c, c)
        return jnp.concatenate([tap.reshape(9 * c, 3 * c), own], axis=1)

    conv_table = table_of(jnp.transpose(taps, (2, 3, 0, 4, 1)), pointwise_weight)
    back_table = table_of(
        jnp.transpose(taps[:, :, ::-1, ::-1, ::-1], (2, 3, 1, 4, 0)), pointwise_weight.T
    )

    turned, slab = call(
        functools.partial(prep_kernel, nx),
        [turned_shape, slab_shape],
        (state, z_state),
        flops=2 * 96 * state.size,
        moved=state.size * 5,
    )
    rim = halos(turned)
    pencil = to_pencil(slab)
    stencil = conv(turned, rim, conv_table)
    modes_in, pencil = per_mode(mix_kernel, pencil, spectral_weight, y_fwd, y_inv)
    slab = to_slab(pencil)
    output, grad, slab = call(
        functools.partial(gelu_kernel, nx),
        [((c, cx, cy, z), BF16), turned_shape, slab_shape],
        (stencil, slab, cotangent, z_spectral, z_grad),
        flops=2 * 192 * state.size,
        moved=state.size * 12,
    )
    grad_rim = halos(grad)
    pencil = to_pencil(slab)
    grad_taps = weight_grad(grad, turned, rim)
    back_modes, pencil = per_mode(mix_back_kernel, pencil, spectral_weight, y_fwd, y_inv)
    grad_modes = outer(modes_in, back_modes, spectral_weight.shape, alpha)
    stencil_back = conv(grad, grad_rim, back_table)
    slab = to_slab(pencil)
    grad_state = call(
        functools.partial(finish_kernel, nx),
        [((c, cx, cy, z), F32)],
        (stencil_back, slab, z_back),
        flops=2 * 96 * state.size,
        moved=state.size * 10,
    )[0]
    total = sum_everywhere(grad_taps, alpha).reshape(3, 3, c, 3, c)
    grad_stencil = jnp.transpose(total, (2, 4, 0, 1, 3))
    grad_point = total[1, 1, :, 1, :]
    return (output, grad_state, grad_modes, grad_stencil.reshape(c, 27 * c), grad_point)


def solution(mesh):
    in_specs = (
        P(None, "gx", "gy", None),
        P(None, "gx", "gy", None),
        P(None, "gx", "gy", None, None),
        P(),
        P(),
    )
    out_specs = (
        P(None, "gx", "gy", None),
        P(None, "gx", "gy", None),
        P(None, "gx", "gy", None, None),
        P(),
        P(),
    )
    return jax.shard_map(body, mesh=mesh, in_specs=in_specs, out_specs=out_specs, check_vma=False)
```

time: 481 us -> 275 us (0.57); the launches traced: 474 us -> 273 us
  matrix products: 181 us -> 5.96 us
  local copies, waits for them, and re-layouts: 115 us -> 32.5 us
  Pallas kernels: 0 us -> 68 us
  other arithmetic: 48.4 us -> 0.34 us
  blocking collectives: 54.1 us -> 82.9 us
  starting transfers between devices: 41.5 us -> 55.9 us
  between operations: 15.3 us -> 1.17 us
  waiting for transfers between devices: 17.8 us -> 26.3 us
    dot_general x77 -> x4, matrix products: 168 us -> 5.96 us  [x_stage(): got = jnp.dot(table, flat, precision=lax.Precision.HIGHEST)]
    all_gather x0 -> x1, blocking collectives: none -> 71 us  [sum_everywhere(): full = lax.all_gather(mine * scale, ('gx', 'gy'), axis=0, tiled=False)]
    pallas_call x0 -> x9, Pallas kernels: none -> 68 us  [the longest x2 43 us: per_mode(): pl.pallas_call(kernel, grid=(mz * mx,), in_specs=[full(data.shape), pl.Bl...]
    psum x1 -> x0, blocking collectives: 41.4 us -> none  [body(): lax.psum((stencil_local, point_local), ('gx', 'gy'))]
    another operation x7 -> x1, local copies, waits for them, and re-layouts: 33 us -> 1.49 us  [body(): total = sum_everywhere(grad_taps, alpha).reshape(3, 3, c, 3, c)]
    squeeze x4, local copies, waits for them, and re-layouts: 27.1 us -> 0.71 us  [the longest x2 0.69 us: halos(): xhi = shift(turned[0], 'gx', -1)]
    mul x6 -> x0, other arithmetic: 15 us -> none  [the longest x1 12 us: body(): alpha * jnp.stack([grad_real, grad_imag]).reshape(2, mz_dev, mx_dev, MY,...]
    conv_general_dilated x2 -> x0, matrix products: 13.2 us -> none  [the longest x1 8.63 us: body(): lax.conv_general_dilated(padded[None], kernel, (1, 1, 1), 'VALID', dimens...]
  transfers between devices with their start and end apart: 16 -> 17, of which waited for: 5 -> 6; matrix products, arithmetic and copies ran while one was open for 54% -> 9% of each run, Pallas kernels for 0% -> 23%
where the time goes in v1:
time: 275 us; the launch traced here: 273 us
  blocking collectives  82.9 us (30%)
  Pallas kernels  68 us (25%)
  starting transfers between devices  55.9 us (20%)
  local copies, waits for them, and re-layouts  32.5 us (12%)
  waiting for transfers between devices  26.3 us (10%)
  matrix products  5.96 us (2%)
    all_gather x1, blocking collectives, sum_everywhere(): full = lax.all_gather(mine * scale, ('gx', 'gy'), axis=0, tiled=False)  71 us
    pallas_call x2, Pallas kernels, per_mode(): pl.pallas_call(kernel, grid=(mz * mx,), in_specs=[full(data.shape), pl.Bl...  43 us
    all_to_all x7, starting transfers between devices, swap(): return lax.all_to_all(block, axis, split_axis=0, concat_axis=0, tiled=True)  29.1 us
    ppermute x8, starting transfers between devices, shift(): return lax.ppermute(block, axis, pairs)  19.3 us
    pallas_call x1, Pallas kernels, outer(): pl.pallas_call(functools.partial(outer_kernel, alpha), grid=(mz * mx,), i...  15 us
    all_to_all x7, waiting for transfers between devices, swap(): return lax.all_to_all(block, axis, split_axis=0, concat_axis=0, tiled=True)  13 us
    unnamed x39, local copies, waits for them, and re-layouts  12.7 us
    all_to_all x1, blocking collectives, swap(): return lax.all_to_all(block, axis, split_axis=0, concat_axis=0, tiled=True)  11.9 us
  transfers between devices with their start and end apart: 17, of which 6 were waited for; matrix products, arithmetic and copies ran while one was open for 9% of the time, Pallas kernels for 23%

profile of v1, /device:TPU:0, one launch (start us, length us, event | category | flops | bytes accessed | tf_op | source)
XLA Modules:
  0.0 273.1 jit_solution(15487747132130815301)
XLA Ops:
  2.9 11.9 %all_to_all.50 = f32[8,16,512]{2,1,0:T(8,128)S(1)} all-to-all(f32[8,16,512]{2,1,0:T(8,128)S(1)} %get-tuple-element.39), channel_id=1, replica_groups=mesh['gx'=8,'gy'=4] {'gx'}, dimensions={0} | all-to-all | bytes 524288 | tf_op jit(solution)/shard_map/all_to_all | solution.py:486
  14.8 1.9 fusion.4
  16.7 4.9 %all-to-all-start.1 = ((f32[4,32,512]{2,1,0:T(8,128)}), f32[4,32,512]{2,1,0:T(8,128)S(1)}, u32[]{:S(2)}, u32[]{:S(2)}) async-start(f32[4,32,512]{2,1,0:T(8,128)} %bitcast.8), calls=%async_computation.1 | async-start | bytes 524288 | tf_op jit(solution)/shard_map/all_to_all | solution.py:486
  23.5 3.0 %collective-permute-start = (bf16[8,64,128]{2,1,0:T(8,128)(2,1)S(1)}, bf16[8,64,128]{2,1,0:T(8,128)(2,1)S(1)}, u32[]{:S(2)}, u32[]{:S(2)}) collective-permute-start(bf16[8,64,128]{2,1,0:T(8,128)(2,1)S(1)} %get-tuple-element.64), channel_id=1, source_target_pairs={{0,4},{4,8},{8,12},{12,16},{16,20},{20,24},{24,28},{1,5},{5,9},{9,... | collective-permute-start | bytes 393224 | tf_op jit(solution)/shard_map/ppermute | solution.py:415
  31.0 3.4 %copy-done = bf16[2,2,8,32,4096]{4,3,2,1,0:T(8,128)(2,1)S(1)} copy-done((bf16[2,2,8,32,4096]{4,3,2,1,0:T(8,128)(2,1)S(1)}, bf16[2,2,8,32,4096]{4,3,2,1,0:T(8,128)(2,1)}, u32[]{:S(2)}) %copy-start) | copy-done | bytes 8388632
  34.3 17.2 %shard_map.166 = (f32[16,32,128]{2,1,0:T(8,128)S(1)}, f32[64,1024]{1,0:T(8,128)S(1)}) custom-call(f32[64,1024]{1,0:T(8,128)S(1)} %reshape.177.data_ref, bf16[2,2,8,32,4096]{4,3,2,1,0:T(8,128)(2,1)S(1)} %copy-done, bf16[64,192]{1,0:T(8,128)(2,1)S(1)} %copy-done.5, bf16[64,192]{1,0:T(8,128)(2,1)S(1)} %copy-done.4), custom_call_target="tpu_custom_call" | custom-call | flops 33554432 | bytes 8388608 | tf_op jit(solution)/shard_map/pallas_call | solution.py:377
  52.7 5.1 %all-to-all-start.2 = ((f32[4,32,512]{2,1,0:T(8,128)}), f32[4,32,512]{2,1,0:T(8,128)S(1)}, u32[]{:S(2)}, u32[]{:S(2)}) async-start(f32[4,32,512]{2,1,0:T(8,128)} %reshape.179), calls=%async_computation.2 | async-start | bytes 524288 | tf_op jit(solution)/shard_map/all_to_all | solution.py:486
  57.8 3.9 %collective-permute-start.2 = (bf16[6,64,128]{2,1,0:T(8,128)(2,1)S(1)}, bf16[6,64,128]{2,1,0:T(8,128)(2,1)S(1)}, u32[]{:S(2)}, u32[]{:S(2)}) collective-permute-start(bf16[6,64,128]{2,1,0:T(8,128)(2,1)S(1)} %pad_maximum_fusion.2), channel_id=1, source_target_pairs={{0,1},{1,2},{2,3},{4,5},{5,6},{6,7},{8,9},{9,10},{10,11},{12,13},{... | collective-permute-start | bytes 294920 | tf_op jit(solution)/shard_map/ppermute | solution.py:415
  61.8 5.3 %all-to-all-done.2 = f32[4,32,512]{2,1,0:T(8,128)S(1)} async-done(((f32[4,32,512]{2,1,0:T(8,128)}), f32[4,32,512]{2,1,0:T(8,128)S(1)}, u32[]{:S(2)}, u32[]{:S(2)}) %all-to-all-start.2) | async-done | bytes 262176 | tf_op jit(solution)/shard_map/all_to_all | solution.py:486
  68.1 3.4 %all-to-all-start.3 = ((f32[8,16,512]{2,1,0:T(8,128)}), f32[8,16,512]{2,1,0:T(8,128)S(1)}, u32[]{:S(2)}, u32[]{:S(2)}) async-start(f32[8,16,512]{2,1,0:T(8,128)} %bitcast.12), calls=%async_computation.3 | async-start | bytes 524288 | tf_op jit(solution)/shard_map/all_to_all | solution.py:486
  73.0 5.6 %collective-permute-done.3.yhi_ref = bf16[6,64,128]{2,1,0:T(8,128)(2,1)S(1)} collective-permute-done((bf16[6,64,128]{2,1,0:T(8,128)(2,1)S(1)}, bf16[6,64,128]{2,1,0:T(8,128)(2,1)S(1)}, u32[]{:S(2)}, u32[]{:S(2)}) %collective-permute-start.3) | collective-permute-done | bytes 98336 | tf_op jit(solution)/shard_map/ppermute | solution.py:415
  78.6 1.9 shard_map.165.stencil_ref
  80.5 2.3 shard_map.167
  82.8 3.8 %all-to-all-start.4 = ((f32[8,16,512]{2,1,0:T(8,128)}), f32[8,16,512]{2,1,0:T(8,128)S(1)}, u32[]{:S(2)}, u32[]{:S(2)}) async-start(f32[8,16,512]{2,1,0:T(8,128)} %get-tuple-element.43), calls=%async_computation.4 | async-start | bytes 524288 | tf_op jit(solution)/shard_map/all_to_all | solution.py:486
  86.7 3.6 %rev.3 = bf16[64,64,3,3,3]{0,4,3,2,1:T(4,128)(2,1)S(1)} reverse(bf16[64,64,3,3,3]{0,4,3,2,1:T(4,128)(2,1)} %copy-done.14), dimensions={2,3,4} | reverse | bytes 442368 | tf_op jit(solution)/shard_map/rev | solution.py:515
  92.8 2.1 shard_map.172
  96.0 4.2 %all-to-all-start.8 = ((f32[8,108,128]{2,1,0:T(8,128)}), f32[8,108,128]{2,1,0:T(8,128)S(1)}, u32[]{:S(2)}, u32[]{:S(2)}) async-start(f32[8,108,128]{2,1,0:T(8,128)} %reshape.193), calls=%async_computation.8 | async-start | bytes 917504 | tf_op jit(solution)/shard_map/all_to_all | solution.py:460
  101.7 3.0 %collective-permute-start.4 = (bf16[8,64,128]{2,1,0:T(8,128)(2,1)S(1)}, bf16[8,64,128]{2,1,0:T(8,128)(2,1)S(1)}, u32[]{:S(2)}, u32[]{:S(2)}) collective-permute-start(bf16[8,64,128]{2,1,0:T(8,128)(2,1)S(1)} %get-tuple-element.60), channel_id=1, source_target_pairs={{0,4},{4,8},{8,12},{12,16},{16,20},{20,24},{24,28},{1,5},{5,9},{9,... | collective-permute-start | bytes 393224 | tf_op jit(solution)/shard_map/ppermute | solution.py:415
  104.8 1.9 fusion.6
  106.7 2.6 all-to-all-done.8
  109.3 3.4 %all-to-all-start.5 = ((f32[4,32,512]{2,1,0:T(8,128)}), f32[4,32,512]{2,1,0:T(8,128)S(1)}, u32[]{:S(2)}, u32[]{:S(2)}) async-start(f32[4,32,512]{2,1,0:T(8,128)} %bitcast.22), calls=%async_computation.5 | async-start | bytes 524288 | tf_op jit(solution)/shard_map/all_to_all | solution.py:486
  113.4 7.7 %all-to-all-done.5 = f32[4,32,512]{2,1,0:T(8,128)S(1)} async-done(((f32[4,32,512]{2,1,0:T(8,128)}), f32[4,32,512]{2,1,0:T(8,128)S(1)}, u32[]{:S(2)}, u32[]{:S(2)}) %all-to-all-start.5) | async-done | bytes 262176 | tf_op jit(solution)/shard_map/all_to_all | solution.py:486
  121.1 3.3 %all-to-all-start.9 = ((f32[4,27,128]{2,1,0:T(8,128)}), f32[4,27,128]{2,1,0:T(8,128)S(1)}, u32[]{:S(2)}, u32[]{:S(2)}) async-start(f32[4,27,128]{2,1,0:T(8,128)} %reshape.194), calls=%async_computation.9 | async-start | bytes 131072 | tf_op jit(solution)/shard_map/all_to_all | solution.py:462
  125.1 3.4 %copy-done.1 = bf16[2,2,8,32,4096]{4,3,2,1,0:T(8,128)(2,1)S(1)} copy-done((bf16[2,2,8,32,4096]{4,3,2,1,0:T(8,128)(2,1)S(1)}, bf16[2,2,8,32,4096]{4,3,2,1,0:T(8,128)(2,1)}, u32[]{:S(2)}) %copy-start.1) | copy-done | bytes 8388632
  128.4 25.9 %shard_map.169 = (f32[16,32,128]{2,1,0:T(8,128)S(1)}, f32[64,1024]{1,0:T(8,128)S(1)}) custom-call(f32[64,1024]{1,0:T(8,128)S(1)} %reshape.188.data_ref, bf16[2,2,8,32,4096]{4,3,2,1,0:T(8,128)(2,1)S(1)} %copy-done.1, bf16[64,192]{1,0:T(8,128)(2,1)S(1)} %copy-done.5, bf16[64,192]{1,0:T(8,128)(2,1)S(1)} %copy-done.4), custom_call_target="tpu_custom_call" | custom-call | flops 33554432 | bytes 8388608 | tf_op jit(solution)/shard_map/pallas_call | solution.py:377
  155.5 5.0 %all-to-all-start.6 = ((f32[4,32,512]{2,1,0:T(8,128)}), f32[4,32,512]{2,1,0:T(8,128)S(1)}, u32[]{:S(2)}, u32[]{:S(2)}) async-start(f32[4,32,512]{2,1,0:T(8,128)} %reshape.190), calls=%async_computation.6 | async-start | bytes 524288 | tf_op jit(solution)/shard_map/all_to_all | solution.py:486
  160.6 3.9 %collective-permute-start.6 = (bf16[6,64,128]{2,1,0:T(8,128)(2,1)S(1)}, bf16[6,64,128]{2,1,0:T(8,128)(2,1)S(1)}, u32[]{:S(2)}, u32[]{:S(2)}) collective-permute-start(bf16[6,64,128]{2,1,0:T(8,128)(2,1)S(1)} %pad_maximum_fusion.4), channel_id=1, source_target_pairs={{0,1},{1,2},{2,3},{4,5},{5,6},{6,7},{8,9},{9,10},{10,11},{12,13},{... | collective-permute-start | bytes 294920 | tf_op jit(solution)/shard_map/ppermute | solution.py:415
  166.7 4.3 %collective-permute-done.7.yhi_ref = bf16[6,64,128]{2,1,0:T(8,128)(2,1)S(1)} collective-permute-done((bf16[6,64,128]{2,1,0:T(8,128)(2,1)S(1)}, bf16[6,64,128]{2,1,0:T(8,128)(2,1)S(1)}, u32[]{:S(2)}, u32[]{:S(2)}) %collective-permute-start.7) | collective-permute-done | bytes 98336 | tf_op jit(solution)/shard_map/ppermute | solution.py:415
  174.0 3.5 %all-to-all-start.7 = ((f32[8,16,512]{2,1,0:T(8,128)}), f32[8,16,512]{2,1,0:T(8,128)S(1)}, u32[]{:S(2)}, u32[]{:S(2)}) async-start(f32[8,16,512]{2,1,0:T(8,128)} %bitcast.26), calls=%async_computation.7 | async-start | bytes 524288 | tf_op jit(solution)/shard_map/all_to_all | solution.py:486
  177.5 71.0 %all-gather.1 = f32[32,27,128]{2,1,0:T(8,128)S(1)} all-gather(f32[1,27,128]{2,1,0:T(8,128)S(1)} %multiply_bitcast_fusion), channel_id=2, replica_groups=mesh['gx'=8,'gy'=4] {'gx','gy'}, dimensions={0}, use_global_device_ids=true | all-gather | bytes 456192 | tf_op jit(solution)/shard_map/all_gather | solution.py:463
  251.6 2.5 copy.55
  256.7 15.0 %shard_map.171 = f32[2,2,8,32,4096]{4,3,2,1,0:T(8,128)} custom-call(f32[16,32,128]{2,1,0:T(8,128)S(1)} %get-tuple-element.45.modes_ref, f32[16,32,128]{2,1,0:T(8,128)S(1)} %get-tuple-element.46.back_ref), custom_call_target="tpu_custom_call" | custom-call | flops 16777216 | bytes 16777216 | tf_op jit(solution)/shard_map/pallas_call | solution.py:400
  (99 shorter events, 32.0 us)
Async XLA Ops:
  0.6 1.0 copy-start.3
  2.4 28.5 %copy-start.4 = (bf16[64,192]{1,0:T(8,128)(2,1)S(1)}, bf16[64,192]{1,0:T(8,128)(2,1)}, u32[]{:S(2)}) copy-start(bf16[64,192]{1,0:T(8,128)(2,1)} %constant.78.clone.inverse_ref) | copy-start | bytes 73732
  2.4 28.5 %copy-start.5 = (bf16[64,192]{1,0:T(8,128)(2,1)S(1)}, bf16[64,192]{1,0:T(8,128)(2,1)}, u32[]{:S(2)}) copy-start(bf16[64,192]{1,0:T(8,128)(2,1)} %constant.77.clone.forward_ref) | copy-start | bytes 73732
  16.7 13.6 %all-to-all-start.1 = ((f32[4,32,512]{2,1,0:T(8,128)}), f32[4,32,512]{2,1,0:T(8,128)S(1)}, u32[]{:S(2)}, u32[]{:S(2)}) async-start(f32[4,32,512]{2,1,0:T(8,128)} %bitcast.8), calls=%async_computation.1 | async-start | bytes 524288 | tf_op jit(solution)/shard_map/all_to_all | solution.py:486
  22.2 35.6 %collective-permute-start.1 = (bf16[8,64,128]{2,1,0:T(8,128)(2,1)}, bf16[8,64,128]{2,1,0:T(8,128)(2,1)S(1)}, u32[]{:S(2)}, u32[]{:S(2)}) collective-permute-start(bf16[8,64,128]{2,1,0:T(8,128)(2,1)} %get-tuple-element.63), channel_id=1, source_target_pairs={{4,0},{8,4},{12,8},{16,12},{20,16},{24,20},{28,24},{5,1},{9,5},{13... | collective-permute-start | bytes 393224 | tf_op jit(solution)/shard_map/ppermute | solution.py:415
  23.5 34.3 %collective-permute-start = (bf16[8,64,128]{2,1,0:T(8,128)(2,1)S(1)}, bf16[8,64,128]{2,1,0:T(8,128)(2,1)S(1)}, u32[]{:S(2)}, u32[]{:S(2)}) collective-permute-start(bf16[8,64,128]{2,1,0:T(8,128)(2,1)S(1)} %get-tuple-element.64), channel_id=1, source_target_pairs={{0,4},{4,8},{8,12},{12,16},{16,20},{20,24},{24,28},{1,5},{5,9},{9,... | collective-permute-start | bytes 393224 | tf_op jit(solution)/shard_map/ppermute | solution.py:415
  28.0 2.7 copy-start.14
  28.0 39.0 %copy-start.15 = (f32[128,128]{1,0:T(8,128)S(1)}, f32[128,128]{1,0:T(8,128)}, u32[]{:S(2)}) copy-start(f32[128,128]{1,0:T(8,128)} %constant.76.clone) | copy-start | bytes 196612
  30.9 3.4 %copy-start = (bf16[2,2,8,32,4096]{4,3,2,1,0:T(8,128)(2,1)S(1)}, bf16[2,2,8,32,4096]{4,3,2,1,0:T(8,128)(2,1)}, u32[]{:S(2)}) copy-start(bf16[2,2,8,32,4096]{4,3,2,1,0:T(8,128)(2,1)} %weight_ref.3) | copy-start | bytes 25165828
  34.3 46.2 %copy-start.2 = (bf16[64,4,8,128]{3,2,1,0:T(8,128)(2,1)S(1)}, bf16[64,4,8,128]{3,2,1,0:T(8,128)(2,1)}, u32[]{:S(2)}) copy-start(bf16[64,4,8,128]{3,2,1,0:T(8,128)(2,1)} %cot_ref.1) | copy-start | bytes 1572868
  34.3 46.2 %copy-start.7 = (bf16[96,128]{1,0:T(8,128)(2,1)S(1)}, bf16[96,128]{1,0:T(8,128)(2,1)}, u32[]{:S(2)}) copy-start(bf16[96,128]{1,0:T(8,128)(2,1)} %constant.73.clone.inverse_ref) | copy-start | bytes 73732
  34.3 46.2 %copy-start.8 = (bf16[96,128]{1,0:T(8,128)(2,1)S(1)}, bf16[96,128]{1,0:T(8,128)(2,1)}, u32[]{:S(2)}) copy-start(bf16[96,128]{1,0:T(8,128)(2,1)} %constant.72.clone.forward_ref) | copy-start | bytes 73732
  51.5 38.8 %copy-start.17 = (bf16[64,64]{1,0:T(8,128)(2,1)S(1)}, bf16[64,64]{1,0:T(8,128)(2,1)}, u32[]{:S(2)}) copy-start(bf16[64,64]{1,0:T(8,128)(2,1)} %param.21) | copy-start | bytes 24580
  52.7 14.4 %all-to-all-start.2 = ((f32[4,32,512]{2,1,0:T(8,128)}), f32[4,32,512]{2,1,0:T(8,128)S(1)}, u32[]{:S(2)}, u32[]{:S(2)}) async-start(f32[4,32,512]{2,1,0:T(8,128)} %reshape.179), calls=%async_computation.2 | async-start | bytes 524288 | tf_op jit(solution)/shard_map/all_to_all | solution.py:486
  57.8 15.1 %collective-permute-start.2 = (bf16[6,64,128]{2,1,0:T(8,128)(2,1)S(1)}, bf16[6,64,128]{2,1,0:T(8,128)(2,1)S(1)}, u32[]{:S(2)}, u32[]{:S(2)}) collective-permute-start(bf16[6,64,128]{2,1,0:T(8,128)(2,1)S(1)} %pad_maximum_fusion.2), channel_id=1, source_target_pairs={{0,1},{1,2},{2,3},{4,5},{5,6},{6,7},{8,9},{9,10},{10,11},{12,13},{... | collective-permute-start | bytes 294920 | tf_op jit(solution)/shard_map/ppermute | solution.py:415
  68.1 12.4 %all-to-all-start.3 = ((f32[8,16,512]{2,1,0:T(8,128)}), f32[8,16,512]{2,1,0:T(8,128)S(1)}, u32[]{:S(2)}, u32[]{:S(2)}) async-start(f32[8,16,512]{2,1,0:T(8,128)} %bitcast.12), calls=%async_computation.3 | async-start | bytes 524288 | tf_op jit(solution)/shard_map/all_to_all | solution.py:486
  71.6 7.0 %collective-permute-start.3 = (bf16[6,64,128]{2,1,0:T(8,128)(2,1)S(1)}, bf16[6,64,128]{2,1,0:T(8,128)(2,1)S(1)}, u32[]{:S(2)}, u32[]{:S(2)}) collective-permute-start(bf16[6,64,128]{2,1,0:T(8,128)(2,1)S(1)} %pad_maximum_fusion.3), channel_id=1, source_target_pairs={{1,0},{2,1},{3,2},{5,4},{6,5},{7,6},{9,8},{10,9},{11,10},{13,12},{... | collective-permute-start | bytes 294920 | tf_op jit(solution)/shard_map/ppermute | solution.py:415
  73.0 7.5 %copy-start.10 = (bf16[6,64,128]{2,1,0:T(8,128)(2,1)}, bf16[6,64,128]{2,1,0:T(8,128)(2,1)S(1)}, u32[]{:S(2)}) copy-start(bf16[6,64,128]{2,1,0:T(8,128)(2,1)S(1)} %collective-permute-done.2.ylo_ref) | copy-start | bytes 294916
  78.6 1.9 copy-start.12
  82.8 13.2 %all-to-all-start.4 = ((f32[8,16,512]{2,1,0:T(8,128)}), f32[8,16,512]{2,1,0:T(8,128)S(1)}, u32[]{:S(2)}, u32[]{:S(2)}) async-start(f32[8,16,512]{2,1,0:T(8,128)} %get-tuple-element.43), calls=%async_computation.4 | async-start | bytes 524288 | tf_op jit(solution)/shard_map/all_to_all | solution.py:486
  96.0 13.2 %all-to-all-start.8 = ((f32[8,108,128]{2,1,0:T(8,128)}), f32[8,108,128]{2,1,0:T(8,128)S(1)}, u32[]{:S(2)}, u32[]{:S(2)}) async-start(f32[8,108,128]{2,1,0:T(8,128)} %reshape.193), calls=%async_computation.8 | async-start | bytes 917504 | tf_op jit(solution)/shard_map/all_to_all | solution.py:460
  100.2 12.5 %collective-permute-start.5 = (bf16[8,64,128]{2,1,0:T(8,128)(2,1)S(1)}, bf16[8,64,128]{2,1,0:T(8,128)(2,1)S(1)}, u32[]{:S(2)}, u32[]{:S(2)}) collective-permute-start(bf16[8,64,128]{2,1,0:T(8,128)(2,1)S(1)} %get-tuple-element.59), channel_id=1, source_target_pairs={{4,0},{8,4},{12,8},{16,12},{20,16},{24,20},{28,24},{5,1},{9,5},{13... | collective-permute-start | bytes 393224 | tf_op jit(solution)/shard_map/ppermute | solution.py:415
  101.7 22.7 %collective-permute-start.4 = (bf16[8,64,128]{2,1,0:T(8,128)(2,1)S(1)}, bf16[8,64,128]{2,1,0:T(8,128)(2,1)S(1)}, u32[]{:S(2)}, u32[]{:S(2)}) collective-permute-start(bf16[8,64,128]{2,1,0:T(8,128)(2,1)S(1)} %get-tuple-element.60), channel_id=1, source_target_pairs={{0,4},{4,8},{8,12},{12,16},{16,20},{20,24},{24,28},{1,5},{5,9},{9,... | collective-permute-start | bytes 393224 | tf_op jit(solution)/shard_map/ppermute | solution.py:415
  109.3 11.9 %all-to-all-start.5 = ((f32[4,32,512]{2,1,0:T(8,128)}), f32[4,32,512]{2,1,0:T(8,128)S(1)}, u32[]{:S(2)}, u32[]{:S(2)}) async-start(f32[4,32,512]{2,1,0:T(8,128)} %bitcast.22), calls=%async_computation.5 | async-start | bytes 524288 | tf_op jit(solution)/shard_map/all_to_all | solution.py:486
  121.1 34.4 %all-to-all-start.9 = ((f32[4,27,128]{2,1,0:T(8,128)}), f32[4,27,128]{2,1,0:T(8,128)S(1)}, u32[]{:S(2)}, u32[]{:S(2)}) async-start(f32[4,27,128]{2,1,0:T(8,128)} %reshape.194), calls=%async_computation.9 | async-start | bytes 131072 | tf_op jit(solution)/shard_map/all_to_all | solution.py:462
  125.1 3.4 %copy-start.1 = (bf16[2,2,8,32,4096]{4,3,2,1,0:T(8,128)(2,1)S(1)}, bf16[2,2,8,32,4096]{4,3,2,1,0:T(8,128)(2,1)}, u32[]{:S(2)}) copy-start(bf16[2,2,8,32,4096]{4,3,2,1,0:T(8,128)(2,1)} %weight_ref.3) | copy-start | bytes 25165828
  128.4 44.5 %copy-start.16 = (f32[128,128]{1,0:T(8,128)S(1)}, f32[128,128]{1,0:T(8,128)}, u32[]{:S(2)}) copy-start(f32[128,128]{1,0:T(8,128)} %constant.76.clone) | copy-start | bytes 196612
  155.5 17.4 %all-to-all-start.6 = ((f32[4,32,512]{2,1,0:T(8,128)}), f32[4,32,512]{2,1,0:T(8,128)S(1)}, u32[]{:S(2)}, u32[]{:S(2)}) async-start(f32[4,32,512]{2,1,0:T(8,128)} %reshape.190), calls=%async_computation.6 | async-start | bytes 524288 | tf_op jit(solution)/shard_map/all_to_all | solution.py:486
  160.6 6.1 %collective-permute-start.6 = (bf16[6,64,128]{2,1,0:T(8,128)(2,1)S(1)}, bf16[6,64,128]{2,1,0:T(8,128)(2,1)S(1)}, u32[]{:S(2)}, u32[]{:S(2)}) collective-permute-start(bf16[6,64,128]{2,1,0:T(8,128)(2,1)S(1)} %pad_maximum_fusion.4), channel_id=1, source_target_pairs={{0,1},{1,2},{2,3},{4,5},{5,6},{6,7},{8,9},{9,10},{10,11},{12,13},{... | collective-permute-start | bytes 294920 | tf_op jit(solution)/shard_map/ppermute | solution.py:415
  164.5 6.5 %collective-permute-start.7 = (bf16[6,64,128]{2,1,0:T(8,128)(2,1)S(1)}, bf16[6,64,128]{2,1,0:T(8,128)(2,1)S(1)}, u32[]{:S(2)}, u32[]{:S(2)}) collective-permute-start(bf16[6,64,128]{2,1,0:T(8,128)(2,1)S(1)} %pad_maximum_fusion.5), channel_id=1, source_target_pairs={{1,0},{2,1},{3,2},{5,4},{6,5},{7,6},{9,8},{10,9},{11,10},{13,12},{... | collective-permute-start | bytes 294920 | tf_op jit(solution)/shard_map/ppermute | solution.py:415
  174.0 97.6 %all-to-all-start.7 = ((f32[8,16,512]{2,1,0:T(8,128)}), f32[8,16,512]{2,1,0:T(8,128)S(1)}, u32[]{:S(2)}, u32[]{:S(2)}) async-start(f32[8,16,512]{2,1,0:T(8,128)} %bitcast.26), calls=%async_computation.7 | async-start | bytes 524288 | tf_op jit(solution)/shard_map/all_to_all | solution.py:486
  256.7 15.0 %copy-start.6 = (bf16[96,128]{1,0:T(8,128)(2,1)S(1)}, bf16[96,128]{1,0:T(8,128)(2,1)}, u32[]{:S(2)}) copy-start(bf16[96,128]{1,0:T(8,128)(2,1)} %constant.74.clone.inverse_ref) | copy-start | bytes 73732
  (3 other events, 2.5 us)

commit v2 on v1

v2 whole, which is shorter than its diff:
```python
import functools
import math

import jax
import jax.numpy as jnp
import numpy as np
from jax import lax
from jax.experimental import pallas as pl
from jax.experimental.pallas import tpu as pltpu
from jax.sharding import PartitionSpec as P

C = 64
MX = 32
MY = 32
MZ = 16
Z = 128
MIB = 1 << 20

F32 = jnp.float32
BF16 = jnp.bfloat16


def angles(places, freqs, length):
    turns = np.outer(np.asarray(places), np.asarray(freqs)) % length
    return turns * (2.0 * np.pi / length)


def centred(count):
    steps = np.arange(count)
    return np.where(steps < count // 2, steps, steps - count)


def split(table, parts):
    rest = np.asarray(table, np.float64)
    out = []
    for _ in range(parts):
        piece = rest.astype(jnp.bfloat16)
        out.append(piece)
        rest = rest - piece.astype(np.float64)
    return out


def z_forward_table(scale):
    def build(nx, mz):
        theta = angles(np.arange(MZ), np.arange(Z), Z)
        pair = np.stack([np.cos(theta), -np.sin(theta)]) * scale[None, :, None]
        rows = pair.reshape(2, nx, mz, Z).transpose(1, 0, 2, 3).reshape(2 * MZ, Z)
        return np.concatenate(split(rows, 3), axis=0)

    return build


def z_inverse_table(nx, mz, scale):
    theta = angles(np.arange(MZ), np.arange(Z), Z)
    pair = np.stack([np.cos(theta), -np.sin(theta)]) * scale[None, :, None]
    rows = pair.reshape(2, nx, mz, Z).transpose(1, 0, 2, 3).reshape(2 * MZ, Z)
    high, low = split(rows, 2)
    return np.concatenate([high, high, low], axis=0)


def rotation(theta, sign):
    cosine, sine = np.cos(theta), sign * np.sin(theta)
    return np.stack([np.stack([cosine, -sine], 1), np.stack([sine, cosine], 1)])


def against_pieces(*tables):
    out = []
    for table in tables:
        high, low = split(table, 2)
        out.append(np.concatenate([high, high, low], axis=1))
    return out


def x_tables(wide, mz):
    theta = angles(centred(MX), np.arange(wide), wide)
    eye = np.eye(mz)
    forward = np.einsum("rkRx,zZ->krzxRZ", rotation(theta, -1.0), eye)
    inverse = np.einsum("rxRk,zZ->xrzkRZ", rotation(theta.T, 1.0), eye)
    size_k, size_x = MX * 2 * mz, wide * 2 * mz
    return against_pieces(forward.reshape(size_k, size_x), inverse.reshape(size_x, size_k))


def y_tables(wide):
    theta = angles(centred(MY), np.arange(wide), wide)
    forward = rotation(theta, -1.0).reshape(2 * MY, 2 * wide)
    inverse = rotation(theta.T, 1.0).reshape(2 * wide, 2 * MY)
    return against_pieces(forward, inverse)


def pieces(values):
    high = values.astype(BF16)
    low = (values - high.astype(F32)).astype(BF16)
    return jnp.concatenate([high, low, high], axis=0)


def z_forward(rows, table, out_ref, x, nx):
    got = lax.dot_general(table, rows, (((1,), (1,)), ((), ())), preferred_element_type=F32)
    size = 2 * MZ
    total = got[:size] + (got[size : 2 * size] + got[2 * size :])
    per = size // nx
    for owner in range(nx):
        out_ref[owner, x * per : (x + 1) * per, :] = total[owner * per : (owner + 1) * per]


def z_inverse(in_ref, table, x, nx):
    per = 2 * MZ // nx
    rows = jnp.concatenate(
        [in_ref[owner, x * per : (x + 1) * per, :] for owner in range(nx)], axis=0
    )
    return lax.dot_general(
        pieces(rows), table, (((0,), (0,)), ((), ())), preferred_element_type=F32
    )


def prep_kernel(nx, field_ref, table_ref, turned_ref, slab_ref):
    c, cx, cy, z = field_ref.shape
    for x in range(cx):
        block = jnp.swapaxes(field_ref[:, x].astype(F32), 0, 1)
        turned = block.astype(BF16)
        turned_ref[x] = turned
        z_forward(turned.reshape(cy * c, z), table_ref[...], slab_ref, x, nx)


def plane_rows(p, cx, body_ref, xlo_ref, xhi_ref, ylo_ref, yhi_ref):
    cy = body_ref.shape[1]
    if p == 0:
        middle = [xlo_ref[y] for y in range(cy)]
    elif p == cx + 1:
        middle = [xhi_ref[y] for y in range(cy)]
    else:
        middle = [body_ref[p - 1, y] for y in range(cy)]
    return [ylo_ref[p]] + middle + [yhi_ref[p]]


def fill_shifts(blocks, rim_ref, flip=False):
    c, z = blocks[0].shape
    lane = lax.broadcasted_iota(jnp.int32, (c, z), 1)
    for y, block in enumerate(blocks):
        wide = block.astype(F32)
        before = jnp.where(lane == 0, 0.0, pltpu.roll(wide, 1, 1))
        after = jnp.where(lane == z - 1, 0.0, pltpu.roll(wide, z - 1, 1))
        if flip:
            before, after = after, before
        columns = slice(y * z, (y + 1) * z)
        rim_ref[0:c, columns] = before.astype(BF16)
        rim_ref[c : 2 * c, columns] = block
        rim_ref[2 * c : 3 * c, columns] = after.astype(BF16)
        rim_ref[3 * c : 4 * c, columns] = block


def conv_kernel(
    flip, body_ref, xlo_ref, xhi_ref, ylo_ref, yhi_ref, weight_ref, out_ref, rim_ref
):
    cx, cy, c, z = body_ref.shape
    for p in range(cx + 2):
        blocks = plane_rows(p, cx, body_ref, xlo_ref, xhi_ref, ylo_ref, yhi_ref)
        fill_shifts(blocks, rim_ref, flip)
        places = [a for a in range(3) if 0 <= p - (2 - a if flip else a) < cx]
        first = places[0]
        got = jnp.dot(
            weight_ref[first * 3 * c : (places[-1] + 1) * 3 * c, :],
            rim_ref[...],
            preferred_element_type=F32,
        )
        for a in places:
            x = p - (2 - a if flip else a)
            total = None
            for b in range(3):
                row = ((a - first) * 3 + b) * c
                skip = 2 - b if flip else b
                term = got[row : row + c, skip * z : (skip + cy) * z]
                total = term if total is None else total + term
            if p == x:
                out_ref[x] = total
            else:
                out_ref[x] += total


def weight_grad_kernel(
    grad_ref, body_ref, xlo_ref, xhi_ref, ylo_ref, yhi_ref, out_ref, rim_ref, wide_ref, sum_ref
):
    cx, cy, c, z = body_ref.shape
    group = 3 * c
    wide_ref[...] = jnp.zeros_like(wide_ref)
    for x in range(cx):
        for b in range(3):
            for y in range(cy):
                row = x * group + b * c
                wide_ref[row : row + c, (y + b) * z : (y + b + 1) * z] = grad_ref[x, y]
    sum_ref[...] = jnp.zeros_like(sum_ref)
    for p in range(cx + 2):
        fill_shifts(plane_rows(p, cx, body_ref, xlo_ref, xhi_ref, ylo_ref, yhi_ref), rim_ref)
        first, last = max(0, p - 2), min(cx - 1, p)
        got = lax.dot_general(
            wide_ref[first * group : (last + 1) * group, :],
            rim_ref[...],
            (((1,), (1,)), ((), ())),
            preferred_element_type=F32,
        )
        for x in range(first, last + 1):
            a = p - x
            sum_ref[a * group : (a + 1) * group, :] += got[
                (x - first) * group : (x - first + 1) * group, :
            ]
    out_ref[: 9 * c] = sum_ref[:, : 2 * c]
    last = [sum_ref[k * c : (k + 1) * c, 2 * c : 3 * c] for k in range(9)]
    last.append(jnp.zeros((c, c), F32))
    for k in range(5):
        row = (9 + k) * c
        out_ref[row : row + c] = jnp.concatenate(last[2 * k : 2 * k + 2], axis=1)


def gelu_kernel(
    nx, stencil_ref, slab_ref, cot_ref, inverse_ref, forward_ref, out_ref, turned_ref, back_ref
):
    c, cx, cy, z = cot_ref.shape
    root = math.sqrt(2.0 / math.pi)
    for x in range(cx):
        spectral = z_inverse(slab_ref, inverse_ref[...], x, nx).reshape(cy, c, z)
        stencil = jnp.stack([stencil_ref[x, :, y * z : (y + 1) * z] for y in range(cy)])
        pre = spectral + stencil
        cot = jnp.swapaxes(cot_ref[:, x].astype(F32), 0, 1)
        square = pre * pre
        bent = jnp.tanh(root * (pre * (1.0 + 0.044715 * square)))
        half = 0.5 + 0.5 * bent
        slope = half + (0.5 * pre) * (1.0 - bent * bent) * (root * (1.0 + 0.134145 * square))
        out_ref[:, x] = jnp.swapaxes(pre * half, 0, 1).astype(BF16)
        grad = (cot * slope).astype(BF16)
        turned_ref[x] = grad
        z_forward(grad.reshape(cy * c, z), forward_ref[...], back_ref, x, nx)


def finish_kernel(nx, stencil_ref, slab_ref, inverse_ref, out_ref):
    c, cx, cy, z = out_ref.shape
    for x in range(cx):
        spectral = z_inverse(slab_ref, inverse_ref[...], x, nx).reshape(cy, c, z)
        stencil = jnp.stack([stencil_ref[x, :, y * z : (y + 1) * z] for y in range(cy)])
        out_ref[:, x] = jnp.swapaxes(spectral + stencil, 0, 1)


def x_kernel(table_ref, data_ref, out_ref):
    out_ref[...] = jnp.dot(table_ref[...], pieces(data_ref[...]), preferred_element_type=F32)


def taps_kernel(taps_ref, point_ref, forward_ref, back_ref, turned_ref):
    turned_ref[...] = taps_ref[...].astype(F32).T
    forward_ref[...] = jnp.zeros_like(forward_ref)
    back_ref[...] = jnp.zeros_like(back_ref)
    for tap in range(27):
        rows = slice(tap // 3 * C, (tap // 3 + 1) * C)
        columns = slice(tap % 3 * C, (tap % 3 + 1) * C)
        block = turned_ref[pl.ds(tap, C, stride=27), :]
        back_ref[rows, columns] = block.astype(BF16)
        forward_ref[rows, columns] = block.T.astype(BF16)
    point = point_ref[...].astype(F32)
    forward_ref[4 * C : 5 * C, 3 * C :] = point.astype(BF16)
    back_ref[4 * C : 5 * C, 3 * C :] = point.T.astype(BF16)


def unpack_kernel(scale, packed_ref, taps_ref, point_ref, turned_ref):
    for tap in range(27):
        group, e = tap // 3, tap % 3
        if e < 2:
            block = packed_ref[group * C : (group + 1) * C, e * C : (e + 1) * C]
        else:
            row = (9 + group // 2) * C
            block = packed_ref[row : row + C, group % 2 * C : (group % 2 + 1) * C]
        block = block * scale
        if tap == 13:
            point_ref[...] = block
        turned_ref[pl.ds(tap, C, stride=27), :] = block.T
    taps_ref[...] = turned_ref[...].T


QUAD = 4
SPAN = 8


def y_forward(data_ref, table_ref, store):
    got = jnp.dot(table_ref[...], pieces(data_ref[...]), preferred_element_type=F32)
    for q in range(got.shape[1] // C):
        block = got[:, q * C : (q + 1) * C]
        for part in range(2):
            store(q // QUAD, part, q % QUAD, block[part * MY : (part + 1) * MY])


def y_inverse(load, count, table_ref, out_ref):
    rows = [
        jnp.concatenate([load(q // QUAD, part, q % QUAD) for q in range(count)], axis=1)
        for part in range(2)
    ]
    out_ref[...] = jnp.dot(
        table_ref[...], pieces(jnp.concatenate(rows, axis=0)), preferred_element_type=F32
    )


def place(part, pair):
    start = (part * QUAD + pair) * MY
    return slice(start, start + MY)


def spread_table(step):
    shape = (3 * C, SPAN * C)
    row = lax.broadcasted_iota(jnp.int32, shape, 0) & (C - 1)
    column = lax.broadcasted_iota(jnp.int32, shape, 1) // C + step * SPAN
    return jnp.where(row == column, 1.0, 0.0).astype(BF16)


def gather_table(step):
    shape = (SPAN * C, C)
    row = lax.broadcasted_iota(jnp.int32, shape, 0) // C + step * SPAN
    column = lax.broadcasted_iota(jnp.int32, shape, 1)
    return jnp.where(row == column, 1.0, 0.0).astype(BF16)


def walk(ref):
    mz, mx = ref.shape[1], ref.shape[2]
    for q in range(mz * mx):
        yield q // QUAD, q % QUAD, q // mx, q % mx


def pair_of(ref, kz, kx, tile):
    columns = slice(tile * 2 * C, (tile + 1) * 2 * C)
    return (
        ref[0, kz, kx, :, columns].astype(F32),
        ref[1, kz, kx, :, columns].astype(F32),
    )


def mix_kernel(data_ref, weight_ref, forward_ref, inverse_ref, modes_ref, out_ref, sum_ref):
    step = pl.program_id(0)
    count = weight_ref.shape[1] * weight_ref.shape[2]

    @pl.when(step == 0)
    def _():
        def store(group, part, pair, values):
            high = values.astype(BF16)
            rest = values - high.astype(F32)
            middle = rest.astype(BF16)
            low = (rest - middle.astype(F32)).astype(BF16)
            modes_ref[group, place(part, pair), :] = jnp.concatenate([high, middle, low], axis=1)

        y_forward(data_ref, forward_ref, store)
        sum_ref[...] = jnp.zeros_like(sum_ref)

    table = spread_table(step)
    spread = {}
    for group, pair, kz, kx in walk(weight_ref):
        if pair == 0:
            spread[group] = jnp.dot(modes_ref[group], table, preferred_element_type=F32)
        real = sum_ref[group, place(0, pair), :]
        imag = sum_ref[group, place(1, pair), :]
        for tile in range(SPAN // 2):
            columns = slice(tile * 2 * C, (tile + 1) * 2 * C)
            mode_re = spread[group][place(0, pair), columns]
            mode_im = spread[group][place(1, pair), columns]
            weight_re, weight_im = pair_of(weight_ref, kz, kx, tile)
            real += mode_re * weight_re - mode_im * weight_im
            imag += mode_re * weight_im + mode_im * weight_re
        sum_ref[group, place(0, pair), :] = real
        sum_ref[group, place(1, pair), :] = imag

    @pl.when(step == pl.num_programs(0) - 1)
    def _():
        def load(group, part, pair):
            values = sum_ref[group, place(part, pair), :]
            return values[:, :C] + values[:, C:]

        y_inverse(load, count, inverse_ref, out_ref)


def mix_back_kernel(
    data_ref, weight_ref, forward_ref, inverse_ref, modes_ref, out_ref, sum_ref, term_ref
):
    step = pl.program_id(0)
    count = weight_ref.shape[1] * weight_ref.shape[2]

    @pl.when(step == 0)
    def _():
        def store(group, part, pair, values):
            modes_ref[group, place(part, pair), :] = jnp.concatenate([values, values], axis=1)

        y_forward(data_ref, forward_ref, store)
        sum_ref[...] = jnp.zeros_like(sum_ref)

    table = gather_table(step)
    for group, pair, kz, kx in walk(weight_ref):
        mode_re = modes_ref[group, place(0, pair), :]
        mode_im = modes_ref[group, place(1, pair), :]
        for tile in range(SPAN // 2):
            columns = slice(tile * 2 * C, (tile + 1) * 2 * C)
            weight_re, weight_im = pair_of(weight_ref, kz, kx, tile)
            real = weight_re * mode_re + weight_im * mode_im
            imag = weight_re * mode_im - weight_im * mode_re
            term_ref[group, place(0, pair), columns] = real.astype(BF16)
            term_ref[group, place(1, pair), columns] = imag.astype(BF16)
        if pair == QUAD - 1:
            sum_ref[group] += jnp.dot(term_ref[group], table, preferred_element_type=F32)

    @pl.when(step == pl.num_programs(0) - 1)
    def _():
        load = lambda group, part, pair: sum_ref[group, place(part, pair), :]
        y_inverse(load, count, inverse_ref, out_ref)


def outer_kernel(alpha, modes_ref, back_ref, out_ref):
    table = spread_table(pl.program_id(0))
    spread = {}
    for group, pair, kz, kx in walk(out_ref):
        if pair == 0:
            spread[group] = jnp.dot(modes_ref[group], table, preferred_element_type=F32)
        back_re = back_ref[group, place(0, pair), :] * alpha
        back_im = back_ref[group, place(1, pair), :] * alpha
        for tile in range(SPAN // 2):
            columns = slice(tile * 2 * C, (tile + 1) * 2 * C)
            mode_re = spread[group][place(0, pair), columns]
            mode_im = spread[group][place(1, pair), columns]
            out_ref[0, kz, kx, :, columns] = mode_re * back_re + mode_im * back_im
            out_ref[1, kz, kx, :, columns] = mode_re * back_im - mode_im * back_re


def whole():
    return pl.BlockSpec(memory_space=pltpu.VMEM)


def params(mib):
    return pltpu.CompilerParams(vmem_limit_bytes=mib * MIB)


def cost(flops, moved):
    return pl.CostEstimate(flops=int(flops), bytes_accessed=int(moved), transcendentals=0)


def call(kernel, outs, args, scratch=(), mib=24, flops=0, moved=0):
    return pl.pallas_call(
        kernel,
        out_shape=[jax.ShapeDtypeStruct(*out) for out in outs],
        in_specs=[whole() for _ in args],
        out_specs=[whole() for _ in outs],
        scratch_shapes=list(scratch),
        compiler_params=params(mib),
        cost_estimate=cost(flops, moved),
    )(*args)


def full(shape):
    return pl.BlockSpec(shape, lambda step: (0,) * len(shape))


def channels(shape):
    return pl.BlockSpec(shape[:4] + (SPAN * C,), lambda step: (0, 0, 0, 0, step))


def per_mode(kernel, data, weight, forward, inverse, modes, scratch):
    _, mz, mx, _, _ = weight.shape
    groups = mz * mx // QUAD
    rows = 2 * QUAD * MY
    modes_shape = (groups, rows, modes[0])
    out_shape = (inverse.shape[0], mz * mx * C)
    return pl.pallas_call(
        kernel,
        grid=(C // SPAN,),
        in_specs=[
            full(data.shape),
            channels(weight.shape),
            full(forward.shape),
            full(inverse.shape),
        ],
        out_specs=[full(modes_shape), full(out_shape)],
        out_shape=[
            jax.ShapeDtypeStruct(modes_shape, modes[1]),
            jax.ShapeDtypeStruct(out_shape, F32),
        ],
        scratch_shapes=[pltpu.VMEM((groups, rows, width), kind) for width, kind in scratch],
        compiler_params=params(56),
        cost_estimate=cost(weight.size * 8, weight.size * 2),
    )(data, weight, forward, inverse)


def outer(modes, back, shape, alpha):
    return pl.pallas_call(
        functools.partial(outer_kernel, alpha),
        grid=(C // SPAN,),
        in_specs=[full(modes.shape), full(back.shape)],
        out_specs=channels(shape),
        out_shape=jax.ShapeDtypeStruct(shape, F32),
        compiler_params=params(24),
        cost_estimate=cost(math.prod(shape) * 4, math.prod(shape) * 4),
    )(modes, back)


def halos(turned):
    def shift(block, axis, step):
        count = lax.axis_size(axis)
        pairs = [(i, i + step) for i in range(count) if 0 <= i + step < count]
        return lax.ppermute(block, axis, pairs)

    xlo = shift(turned[-1], "gx", 1)
    xhi = shift(turned[0], "gx", -1)
    edge = lambda y: jnp.concatenate([xlo[None, y], turned[:, y], xhi[None, y]], axis=0)
    ylo = shift(edge(-1), "gy", 1)
    yhi = shift(edge(0), "gy", -1)
    return xlo, xhi, ylo, yhi


def conv(turned, rim, weight, flip):
    cx, cy, c, z = turned.shape
    return call(
        functools.partial(conv_kernel, flip),
        [((cx, c, cy * z), F32)],
        (turned, *rim, weight),
        [pltpu.VMEM((4 * c, (cy + 2) * z), BF16)],
        mib=32,
        flops=2 * 27 * c * c * cx * cy * z,
        moved=turned.size * 8,
    )[0]


def weight_grad(grad, turned, rim):
    cx, cy, c, z = turned.shape
    return call(
        weight_grad_kernel,
        [((14 * c, 2 * c), F32)],
        (grad, turned, *rim),
        [
            pltpu.VMEM((4 * c, (cy + 2) * z), BF16),
            pltpu.VMEM((cx * 3 * c, (cy + 2) * z), BF16),
            pltpu.VMEM((9 * c, 4 * c), F32),
        ],
        mib=32,
        flops=2 * 27 * c * c * cx * cy * z,
        moved=turned.size * 8,
    )[0]


def sum_everywhere(part):
    nx, ny = lax.axis_size("gx"), lax.axis_size("gy")

    def swap(block, axis):
        return lax.all_to_all(block, axis, split_axis=0, concat_axis=0, tiled=True)

    def everyone(block, count):
        return jnp.broadcast_to(block[None], (count, *block.shape))

    mine = swap(part.reshape(nx, -1, part.shape[1]), "gx").sum(0)
    mine = swap(everyone(mine, ny), "gy").sum(0)
    return swap(everyone(mine, nx), "gx").reshape(part.shape)


def body(state, cotangent, spectral_weight, stencil_weight, pointwise_weight):
    nx, ny = lax.axis_size("gx"), lax.axis_size("gy")
    c, cx, cy, z = state.shape
    _, mz, mx, _, _ = spectral_weight.shape
    wide_x, wide_y = cx * nx, cy * ny
    alpha = 1.0 / math.sqrt(wide_x * wide_y * z)
    beta = 1.0 / math.sqrt(2 * MX * MY * MZ)
    double = np.where(np.arange(MZ) == 0, 1.0, 2.0)
    ones = np.ones(MZ)
    z_state = jnp.asarray(z_forward_table(alpha * ones)(nx, mz))
    z_grad = jnp.asarray(z_forward_table(double)(nx, mz))
    z_spectral = jnp.asarray(z_inverse_table(nx, mz, beta * double))
    z_back = jnp.asarray(z_inverse_table(nx, mz, alpha * beta * ones))
    x_fwd, x_inv = (jnp.asarray(t) for t in x_tables(wide_x, mz))
    y_fwd, y_inv = (jnp.asarray(t) for t in y_tables(wide_y))
    lanes = cy * c
    x_rows = cx * 2 * mz

    def swap(block, axis):
        return lax.all_to_all(block, axis, split_axis=0, concat_axis=0, tiled=True)

    def x_stage(table, block, lead):
        flat = block.reshape(-1, lanes)
        got = call(
            x_kernel,
            [((table.shape[0], lanes), F32)],
            (table, flat),
            mib=16,
            flops=2 * table.size * lanes,
            moved=8 * flat.size,
        )[0]
        return got.reshape(lead, -1, lanes)

    def to_pencil(slab):
        block = swap(x_stage(x_fwd, swap(slab, "gx"), ny), "gy")
        block = block.reshape(ny, mx, 2, mz, cy, c).transpose(2, 0, 4, 3, 1, 5)
        return block.reshape(2 * wide_y, mz * mx * c)

    def to_slab(pencil):
        block = pencil.reshape(2, ny, cy, mz, mx, c).transpose(1, 4, 0, 3, 2, 5)
        block = swap(block.reshape(ny, mx * 2 * mz, lanes), "gy")
        return swap(x_stage(x_inv, block, nx), "gx")

    slab_shape = ((nx, x_rows, lanes), F32)
    turned_shape = ((cx, cy, c, z), BF16)

    conv_table, back_table = call(
        taps_kernel,
        [((9 * c, 4 * c), BF16)] * 2,
        (stencil_weight, pointwise_weight),
        [pltpu.VMEM((27 * c, c), F32)],
        moved=stencil_weight.size * 6,
    )
    turned, slab = call(
        functools.partial(prep_kernel, nx),
        [turned_shape, slab_shape],
        (state, z_state),
        flops=2 * 96 * state.size,
        moved=state.size * 5,
    )
    rim = halos(turned)
    pencil = to_pencil(slab)
    stencil = conv(turned, rim, conv_table, False)
    modes_in, pencil = per_mode(
        mix_kernel, pencil, spectral_weight, y_fwd, y_inv, (3 * c, BF16), [(2 * c, F32)]
    )
    slab = to_slab(pencil)
    output, grad, slab = call(
        functools.partial(gelu_kernel, nx),
        [((c, cx, cy, z), BF16), turned_shape, slab_shape],
        (stencil, slab, cotangent, z_spectral, z_grad),
        flops=2 * 192 * state.size,
        moved=state.size * 12,
    )
    grad_rim = halos(grad)
    pencil = to_pencil(slab)
    grad_taps = weight_grad(grad, turned, rim)
    back_modes, pencil = per_mode(
        mix_back_kernel,
        pencil,
        spectral_weight,
        y_fwd,
        y_inv,
        (2 * c, F32),
        [(c, F32), (SPAN * c, BF16)],
    )
    grad_modes = outer(modes_in, back_modes, spectral_weight.shape, alpha)
    stencil_back = conv(grad, grad_rim, back_table, True)
    slab = to_slab(pencil)
    grad_state = call(
        functools.partial(finish_kernel, nx),
        [((c, cx, cy, z), F32)],
        (stencil_back, slab, z_back),
        flops=2 * 96 * state.size,
        moved=state.size * 10,
    )[0]
    grad_stencil, grad_point = call(
        functools.partial(unpack_kernel, alpha),
        [((c, 27 * c), F32), ((c, c), F32)],
        (sum_everywhere(grad_taps),),
        [pltpu.VMEM((27 * c, c), F32)],
        moved=grad_taps.size * 8,
    )
    return (output, grad_state, grad_modes, grad_stencil, grad_point)


def solution(mesh):
    in_specs = (
        P(None, "gx", "gy", None),
        P(None, "gx", "gy", None),
        P(None, "gx", "gy", None, None),
        P(),
        P(),
    )
    out_specs = (
        P(None, "gx", "gy", None),
        P(None, "gx", "gy", None),
        P(None, "gx", "gy", None, None),
        P(),
        P(),
    )
    return jax.shard_map(body, mesh=mesh, in_specs=in_specs, out_specs=out_specs, check_vma=False)
```

time: 275 us -> 176 us (0.64)
  blocking collectives: 82.9 us -> 11.9 us
  Pallas kernels: 68 us -> 46.2 us
  local copies, waits for them, and re-layouts: 32.5 us -> 16.4 us
  waiting for transfers between devices: 26.3 us -> 40.7 us
  matrix products: 5.96 us -> 0 us
    all_gather x1 -> x0, blocking collectives: 71 us -> none  [sum_everywhere(): full = lax.all_gather(mine * scale, ('gx', 'gy'), axis=0, tiled=False)]
    pallas_call x3, Pallas kernels: 58 us -> 29.3 us  [the longest x2 21 us: per_mode(): pl.pallas_call(kernel, grid=(C // SPAN,), in_specs=[full(data.shape), cha...]
    all_to_all x7 -> x10, waiting for transfers between devices: 13 us -> 30.5 us  [swap(): return lax.all_to_all(block, axis, split_axis=0, concat_axis=0, tiled=True)]
    all_to_all x7 -> x10, starting transfers between devices: 29.1 us -> 38.8 us  [swap(): return lax.all_to_all(block, axis, split_axis=0, concat_axis=0, tiled=True)]
    all_to_all x2 -> x0, starting transfers between devices: 7.47 us -> none  [the longest x1 4.18 us: sum_everywhere(): lax.all_to_all(mine, 'gx', split_axis=0, concat_axis=0, tiled=True).sum(0)]
    pallas_call x6 -> x12, Pallas kernels: 10 us -> 16.9 us  [call(): pl.pallas_call(kernel, out_shape=[jax.ShapeDtypeStruct(*out) for out in o...]
    dot_general x4 -> x0, matrix products: 5.96 us -> none  [x_stage(): got = jnp.dot(table, flat, precision=lax.Precision.HIGHEST)]
    reshape x8 -> x0, local copies, waits for them, and re-layouts: 5.61 us -> none  [the longest x4 2.04 us: table_of(): return jnp.concatenate([tap.reshape(9 * c, 3 * c), own], axis=1)]
  transfers between devices with their start and end apart: 17 -> 18, of which waited for: 6 -> 9; matrix products, arithmetic and copies ran while one was open for 9% -> 5% of each run, Pallas kernels for 23% -> 24%
where the time goes in v2:
time: 176 us; the launch traced here: 174 us
  starting transfers between devices  57.3 us (33%)
  Pallas kernels  46.2 us (26%)
  waiting for transfers between devices  40.7 us (23%)
  local copies, waits for them, and re-layouts  16.4 us (9%)
  blocking collectives  11.9 us (7%)
    all_to_all x10, starting transfers between devices, swap(): return lax.all_to_all(block, axis, split_axis=0, concat_axis=0, tiled=True)  38.8 us
    all_to_all x10, waiting for transfers between devices, swap(): return lax.all_to_all(block, axis, split_axis=0, concat_axis=0, tiled=True)  30.5 us
    pallas_call x2, Pallas kernels, per_mode(): pl.pallas_call(kernel, grid=(C // SPAN,), in_specs=[full(data.shape), cha...  21 us
    ppermute x8, starting transfers between devices, shift(): return lax.ppermute(block, axis, pairs)  18.5 us
    pallas_call x12, Pallas kernels, call(): pl.pallas_call(kernel, out_shape=[jax.ShapeDtypeStruct(*out) for out in o...  16.9 us
    all_to_all x1, blocking collectives, swap(): return lax.all_to_all(block, axis, split_axis=0, concat_axis=0, tiled=True)  11.9 us
    ppermute x8, waiting for transfers between devices, shift(): return lax.ppermute(block, axis, pairs)  10.2 us
    pallas_call x1, Pallas kernels, outer(): pl.pallas_call(functools.partial(outer_kernel, alpha), grid=(C // SPAN,),...  8.34 us
  transfers between devices with their start and end apart: 18, of which 9 were waited for; matrix products, arithmetic and copies ran while one was open for 5% of the time, Pallas kernels for 24%

profile of v2, /device:TPU:0, one launch (start us, length us, event | category | flops | bytes accessed | tf_op | source)
XLA Modules:
  0.0 173.7 jit_solution(2853812107111224299)
XLA Ops:
  2.9 11.9 %all_to_all.55 = f32[8,16,512]{2,1,0:T(8,128)S(1)} all-to-all(f32[8,16,512]{2,1,0:T(8,128)S(1)} %get-tuple-element.20), channel_id=1, replica_groups=mesh['gx'=8,'gy'=4] {'gx'}, dimensions={0} | all-to-all | bytes 524288 | tf_op jit(solution)/shard_map/all_to_all | solution.py:569
  16.6 4.9 %all-to-all-start.1 = ((f32[4,32,512]{2,1,0:T(8,128)}), f32[4,32,512]{2,1,0:T(8,128)S(1)}, u32[]{:S(2)}, u32[]{:S(2)}) async-start(f32[4,32,512]{2,1,0:T(8,128)} %bitcast.5), calls=%async_computation.1 | async-start | bytes 524288 | tf_op jit(solution)/shard_map/all_to_all | solution.py:569
  22.8 3.0 %collective-permute-start = (bf16[8,64,128]{2,1,0:T(8,128)(2,1)S(1)}, bf16[8,64,128]{2,1,0:T(8,128)(2,1)S(1)}, u32[]{:S(2)}, u32[]{:S(2)}) collective-permute-start(bf16[8,64,128]{2,1,0:T(8,128)(2,1)S(1)} %get-tuple-element.38), channel_id=1, source_target_pairs={{0,4},{4,8},{8,12},{12,16},{16,20},{20,24},{24,28},{1,5},{5,9},{9,... | collective-permute-start | bytes 393224 | tf_op jit(solution)/shard_map/ppermute | solution.py:496
  25.9 3.8 %all-to-all-done.1 = f32[4,32,512]{2,1,0:T(8,128)S(1)} async-done(((f32[4,32,512]{2,1,0:T(8,128)}), f32[4,32,512]{2,1,0:T(8,128)S(1)}, u32[]{:S(2)}, u32[]{:S(2)}) %all-to-all-start.1) | async-done | bytes 262176 | tf_op jit(solution)/shard_map/all_to_all | solution.py:569
  31.1 10.4 %shard_map.168 = (bf16[4,256,192]{2,1,0:T(8,128)(2,1)}, f32[64,1024]{1,0:T(8,128)}) custom-call(f32[64,1024]{1,0:T(8,128)} %reshape.69.data_ref, bf16[2,2,8,32,4096]{4,3,2,1,0:T(8,128)(2,1)} %weight_ref.3, bf16[64,192]{1,0:T(8,128)(2,1)} %constant.24.clone.forward_ref, bf16[64,192]{1,0:T(8,128)(2,1)} %constant.25.clone.inverse_ref), custom_call_target="tpu_custom_call" | custom-call | flops 33554432 | bytes 8388608 | tf_op jit(solution)/shard_map/pallas_call | solution.py:460
  43.6 3.4 %all-to-all-start.2 = ((f32[4,32,512]{2,1,0:T(8,128)}), f32[4,32,512]{2,1,0:T(8,128)S(1)}, u32[]{:S(2)}, u32[]{:S(2)}) async-start(f32[4,32,512]{2,1,0:T(8,128)} %reshape.71), calls=%async_computation.2 | async-start | bytes 524288 | tf_op jit(solution)/shard_map/all_to_all | solution.py:569
  47.1 3.9 %collective-permute-start.2 = (bf16[6,64,128]{2,1,0:T(8,128)(2,1)S(1)}, bf16[6,64,128]{2,1,0:T(8,128)(2,1)S(1)}, u32[]{:S(2)}, u32[]{:S(2)}) collective-permute-start(bf16[6,64,128]{2,1,0:T(8,128)(2,1)S(1)} %pad_maximum_fusion), channel_id=1, source_target_pairs={{0,1},{1,2},{2,3},{4,5},{5,6},{6,7},{8,9},{9,10},{10,11},{12,13},{... | collective-permute-start | bytes 294920 | tf_op jit(solution)/shard_map/ppermute | solution.py:496
  51.0 2.9 %all-to-all-done.2 = f32[4,32,512]{2,1,0:T(8,128)S(1)} async-done(((f32[4,32,512]{2,1,0:T(8,128)}), f32[4,32,512]{2,1,0:T(8,128)S(1)}, u32[]{:S(2)}, u32[]{:S(2)}) %all-to-all-start.2) | async-done | bytes 262176 | tf_op jit(solution)/shard_map/all_to_all | solution.py:569
  54.8 3.6 %all-to-all-start.3 = ((f32[8,16,512]{2,1,0:T(8,128)}), f32[8,16,512]{2,1,0:T(8,128)S(1)}, u32[]{:S(2)}, u32[]{:S(2)}) async-start(f32[8,16,512]{2,1,0:T(8,128)} %bitcast.9), calls=%async_computation.3 | async-start | bytes 524288 | tf_op jit(solution)/shard_map/all_to_all | solution.py:569
  61.1 4.5 %collective-permute-done.3.yhi_ref = bf16[6,64,128]{2,1,0:T(8,128)(2,1)S(1)} collective-permute-done((bf16[6,64,128]{2,1,0:T(8,128)(2,1)S(1)}, bf16[6,64,128]{2,1,0:T(8,128)(2,1)S(1)}, u32[]{:S(2)}, u32[]{:S(2)}) %collective-permute-start.3) | collective-permute-done | bytes 98336 | tf_op jit(solution)/shard_map/ppermute | solution.py:496
  65.5 1.9 %shard_map.166.stencil_ref = f32[4,64,1024]{2,1,0:T(8,128)S(1)} custom-call(bf16[4,8,64,128]{3,2,1,0:T(8,128)(2,1)S(1)} %get-tuple-element.18.body_ref, bf16[8,64,128]{2,1,0:T(8,128)(2,1)S(1)} %collective-permute-done.xlo_ref, bf16[8,64,128]{2,1,0:T(8,128)(2,1)S(1)} %collective-permute-done.1.xhi_ref, ...), custom_call_target="tpu_custom_call" | custom-call | flops 905969664 | bytes 2097152 | tf_op jit(solution)/shard_map/pallas_call | solution.py:435
  68.1 2.3 %shard_map.170 = (bf16[64,4,8,128]{3,2,1,0:T(8,128)(2,1)}, bf16[4,8,64,128]{3,2,1,0:T(8,128)(2,1)S(1)}, f32[8,16,512]{2,1,0:T(8,128)}) custom-call(f32[4,64,1024]{2,1,0:T(8,128)S(1)} %shard_map.166.stencil_ref, f32[8,16,512]{2,1,0:T(8,128)S(1)} %all-to-all-done.3.slab_ref, bf16[64,4,8,128]{3,2,1,0:T(8,128)(2,1)S(1)} %copy-done, ...), custom_call_target="tpu_custom_call" | custom-call | flops 100663296 | bytes 3145728 | tf_op jit(solution)/shard_map/pallas_call | solution.py:435
  70.4 3.8 %all-to-all-start.4 = ((f32[8,16,512]{2,1,0:T(8,128)}), f32[8,16,512]{2,1,0:T(8,128)S(1)}, u32[]{:S(2)}, u32[]{:S(2)}) async-start(f32[8,16,512]{2,1,0:T(8,128)} %get-tuple-element.25), calls=%async_computation.4 | async-start | bytes 524288 | tf_op jit(solution)/shard_map/all_to_all | solution.py:569
  76.2 3.0 %shard_map.177 = f32[896,128]{1,0:T(8,128)} custom-call(bf16[4,8,64,128]{3,2,1,0:T(8,128)(2,1)S(1)} %get-tuple-element.23.body_ref.grad_ref, bf16[4,8,64,128]{3,2,1,0:T(8,128)(2,1)S(1)} %copy-done.8, bf16[8,64,128]{2,1,0:T(8,128)(2,1)S(1)} %collective-permute-done.xlo_ref, bf16[8,64,128]{2,1,0:T(8,128)(2,1)S(1)} %collective-permute-done.1.xhi_ref, ...), custom_call_target="tpu_custom_call" | custom-call | flops 905969664 | bytes 2097152 | tf_op jit(solution)/shard_map/pallas_call | solution.py:435
  79.2 2.0 %all-to-all-done.4 = f32[8,16,512]{2,1,0:T(8,128)S(1)} async-done(((f32[8,16,512]{2,1,0:T(8,128)}), f32[8,16,512]{2,1,0:T(8,128)S(1)}, u32[]{:S(2)}, u32[]{:S(2)}) %all-to-all-start.4) | async-done | bytes 262176 | tf_op jit(solution)/shard_map/all_to_all | solution.py:569
  81.2 3.5 %all-to-all-start.8 = ((f32[8,112,128]{2,1,0:T(8,128)}), f32[8,112,128]{2,1,0:T(8,128)S(1)}, u32[]{:S(2)}, u32[]{:S(2)}) async-start(f32[8,112,128]{2,1,0:T(8,128)} %bitcast.20), calls=%async_computation.8 | async-start | bytes 917504 | tf_op jit(solution)/shard_map/all_to_all | solution.py:540
  85.6 8.0 %all-to-all-done.8 = f32[8,112,128]{2,1,0:T(8,128)S(1)} async-done(((f32[8,112,128]{2,1,0:T(8,128)}), f32[8,112,128]{2,1,0:T(8,128)S(1)}, u32[]{:S(2)}, u32[]{:S(2)}) %all-to-all-start.8) | async-done | bytes 458784 | tf_op jit(solution)/shard_map/all_to_all | solution.py:540
  93.6 3.4 %all-to-all-start.5 = ((f32[4,32,512]{2,1,0:T(8,128)}), f32[4,32,512]{2,1,0:T(8,128)S(1)}, u32[]{:S(2)}, u32[]{:S(2)}) async-start(f32[4,32,512]{2,1,0:T(8,128)} %bitcast.15), calls=%async_computation.5 | async-start | bytes 524288 | tf_op jit(solution)/shard_map/all_to_all | solution.py:569
  97.1 6.7 %all-to-all-done.5 = f32[4,32,512]{2,1,0:T(8,128)S(1)} async-done(((f32[4,32,512]{2,1,0:T(8,128)}), f32[4,32,512]{2,1,0:T(8,128)S(1)}, u32[]{:S(2)}, u32[]{:S(2)}) %all-to-all-start.5) | async-done | bytes 262176 | tf_op jit(solution)/shard_map/all_to_all | solution.py:569
  104.5 3.6 %all-to-all-start.9 = ((f32[4,112,128]{2,1,0:T(8,128)}), f32[4,112,128]{2,1,0:T(8,128)S(1)}, u32[]{:S(2)}, u32[]{:S(2)}) async-start(f32[4,112,128]{2,1,0:T(8,128)} %broadcast_in_dim.4), calls=%async_computation.9 | async-start | bytes 458752 | tf_op jit(solution)/shard_map/all_to_all | solution.py:540
  109.4 10.6 %shard_map.173 = (f32[4,256,128]{2,1,0:T(8,128)}, f32[64,1024]{1,0:T(8,128)}) custom-call(f32[64,1024]{1,0:T(8,128)} %reshape.77.data_ref, bf16[2,2,8,32,4096]{4,3,2,1,0:T(8,128)(2,1)} %weight_ref.3, bf16[64,192]{1,0:T(8,128)(2,1)} %constant.24.clone.forward_ref, bf16[64,192]{1,0:T(8,128)(2,1)} %constant.25.clone.inverse_ref), custom_call_target="tpu_custom_call" | custom-call | flops 33554432 | bytes 8388608 | tf_op jit(solution)/shard_map/pallas_call | solution.py:460
  122.1 4.9 %all-to-all-start.6 = ((f32[4,32,512]{2,1,0:T(8,128)}), f32[4,32,512]{2,1,0:T(8,128)S(1)}, u32[]{:S(2)}, u32[]{:S(2)}) async-start(f32[4,32,512]{2,1,0:T(8,128)} %reshape.79), calls=%async_computation.6 | async-start | bytes 524288 | tf_op jit(solution)/shard_map/all_to_all | solution.py:569
  128.3 3.0 %collective-permute-start.4 = (bf16[8,64,128]{2,1,0:T(8,128)(2,1)S(1)}, bf16[8,64,128]{2,1,0:T(8,128)(2,1)S(1)}, u32[]{:S(2)}, u32[]{:S(2)}) collective-permute-start(bf16[8,64,128]{2,1,0:T(8,128)(2,1)S(1)} %get-tuple-element.34), channel_id=1, source_target_pairs={{0,4},{4,8},{8,12},{12,16},{16,20},{20,24},{24,28},{1,5},{5,9},{9,... | collective-permute-start | bytes 393224 | tf_op jit(solution)/shard_map/ppermute | solution.py:496
  131.4 2.4 %all-to-all-done.6 = f32[4,32,512]{2,1,0:T(8,128)S(1)} async-done(((f32[4,32,512]{2,1,0:T(8,128)}), f32[4,32,512]{2,1,0:T(8,128)S(1)}, u32[]{:S(2)}, u32[]{:S(2)}) %all-to-all-start.6) | async-done | bytes 262176 | tf_op jit(solution)/shard_map/all_to_all | solution.py:569
  134.6 4.4 %all-to-all-start.10 = ((f32[8,112,128]{2,1,0:T(8,128)}), f32[8,112,128]{2,1,0:T(8,128)S(1)}, u32[]{:S(2)}, u32[]{:S(2)}) async-start(f32[8,112,128]{2,1,0:T(8,128)} %broadcast_in_dim.5), calls=%async_computation.10 | async-start | bytes 917504 | tf_op jit(solution)/shard_map/all_to_all | solution.py:540
  139.0 3.4 %collective-permute-start.6 = (bf16[6,64,128]{2,1,0:T(8,128)(2,1)S(1)}, bf16[6,64,128]{2,1,0:T(8,128)(2,1)S(1)}, u32[]{:S(2)}, u32[]{:S(2)}) collective-permute-start(bf16[6,64,128]{2,1,0:T(8,128)(2,1)S(1)} %pad_maximum_fusion.2), channel_id=1, source_target_pairs={{0,1},{1,2},{2,3},{4,5},{5,6},{6,7},{8,9},{9,10},{10,11},{12,13},{... | collective-permute-start | bytes 294920 | tf_op jit(solution)/shard_map/ppermute | solution.py:496
  143.3 4.7 %all-to-all-done.10 = f32[8,112,128]{2,1,0:T(8,128)S(1)} async-done(((f32[8,112,128]{2,1,0:T(8,128)}), f32[8,112,128]{2,1,0:T(8,128)S(1)}, u32[]{:S(2)}, u32[]{:S(2)}) %all-to-all-start.10) | async-done | bytes 458784 | tf_op jit(solution)/shard_map/all_to_all | solution.py:540
  148.0 3.4 %all-to-all-start.7 = ((f32[8,16,512]{2,1,0:T(8,128)}), f32[8,16,512]{2,1,0:T(8,128)S(1)}, u32[]{:S(2)}, u32[]{:S(2)}) async-start(f32[8,16,512]{2,1,0:T(8,128)} %bitcast.19), calls=%async_computation.7 | async-start | bytes 524288 | tf_op jit(solution)/shard_map/all_to_all | solution.py:569
  152.8 5.7 %collective-permute-done.7.yhi_ref = bf16[6,64,128]{2,1,0:T(8,128)(2,1)S(1)} collective-permute-done((bf16[6,64,128]{2,1,0:T(8,128)(2,1)S(1)}, bf16[6,64,128]{2,1,0:T(8,128)(2,1)S(1)}, u32[]{:S(2)}, u32[]{:S(2)}) %collective-permute-start.7) | collective-permute-done | bytes 98336 | tf_op jit(solution)/shard_map/ppermute | solution.py:496
  159.4 2.0 %shard_map.171.stencil_ref = f32[4,64,1024]{2,1,0:T(8,128)S(1)} custom-call(bf16[4,8,64,128]{3,2,1,0:T(8,128)(2,1)S(1)} %get-tuple-element.23.body_ref.grad_ref, bf16[8,64,128]{2,1,0:T(8,128)(2,1)S(1)} %collective-permute-done.4.xlo_ref, bf16[8,64,128]{2,1,0:T(8,128)(2,1)S(1)} %collective-permute-done.5.xhi_ref, ...), custom_call_target="tpu_custom_call" | custom-call | flops 905969664 | bytes 2097152 | tf_op jit(solution)/shard_map/pallas_call | solution.py:435
  162.4 8.3 %shard_map.176 = f32[2,2,8,32,4096]{4,3,2,1,0:T(8,128)} custom-call(bf16[4,256,192]{2,1,0:T(8,128)(2,1)S(1)} %copy-done.1, f32[4,256,128]{2,1,0:T(8,128)S(1)} %copy-done.2), custom_call_target="tpu_custom_call" | custom-call | flops 16777216 | bytes 16777216 | tf_op jit(solution)/shard_map/pallas_call | solution.py:481
  170.8 1.5 shard_map.178
  (86 shorter events, 28.0 us)
Async XLA Ops:
  0.6 1.0 copy-start.3
  2.4 51.5 %copy-start.4 = (bf16[128,384]{1,0:T(8,128)(2,1)S(1)}, bf16[128,384]{1,0:T(8,128)(2,1)}, u32[]{:S(2)}) copy-start(bf16[128,384]{1,0:T(8,128)(2,1)} %constant.23.clone.table_ref) | copy-start | bytes 294916
  2.4 57.3 %copy-start.9 = (bf16[64,1728]{1,0:T(8,128)(2,1)S(1)}, bf16[64,1728]{1,0:T(8,128)(2,1)}, u32[]{:S(2)}) copy-start(bf16[64,1728]{1,0:T(8,128)(2,1)} %taps_ref.1) | copy-start | bytes 663556
  2.4 57.3 %copy-start.14 = (bf16[64,64]{1,0:T(8,128)(2,1)S(1)}, bf16[64,64]{1,0:T(8,128)(2,1)}, u32[]{:S(2)}) copy-start(bf16[64,64]{1,0:T(8,128)(2,1)} %point_ref.1) | copy-start | bytes 24580
  2.4 65.6 %copy-start = (bf16[64,4,8,128]{3,2,1,0:T(8,128)(2,1)S(1)}, bf16[64,4,8,128]{3,2,1,0:T(8,128)(2,1)}, u32[]{:S(2)}) copy-start(bf16[64,4,8,128]{3,2,1,0:T(8,128)(2,1)} %cot_ref.1) | copy-start | bytes 1572868
  2.4 65.6 %copy-start.11 = (bf16[96,128]{1,0:T(8,128)(2,1)S(1)}, bf16[96,128]{1,0:T(8,128)(2,1)}, u32[]{:S(2)}) copy-start(bf16[96,128]{1,0:T(8,128)(2,1)} %constant.20.clone.inverse_ref) | copy-start | bytes 73732
  2.4 65.6 %copy-start.12 = (bf16[96,128]{1,0:T(8,128)(2,1)S(1)}, bf16[96,128]{1,0:T(8,128)(2,1)}, u32[]{:S(2)}) copy-start(bf16[96,128]{1,0:T(8,128)(2,1)} %constant.19.clone.forward_ref) | copy-start | bytes 73732
  2.4 82.2 %copy-start.6 = (bf16[128,384]{1,0:T(8,128)(2,1)S(1)}, bf16[128,384]{1,0:T(8,128)(2,1)}, u32[]{:S(2)}) copy-start(bf16[128,384]{1,0:T(8,128)(2,1)} %constant.22.clone.table_ref) | copy-start | bytes 294916
  2.9 64.5 %copy-start.7 = (bf16[4,8,64,128]{3,2,1,0:T(8,128)(2,1)}, bf16[4,8,64,128]{3,2,1,0:T(8,128)(2,1)S(1)}, u32[]{:S(2)}) copy-start(bf16[4,8,64,128]{3,2,1,0:T(8,128)(2,1)S(1)} %get-tuple-element.18.body_ref) | copy-start | bytes 1572868
  16.6 13.1 %all-to-all-start.1 = ((f32[4,32,512]{2,1,0:T(8,128)}), f32[4,32,512]{2,1,0:T(8,128)S(1)}, u32[]{:S(2)}, u32[]{:S(2)}) async-start(f32[4,32,512]{2,1,0:T(8,128)} %bitcast.5), calls=%async_computation.1 | async-start | bytes 524288 | tf_op jit(solution)/shard_map/all_to_all | solution.py:569
  21.5 25.5 %collective-permute-start.1 = (bf16[8,64,128]{2,1,0:T(8,128)(2,1)S(1)}, bf16[8,64,128]{2,1,0:T(8,128)(2,1)S(1)}, u32[]{:S(2)}, u32[]{:S(2)}) collective-permute-start(bf16[8,64,128]{2,1,0:T(8,128)(2,1)S(1)} %get-tuple-element.37), channel_id=1, source_target_pairs={{4,0},{8,4},{12,8},{16,12},{20,16},{24,20},{28,24},{5,1},{9,5},{13... | collective-permute-start | bytes 393224 | tf_op jit(solution)/shard_map/ppermute | solution.py:496
  22.8 24.2 %collective-permute-start = (bf16[8,64,128]{2,1,0:T(8,128)(2,1)S(1)}, bf16[8,64,128]{2,1,0:T(8,128)(2,1)S(1)}, u32[]{:S(2)}, u32[]{:S(2)}) collective-permute-start(bf16[8,64,128]{2,1,0:T(8,128)(2,1)S(1)} %get-tuple-element.38), channel_id=1, source_target_pairs={{0,4},{4,8},{8,12},{12,16},{16,20},{20,24},{24,28},{1,5},{5,9},{9,... | collective-permute-start | bytes 393224 | tf_op jit(solution)/shard_map/ppermute | solution.py:496
  43.6 10.3 %all-to-all-start.2 = ((f32[4,32,512]{2,1,0:T(8,128)}), f32[4,32,512]{2,1,0:T(8,128)S(1)}, u32[]{:S(2)}, u32[]{:S(2)}) async-start(f32[4,32,512]{2,1,0:T(8,128)} %reshape.71), calls=%async_computation.2 | async-start | bytes 524288 | tf_op jit(solution)/shard_map/all_to_all | solution.py:569
  47.1 14.0 %collective-permute-start.2 = (bf16[6,64,128]{2,1,0:T(8,128)(2,1)S(1)}, bf16[6,64,128]{2,1,0:T(8,128)(2,1)S(1)}, u32[]{:S(2)}, u32[]{:S(2)}) collective-permute-start(bf16[6,64,128]{2,1,0:T(8,128)(2,1)S(1)} %pad_maximum_fusion), channel_id=1, source_target_pairs={{0,1},{1,2},{2,3},{4,5},{5,6},{6,7},{8,9},{9,10},{10,11},{12,13},{... | collective-permute-start | bytes 294920 | tf_op jit(solution)/shard_map/ppermute | solution.py:496
  54.8 13.2 %all-to-all-start.3 = ((f32[8,16,512]{2,1,0:T(8,128)}), f32[8,16,512]{2,1,0:T(8,128)S(1)}, u32[]{:S(2)}, u32[]{:S(2)}) async-start(f32[8,16,512]{2,1,0:T(8,128)} %bitcast.9), calls=%async_computation.3 | async-start | bytes 524288 | tf_op jit(solution)/shard_map/all_to_all | solution.py:569
  58.4 7.1 %collective-permute-start.3 = (bf16[6,64,128]{2,1,0:T(8,128)(2,1)S(1)}, bf16[6,64,128]{2,1,0:T(8,128)(2,1)S(1)}, u32[]{:S(2)}, u32[]{:S(2)}) collective-permute-start(bf16[6,64,128]{2,1,0:T(8,128)(2,1)S(1)} %pad_maximum_fusion.1), channel_id=1, source_target_pairs={{1,0},{2,1},{3,2},{5,4},{6,5},{7,6},{9,8},{10,9},{11,10},{13,12},{... | collective-permute-start | bytes 294920 | tf_op jit(solution)/shard_map/ppermute | solution.py:496
  65.5 95.9 %copy-start.1 = (bf16[4,256,192]{2,1,0:T(8,128)(2,1)S(1)}, bf16[4,256,192]{2,1,0:T(8,128)(2,1)}, u32[]{:S(2)}) copy-start(bf16[4,256,192]{2,1,0:T(8,128)(2,1)} %get-tuple-element.27.modes_ref) | copy-start | bytes 1179652
  70.4 10.8 %all-to-all-start.4 = ((f32[8,16,512]{2,1,0:T(8,128)}), f32[8,16,512]{2,1,0:T(8,128)S(1)}, u32[]{:S(2)}, u32[]{:S(2)}) async-start(f32[8,16,512]{2,1,0:T(8,128)} %get-tuple-element.25), calls=%async_computation.4 | async-start | bytes 524288 | tf_op jit(solution)/shard_map/all_to_all | solution.py:569
  74.2 1.0 copy-start.8
  81.2 12.5 %all-to-all-start.8 = ((f32[8,112,128]{2,1,0:T(8,128)}), f32[8,112,128]{2,1,0:T(8,128)S(1)}, u32[]{:S(2)}, u32[]{:S(2)}) async-start(f32[8,112,128]{2,1,0:T(8,128)} %bitcast.20), calls=%async_computation.8 | async-start | bytes 917504 | tf_op jit(solution)/shard_map/all_to_all | solution.py:540
  93.6 10.2 %all-to-all-start.5 = ((f32[4,32,512]{2,1,0:T(8,128)}), f32[4,32,512]{2,1,0:T(8,128)S(1)}, u32[]{:S(2)}, u32[]{:S(2)}) async-start(f32[4,32,512]{2,1,0:T(8,128)} %bitcast.15), calls=%async_computation.5 | async-start | bytes 524288 | tf_op jit(solution)/shard_map/all_to_all | solution.py:569
  104.5 17.6 %all-to-all-start.9 = ((f32[4,112,128]{2,1,0:T(8,128)}), f32[4,112,128]{2,1,0:T(8,128)S(1)}, u32[]{:S(2)}, u32[]{:S(2)}) async-start(f32[4,112,128]{2,1,0:T(8,128)} %broadcast_in_dim.4), calls=%async_computation.9 | async-start | bytes 458752 | tf_op jit(solution)/shard_map/all_to_all | solution.py:540
  109.4 62.9 %copy-start.10 = (bf16[96,128]{1,0:T(8,128)(2,1)S(1)}, bf16[96,128]{1,0:T(8,128)(2,1)}, u32[]{:S(2)}) copy-start(bf16[96,128]{1,0:T(8,128)(2,1)} %constant.21.clone.inverse_ref) | copy-start | bytes 73732
  122.1 11.7 %all-to-all-start.6 = ((f32[4,32,512]{2,1,0:T(8,128)}), f32[4,32,512]{2,1,0:T(8,128)S(1)}, u32[]{:S(2)}, u32[]{:S(2)}) async-start(f32[4,32,512]{2,1,0:T(8,128)} %reshape.79), calls=%async_computation.6 | async-start | bytes 524288 | tf_op jit(solution)/shard_map/all_to_all | solution.py:569
  127.0 11.9 %collective-permute-start.5 = (bf16[8,64,128]{2,1,0:T(8,128)(2,1)S(1)}, bf16[8,64,128]{2,1,0:T(8,128)(2,1)S(1)}, u32[]{:S(2)}, u32[]{:S(2)}) collective-permute-start(bf16[8,64,128]{2,1,0:T(8,128)(2,1)S(1)} %get-tuple-element.33), channel_id=1, source_target_pairs={{4,0},{8,4},{12,8},{16,12},{20,16},{24,20},{28,24},{5,1},{9,5},{13... | collective-permute-start | bytes 393224 | tf_op jit(solution)/shard_map/ppermute | solution.py:496
  128.3 10.6 %collective-permute-start.4 = (bf16[8,64,128]{2,1,0:T(8,128)(2,1)S(1)}, bf16[8,64,128]{2,1,0:T(8,128)(2,1)S(1)}, u32[]{:S(2)}, u32[]{:S(2)}) collective-permute-start(bf16[8,64,128]{2,1,0:T(8,128)(2,1)S(1)} %get-tuple-element.34), channel_id=1, source_target_pairs={{0,4},{4,8},{8,12},{12,16},{16,20},{20,24},{24,28},{1,5},{5,9},{9,... | collective-permute-start | bytes 393224 | tf_op jit(solution)/shard_map/ppermute | solution.py:496
  134.6 13.4 %all-to-all-start.10 = ((f32[8,112,128]{2,1,0:T(8,128)}), f32[8,112,128]{2,1,0:T(8,128)S(1)}, u32[]{:S(2)}, u32[]{:S(2)}) async-start(f32[8,112,128]{2,1,0:T(8,128)} %broadcast_in_dim.5), calls=%async_computation.10 | async-start | bytes 917504 | tf_op jit(solution)/shard_map/all_to_all | solution.py:540
  139.0 13.7 %collective-permute-start.6 = (bf16[6,64,128]{2,1,0:T(8,128)(2,1)S(1)}, bf16[6,64,128]{2,1,0:T(8,128)(2,1)S(1)}, u32[]{:S(2)}, u32[]{:S(2)}) collective-permute-start(bf16[6,64,128]{2,1,0:T(8,128)(2,1)S(1)} %pad_maximum_fusion.2), channel_id=1, source_target_pairs={{0,1},{1,2},{2,3},{4,5},{5,6},{6,7},{8,9},{9,10},{10,11},{12,13},{... | collective-permute-start | bytes 294920 | tf_op jit(solution)/shard_map/ppermute | solution.py:496
  148.0 24.3 %all-to-all-start.7 = ((f32[8,16,512]{2,1,0:T(8,128)}), f32[8,16,512]{2,1,0:T(8,128)S(1)}, u32[]{:S(2)}, u32[]{:S(2)}) async-start(f32[8,16,512]{2,1,0:T(8,128)} %bitcast.19), calls=%async_computation.7 | async-start | bytes 524288 | tf_op jit(solution)/shard_map/all_to_all | solution.py:569
  151.4 7.0 %collective-permute-start.7 = (bf16[6,64,128]{2,1,0:T(8,128)(2,1)S(1)}, bf16[6,64,128]{2,1,0:T(8,128)(2,1)S(1)}, u32[]{:S(2)}, u32[]{:S(2)}) collective-permute-start(bf16[6,64,128]{2,1,0:T(8,128)(2,1)S(1)} %pad_maximum_fusion.3), channel_id=1, source_target_pairs={{1,0},{2,1},{3,2},{5,4},{6,5},{7,6},{9,8},{10,9},{11,10},{13,12},{... | collective-permute-start | bytes 294920 | tf_op jit(solution)/shard_map/ppermute | solution.py:496
  158.5 1.0 copy-start.16
  161.4 1.0 copy-start.2
  (5 other events, 3.9 us)

commit v3 on v2

--- a/solution.py
+++ b/solution.py
@@ -208,6 +208,7 @@
     for k in range(5):
         row = (9 + k) * c
         out_ref[row : row + c] = jnp.concatenate(last[2 * k : 2 * k + 2], axis=1)
+    out_ref[14 * c :] = jnp.zeros((2 * c, 2 * c), F32)
 
 
 def gelu_kernel(
@@ -239,7 +240,18 @@
 
 
 def x_kernel(table_ref, data_ref, out_ref):
-    out_ref[...] = jnp.dot(table_ref[...], pieces(data_ref[...]), preferred_element_type=F32)
+    data = data_ref[...].astype(F32)
+    lanes = data.shape[2]
+    rows = table_ref.shape[1] // (3 * data.shape[0])
+    flat = pieces(data[:, :rows].reshape(-1, lanes))
+    got = jnp.dot(table_ref[...], flat, preferred_element_type=F32).astype(out_ref.dtype)
+    count = got.shape[0] // out_ref.shape[0]
+    for owner in range(out_ref.shape[0]):
+        out_ref[owner, :count] = got[owner * count : (owner + 1) * count]
+    if data.shape[1] > rows:
+        extra = data[:, rows:].sum(0)
+        for owner in range(out_ref.shape[0]):
+            out_ref[owner, count:] = extra
 
 
 def taps_kernel(taps_ref, point_ref, forward_ref, back_ref, turned_ref):
@@ -257,7 +269,13 @@
     back_ref[4 * C : 5 * C, 3 * C :] = point.T.astype(BF16)
 
 
-def unpack_kernel(scale, packed_ref, taps_ref, point_ref, turned_ref):
+def unpack_kernel(scale, skip, message_ref, taps_ref, point_ref, packed_ref, turned_ref):
+    devices, rows, lanes = message_ref.shape
+    per, tiles_in = rows - skip, lanes // 128
+    for owner in range(devices):
+        for tile in range(tiles_in):
+            row = (owner * tiles_in + tile) * per
+            packed_ref[row : row + per] = message_ref[owner, skip:, tile * 128 : (tile + 1) * 128]
     for tap in range(27):
         group, e = tap // 3, tap % 3
         if e < 2:
@@ -273,20 +291,28 @@
 
 
 QUAD = 4
-SPAN = 8
+SPAN = 8 * C
 
 
 def y_forward(data_ref, table_ref, store):
-    got = jnp.dot(table_ref[...], pieces(data_ref[...]), preferred_element_type=F32)
+    data = pieces(data_ref[...].astype(F32))
+    got = jnp.dot(table_ref[...], data, preferred_element_type=F32)
     for q in range(got.shape[1] // C):
         block = got[:, q * C : (q + 1) * C]
         for part in range(2):
             store(q // QUAD, part, q % QUAD, block[part * MY : (part + 1) * MY])
 
 
-def y_inverse(load, count, table_ref, out_ref):
+def y_inverse(sum_ref, table_ref, out_ref):
     rows = [
-        jnp.concatenate([load(q // QUAD, part, q % QUAD) for q in range(count)], axis=1)
+        jnp.concatenate(
+            [
+                sum_ref[group, place(part, pair), :]
+                for group in range(sum_ref.shape[0])
+                for pair in range(QUAD)
+            ],
+            axis=1,
+        )
         for part in range(2)
     ]
     out_ref[...] = jnp.dot(
@@ -299,37 +325,40 @@
     return slice(start, start + MY)
 
 
-def spread_table(step):
-    shape = (3 * C, SPAN * C)
-    row = lax.broadcasted_iota(jnp.int32, shape, 0) & (C - 1)
-    column = lax.broadcasted_iota(jnp.int32, shape, 1) // C + step * SPAN
-    return jnp.where(row == column, 1.0, 0.0).astype(BF16)
-
-
-def gather_table(step):
-    shape = (SPAN * C, C)
-    row = lax.broadcasted_iota(jnp.int32, shape, 0) // C + step * SPAN
-    column = lax.broadcasted_iota(jnp.int32, shape, 1)
-    return jnp.where(row == column, 1.0, 0.0).astype(BF16)
-
-
-def walk(ref):
-    mz, mx = ref.shape[1], ref.shape[2]
-    for q in range(mz * mx):
-        yield q // QUAD, q % QUAD, q // mx, q % mx
-
-
-def pair_of(ref, kz, kx, tile):
-    columns = slice(tile * 2 * C, (tile + 1) * 2 * C)
-    return (
-        ref[0, kz, kx, :, columns].astype(F32),
-        ref[1, kz, kx, :, columns].astype(F32),
-    )
-
-
-def mix_kernel(data_ref, weight_ref, forward_ref, inverse_ref, modes_ref, out_ref, sum_ref):
+def spread_table():
+    return np.tile(np.kron(np.eye(C), np.ones((1, C))), (3, 1)).astype(jnp.bfloat16)
+
+
+def gather_table():
+    return np.kron(np.eye(C), np.ones((C, 1))).astype(jnp.bfloat16)
+
+
+def tiles():
+    for piece in range(C * C // SPAN):
+        for tile in range(SPAN // (2 * C)):
+            start = piece * SPAN + tile * 2 * C
+            yield piece, tile, slice(start, start + 2 * C)
+
+
+def spread_modes(modes, table_ref):
+    count = C * C // SPAN
+    made = {}
+
+    def get(piece):
+        for p in range(piece, min(piece + 2, count)):
+            if p not in made:
+                made[p] = jnp.dot(
+                    modes, table_ref[:, p * SPAN : (p + 1) * SPAN], preferred_element_type=F32
+                )
+        return made[piece]
+
+    return get
+
+
+def mix_kernel(
+    data_ref, weight_ref, table_ref, forward_ref, inverse_ref, modes_ref, out_ref, sum_ref
+):
     step = pl.program_id(0)
-    count = weight_ref.shape[1] * weight_ref.shape[2]
 
     @pl.when(step == 0)
     def _():
@@ -341,39 +370,33 @@
             modes_ref[group, place(part, pair), :] = jnp.concatenate([high, middle, low], axis=1)
 
         y_forward(data_ref, forward_ref, store)
-        sum_ref[...] = jnp.zeros_like(sum_ref)
-
-    table = spread_table(step)
-    spread = {}
-    for group, pair, kz, kx in walk(weight_ref):
-        if pair == 0:
-            spread[group] = jnp.dot(modes_ref[group], table, preferred_element_type=F32)
-        real = sum_ref[group, place(0, pair), :]
-        imag = sum_ref[group, place(1, pair), :]
-        for tile in range(SPAN // 2):
-            columns = slice(tile * 2 * C, (tile + 1) * 2 * C)
-            mode_re = spread[group][place(0, pair), columns]
-            mode_im = spread[group][place(1, pair), columns]
-            weight_re, weight_im = pair_of(weight_ref, kz, kx, tile)
-            real += mode_re * weight_re - mode_im * weight_im
-            imag += mode_re * weight_im + mode_im * weight_re
-        sum_ref[group, place(0, pair), :] = real
-        sum_ref[group, place(1, pair), :] = imag
+
+    spread = spread_modes(modes_ref[step], table_ref)
+    real = [jnp.zeros((MY, 2 * C), F32)] * QUAD
+    imag = [jnp.zeros((MY, 2 * C), F32)] * QUAD
+    for piece, tile, columns in tiles():
+        modes = spread(piece)
+        inside = slice(tile * 2 * C, (tile + 1) * 2 * C)
+        for pair in range(QUAD):
+            mode_re = modes[place(0, pair), inside]
+            mode_im = modes[place(1, pair), inside]
+            weight_re = weight_ref[0, 0, pair, :, columns].astype(F32)
+            weight_im = weight_ref[1, 0, pair, :, columns].astype(F32)
+            real[pair] += mode_re * weight_re - mode_im * weight_im
+            imag[pair] += mode_re * weight_im + mode_im * weight_re
+    for pair in range(QUAD):
+        sum_ref[step, place(0, pair), :] = real[pair][:, :C] + real[pair][:, C:]
+        sum_ref[step, place(1, pair), :] = imag[pair][:, :C] + imag[pair][:, C:]
 
     @pl.when(step == pl.num_programs(0) - 1)
     def _():
-        def load(group, part, pair):
-            values = sum_ref[group, place(part, pair), :]
-            return values[:, :C] + values[:, C:]
-
-        y_inverse(load, count, inverse_ref, out_ref)
+        y_inverse(sum_ref, inverse_ref, out_ref)
 
 
 def mix_back_kernel(
-    data_ref, weight_ref, forward_ref, inverse_ref, modes_ref, out_ref, sum_ref, term_ref
+    data_ref, weight_ref, table_ref, forward_ref, inverse_ref, modes_ref, out_ref, sum_ref, term_ref
 ):
     step = pl.program_id(0)
-    count = weight_ref.shape[1] * weight_ref.shape[2]
 
     @pl.when(step == 0)
     def _():
@@ -381,42 +404,45 @@
             modes_ref[group, place(part, pair), :] = jnp.concatenate([values, values], axis=1)
 
         y_forward(data_ref, forward_ref, store)
-        sum_ref[...] = jnp.zeros_like(sum_ref)
-
-    table = gather_table(step)
-    for group, pair, kz, kx in walk(weight_ref):
-        mode_re = modes_ref[group, place(0, pair), :]
-        mode_im = modes_ref[group, place(1, pair), :]
-        for tile in range(SPAN // 2):
-            columns = slice(tile * 2 * C, (tile + 1) * 2 * C)
-            weight_re, weight_im = pair_of(weight_ref, kz, kx, tile)
-            real = weight_re * mode_re + weight_im * mode_im
-            imag = weight_re * mode_im - weight_im * mode_re
-            term_ref[group, place(0, pair), columns] = real.astype(BF16)
-            term_ref[group, place(1, pair), columns] = imag.astype(BF16)
-        if pair == QUAD - 1:
-            sum_ref[group] += jnp.dot(term_ref[group], table, preferred_element_type=F32)
+
+    total = None
+    for piece, tile, columns in tiles():
+        for pair in range(QUAD):
+            mode_re = modes_ref[step, place(0, pair), :]
+            mode_im = modes_ref[step, place(1, pair), :]
+            weight_re = weight_ref[0, 0, pair, :, columns].astype(F32)
+            weight_im = weight_ref[1, 0, pair, :, columns].astype(F32)
+            term_ref[place(0, pair), columns] = (
+                weight_re * mode_re + weight_im * mode_im
+            ).astype(BF16)
+            term_ref[place(1, pair), columns] = (
+                weight_re * mode_im - weight_im * mode_re
+            ).astype(BF16)
+        if columns.stop % SPAN == 0:
+            whole_piece = slice(piece * SPAN, (piece + 1) * SPAN)
+            got = jnp.dot(
+                term_ref[:, whole_piece], table_ref[whole_piece, :], preferred_element_type=F32
+            )
+            total = got if total is None else total + got
+    sum_ref[step] = total
 
     @pl.when(step == pl.num_programs(0) - 1)
     def _():
-        load = lambda group, part, pair: sum_ref[group, place(part, pair), :]
-        y_inverse(load, count, inverse_ref, out_ref)
-
-
-def outer_kernel(alpha, modes_ref, back_ref, out_ref):
-    table = spread_table(pl.program_id(0))
-    spread = {}
-    for group, pair, kz, kx in walk(out_ref):
-        if pair == 0:
-            spread[group] = jnp.dot(modes_ref[group], table, preferred_element_type=F32)
-        back_re = back_ref[group, place(0, pair), :] * alpha
-        back_im = back_ref[group, place(1, pair), :] * alpha
-        for tile in range(SPAN // 2):
-            columns = slice(tile * 2 * C, (tile + 1) * 2 * C)
-            mode_re = spread[group][place(0, pair), columns]
-            mode_im = spread[group][place(1, pair), columns]
-            out_ref[0, kz, kx, :, columns] = mode_re * back_re + mode_im * back_im
-            out_ref[1, kz, kx, :, columns] = mode_re * back_im - mode_im * back_re
+        y_inverse(sum_ref, inverse_ref, out_ref)
+
+
+def outer_kernel(alpha, modes_ref, back_ref, table_ref, out_ref):
+    spread = spread_modes(modes_ref[0], table_ref)
+    for piece, tile, columns in tiles():
+        modes = spread(piece)
+        inside = slice(tile * 2 * C, (tile + 1) * 2 * C)
+        for pair in range(QUAD):
+            back_re = back_ref[0, place(0, pair), :] * alpha
+            back_im = back_ref[0, place(1, pair), :] * alpha
+            mode_re = modes[place(0, pair), inside]
+            mode_im = modes[place(1, pair), inside]
+            out_ref[0, 0, pair, :, columns] = mode_re * back_re + mode_im * back_im
+            out_ref[1, 0, pair, :, columns] = mode_re * back_im - mode_im * back_re
 
 
 def whole():
@@ -447,60 +473,60 @@
     return pl.BlockSpec(shape, lambda step: (0,) * len(shape))
 
 
-def channels(shape):
-    return pl.BlockSpec(shape[:4] + (SPAN * C,), lambda step: (0, 0, 0, 0, step))
-
-
-def per_mode(kernel, data, weight, forward, inverse, modes, scratch):
+def group_block(shape):
+    per = shape[2] // QUAD
+    return pl.BlockSpec(
+        (2, 1, QUAD) + shape[3:], lambda step: (0, step // per, step % per, 0, 0)
+    )
+
+
+def per_mode(kernel, data, weight, tables, modes, scratch=()):
     _, mz, mx, _, _ = weight.shape
     groups = mz * mx // QUAD
     rows = 2 * QUAD * MY
     modes_shape = (groups, rows, modes[0])
-    out_shape = (inverse.shape[0], mz * mx * C)
+    out_shape = (tables[-1].shape[0], mz * mx * C)
     return pl.pallas_call(
         kernel,
-        grid=(C // SPAN,),
-        in_specs=[
-            full(data.shape),
-            channels(weight.shape),
-            full(forward.shape),
-            full(inverse.shape),
-        ],
+        grid=(groups,),
+        in_specs=[full(data.shape), group_block(weight.shape)] + [full(t.shape) for t in tables],
         out_specs=[full(modes_shape), full(out_shape)],
         out_shape=[
             jax.ShapeDtypeStruct(modes_shape, modes[1]),
             jax.ShapeDtypeStruct(out_shape, F32),
         ],
-        scratch_shapes=[pltpu.VMEM((groups, rows, width), kind) for width, kind in scratch],
+        scratch_shapes=[pltpu.VMEM((groups, rows, C), F32), *scratch],
         compiler_params=params(56),
         cost_estimate=cost(weight.size * 8, weight.size * 2),
-    )(data, weight, forward, inverse)
-
-
-def outer(modes, back, shape, alpha):
+    )(data, weight, *tables)
+
+
+def outer(modes, back, table, shape, alpha):
+    group = lambda ref: pl.BlockSpec((1,) + ref.shape[1:], lambda step: (step, 0, 0))
     return pl.pallas_call(
         functools.partial(outer_kernel, alpha),
-        grid=(C // SPAN,),
-        in_specs=[full(modes.shape), full(back.shape)],
-        out_specs=channels(shape),
+        grid=(modes.shape[0],),
+        in_specs=[group(modes), group(back), full(table.shape)],
+        out_specs=group_block(shape),
         out_shape=jax.ShapeDtypeStruct(shape, F32),
-        compiler_params=params(24),
+        compiler_params=params(32),
         cost_estimate=cost(math.prod(shape) * 4, math.prod(shape) * 4),
-    )(modes, back)
-
-
-def halos(turned):
-    def shift(block, axis, step):
-        count = lax.axis_size(axis)
-        pairs = [(i, i + step) for i in range(count) if 0 <= i + step < count]
-        return lax.ppermute(block, axis, pairs)
-
-    xlo = shift(turned[-1], "gx", 1)
-    xhi = shift(turned[0], "gx", -1)
+    )(modes, back, table)
+
+
+def shift(block, axis, step):
+    count = lax.axis_size(axis)
+    pairs = [(i, i + step) for i in range(count) if 0 <= i + step < count]
+    return lax.ppermute(block, axis, pairs)
+
+
+def x_halos(turned):
+    return shift(turned[-1], "gx", 1), shift(turned[0], "gx", -1)
+
+
+def y_halos(turned, xlo, xhi):
     edge = lambda y: jnp.concatenate([xlo[None, y], turned[:, y], xhi[None, y]], axis=0)
-    ylo = shift(edge(-1), "gy", 1)
-    yhi = shift(edge(0), "gy", -1)
-    return xlo, xhi, ylo, yhi
+    return shift(edge(-1), "gy", 1), shift(edge(0), "gy", -1)
 
 
 def conv(turned, rim, weight, flip):
@@ -520,7 +546,7 @@
     cx, cy, c, z = turned.shape
     return call(
         weight_grad_kernel,
-        [((14 * c, 2 * c), F32)],
+        [((16 * c, 2 * c), F32)],
         (grad, turned, *rim),
         [
             pltpu.VMEM((4 * c, (cy + 2) * z), BF16),
@@ -533,18 +559,12 @@
     )[0]
 
 
-def sum_everywhere(part):
-    nx, ny = lax.axis_size("gx"), lax.axis_size("gy")
-
-    def swap(block, axis):
-        return lax.all_to_all(block, axis, split_axis=0, concat_axis=0, tiled=True)
-
-    def everyone(block, count):
-        return jnp.broadcast_to(block[None], (count, *block.shape))
-
-    mine = swap(part.reshape(nx, -1, part.shape[1]), "gx").sum(0)
-    mine = swap(everyone(mine, ny), "gy").sum(0)
-    return swap(everyone(mine, nx), "gx").reshape(part.shape)
+def swap(block, axis):
+    return lax.all_to_all(block, axis, split_axis=0, concat_axis=0, tiled=True)
+
+
+def together(*values):
+    return lax.optimization_barrier(values)
 
 
 def body(state, cotangent, spectral_weight, stencil_weight, pointwise_weight):
@@ -562,33 +582,28 @@
     z_back = jnp.asarray(z_inverse_table(nx, mz, alpha * beta * ones))
     x_fwd, x_inv = (jnp.asarray(t) for t in x_tables(wide_x, mz))
     y_fwd, y_inv = (jnp.asarray(t) for t in y_tables(wide_y))
+    spread, gather = jnp.asarray(spread_table()), jnp.asarray(gather_table())
     lanes = cy * c
     x_rows = cx * 2 * mz
 
-    def swap(block, axis):
-        return lax.all_to_all(block, axis, split_axis=0, concat_axis=0, tiled=True)
-
-    def x_stage(table, block, lead):
-        flat = block.reshape(-1, lanes)
-        got = call(
+    def x_stage(table, block, lead, kind=F32, extra=0):
+        rows = table.shape[0] // lead + extra
+        return call(
             x_kernel,
-            [((table.shape[0], lanes), F32)],
-            (table, flat),
+            [((lead, rows, lanes), kind)],
+            (table, block),
             mib=16,
             flops=2 * table.size * lanes,
-            moved=8 * flat.size,
+            moved=8 * block.size,
         )[0]
-        return got.reshape(lead, -1, lanes)
-
-    def to_pencil(slab):
-        block = swap(x_stage(x_fwd, swap(slab, "gx"), ny), "gy")
+
+    def to_rows(block):
         block = block.reshape(ny, mx, 2, mz, cy, c).transpose(2, 0, 4, 3, 1, 5)
         return block.reshape(2 * wide_y, mz * mx * c)
 
-    def to_slab(pencil):
-        block = pencil.reshape(2, ny, cy, mz, mx, c).transpose(1, 4, 0, 3, 2, 5)
-        block = swap(block.reshape(ny, mx * 2 * mz, lanes), "gy")
-        return swap(x_stage(x_inv, block, nx), "gx")
+    def to_blocks(rows):
+        block = rows.reshape(2, ny, cy, mz, mx, c).transpose(1, 4, 0, 3, 2, 5)
+        return block.reshape(ny, mx * 2 * mz, lanes)
 
     slab_shape = ((nx, x_rows, lanes), F32)
     turned_shape = ((cx, cy, c, z), BF16)
@@ -607,47 +622,59 @@
         flops=2 * 96 * state.size,
         moved=state.size * 5,
     )
-    rim = halos(turned)
-    pencil = to_pencil(slab)
+    block = x_stage(x_fwd, swap(slab, "gx"), ny)
+    block, *faces = together(block, *x_halos(turned))
+    rows = to_rows(swap(block, "gy"))
+    modes_in, rows = per_mode(
+        mix_kernel, rows, spectral_weight, (spread, y_fwd, y_inv), (3 * c, BF16)
+    )
+    block, *edges = together(to_blocks(rows), *y_halos(turned, *faces))
+    rim = (*faces, *edges)
+    block = x_stage(x_inv, swap(block, "gy"), nx)
     stencil = conv(turned, rim, conv_table, False)
-    modes_in, pencil = per_mode(
-        mix_kernel, pencil, spectral_weight, y_fwd, y_inv, (3 * c, BF16), [(2 * c, F32)]
-    )
-    slab = to_slab(pencil)
     output, grad, slab = call(
         functools.partial(gelu_kernel, nx),
         [((c, cx, cy, z), BF16), turned_shape, slab_shape],
-        (stencil, slab, cotangent, z_spectral, z_grad),
+        (stencil, swap(block, "gx"), cotangent, z_spectral, z_grad),
         flops=2 * 192 * state.size,
         moved=state.size * 12,
     )
-    grad_rim = halos(grad)
-    pencil = to_pencil(slab)
+
+    block = x_stage(x_fwd, swap(slab, "gx"), ny, BF16)
     grad_taps = weight_grad(grad, turned, rim)
-    back_modes, pencil = per_mode(
+    block, *faces = together(block, *x_halos(grad))
+    block, grad_taps = together(swap(block, "gy"), grad_taps)
+    mine = swap(grad_taps.reshape(nx, -1, 2 * c), "gx").sum(0)
+    back_modes, rows = per_mode(
         mix_back_kernel,
-        pencil,
+        to_rows(block),
         spectral_weight,
-        y_fwd,
-        y_inv,
+        (gather, y_fwd, y_inv),
         (2 * c, F32),
-        [(c, F32), (SPAN * c, BF16)],
-    )
-    grad_modes = outer(modes_in, back_modes, spectral_weight.shape, alpha)
-    stencil_back = conv(grad, grad_rim, back_table, True)
-    slab = to_slab(pencil)
+        [pltpu.VMEM((2 * QUAD * MY, c * c), BF16)],
+    )
+    packed = jnp.concatenate(jnp.split(mine, lanes // (2 * c)), axis=1)
+    extra = packed.shape[0]
+    packed = jnp.broadcast_to(packed[None], (ny, extra, lanes))
+    block = jnp.concatenate([to_blocks(rows), packed], axis=1).astype(BF16)
+    block, *edges = together(block, *y_halos(grad, *faces))
+    block = x_stage(x_inv, swap(block, "gy"), nx, F32, extra)
+    stencil_back = conv(grad, (*faces, *edges), back_table, True)
+    block, stencil_back = together(block, stencil_back)
+    message = swap(block, "gx")
+    grad_modes = outer(modes_in, back_modes, spread, spectral_weight.shape, alpha)
     grad_state = call(
         functools.partial(finish_kernel, nx),
         [((c, cx, cy, z), F32)],
-        (stencil_back, slab, z_back),
+        (stencil_back, message, z_back),
         flops=2 * 96 * state.size,
         moved=state.size * 10,
     )[0]
     grad_stencil, grad_point = call(
-        functools.partial(unpack_kernel, alpha),
+        functools.partial(unpack_kernel, alpha, x_rows),
         [((c, 27 * c), F32), ((c, c), F32)],
-        (sum_everywhere(grad_taps),),
-        [pltpu.VMEM((27 * c, c), F32)],
+        (message,),
+        [pltpu.VMEM(grad_taps.shape, F32), pltpu.VMEM((27 * c, c), F32)],
         moved=grad_taps.size * 8,
     )
     return (output, grad_state, grad_modes, grad_stencil, grad_point)

time: 176 us -> 156 us (0.89)
  waiting for transfers between devices: 40.7 us -> 19.7 us
  local copies, waits for them, and re-layouts: 16.4 us -> 21.4 us
  starting transfers between devices: 57.3 us -> 53.2 us
  other arithmetic: 0.11 us -> 3.71 us
    all_to_all x10 -> x8, waiting for transfers between devices: 30.5 us -> 19.7 us  [swap(): return lax.all_to_all(block, axis, split_axis=0, concat_axis=0, tiled=True)]
    ppermute x8, waiting for transfers between devices: 10.2 us -> 0.02 us  [shift(): return lax.ppermute(block, axis, pairs)]
    unnamed x38 -> x66, local copies, waits for them, and re-layouts: 7.97 us -> 13.7 us
    all_to_all x10 -> x8, starting transfers between devices: 38.8 us -> 34.5 us  [swap(): return lax.all_to_all(block, axis, split_axis=0, concat_axis=0, tiled=True)]
    concatenate x4 -> x5, other arithmetic: 0.06 us -> 2.71 us  [the longest x4 1.98 us: y_halos(): jnp.concatenate([xlo[None, y], turned[:, y], xhi[None, y]], axis=0)]
    pallas_call x3, Pallas kernels: 29.3 us -> 26.9 us  [the longest x2 19.2 us: per_mode(): pl.pallas_call(kernel, grid=(groups,), in_specs=[full(data.shape), group_...]
    reshape x8 -> x12, local copies, waits for them, and re-layouts: 5.94 us -> 7.66 us  [the longest x4 3.89 us: to_blocks(): block = rows.reshape(2, ny, cy, mz, mx, c).transpose(1, 4, 0, 3, 2, 5)]
  transfers between devices with their start and end apart: 18 -> 16, of which waited for: 9 -> 6; matrix products, arithmetic and copies ran while one was open for 5% -> 7% of each run, Pallas kernels for 24% -> 23%
where the time goes in v3:
time: 156 us; the launch traced here: 154 us
  starting transfers between devices  53.2 us (34%)
  Pallas kernels  44.5 us (29%)
  local copies, waits for them, and re-layouts  21.4 us (14%)
  waiting for transfers between devices  19.7 us (13%)
  blocking collectives  10.3 us (7%)
  other arithmetic  3.71 us (2%)
    all_to_all x8, starting transfers between devices, swap(): return lax.all_to_all(block, axis, split_axis=0, concat_axis=0, tiled=True)  34.5 us
    all_to_all x8, waiting for transfers between devices, swap(): return lax.all_to_all(block, axis, split_axis=0, concat_axis=0, tiled=True)  19.7 us
    pallas_call x2, Pallas kernels, per_mode(): pl.pallas_call(kernel, grid=(groups,), in_specs=[full(data.shape), group_...  19.2 us
    ppermute x8, starting transfers between devices, shift(): return lax.ppermute(block, axis, pairs)  18.7 us
    pallas_call x12, Pallas kernels, call(): pl.pallas_call(kernel, out_shape=[jax.ShapeDtypeStruct(*out) for out in o...  17.6 us
    unnamed x66, local copies, waits for them, and re-layouts  13.7 us
    all_to_all x1, blocking collectives, swap(): return lax.all_to_all(block, axis, split_axis=0, concat_axis=0, tiled=True)  10.3 us
    pallas_call x1, Pallas kernels, outer(): pl.pallas_call(functools.partial(outer_kernel, alpha), grid=(modes.shape[...  7.64 us
  transfers between devices with their start and end apart: 16, of which 6 were waited for; matrix products, arithmetic and copies ran while one was open for 7% of the time, Pallas kernels for 23%

profile of v3, /device:TPU:0, one launch (start us, length us, event | category | flops | bytes accessed | tf_op | source)
XLA Modules:
  0.0 154.0 jit_solution(11402143139833757335)
XLA Ops:
  3.6 5.2 %all-to-all-start = ((f32[8,16,512]{2,1,0:T(8,128)}), f32[8,16,512]{2,1,0:T(8,128)S(1)}, u32[]{:S(2)}, u32[]{:S(2)}) async-start(f32[8,16,512]{2,1,0:T(8,128)} %get-tuple-element.35), calls=%async_computation | async-start | bytes 524288 | tf_op jit(solution)/shard_map/all_to_all | solution.py:563
  8.7 1.3 collective-permute-start.1
  10.0 3.0 %collective-permute-start = (bf16[8,64,128]{2,1,0:T(8,128)(2,1)S(1)}, bf16[8,64,128]{2,1,0:T(8,128)(2,1)S(1)}, u32[]{:S(2)}, u32[]{:S(2)}) collective-permute-start(bf16[8,64,128]{2,1,0:T(8,128)(2,1)S(1)} %get-tuple-element.70), channel_id=1, source_target_pairs={{0,4},{4,8},{8,12},{12,16},{16,20},{20,24},{24,28},{1,5},{5,9},{9,... | collective-permute-start | bytes 393224 | tf_op jit(solution)/shard_map/ppermute | solution.py:520
  13.1 2.5 %all-to-all-done.data_ref = f32[8,16,512]{2,1,0:T(8,128)S(1)} async-done(((f32[8,16,512]{2,1,0:T(8,128)}), f32[8,16,512]{2,1,0:T(8,128)S(1)}, u32[]{:S(2)}, u32[]{:S(2)}) %all-to-all-start) | async-done | bytes 262176 | tf_op jit(solution)/shard_map/all_to_all | solution.py:563
  17.5 4.9 %all-to-all-start.1 = ((f32[4,32,512]{2,1,0:T(8,128)}), f32[4,32,512]{2,1,0:T(8,128)S(1)}, u32[]{:S(2)}, u32[]{:S(2)}) async-start(f32[4,32,512]{2,1,0:T(8,128)} %shard_map.183), calls=%async_computation.1 | async-start | bytes 524288 | tf_op jit(solution)/shard_map/all_to_all | solution.py:563
  22.4 4.1 %collective-permute-start.2 = (bf16[6,64,128]{2,1,0:T(8,128)(2,1)S(1)}, bf16[6,64,128]{2,1,0:T(8,128)(2,1)S(1)}, u32[]{:S(2)}, u32[]{:S(2)}) collective-permute-start(bf16[6,64,128]{2,1,0:T(8,128)(2,1)S(1)} %pad_maximum_fusion.1), channel_id=1, source_target_pairs={{0,1},{1,2},{2,3},{4,5},{5,6},{6,7},{8,9},{9,10},{10,11},{12,13},{... | collective-permute-start | bytes 294920 | tf_op jit(solution)/shard_map/ppermute | solution.py:520
  28.4 2.3 %all-to-all-done.1 = f32[4,32,512]{2,1,0:T(8,128)S(1)} async-done(((f32[4,32,512]{2,1,0:T(8,128)}), f32[4,32,512]{2,1,0:T(8,128)S(1)}, u32[]{:S(2)}, u32[]{:S(2)}) %all-to-all-start.1) | async-done | bytes 262176 | tf_op jit(solution)/shard_map/all_to_all | solution.py:563
  32.1 9.5 %shard_map.184 = (bf16[4,256,192]{2,1,0:T(8,128)(2,1)}, f32[64,1024]{1,0:T(8,128)}) custom-call(f32[64,1024]{1,0:T(8,128)} %reshape.41.data_ref, bf16[2,2,8,32,4096]{4,3,2,1,0:T(8,128)(2,1)} %weight_ref.3, bf16[192,4096]{1,0:T(8,128)(2,1)} %constant.30.clone.table_ref, bf16[64,192]{1,0:T(8,128)(2,1)} %constant.28.clone.forward_ref, ...), custom_call_target="tpu_custom_call" | custom-call | flops 33554432 | bytes 8388608 | tf_op jit(solution)/shard_map/pallas_call | solution.py:489
  43.1 10.3 %all_to_all.45.data_ref = f32[4,32,512]{2,1,0:T(8,128)S(1)} all-to-all(f32[4,32,512]{2,1,0:T(8,128)S(1)} %reshape.43), channel_id=1, replica_groups=mesh['gx'=8,'gy'=4] {'gy'}, dimensions={0} | all-to-all | bytes 524288 | tf_op jit(solution)/shard_map/all_to_all | solution.py:563
  54.3 4.8 %all-to-all-start.3 = ((f32[8,16,512]{2,1,0:T(8,128)}), f32[8,16,512]{2,1,0:T(8,128)S(1)}, u32[]{:S(2)}, u32[]{:S(2)}) async-start(f32[8,16,512]{2,1,0:T(8,128)} %shard_map.187), calls=%async_computation.3 | async-start | bytes 524288 | tf_op jit(solution)/shard_map/all_to_all | solution.py:563
  60.8 1.9 %shard_map.186.stencil_ref = f32[4,64,1024]{2,1,0:T(8,128)S(1)} custom-call(bf16[4,8,64,128]{3,2,1,0:T(8,128)(2,1)S(1)} %get-tuple-element.34.body_ref, bf16[8,64,128]{2,1,0:T(8,128)(2,1)S(1)} %collective-permute-done.xlo_ref, bf16[8,64,128]{2,1,0:T(8,128)(2,1)S(1)} %collective-permute-done.1.xhi_ref, ...), custom_call_target="tpu_custom_call" | custom-call | flops 905969664 | bytes 2097152 | tf_op jit(solution)/shard_map/pallas_call | solution.py:461
  62.7 3.4 %all-to-all-done.3.slab_ref = f32[8,16,512]{2,1,0:T(8,128)S(1)} async-done(((f32[8,16,512]{2,1,0:T(8,128)}), f32[8,16,512]{2,1,0:T(8,128)S(1)}, u32[]{:S(2)}, u32[]{:S(2)}) %all-to-all-start.3) | async-done | bytes 262176 | tf_op jit(solution)/shard_map/all_to_all | solution.py:563
  66.1 2.3 %shard_map.188 = (bf16[64,4,8,128]{3,2,1,0:T(8,128)(2,1)}, bf16[4,8,64,128]{3,2,1,0:T(8,128)(2,1)S(1)}, f32[8,16,512]{2,1,0:T(8,128)}) custom-call(f32[4,64,1024]{2,1,0:T(8,128)S(1)} %shard_map.186.stencil_ref, f32[8,16,512]{2,1,0:T(8,128)S(1)} %all-to-all-done.3.slab_ref, bf16[64,4,8,128]{3,2,1,0:T(8,128)(2,1)S(1)} %copy-done.1, ...), custom_call_target="tpu_custom_call" | custom-call | flops 100663296 | bytes 3145728 | tf_op jit(solution)/shard_map/pallas_call | solution.py:461
  68.4 3.4 %all-to-all-start.4 = ((f32[8,16,512]{2,1,0:T(8,128)}), f32[8,16,512]{2,1,0:T(8,128)S(1)}, u32[]{:S(2)}, u32[]{:S(2)}) async-start(f32[8,16,512]{2,1,0:T(8,128)} %get-tuple-element.45), calls=%async_computation.4 | async-start | bytes 524288 | tf_op jit(solution)/shard_map/all_to_all | solution.py:563
  71.9 1.3 collective-permute-start.5
  73.2 3.0 %collective-permute-start.4 = (bf16[8,64,128]{2,1,0:T(8,128)(2,1)S(1)}, bf16[8,64,128]{2,1,0:T(8,128)(2,1)S(1)}, u32[]{:S(2)}, u32[]{:S(2)}) collective-permute-start(bf16[8,64,128]{2,1,0:T(8,128)(2,1)S(1)} %get-tuple-element.66), channel_id=1, source_target_pairs={{0,4},{4,8},{8,12},{12,16},{16,20},{20,24},{24,28},{1,5},{5,9},{9,... | collective-permute-start | bytes 393224 | tf_op jit(solution)/shard_map/ppermute | solution.py:520
  78.9 3.1 %shard_map.190 = f32[1024,128]{1,0:T(8,128)} custom-call(bf16[4,8,64,128]{3,2,1,0:T(8,128)(2,1)S(1)} %get-tuple-element.46.grad_ref.body_ref, bf16[4,8,64,128]{3,2,1,0:T(8,128)(2,1)S(1)} %get-tuple-element.34.body_ref, bf16[8,64,128]{2,1,0:T(8,128)(2,1)S(1)} %copy-done.21, bf16[8,64,128]{2,1,0:T(8,128)(2,1)S(1)} %collective-permute-done.1.xhi_ref, ...), custom_call_target="tpu_custom_call" | custom-call | flops 905969664 | bytes 2097152 | tf_op jit(solution)/shard_map/pallas_call | solution.py:461
  82.9 3.3 %all-to-all-start.5 = ((bf16[4,32,512]{2,1,0:T(8,128)(2,1)}), bf16[4,32,512]{2,1,0:T(8,128)(2,1)S(1)}, u32[]{:S(2)}, u32[]{:S(2)}) async-start(bf16[4,32,512]{2,1,0:T(8,128)(2,1)} %shard_map.189), calls=%async_computation.5 | async-start | bytes 262144 | tf_op jit(solution)/shard_map/all_to_all | solution.py:563
  86.2 6.0 %all-to-all-done.5 = bf16[4,32,512]{2,1,0:T(8,128)(2,1)S(1)} async-done(((bf16[4,32,512]{2,1,0:T(8,128)(2,1)}), bf16[4,32,512]{2,1,0:T(8,128)(2,1)S(1)}, u32[]{:S(2)}, u32[]{:S(2)}) %all-to-all-start.5) | async-done | bytes 131104 | tf_op jit(solution)/shard_map/all_to_all | solution.py:563
  92.2 4.5 %all-to-all-start.6 = ((f32[8,128,128]{2,1,0:T(8,128)}), f32[8,128,128]{2,1,0:T(8,128)S(1)}, u32[]{:S(2)}, u32[]{:S(2)}) async-start(f32[8,128,128]{2,1,0:T(8,128)} %bitcast.10), calls=%async_computation.6 | async-start | bytes 1048576 | tf_op jit(solution)/shard_map/all_to_all | solution.py:563
  97.4 3.3 %collective-permute-start.6 = (bf16[6,64,128]{2,1,0:T(8,128)(2,1)}, bf16[6,64,128]{2,1,0:T(8,128)(2,1)S(1)}, u32[]{:S(2)}, u32[]{:S(2)}) collective-permute-start(bf16[6,64,128]{2,1,0:T(8,128)(2,1)} %pad_maximum_fusion.3), channel_id=1, source_target_pairs={{0,1},{1,2},{2,3},{4,5},{5,6},{6,7},{8,9},{9,10},{10,11},{12,13},{... | collective-permute-start | bytes 294920 | tf_op jit(solution)/shard_map/ppermute | solution.py:520
  101.3 1.5 collective-permute-start.7
  103.9 9.8 %shard_map.191 = (f32[4,256,128]{2,1,0:T(8,128)}, f32[64,1024]{1,0:T(8,128)}) custom-call(bf16[64,1024]{1,0:T(8,128)(2,1)} %reshape.45.data_ref, bf16[2,2,8,32,4096]{4,3,2,1,0:T(8,128)(2,1)} %weight_ref.3, bf16[4096,64]{1,0:T(8,128)(2,1)} %constant.31.clone.table_ref, bf16[64,192]{1,0:T(8,128)(2,1)} %constant.28.clone.forward_ref, ...), custom_call_target="tpu_custom_call" | custom-call | flops 33554432 | bytes 8388608 | tf_op jit(solution)/shard_map/pallas_call | solution.py:489
  115.6 1.7 %copy.38 = bf16[2,4,8,2,8,64]{5,2,3,0,4,1:T(8,128)(2,1)} copy(bf16[2,4,8,2,8,64]{5,4,3,2,1,0:T(8,128)(2,1)} %reshape.46) | data formatting | bytes 262144 | tf_op jit(solution)/shard_map/reshape | solution.py:605
  119.9 4.6 %all-to-all-start.7 = ((bf16[4,64,512]{2,1,0:T(8,128)(2,1)}), bf16[4,64,512]{2,1,0:T(8,128)(2,1)S(1)}, u32[]{:S(2)}, u32[]{:S(2)}) async-start(bf16[4,64,512]{2,1,0:T(8,128)(2,1)} %pad_maximum_fusion), calls=%async_computation.7 | async-start | bytes 524288 | tf_op jit(solution)/shard_map/all_to_all | solution.py:563
  129.1 1.9 %shard_map.193.stencil_ref = f32[4,64,1024]{2,1,0:T(8,128)S(1)} custom-call(bf16[4,8,64,128]{3,2,1,0:T(8,128)(2,1)S(1)} %copy-done.9, bf16[8,64,128]{2,1,0:T(8,128)(2,1)S(1)} %copy-done.19, bf16[8,64,128]{2,1,0:T(8,128)(2,1)S(1)} %copy-done.17, bf16[6,64,128]{2,1,0:T(8,128)(2,1)S(1)} %copy-done.30, bf16[6,64,128]{2,1,0:T(8,128)(2,1)S(1)} %copy-done.32, ...), custom_call_target="tpu_custom_call" | custom-call | flops 905969664 | bytes 2097152 | tf_op jit(solution)/shard_map/pallas_call | solution.py:461
  131.0 2.6 %all-to-all-done.7.data_ref = bf16[4,64,512]{2,1,0:T(8,128)(2,1)S(1)} async-done(((bf16[4,64,512]{2,1,0:T(8,128)(2,1)}), bf16[4,64,512]{2,1,0:T(8,128)(2,1)S(1)}, u32[]{:S(2)}, u32[]{:S(2)}) %all-to-all-start.7) | async-done | bytes 262176 | tf_op jit(solution)/shard_map/all_to_all | solution.py:563
  134.7 3.8 %all-to-all-start.8 = ((f32[8,48,512]{2,1,0:T(8,128)}), f32[8,48,512]{2,1,0:T(8,128)S(1)}, u32[]{:S(2)}, u32[]{:S(2)}) async-start(f32[8,48,512]{2,1,0:T(8,128)} %shard_map.192), calls=%async_computation.8 | async-start | bytes 1572864 | tf_op jit(solution)/shard_map/all_to_all | solution.py:563
  140.6 7.6 %shard_map.195 = f32[2,2,8,32,4096]{4,3,2,1,0:T(8,128)} custom-call(bf16[4,256,192]{2,1,0:T(8,128)(2,1)S(1)} %copy-done.2, f32[4,256,128]{2,1,0:T(8,128)S(1)} %copy-done.3, bf16[192,4096]{1,0:T(8,128)(2,1)S(1)} %copy-done), custom_call_target="tpu_custom_call" | custom-call | flops 16777216 | bytes 16777216 | tf_op jit(solution)/shard_map/pallas_call | solution.py:506
  148.2 2.9 %all-to-all-done.8.slab_ref.message_ref = f32[8,48,512]{2,1,0:T(8,128)S(1)} async-done(((f32[8,48,512]{2,1,0:T(8,128)}), f32[8,48,512]{2,1,0:T(8,128)S(1)}, u32[]{:S(2)}, u32[]{:S(2)}) %all-to-all-start.8) | async-done | bytes 786464 | tf_op jit(solution)/shard_map/all_to_all | solution.py:563
  151.1 1.5 shard_map.196
  152.6 1.4 shard_map.194
  (111 shorter events, 30.4 us)
Async XLA Ops:
  3.6 12.1 %all-to-all-start = ((f32[8,16,512]{2,1,0:T(8,128)}), f32[8,16,512]{2,1,0:T(8,128)S(1)}, u32[]{:S(2)}, u32[]{:S(2)}) async-start(f32[8,16,512]{2,1,0:T(8,128)} %get-tuple-element.35), calls=%async_computation | async-start | bytes 524288 | tf_op jit(solution)/shard_map/all_to_all | solution.py:563
  8.7 8.7 %collective-permute-start.1 = (bf16[8,64,128]{2,1,0:T(8,128)(2,1)S(1)}, bf16[8,64,128]{2,1,0:T(8,128)(2,1)S(1)}, u32[]{:S(2)}, u32[]{:S(2)}) collective-permute-start(bf16[8,64,128]{2,1,0:T(8,128)(2,1)S(1)} %get-tuple-element.69), channel_id=1, source_target_pairs={{4,0},{8,4},{12,8},{16,12},{20,16},{24,20},{28,24},{5,1},{9,5},{13... | collective-permute-start | bytes 393224 | tf_op jit(solution)/shard_map/ppermute | solution.py:520
  10.0 7.5 %collective-permute-start = (bf16[8,64,128]{2,1,0:T(8,128)(2,1)S(1)}, bf16[8,64,128]{2,1,0:T(8,128)(2,1)S(1)}, u32[]{:S(2)}, u32[]{:S(2)}) collective-permute-start(bf16[8,64,128]{2,1,0:T(8,128)(2,1)S(1)} %get-tuple-element.70), channel_id=1, source_target_pairs={{0,4},{4,8},{8,12},{12,16},{16,20},{20,24},{24,28},{1,5},{5,9},{9,... | collective-permute-start | bytes 393224 | tf_op jit(solution)/shard_map/ppermute | solution.py:520
  17.5 42.3 %copy-start.20 = (bf16[8,64,128]{2,1,0:T(8,128)(2,1)}, bf16[8,64,128]{2,1,0:T(8,128)(2,1)S(1)}, u32[]{:S(2)}) copy-start(bf16[8,64,128]{2,1,0:T(8,128)(2,1)S(1)} %collective-permute-done.xlo_ref) | copy-start | bytes 393220
  17.5 13.3 %all-to-all-start.1 = ((f32[4,32,512]{2,1,0:T(8,128)}), f32[4,32,512]{2,1,0:T(8,128)S(1)}, u32[]{:S(2)}, u32[]{:S(2)}) async-start(f32[4,32,512]{2,1,0:T(8,128)} %shard_map.183), calls=%async_computation.1 | async-start | bytes 524288 | tf_op jit(solution)/shard_map/all_to_all | solution.py:563
  22.4 31.0 %copy-start.5 = (bf16[128,384]{1,0:T(8,128)(2,1)S(1)}, bf16[128,384]{1,0:T(8,128)(2,1)}, u32[]{:S(2)}) copy-start(bf16[128,384]{1,0:T(8,128)(2,1)} %constant.27.clone.table_ref) | copy-start | bytes 294916
  22.4 20.6 %collective-permute-start.2 = (bf16[6,64,128]{2,1,0:T(8,128)(2,1)S(1)}, bf16[6,64,128]{2,1,0:T(8,128)(2,1)S(1)}, u32[]{:S(2)}, u32[]{:S(2)}) collective-permute-start(bf16[6,64,128]{2,1,0:T(8,128)(2,1)S(1)} %pad_maximum_fusion.1), channel_id=1, source_target_pairs={{0,1},{1,2},{2,3},{4,5},{5,6},{6,7},{8,9},{9,10},{10,11},{12,13},{... | collective-permute-start | bytes 294920 | tf_op jit(solution)/shard_map/ppermute | solution.py:520
  27.1 15.9 %collective-permute-start.3 = (bf16[6,64,128]{2,1,0:T(8,128)(2,1)}, bf16[6,64,128]{2,1,0:T(8,128)(2,1)S(1)}, u32[]{:S(2)}, u32[]{:S(2)}) collective-permute-start(bf16[6,64,128]{2,1,0:T(8,128)(2,1)} %pad_maximum_fusion.2), channel_id=1, source_target_pairs={{1,0},{2,1},{3,2},{5,4},{6,5},{7,6},{9,8},{10,9},{11,10},{13,12},{... | collective-permute-start | bytes 294920 | tf_op jit(solution)/shard_map/ppermute | solution.py:520
  30.9 28.3 %copy-start.10 = (bf16[64,1728]{1,0:T(8,128)(2,1)S(1)}, bf16[64,1728]{1,0:T(8,128)(2,1)}, u32[]{:S(2)}) copy-start(bf16[64,1728]{1,0:T(8,128)(2,1)} %taps_ref.1) | copy-start | bytes 663556
  30.9 28.3 %copy-start.15 = (bf16[64,64]{1,0:T(8,128)(2,1)S(1)}, bf16[64,64]{1,0:T(8,128)(2,1)}, u32[]{:S(2)}) copy-start(bf16[64,64]{1,0:T(8,128)(2,1)} %point_ref.1) | copy-start | bytes 24580
  32.1 34.0 %copy-start.1 = (bf16[64,4,8,128]{3,2,1,0:T(8,128)(2,1)S(1)}, bf16[64,4,8,128]{3,2,1,0:T(8,128)(2,1)}, u32[]{:S(2)}) copy-start(bf16[64,4,8,128]{3,2,1,0:T(8,128)(2,1)} %cot_ref.1) | copy-start | bytes 1572868
  32.1 34.0 %copy-start.12 = (bf16[96,128]{1,0:T(8,128)(2,1)S(1)}, bf16[96,128]{1,0:T(8,128)(2,1)}, u32[]{:S(2)}) copy-start(bf16[96,128]{1,0:T(8,128)(2,1)} %constant.24.clone.inverse_ref) | copy-start | bytes 73732
  32.1 34.0 %copy-start.13 = (bf16[96,128]{1,0:T(8,128)(2,1)S(1)}, bf16[96,128]{1,0:T(8,128)(2,1)}, u32[]{:S(2)}) copy-start(bf16[96,128]{1,0:T(8,128)(2,1)} %constant.23.clone.forward_ref) | copy-start | bytes 73732
  41.6 40.4 %copy-start.7 = (bf16[128,384]{1,0:T(8,128)(2,1)S(1)}, bf16[128,384]{1,0:T(8,128)(2,1)}, u32[]{:S(2)}) copy-start(bf16[128,384]{1,0:T(8,128)(2,1)} %constant.26.clone.table_ref) | copy-start | bytes 294916
  43.0 19.7 %copy-start.24 = (bf16[6,64,128]{2,1,0:T(8,128)(2,1)}, bf16[6,64,128]{2,1,0:T(8,128)(2,1)S(1)}, u32[]{:S(2)}) copy-start(bf16[6,64,128]{2,1,0:T(8,128)(2,1)S(1)} %collective-permute-done.2.ylo_ref) | copy-start | bytes 294916
  43.1 11.3 %copy-start.26 = (bf16[6,64,128]{2,1,0:T(8,128)(2,1)}, bf16[6,64,128]{2,1,0:T(8,128)(2,1)S(1)}, u32[]{:S(2)}) copy-start(bf16[6,64,128]{2,1,0:T(8,128)(2,1)S(1)} %collective-permute-done.3.yhi_ref) | copy-start | bytes 294916
  54.3 11.8 %all-to-all-start.3 = ((f32[8,16,512]{2,1,0:T(8,128)}), f32[8,16,512]{2,1,0:T(8,128)S(1)}, u32[]{:S(2)}, u32[]{:S(2)}) async-start(f32[8,16,512]{2,1,0:T(8,128)} %shard_map.187), calls=%async_computation.3 | async-start | bytes 524288 | tf_op jit(solution)/shard_map/all_to_all | solution.py:563
  68.4 34.6 %copy-start.8 = (bf16[4,8,64,128]{3,2,1,0:T(8,128)(2,1)}, bf16[4,8,64,128]{3,2,1,0:T(8,128)(2,1)S(1)}, u32[]{:S(2)}) copy-start(bf16[4,8,64,128]{3,2,1,0:T(8,128)(2,1)S(1)} %get-tuple-element.46.grad_ref.body_ref) | copy-start | bytes 1572868
  68.4 13.5 %all-to-all-start.4 = ((f32[8,16,512]{2,1,0:T(8,128)}), f32[8,16,512]{2,1,0:T(8,128)S(1)}, u32[]{:S(2)}, u32[]{:S(2)}) async-start(f32[8,16,512]{2,1,0:T(8,128)} %get-tuple-element.45), calls=%async_computation.4 | async-start | bytes 524288 | tf_op jit(solution)/shard_map/all_to_all | solution.py:563
  71.9 11.0 %collective-permute-start.5 = (bf16[8,64,128]{2,1,0:T(8,128)(2,1)S(1)}, bf16[8,64,128]{2,1,0:T(8,128)(2,1)S(1)}, u32[]{:S(2)}, u32[]{:S(2)}) collective-permute-start(bf16[8,64,128]{2,1,0:T(8,128)(2,1)S(1)} %get-tuple-element.65), channel_id=1, source_target_pairs={{4,0},{8,4},{12,8},{16,12},{20,16},{24,20},{28,24},{5,1},{9,5},{13... | collective-permute-start | bytes 393224 | tf_op jit(solution)/shard_map/ppermute | solution.py:520
  73.2 9.7 %collective-permute-start.4 = (bf16[8,64,128]{2,1,0:T(8,128)(2,1)S(1)}, bf16[8,64,128]{2,1,0:T(8,128)(2,1)S(1)}, u32[]{:S(2)}, u32[]{:S(2)}) collective-permute-start(bf16[8,64,128]{2,1,0:T(8,128)(2,1)S(1)} %get-tuple-element.66), channel_id=1, source_target_pairs={{0,4},{4,8},{8,12},{12,16},{16,20},{20,24},{24,28},{1,5},{5,9},{9,... | collective-permute-start | bytes 393224 | tf_op jit(solution)/shard_map/ppermute | solution.py:520
  82.9 41.7 %copy-start.16 = (bf16[8,64,128]{2,1,0:T(8,128)(2,1)}, bf16[8,64,128]{2,1,0:T(8,128)(2,1)S(1)}, u32[]{:S(2)}) copy-start(bf16[8,64,128]{2,1,0:T(8,128)(2,1)S(1)} %collective-permute-done.5.xhi_ref) | copy-start | bytes 393220
  82.9 41.7 %copy-start.18 = (bf16[8,64,128]{2,1,0:T(8,128)(2,1)}, bf16[8,64,128]{2,1,0:T(8,128)(2,1)S(1)}, u32[]{:S(2)}) copy-start(bf16[8,64,128]{2,1,0:T(8,128)(2,1)S(1)} %collective-permute-done.4.xlo_ref) | copy-start | bytes 393220
  82.9 9.3 %all-to-all-start.5 = ((bf16[4,32,512]{2,1,0:T(8,128)(2,1)}), bf16[4,32,512]{2,1,0:T(8,128)(2,1)S(1)}, u32[]{:S(2)}, u32[]{:S(2)}) async-start(bf16[4,32,512]{2,1,0:T(8,128)(2,1)} %shard_map.189), calls=%async_computation.5 | async-start | bytes 262144 | tf_op jit(solution)/shard_map/all_to_all | solution.py:563
  92.2 26.2 %all-to-all-start.6 = ((f32[8,128,128]{2,1,0:T(8,128)}), f32[8,128,128]{2,1,0:T(8,128)S(1)}, u32[]{:S(2)}, u32[]{:S(2)}) async-start(f32[8,128,128]{2,1,0:T(8,128)} %bitcast.10), calls=%async_computation.6 | async-start | bytes 1048576 | tf_op jit(solution)/shard_map/all_to_all | solution.py:563
  97.4 21.9 %collective-permute-start.6 = (bf16[6,64,128]{2,1,0:T(8,128)(2,1)}, bf16[6,64,128]{2,1,0:T(8,128)(2,1)S(1)}, u32[]{:S(2)}, u32[]{:S(2)}) collective-permute-start(bf16[6,64,128]{2,1,0:T(8,128)(2,1)} %pad_maximum_fusion.3), channel_id=1, source_target_pairs={{0,1},{1,2},{2,3},{4,5},{5,6},{6,7},{8,9},{9,10},{10,11},{12,13},{... | collective-permute-start | bytes 294920 | tf_op jit(solution)/shard_map/ppermute | solution.py:520
  101.3 18.0 %collective-permute-start.7 = (bf16[6,64,128]{2,1,0:T(8,128)(2,1)}, bf16[6,64,128]{2,1,0:T(8,128)(2,1)S(1)}, u32[]{:S(2)}, u32[]{:S(2)}) collective-permute-start(bf16[6,64,128]{2,1,0:T(8,128)(2,1)} %pad_maximum_fusion.4), channel_id=1, source_target_pairs={{1,0},{2,1},{3,2},{5,4},{6,5},{7,6},{9,8},{10,9},{11,10},{13,12},{... | collective-permute-start | bytes 294920 | tf_op jit(solution)/shard_map/ppermute | solution.py:520
  103.9 20.6 %copy-start.9 = (bf16[4,8,64,128]{3,2,1,0:T(8,128)(2,1)S(1)}, bf16[4,8,64,128]{3,2,1,0:T(8,128)(2,1)}, u32[]{:S(2)}) copy-start(bf16[4,8,64,128]{3,2,1,0:T(8,128)(2,1)} %copy-done.8) | copy-start | bytes 1572868
  103.9 34.6 %copy-start = (bf16[192,4096]{1,0:T(8,128)(2,1)S(1)}, bf16[192,4096]{1,0:T(8,128)(2,1)}, u32[]{:S(2)}) copy-start(bf16[192,4096]{1,0:T(8,128)(2,1)} %constant.30.clone.table_ref) | copy-start | bytes 4718596
  119.9 13.6 %all-to-all-start.7 = ((bf16[4,64,512]{2,1,0:T(8,128)(2,1)}), bf16[4,64,512]{2,1,0:T(8,128)(2,1)S(1)}, u32[]{:S(2)}, u32[]{:S(2)}) async-start(bf16[4,64,512]{2,1,0:T(8,128)(2,1)} %pad_maximum_fusion), calls=%async_computation.7 | async-start | bytes 524288 | tf_op jit(solution)/shard_map/all_to_all | solution.py:563
  134.7 16.4 %all-to-all-start.8 = ((f32[8,48,512]{2,1,0:T(8,128)}), f32[8,48,512]{2,1,0:T(8,128)S(1)}, u32[]{:S(2)}, u32[]{:S(2)}) async-start(f32[8,48,512]{2,1,0:T(8,128)} %shard_map.192), calls=%async_computation.8 | async-start | bytes 1572864 | tf_op jit(solution)/shard_map/all_to_all | solution.py:563
  140.6 12.0 %copy-start.11 = (bf16[96,128]{1,0:T(8,128)(2,1)S(1)}, bf16[96,128]{1,0:T(8,128)(2,1)}, u32[]{:S(2)}) copy-start(bf16[96,128]{1,0:T(8,128)(2,1)} %constant.25.clone.inverse_ref) | copy-start | bytes 73732
  (17 other events, 21.9 us)

commit v4 on v3

--- a/solution.py
+++ b/solution.py
@@ -71,12 +71,14 @@
     return out
 
 
-def x_tables(wide, mz):
+def x_tables(wide, mz, mx):
     theta = angles(centred(MX), np.arange(wide), wide)
     eye = np.eye(mz)
     forward = np.einsum("rkRx,zZ->krzxRZ", rotation(theta, -1.0), eye)
     inverse = np.einsum("rxRk,zZ->xrzkRZ", rotation(theta.T, 1.0), eye)
     size_k, size_x = MX * 2 * mz, wide * 2 * mz
+    forward = forward.reshape(MX // mx, mx, 2, mz, size_x).transpose(0, 2, 3, 1, 4)
+    inverse = inverse.reshape(size_x, MX // mx, mx, 2, mz).transpose(0, 1, 3, 4, 2)
     return against_pieces(forward.reshape(size_k, size_x), inverse.reshape(size_x, size_k))
 
 
@@ -294,16 +296,31 @@
 SPAN = 8 * C
 
 
-def y_forward(data_ref, table_ref, store):
-    data = pieces(data_ref[...].astype(F32))
-    got = jnp.dot(table_ref[...], data, preferred_element_type=F32)
-    for q in range(got.shape[1] // C):
+def y_forward(mz, data_ref, table_ref, rows_ref, store):
+    ny, _, lanes = data_ref.shape
+    cy = lanes // C
+    count = rows_ref.shape[1] // C
+    for owner in range(ny):
+        data = data_ref[owner].astype(F32)
+        for part in range(2):
+            for kz in range(mz):
+                mx = count // mz
+                start = (part * mz + kz) * mx
+                block = data[start : start + mx]
+                block = jnp.stack([block[:, y * C : (y + 1) * C] for y in range(cy)])
+                block = jnp.swapaxes(block, 0, 1)
+                row = (part * ny + owner) * cy
+                for kx in range(mx):
+                    column = (kz * mx + kx) * C
+                    rows_ref[row : row + cy, column : column + C] = block[kx]
+    got = jnp.dot(table_ref[...], pieces(rows_ref[...]), preferred_element_type=F32)
+    for q in range(count):
         block = got[:, q * C : (q + 1) * C]
         for part in range(2):
             store(q // QUAD, part, q % QUAD, block[part * MY : (part + 1) * MY])
 
 
-def y_inverse(sum_ref, table_ref, out_ref):
+def y_inverse(mz, sum_ref, table_ref, out_ref, block_ref):
     rows = [
         jnp.concatenate(
             [
@@ -315,9 +332,24 @@
         )
         for part in range(2)
     ]
-    out_ref[...] = jnp.dot(
+    got = jnp.dot(
         table_ref[...], pieces(jnp.concatenate(rows, axis=0)), preferred_element_type=F32
     )
+    ny, _, lanes = out_ref.shape
+    cy = lanes // C
+    count = got.shape[1] // C
+    mx = count // mz
+    for owner in range(ny):
+        for part in range(2):
+            for kz in range(mz):
+                row = (part * ny + owner) * cy
+                block = got[row : row + cy, kz * mx * C : (kz + 1) * mx * C]
+                block = jnp.stack([block[:, kx * C : (kx + 1) * C] for kx in range(mx)])
+                block = jnp.swapaxes(block, 0, 1)
+                start = (part * mz + kz) * mx
+                for y in range(cy):
+                    block_ref[owner, start : start + mx, y * C : (y + 1) * C] = block[y]
+    out_ref[...] = block_ref[...].astype(out_ref.dtype)
 
 
 def place(part, pair):
@@ -326,11 +358,11 @@
 
 
 def spread_table():
-    return np.tile(np.kron(np.eye(C), np.ones((1, C))), (3, 1)).astype(jnp.bfloat16)
+    return np.tile(np.kron(np.eye(C), np.ones((1, C))), (2, 1)).astype(jnp.bfloat16)
 
 
 def gather_table():
-    return np.kron(np.eye(C), np.ones((C, 1))).astype(jnp.bfloat16)
+    return np.kron(np.eye(SPAN // C), np.ones((1, C))).astype(jnp.bfloat16)
 
 
 def tiles():
@@ -356,7 +388,17 @@
 
 
 def mix_kernel(
-    data_ref, weight_ref, table_ref, forward_ref, inverse_ref, modes_ref, out_ref, sum_ref
+    mz,
+    data_ref,
+    weight_ref,
+    table_ref,
+    forward_ref,
+    inverse_ref,
+    modes_ref,
+    out_ref,
+    sum_ref,
+    rows_ref,
+    block_ref,
 ):
     step = pl.program_id(0)
 
@@ -364,12 +406,10 @@
     def _():
         def store(group, part, pair, values):
             high = values.astype(BF16)
-            rest = values - high.astype(F32)
-            middle = rest.astype(BF16)
-            low = (rest - middle.astype(F32)).astype(BF16)
-            modes_ref[group, place(part, pair), :] = jnp.concatenate([high, middle, low], axis=1)
-
-        y_forward(data_ref, forward_ref, store)
+            low = (values - high.astype(F32)).astype(BF16)
+            modes_ref[group, place(part, pair), :] = jnp.concatenate([high, low], axis=1)
+
+        y_forward(mz, data_ref, forward_ref, rows_ref, store)
 
     spread = spread_modes(modes_ref[step], table_ref)
     real = [jnp.zeros((MY, 2 * C), F32)] * QUAD
@@ -390,11 +430,22 @@
 
     @pl.when(step == pl.num_programs(0) - 1)
     def _():
-        y_inverse(sum_ref, inverse_ref, out_ref)
+        y_inverse(mz, sum_ref, inverse_ref, out_ref, block_ref)
 
 
 def mix_back_kernel(
-    data_ref, weight_ref, table_ref, forward_ref, inverse_ref, modes_ref, out_ref, sum_ref, term_ref
+    mz,
+    data_ref,
+    weight_ref,
+    table_ref,
+    forward_ref,
+    inverse_ref,
+    modes_ref,
+    out_ref,
+    sum_ref,
+    rows_ref,
+    block_ref,
+    term_ref,
 ):
     step = pl.program_id(0)
 
@@ -403,9 +454,9 @@
         def store(group, part, pair, values):
             modes_ref[group, place(part, pair), :] = jnp.concatenate([values, values], axis=1)
 
-        y_forward(data_ref, forward_ref, store)
-
-    total = None
+        y_forward(mz, data_ref, forward_ref, rows_ref, store)
+
+    total = []
     for piece, tile, columns in tiles():
         for pair in range(QUAD):
             mode_re = modes_ref[step, place(0, pair), :]
@@ -420,15 +471,19 @@
             ).astype(BF16)
         if columns.stop % SPAN == 0:
             whole_piece = slice(piece * SPAN, (piece + 1) * SPAN)
-            got = jnp.dot(
-                term_ref[:, whole_piece], table_ref[whole_piece, :], preferred_element_type=F32
+            total.append(
+                lax.dot_general(
+                    table_ref[...],
+                    term_ref[:, whole_piece],
+                    (((1,), (1,)), ((), ())),
+                    preferred_element_type=F32,
+                )
             )
-            total = got if total is None else total + got
-    sum_ref[step] = total
+    sum_ref[step] = jnp.concatenate(total, axis=0).T
 
     @pl.when(step == pl.num_programs(0) - 1)
     def _():
-        y_inverse(sum_ref, inverse_ref, out_ref)
+        y_inverse(mz, sum_ref, inverse_ref, out_ref, block_ref)
 
 
 def outer_kernel(alpha, modes_ref, back_ref, table_ref, out_ref):
@@ -473,45 +528,56 @@
     return pl.BlockSpec(shape, lambda step: (0,) * len(shape))
 
 
-def group_block(shape):
+def group_block(shape, start=0):
     per = shape[2] // QUAD
     return pl.BlockSpec(
-        (2, 1, QUAD) + shape[3:], lambda step: (0, step // per, step % per, 0, 0)
-    )
-
-
-def per_mode(kernel, data, weight, tables, modes, scratch=()):
+        (2, 1, QUAD) + shape[3:],
+        lambda step: (0, (step + start) // per, (step + start) % per, 0, 0),
+    )
+
+
+def per_mode(kernel, data, weight, tables, modes, kind, scratch=()):
     _, mz, mx, _, _ = weight.shape
     groups = mz * mx // QUAD
     rows = 2 * QUAD * MY
     modes_shape = (groups, rows, modes[0])
-    out_shape = (tables[-1].shape[0], mz * mx * C)
+    return pl.pallas_call(
+        functools.partial(kernel, mz),
+        grid=(groups,),
+        in_specs=[full(data.shape), group_block(weight.shape)] + [full(t.shape) for t in tables],
+        out_specs=[full(modes_shape), full(data.shape)],
+        out_shape=[
+            jax.ShapeDtypeStruct(modes_shape, modes[1]),
+            jax.ShapeDtypeStruct(data.shape, kind),
+        ],
+        scratch_shapes=[
+            pltpu.VMEM((groups, rows, C), F32),
+            pltpu.VMEM((tables[-1].shape[0], mz * mx * C), F32),
+            pltpu.VMEM(data.shape, F32),
+            *scratch,
+        ],
+        compiler_params=params(48),
+        cost_estimate=cost(weight.size * 8, weight.size * 2),
+    )(data, weight, *tables)
+
+
+def outer(modes, back, table, shape, alpha, start, count, prior=None):
+    def kernel(*refs):
+        outer_kernel(alpha, *refs[:3], refs[-1])
+
+    group = lambda ref: pl.BlockSpec((1,) + ref.shape[1:], lambda step: (step + start, 0, 0))
+    given = () if prior is None else (prior,)
     return pl.pallas_call(
         kernel,
-        grid=(groups,),
-        in_specs=[full(data.shape), group_block(weight.shape)] + [full(t.shape) for t in tables],
-        out_specs=[full(modes_shape), full(out_shape)],
-        out_shape=[
-            jax.ShapeDtypeStruct(modes_shape, modes[1]),
-            jax.ShapeDtypeStruct(out_shape, F32),
-        ],
-        scratch_shapes=[pltpu.VMEM((groups, rows, C), F32), *scratch],
-        compiler_params=params(56),
-        cost_estimate=cost(weight.size * 8, weight.size * 2),
-    )(data, weight, *tables)
-
-
-def outer(modes, back, table, shape, alpha):
-    group = lambda ref: pl.BlockSpec((1,) + ref.shape[1:], lambda step: (step, 0, 0))
-    return pl.pallas_call(
-        functools.partial(outer_kernel, alpha),
-        grid=(modes.shape[0],),
-        in_specs=[group(modes), group(back), full(table.shape)],
-        out_specs=group_block(shape),
+        grid=(count,),
+        in_specs=[group(modes), group(back), full(table.shape)]
+        + [pl.BlockSpec(memory_space=pl.ANY)] * len(given),
+        out_specs=group_block(shape, start),
         out_shape=jax.ShapeDtypeStruct(shape, F32),
-        compiler_params=params(32),
+        input_output_aliases={3: 0} if given else {},
+        compiler_params=params(24),
         cost_estimate=cost(math.prod(shape) * 4, math.prod(shape) * 4),
-    )(modes, back, table)
+    )(modes, back, table, *given)
 
 
 def shift(block, axis, step):
@@ -580,7 +646,7 @@
     z_grad = jnp.asarray(z_forward_table(double)(nx, mz))
     z_spectral = jnp.asarray(z_inverse_table(nx, mz, beta * double))
     z_back = jnp.asarray(z_inverse_table(nx, mz, alpha * beta * ones))
-    x_fwd, x_inv = (jnp.asarray(t) for t in x_tables(wide_x, mz))
+    x_fwd, x_inv = (jnp.asarray(t) for t in x_tables(wide_x, mz, mx))
     y_fwd, y_inv = (jnp.asarray(t) for t in y_tables(wide_y))
     spread, gather = jnp.asarray(spread_table()), jnp.asarray(gather_table())
     lanes = cy * c
@@ -597,14 +663,6 @@
             moved=8 * block.size,
         )[0]
 
-    def to_rows(block):
-        block = block.reshape(ny, mx, 2, mz, cy, c).transpose(2, 0, 4, 3, 1, 5)
-        return block.reshape(2 * wide_y, mz * mx * c)
-
-    def to_blocks(rows):
-        block = rows.reshape(2, ny, cy, mz, mx, c).transpose(1, 4, 0, 3, 2, 5)
-        return block.reshape(ny, mx * 2 * mz, lanes)
-
     slab_shape = ((nx, x_rows, lanes), F32)
     turned_shape = ((cx, cy, c, z), BF16)
 
@@ -624,13 +682,19 @@
     )
     block = x_stage(x_fwd, swap(slab, "gx"), ny)
     block, *faces = together(block, *x_halos(turned))
-    rows = to_rows(swap(block, "gy"))
-    modes_in, rows = per_mode(
-        mix_kernel, rows, spectral_weight, (spread, y_fwd, y_inv), (3 * c, BF16)
-    )
-    block, *edges = together(to_blocks(rows), *y_halos(turned, *faces))
+    modes_in, block = per_mode(
+        mix_kernel,
+        swap(block, "gy"),
+        spectral_weight,
+        (spread, y_fwd, y_inv),
+        (2 * c, BF16),
+        F32,
+    )
+    block, *faces = together(block, *faces)
+    edges = y_halos(turned, *faces)
+    block = x_stage(x_inv, swap(block, "gy"), nx)
+    block, *edges = together(block, *edges)
     rim = (*faces, *edges)
-    block = x_stage(x_inv, swap(block, "gy"), nx)
     stencil = conv(turned, rim, conv_table, False)
     output, grad, slab = call(
         functools.partial(gelu_kernel, nx),
@@ -640,29 +704,39 @@
         moved=state.size * 12,
     )
 
+    grad_taps = weight_grad(grad, turned, rim)
     block = x_stage(x_fwd, swap(slab, "gx"), ny, BF16)
-    grad_taps = weight_grad(grad, turned, rim)
     block, *faces = together(block, *x_halos(grad))
-    block, grad_taps = together(swap(block, "gy"), grad_taps)
+    edges = y_halos(grad, *faces)
+    block, grad_taps, *edges = together(swap(block, "gy"), grad_taps, *edges)
     mine = swap(grad_taps.reshape(nx, -1, 2 * c), "gx").sum(0)
-    back_modes, rows = per_mode(
+    back_modes, block = per_mode(
         mix_back_kernel,
-        to_rows(block),
+        block,
         spectral_weight,
         (gather, y_fwd, y_inv),
         (2 * c, F32),
+        BF16,
         [pltpu.VMEM((2 * QUAD * MY, c * c), BF16)],
     )
-    packed = jnp.concatenate(jnp.split(mine, lanes // (2 * c)), axis=1)
+    packed = jnp.concatenate(jnp.split(mine, lanes // (2 * c)), axis=1).astype(BF16)
     extra = packed.shape[0]
     packed = jnp.broadcast_to(packed[None], (ny, extra, lanes))
-    block = jnp.concatenate([to_blocks(rows), packed], axis=1).astype(BF16)
-    block, *edges = together(block, *y_halos(grad, *faces))
-    block = x_stage(x_inv, swap(block, "gy"), nx, F32, extra)
+    block = x_stage(
+        x_inv, swap(jnp.concatenate([block, packed], axis=1), "gy"), nx, F32, extra
+    )
     stencil_back = conv(grad, (*faces, *edges), back_table, True)
-    block, stencil_back = together(block, stencil_back)
+    shape = spectral_weight.shape
+    groups = modes_in.shape[0]
+    early = groups // 2
+    grad_modes = None
+    if early:
+        grad_modes = outer(modes_in, back_modes, spread, shape, alpha, 0, early)
+        block, stencil_back, grad_modes = together(block, stencil_back, grad_modes)
     message = swap(block, "gx")
-    grad_modes = outer(modes_in, back_modes, spread, spectral_weight.shape, alpha)
+    grad_modes = outer(
+        modes_in, back_modes, spread, shape, alpha, early, groups - early, grad_modes
+    )
     grad_state = call(
         functools.partial(finish_kernel, nx),
         [((c, cx, cy, z), F32)],

time: 156 us -> 159 us (1.019)
  blocking collectives: 10.3 us -> 0 us
  starting transfers between devices: 53.2 us -> 60.6 us
  waiting for transfers between devices: 19.7 us -> 24.4 us
  local copies, waits for them, and re-layouts: 21.4 us -> 24.4 us
  other arithmetic: 3.71 us -> 1.87 us
    all_to_all x1 -> x0, blocking collectives: 10.3 us -> none  [swap(): return lax.all_to_all(block, axis, split_axis=0, concat_axis=0, tiled=True)]
    unnamed x66 -> x80, local copies, waits for them, and re-layouts: 13.7 us -> 22.5 us
    reshape x12 -> x0, local copies, waits for them, and re-layouts: 7.66 us -> none  [the longest x4 3.89 us: to_blocks(): block = rows.reshape(2, ny, cy, mz, mx, c).transpose(1, 4, 0, 3, 2, 5)]
    all_to_all x8 -> x9, starting transfers between devices: 34.5 us -> 41.6 us  [swap(): return lax.all_to_all(block, axis, split_axis=0, concat_axis=0, tiled=True)]
    all_to_all x8 -> x9, waiting for transfers between devices: 19.7 us -> 22.7 us  [swap(): return lax.all_to_all(block, axis, split_axis=0, concat_axis=0, tiled=True)]
    concatenate x4, other arithmetic: 1.98 us -> 0.06 us  [y_halos(): jnp.concatenate([xlo[None, y], turned[:, y], xhi[None, y]], axis=0)]
    ppermute x8, waiting for transfers between devices: 0.02 us -> 1.66 us  [shift(): return lax.ppermute(block, axis, pairs)]
    pallas_call x3 -> x4, Pallas kernels: 26.9 us -> 26.5 us  [the longest x2 17.5 us: per_mode(): pl.pallas_call(functools.partial(kernel, mz), grid=(groups,), in_specs=[f...]
  transfers between devices with their start and end apart: 16 -> 17, of which waited for: 6 -> 7; matrix products, arithmetic and copies ran while one was open for 7% -> 1% of each run, Pallas kernels for 23% -> 18%
where the time goes in v4:
time: 159 us; the launch traced here: 157 us
  starting transfers between devices  60.6 us (38%)
  Pallas kernels  44.3 us (28%)
  local copies, waits for them, and re-layouts  24.4 us (15%)
  waiting for transfers between devices  24.4 us (15%)
  other arithmetic  1.87 us (1%)
    all_to_all x9, starting transfers between devices, swap(): return lax.all_to_all(block, axis, split_axis=0, concat_axis=0, tiled=True)  41.6 us
    all_to_all x9, waiting for transfers between devices, swap(): return lax.all_to_all(block, axis, split_axis=0, concat_axis=0, tiled=True)  22.7 us
    unnamed x80, local copies, waits for them, and re-layouts  22.5 us
    ppermute x8, starting transfers between devices, shift(): return lax.ppermute(block, axis, pairs)  19.1 us
    pallas_call x12, Pallas kernels, call(): pl.pallas_call(kernel, out_shape=[jax.ShapeDtypeStruct(*out) for out in o...  17.7 us
    pallas_call x2, Pallas kernels, per_mode(): pl.pallas_call(functools.partial(kernel, mz), grid=(groups,), in_specs=[f...  17.5 us
    pallas_call x2, Pallas kernels, outer(): pl.pallas_call(kernel, grid=(count,), in_specs=[group(modes), group(back)...  9 us
  transfers between devices with their start and end apart: 17, of which 7 were waited for; matrix products, arithmetic and copies ran while one was open for 1% of the time, Pallas kernels for 18%

profile of v4, /device:TPU:0, one launch (start us, length us, event | category | flops | bytes accessed | tf_op | source)
XLA Modules:
  0.0 156.5 jit_solution(14088625493967941701)
XLA Ops:
  3.6 5.2 %all-to-all-start = ((f32[8,16,512]{2,1,0:T(8,128)}), f32[8,16,512]{2,1,0:T(8,128)S(1)}, u32[]{:S(2)}, u32[]{:S(2)}) async-start(f32[8,16,512]{2,1,0:T(8,128)} %get-tuple-element.38), calls=%async_computation | async-start | bytes 524288 | tf_op jit(solution)/shard_map/all_to_all | solution.py:629
  8.8 1.3 collective-permute-start.1
  10.1 3.0 %collective-permute-start = (bf16[8,64,128]{2,1,0:T(8,128)(2,1)S(1)}, bf16[8,64,128]{2,1,0:T(8,128)(2,1)S(1)}, u32[]{:S(2)}, u32[]{:S(2)}) collective-permute-start(bf16[8,64,128]{2,1,0:T(8,128)(2,1)S(1)} %get-tuple-element.76), channel_id=1, source_target_pairs={{0,4},{4,8},{8,12},{12,16},{16,20},{20,24},{24,28},{1,5},{5,9},{9,... | collective-permute-start | bytes 393224 | tf_op jit(solution)/shard_map/ppermute | solution.py:586
  13.1 2.6 %all-to-all-done.data_ref = f32[8,16,512]{2,1,0:T(8,128)S(1)} async-done(((f32[8,16,512]{2,1,0:T(8,128)}), f32[8,16,512]{2,1,0:T(8,128)S(1)}, u32[]{:S(2)}, u32[]{:S(2)}) %all-to-all-start) | async-done | bytes 262176 | tf_op jit(solution)/shard_map/all_to_all | solution.py:629
  17.6 4.9 %all-to-all-start.1 = ((f32[4,32,512]{2,1,0:T(8,128)}), f32[4,32,512]{2,1,0:T(8,128)S(1)}, u32[]{:S(2)}, u32[]{:S(2)}) async-start(f32[4,32,512]{2,1,0:T(8,128)} %shard_map.183), calls=%async_computation.1 | async-start | bytes 524288 | tf_op jit(solution)/shard_map/all_to_all | solution.py:629
  22.5 8.3 %all-to-all-done.1.data_ref = f32[4,32,512]{2,1,0:T(8,128)S(1)} async-done(((f32[4,32,512]{2,1,0:T(8,128)}), f32[4,32,512]{2,1,0:T(8,128)S(1)}, u32[]{:S(2)}, u32[]{:S(2)}) %all-to-all-start.1) | async-done | bytes 262176 | tf_op jit(solution)/shard_map/all_to_all | solution.py:629
  33.5 9.1 %shard_map.184 = (bf16[4,256,128]{2,1,0:T(8,128)(2,1)S(1)}, f32[4,32,512]{2,1,0:T(8,128)}) custom-call(f32[4,32,512]{2,1,0:T(8,128)S(1)} %all-to-all-done.1.data_ref, bf16[2,2,8,32,4096]{4,3,2,1,0:T(8,128)(2,1)} %weight_ref.3, bf16[128,4096]{1,0:T(8,128)(2,1)S(1)} %copy-done, bf16[64,192]{1,0:T(8,128)(2,1)S(1)} %copy-done.19, bf16[64,192]{1,0:T(8,128)(2,1)S(1)} %copy-done.17), custom_call_target="tpu_custom_call" | custom-call | flops 33554432 | bytes 8388608 | tf_op jit(solution)/shard_map/pallas_call | solution.py:544
  42.5 3.4 %all-to-all-start.2 = ((f32[4,32,512]{2,1,0:T(8,128)}), f32[4,32,512]{2,1,0:T(8,128)S(1)}, u32[]{:S(2)}, u32[]{:S(2)}) async-start(f32[4,32,512]{2,1,0:T(8,128)} %get-tuple-element.45), calls=%async_computation.2 | async-start | bytes 524288 | tf_op jit(solution)/shard_map/all_to_all | solution.py:629
  46.0 3.9 %collective-permute-start.2 = (bf16[6,64,128]{2,1,0:T(8,128)(2,1)S(1)}, bf16[6,64,128]{2,1,0:T(8,128)(2,1)S(1)}, u32[]{:S(2)}, u32[]{:S(2)}) collective-permute-start(bf16[6,64,128]{2,1,0:T(8,128)(2,1)S(1)} %pad_maximum_fusion.1), channel_id=1, source_target_pairs={{0,1},{1,2},{2,3},{4,5},{5,6},{6,7},{8,9},{9,10},{10,11},{12,13},{... | collective-permute-start | bytes 294920 | tf_op jit(solution)/shard_map/ppermute | solution.py:586
  51.2 1.7 %all-to-all-done.2.data_ref = f32[4,32,512]{2,1,0:T(8,128)S(1)} async-done(((f32[4,32,512]{2,1,0:T(8,128)}), f32[4,32,512]{2,1,0:T(8,128)S(1)}, u32[]{:S(2)}, u32[]{:S(2)}) %all-to-all-start.2) | async-done | bytes 262176 | tf_op jit(solution)/shard_map/all_to_all | solution.py:629
  54.8 1.6 %collective-permute-done.3.yhi_ref = bf16[6,64,128]{2,1,0:T(8,128)(2,1)S(1)} collective-permute-done((bf16[6,64,128]{2,1,0:T(8,128)(2,1)S(1)}, bf16[6,64,128]{2,1,0:T(8,128)(2,1)S(1)}, u32[]{:S(2)}, u32[]{:S(2)}) %collective-permute-start.3) | collective-permute-done | bytes 98336 | tf_op jit(solution)/shard_map/ppermute | solution.py:586
  57.1 3.9 %all-to-all-start.3 = ((f32[8,16,512]{2,1,0:T(8,128)}), f32[8,16,512]{2,1,0:T(8,128)S(1)}, u32[]{:S(2)}, u32[]{:S(2)}) async-start(f32[8,16,512]{2,1,0:T(8,128)} %shard_map.185), calls=%async_computation.3 | async-start | bytes 524288 | tf_op jit(solution)/shard_map/all_to_all | solution.py:629
  67.7 1.9 %shard_map.187.stencil_ref = f32[4,64,1024]{2,1,0:T(8,128)S(1)} custom-call(bf16[4,8,64,128]{3,2,1,0:T(8,128)(2,1)S(1)} %copy-done.11, bf16[8,64,128]{2,1,0:T(8,128)(2,1)S(1)} %copy-done.28, bf16[8,64,128]{2,1,0:T(8,128)(2,1)S(1)} %collective-permute-done.1.xhi_ref, bf16[6,64,128]{2,1,0:T(8,128)(2,1)S(1)} %copy-done.33, bf16[6,64,128]{2,1,0:T(8,128)(2,1)S(1)} %copy-done.36, ...), custom_call_target="tpu_custom_call" | custom-call | flops 905969664 | bytes 2097152 | tf_op jit(solution)/shard_map/pallas_call | solution.py:516
  69.6 2.3 %shard_map.188 = (bf16[64,4,8,128]{3,2,1,0:T(8,128)(2,1)}, bf16[4,8,64,128]{3,2,1,0:T(8,128)(2,1)S(1)}, f32[8,16,512]{2,1,0:T(8,128)}) custom-call(f32[4,64,1024]{2,1,0:T(8,128)S(1)} %shard_map.187.stencil_ref, f32[8,16,512]{2,1,0:T(8,128)S(1)} %all-to-all-done.3.slab_ref, bf16[64,4,8,128]{3,2,1,0:T(8,128)(2,1)S(1)} %copy-done.4, ...), custom_call_target="tpu_custom_call" | custom-call | flops 100663296 | bytes 3145728 | tf_op jit(solution)/shard_map/pallas_call | solution.py:516
  72.7 4.2 %all-to-all-start.4 = ((f32[8,16,512]{2,1,0:T(8,128)}), f32[8,16,512]{2,1,0:T(8,128)S(1)}, u32[]{:S(2)}, u32[]{:S(2)}) async-start(f32[8,16,512]{2,1,0:T(8,128)} %get-tuple-element.51), calls=%async_computation.4 | async-start | bytes 524288 | tf_op jit(solution)/shard_map/all_to_all | solution.py:629
  77.9 1.3 collective-permute-start.5
  79.2 3.0 %collective-permute-start.4 = (bf16[8,64,128]{2,1,0:T(8,128)(2,1)S(1)}, bf16[8,64,128]{2,1,0:T(8,128)(2,1)S(1)}, u32[]{:S(2)}, u32[]{:S(2)}) collective-permute-start(bf16[8,64,128]{2,1,0:T(8,128)(2,1)S(1)} %get-tuple-element.72), channel_id=1, source_target_pairs={{0,4},{4,8},{8,12},{12,16},{16,20},{20,24},{24,28},{1,5},{5,9},{9,... | collective-permute-start | bytes 393224 | tf_op jit(solution)/shard_map/ppermute | solution.py:586
  84.7 3.6 %all-to-all-start.5 = ((bf16[4,32,512]{2,1,0:T(8,128)(2,1)}), bf16[4,32,512]{2,1,0:T(8,128)(2,1)S(1)}, u32[]{:S(2)}, u32[]{:S(2)}) async-start(bf16[4,32,512]{2,1,0:T(8,128)(2,1)} %shard_map.189), calls=%async_computation.5 | async-start | bytes 262144 | tf_op jit(solution)/shard_map/all_to_all | solution.py:629
  88.4 3.9 %collective-permute-start.6 = (bf16[6,64,128]{2,1,0:T(8,128)(2,1)S(1)}, bf16[6,64,128]{2,1,0:T(8,128)(2,1)S(1)}, u32[]{:S(2)}, u32[]{:S(2)}) collective-permute-start(bf16[6,64,128]{2,1,0:T(8,128)(2,1)S(1)} %pad_maximum_fusion.3), channel_id=1, source_target_pairs={{0,1},{1,2},{2,3},{4,5},{5,6},{6,7},{8,9},{9,10},{10,11},{12,13},{... | collective-permute-start | bytes 294920 | tf_op jit(solution)/shard_map/ppermute | solution.py:586
  92.4 1.3 collective-permute-start.7
  98.5 3.1 %shard_map.190 = f32[1024,128]{1,0:T(8,128)} custom-call(bf16[4,8,64,128]{3,2,1,0:T(8,128)(2,1)S(1)} %copy-done.14, bf16[4,8,64,128]{3,2,1,0:T(8,128)(2,1)S(1)} %copy-done.12, bf16[8,64,128]{2,1,0:T(8,128)(2,1)S(1)} %copy-done.29, bf16[8,64,128]{2,1,0:T(8,128)(2,1)S(1)} %collective-permute-done.1.xhi_ref, bf16[6,64,128]{2,1,0:T(8,128)(2,1)S(1)} %copy-done.34, ...), custom_call_target="tpu_custom_call" | custom-call | flops 905969664 | bytes 2097152 | tf_op jit(solution)/shard_map/pallas_call | solution.py:516
  102.2 6.9 %all-to-all-start.6 = ((f32[8,128,128]{2,1,0:T(8,128)}), f32[8,128,128]{2,1,0:T(8,128)}, u32[]{:S(2)}, u32[]{:S(2)}) async-start(f32[8,128,128]{2,1,0:T(8,128)} %bitcast.8), calls=%async_computation.6 | async-start | bytes 1048576 | tf_op jit(solution)/shard_map/all_to_all | solution.py:629
  109.1 8.5 %shard_map.191 = (f32[4,256,128]{2,1,0:T(8,128)S(1)}, bf16[4,32,512]{2,1,0:T(8,128)(2,1)S(1)}) custom-call(bf16[4,32,512]{2,1,0:T(8,128)(2,1)S(1)} %all-to-all-done.5.data_ref, bf16[2,2,8,32,4096]{4,3,2,1,0:T(8,128)(2,1)} %weight_ref.3, bf16[8,512]{1,0:T(8,128)(2,1)S(1)} %copy-done.26, bf16[64,192]{1,0:T(8,128)(2,1)S(1)} %copy-done.20, ...), custom_call_target="tpu_custom_call" | custom-call | flops 33554432 | bytes 8388608 | tf_op jit(solution)/shard_map/pallas_call | solution.py:544
  117.6 1.4 all-to-all-done.6
  120.8 5.7 %all-to-all-start.7 = ((bf16[4,64,512]{2,1,0:T(8,128)(2,1)}), bf16[4,64,512]{2,1,0:T(8,128)(2,1)S(1)}, u32[]{:S(2)}, u32[]{:S(2)}) async-start(bf16[4,64,512]{2,1,0:T(8,128)(2,1)} %pad_maximum_fusion), calls=%async_computation.7 | async-start | bytes 524288 | tf_op jit(solution)/shard_map/all_to_all | solution.py:629
  126.5 4.5 %shard_map.194.refs_3_ = f32[2,2,8,32,4096]{4,3,2,1,0:T(8,128)} custom-call(bf16[4,256,128]{2,1,0:T(8,128)(2,1)S(1)} %get-tuple-element.62.refs_0_, f32[4,256,128]{2,1,0:T(8,128)S(1)} %get-tuple-element.63.refs_1_, bf16[128,4096]{1,0:T(8,128)(2,1)S(1)} %copy-done.1), custom_call_target="tpu_custom_call" | custom-call | flops 16777216 | bytes 16777216 | tf_op jit(solution)/shard_map/pallas_call | solution.py:570
  131.9 1.9 %shard_map.193.stencil_ref = f32[4,64,1024]{2,1,0:T(8,128)S(1)} custom-call(bf16[4,8,64,128]{3,2,1,0:T(8,128)(2,1)S(1)} %copy-done.15, bf16[8,64,128]{2,1,0:T(8,128)(2,1)S(1)} %collective-permute-done.4.xlo_ref, bf16[8,64,128]{2,1,0:T(8,128)(2,1)S(1)} %collective-permute-done.5.xhi_ref, bf16[6,64,128]{2,1,0:T(8,128)(2,1)S(1)} %collective-permute-done.6.ylo_ref, ...), custom_call_target="tpu_custom_call" | custom-call | flops 905969664 | bytes 2097152 | tf_op jit(solution)/shard_map/pallas_call | solution.py:516
  136.0 3.8 %all-to-all-start.8 = ((f32[8,48,512]{2,1,0:T(8,128)}), f32[8,48,512]{2,1,0:T(8,128)S(1)}, u32[]{:S(2)}, u32[]{:S(2)}) async-start(f32[8,48,512]{2,1,0:T(8,128)} %shard_map.192), calls=%async_computation.8 | async-start | bytes 1572864 | tf_op jit(solution)/shard_map/all_to_all | solution.py:629
  139.8 4.5 %shard_map.196 = f32[2,2,8,32,4096]{4,3,2,1,0:T(8,128)} custom-call(bf16[4,256,128]{2,1,0:T(8,128)(2,1)S(1)} %get-tuple-element.62.refs_0_, f32[4,256,128]{2,1,0:T(8,128)S(1)} %get-tuple-element.63.refs_1_, bf16[128,4096]{1,0:T(8,128)(2,1)S(1)} %copy-done.1, f32[2,2,8,32,4096]{4,3,2,1,0:T(8,128)} %shard_map.194.refs_3_), custom_call_target="tpu_custom_call", output_to_operand_aliasing={{}: (3, {})} | custom-call | flops 16777216 | bytes 16777216 | tf_op jit(solution)/shard_map/pallas_call | solution.py:570
  144.3 8.1 %all-to-all-done.8.slab_ref.message_ref = f32[8,48,512]{2,1,0:T(8,128)S(1)} async-done(((f32[8,48,512]{2,1,0:T(8,128)}), f32[8,48,512]{2,1,0:T(8,128)S(1)}, u32[]{:S(2)}, u32[]{:S(2)}) %all-to-all-start.8) | async-done | bytes 786464 | tf_op jit(solution)/shard_map/all_to_all | solution.py:629
  152.3 1.5 shard_map.197
  155.1 1.4 shard_map.195
  (114 shorter events, 34.0 us)
Async XLA Ops:
  2.4 67.1 %copy-start.4 = (bf16[64,4,8,128]{3,2,1,0:T(8,128)(2,1)S(1)}, bf16[64,4,8,128]{3,2,1,0:T(8,128)(2,1)}, u32[]{:S(2)}) copy-start(bf16[64,4,8,128]{3,2,1,0:T(8,128)(2,1)} %cot_ref.1) | copy-start | bytes 1572868
  2.4 67.1 %copy-start.22 = (bf16[96,128]{1,0:T(8,128)(2,1)S(1)}, bf16[96,128]{1,0:T(8,128)(2,1)}, u32[]{:S(2)}) copy-start(bf16[96,128]{1,0:T(8,128)(2,1)} %constant.24.clone.inverse_ref) | copy-start | bytes 73732
  2.4 67.2 %copy-start.23 = (bf16[96,128]{1,0:T(8,128)(2,1)S(1)}, bf16[96,128]{1,0:T(8,128)(2,1)}, u32[]{:S(2)}) copy-start(bf16[96,128]{1,0:T(8,128)(2,1)} %constant.23.clone.forward_ref) | copy-start | bytes 73732
  2.4 81.4 %copy-start.9 = (bf16[128,384]{1,0:T(8,128)(2,1)S(1)}, bf16[128,384]{1,0:T(8,128)(2,1)}, u32[]{:S(2)}) copy-start(bf16[128,384]{1,0:T(8,128)(2,1)} %constant.26.clone.table_ref) | copy-start | bytes 294916
  2.4 106.7 %copy-start.18 = (bf16[64,192]{1,0:T(8,128)(2,1)S(1)}, bf16[64,192]{1,0:T(8,128)(2,1)}, u32[]{:S(2)}) copy-start(bf16[64,192]{1,0:T(8,128)(2,1)} %constant.29.clone.inverse_ref) | copy-start | bytes 73732
  2.4 106.6 %copy-start.20 = (bf16[64,192]{1,0:T(8,128)(2,1)S(1)}, bf16[64,192]{1,0:T(8,128)(2,1)}, u32[]{:S(2)}) copy-start(bf16[64,192]{1,0:T(8,128)(2,1)} %constant.28.clone.forward_ref) | copy-start | bytes 73732
  2.4 106.6 %copy-start.26 = (bf16[8,512]{1,0:T(8,128)(2,1)S(1)}, bf16[8,512]{1,0:T(8,128)(2,1)}, u32[]{:S(2)}) copy-start(bf16[8,512]{1,0:T(8,128)(2,1)} %constant.31.clone.table_ref) | copy-start | bytes 24580
  3.6 18.9 %copy-start.10 = (bf16[4,8,64,128]{3,2,1,0:T(8,128)(2,1)}, bf16[4,8,64,128]{3,2,1,0:T(8,128)(2,1)S(1)}, u32[]{:S(2)}) copy-start(bf16[4,8,64,128]{3,2,1,0:T(8,128)(2,1)S(1)} %get-tuple-element.37.body_ref) | copy-start | bytes 1572868
  3.6 12.1 %all-to-all-start = ((f32[8,16,512]{2,1,0:T(8,128)}), f32[8,16,512]{2,1,0:T(8,128)S(1)}, u32[]{:S(2)}, u32[]{:S(2)}) async-start(f32[8,16,512]{2,1,0:T(8,128)} %get-tuple-element.38), calls=%async_computation | async-start | bytes 524288 | tf_op jit(solution)/shard_map/all_to_all | solution.py:629
  8.8 8.7 %collective-permute-start.1 = (bf16[8,64,128]{2,1,0:T(8,128)(2,1)S(1)}, bf16[8,64,128]{2,1,0:T(8,128)(2,1)S(1)}, u32[]{:S(2)}, u32[]{:S(2)}) collective-permute-start(bf16[8,64,128]{2,1,0:T(8,128)(2,1)S(1)} %get-tuple-element.75), channel_id=1, source_target_pairs={{4,0},{8,4},{12,8},{16,12},{20,16},{24,20},{28,24},{5,1},{9,5},{13... | collective-permute-start | bytes 393224 | tf_op jit(solution)/shard_map/ppermute | solution.py:586
  10.1 7.5 %collective-permute-start = (bf16[8,64,128]{2,1,0:T(8,128)(2,1)S(1)}, bf16[8,64,128]{2,1,0:T(8,128)(2,1)S(1)}, u32[]{:S(2)}, u32[]{:S(2)}) collective-permute-start(bf16[8,64,128]{2,1,0:T(8,128)(2,1)S(1)} %get-tuple-element.76), channel_id=1, source_target_pairs={{0,4},{4,8},{8,12},{12,16},{16,20},{20,24},{24,28},{1,5},{5,9},{9,... | collective-permute-start | bytes 393224 | tf_op jit(solution)/shard_map/ppermute | solution.py:586
  17.5 45.6 %copy-start.27 = (bf16[8,64,128]{2,1,0:T(8,128)(2,1)}, bf16[8,64,128]{2,1,0:T(8,128)(2,1)S(1)}, u32[]{:S(2)}) copy-start(bf16[8,64,128]{2,1,0:T(8,128)(2,1)S(1)} %collective-permute-done.xlo_ref) | copy-start | bytes 393220
  17.6 13.2 %all-to-all-start.1 = ((f32[4,32,512]{2,1,0:T(8,128)}), f32[4,32,512]{2,1,0:T(8,128)S(1)}, u32[]{:S(2)}, u32[]{:S(2)}) async-start(f32[4,32,512]{2,1,0:T(8,128)} %shard_map.183), calls=%async_computation.1 | async-start | bytes 524288 | tf_op jit(solution)/shard_map/all_to_all | solution.py:629
  33.5 93.0 %copy-start.1 = (bf16[128,4096]{1,0:T(8,128)(2,1)S(1)}, bf16[128,4096]{1,0:T(8,128)(2,1)}, u32[]{:S(2)}) copy-start(bf16[128,4096]{1,0:T(8,128)(2,1)} %constant.30.clone.table_ref.refs_2_) | copy-start | bytes 3145732
  42.5 10.4 %all-to-all-start.2 = ((f32[4,32,512]{2,1,0:T(8,128)}), f32[4,32,512]{2,1,0:T(8,128)S(1)}, u32[]{:S(2)}, u32[]{:S(2)}) async-start(f32[4,32,512]{2,1,0:T(8,128)} %get-tuple-element.45), calls=%async_computation.2 | async-start | bytes 524288 | tf_op jit(solution)/shard_map/all_to_all | solution.py:629
  46.0 8.8 %collective-permute-start.2 = (bf16[6,64,128]{2,1,0:T(8,128)(2,1)S(1)}, bf16[6,64,128]{2,1,0:T(8,128)(2,1)S(1)}, u32[]{:S(2)}, u32[]{:S(2)}) collective-permute-start(bf16[6,64,128]{2,1,0:T(8,128)(2,1)S(1)} %pad_maximum_fusion.1), channel_id=1, source_target_pairs={{0,1},{1,2},{2,3},{4,5},{5,6},{6,7},{8,9},{9,10},{10,11},{12,13},{... | collective-permute-start | bytes 294920 | tf_op jit(solution)/shard_map/ppermute | solution.py:586
  49.9 6.5 %collective-permute-start.3 = (bf16[6,64,128]{2,1,0:T(8,128)(2,1)S(1)}, bf16[6,64,128]{2,1,0:T(8,128)(2,1)S(1)}, u32[]{:S(2)}, u32[]{:S(2)}) collective-permute-start(bf16[6,64,128]{2,1,0:T(8,128)(2,1)S(1)} %pad_maximum_fusion.2), channel_id=1, source_target_pairs={{1,0},{2,1},{3,2},{5,4},{6,5},{7,6},{9,8},{10,9},{11,10},{13,12},{... | collective-permute-start | bytes 294920 | tf_op jit(solution)/shard_map/ppermute | solution.py:586
  54.8 1.7 %copy-start.32 = (bf16[6,64,128]{2,1,0:T(8,128)(2,1)}, bf16[6,64,128]{2,1,0:T(8,128)(2,1)S(1)}, u32[]{:S(2)}) copy-start(bf16[6,64,128]{2,1,0:T(8,128)(2,1)S(1)} %collective-permute-done.2.ylo_ref) | copy-start | bytes 294916
  57.1 12.5 %all-to-all-start.3 = ((f32[8,16,512]{2,1,0:T(8,128)}), f32[8,16,512]{2,1,0:T(8,128)S(1)}, u32[]{:S(2)}, u32[]{:S(2)}) async-start(f32[8,16,512]{2,1,0:T(8,128)} %shard_map.185), calls=%async_computation.3 | async-start | bytes 524288 | tf_op jit(solution)/shard_map/all_to_all | solution.py:629
  72.7 11.1 %all-to-all-start.4 = ((f32[8,16,512]{2,1,0:T(8,128)}), f32[8,16,512]{2,1,0:T(8,128)S(1)}, u32[]{:S(2)}, u32[]{:S(2)}) async-start(f32[8,16,512]{2,1,0:T(8,128)} %get-tuple-element.51), calls=%async_computation.4 | async-start | bytes 524288 | tf_op jit(solution)/shard_map/all_to_all | solution.py:629
  77.9 6.8 %collective-permute-start.5 = (bf16[8,64,128]{2,1,0:T(8,128)(2,1)S(1)}, bf16[8,64,128]{2,1,0:T(8,128)(2,1)S(1)}, u32[]{:S(2)}, u32[]{:S(2)}) collective-permute-start(bf16[8,64,128]{2,1,0:T(8,128)(2,1)S(1)} %get-tuple-element.71), channel_id=1, source_target_pairs={{4,0},{8,4},{12,8},{16,12},{20,16},{24,20},{28,24},{5,1},{9,5},{13... | collective-permute-start | bytes 393224 | tf_op jit(solution)/shard_map/ppermute | solution.py:586
  79.2 5.5 %collective-permute-start.4 = (bf16[8,64,128]{2,1,0:T(8,128)(2,1)S(1)}, bf16[8,64,128]{2,1,0:T(8,128)(2,1)S(1)}, u32[]{:S(2)}, u32[]{:S(2)}) collective-permute-start(bf16[8,64,128]{2,1,0:T(8,128)(2,1)S(1)} %get-tuple-element.72), channel_id=1, source_target_pairs={{0,4},{4,8},{8,12},{12,16},{16,20},{20,24},{24,28},{1,5},{5,9},{9,... | collective-permute-start | bytes 393224 | tf_op jit(solution)/shard_map/ppermute | solution.py:586
  84.7 17.4 %all-to-all-start.5 = ((bf16[4,32,512]{2,1,0:T(8,128)(2,1)}), bf16[4,32,512]{2,1,0:T(8,128)(2,1)S(1)}, u32[]{:S(2)}, u32[]{:S(2)}) async-start(bf16[4,32,512]{2,1,0:T(8,128)(2,1)} %shard_map.189), calls=%async_computation.5 | async-start | bytes 262144 | tf_op jit(solution)/shard_map/all_to_all | solution.py:629
  88.4 13.1 %collective-permute-start.6 = (bf16[6,64,128]{2,1,0:T(8,128)(2,1)S(1)}, bf16[6,64,128]{2,1,0:T(8,128)(2,1)S(1)}, u32[]{:S(2)}, u32[]{:S(2)}) collective-permute-start(bf16[6,64,128]{2,1,0:T(8,128)(2,1)S(1)} %pad_maximum_fusion.3), channel_id=1, source_target_pairs={{0,1},{1,2},{2,3},{4,5},{5,6},{6,7},{8,9},{9,10},{10,11},{12,13},{... | collective-permute-start | bytes 294920 | tf_op jit(solution)/shard_map/ppermute | solution.py:586
  92.4 9.2 %collective-permute-start.7 = (bf16[6,64,128]{2,1,0:T(8,128)(2,1)S(1)}, bf16[6,64,128]{2,1,0:T(8,128)(2,1)S(1)}, u32[]{:S(2)}, u32[]{:S(2)}) collective-permute-start(bf16[6,64,128]{2,1,0:T(8,128)(2,1)S(1)} %pad_maximum_fusion.4), channel_id=1, source_target_pairs={{1,0},{2,1},{3,2},{5,4},{6,5},{7,6},{9,8},{10,9},{11,10},{13,12},{... | collective-permute-start | bytes 294920 | tf_op jit(solution)/shard_map/ppermute | solution.py:586
  98.5 32.5 %copy-start.15 = (bf16[4,8,64,128]{3,2,1,0:T(8,128)(2,1)S(1)}, bf16[4,8,64,128]{3,2,1,0:T(8,128)(2,1)}, u32[]{:S(2)}) copy-start(bf16[4,8,64,128]{3,2,1,0:T(8,128)(2,1)} %copy-done.13) | copy-start | bytes 1572868
  101.5 33.3 %copy-start.7 = (bf16[128,384]{1,0:T(8,128)(2,1)S(1)}, bf16[128,384]{1,0:T(8,128)(2,1)}, u32[]{:S(2)}) copy-start(bf16[128,384]{1,0:T(8,128)(2,1)} %constant.27.clone.table_ref) | copy-start | bytes 294916
  102.2 28.8 %copy-start.39 = (bf16[6,64,128]{2,1,0:T(8,128)(2,1)S(1)}, bf16[6,64,128]{2,1,0:T(8,128)(2,1)}, u32[]{:S(2)}) copy-start(bf16[6,64,128]{2,1,0:T(8,128)(2,1)} %copy-done.38) | copy-start | bytes 294916
  102.2 16.7 %all-to-all-start.6 = ((f32[8,128,128]{2,1,0:T(8,128)}), f32[8,128,128]{2,1,0:T(8,128)}, u32[]{:S(2)}, u32[]{:S(2)}) async-start(f32[8,128,128]{2,1,0:T(8,128)} %bitcast.8), calls=%async_computation.6 | async-start | bytes 1048576 | tf_op jit(solution)/shard_map/all_to_all | solution.py:629
  120.8 14.0 %all-to-all-start.7 = ((bf16[4,64,512]{2,1,0:T(8,128)(2,1)}), bf16[4,64,512]{2,1,0:T(8,128)(2,1)S(1)}, u32[]{:S(2)}, u32[]{:S(2)}) async-start(bf16[4,64,512]{2,1,0:T(8,128)(2,1)} %pad_maximum_fusion), calls=%async_computation.7 | async-start | bytes 524288 | tf_op jit(solution)/shard_map/all_to_all | solution.py:629
  136.0 16.4 %all-to-all-start.8 = ((f32[8,48,512]{2,1,0:T(8,128)}), f32[8,48,512]{2,1,0:T(8,128)S(1)}, u32[]{:S(2)}, u32[]{:S(2)}) async-start(f32[8,48,512]{2,1,0:T(8,128)} %shard_map.192), calls=%async_computation.8 | async-start | bytes 1572864 | tf_op jit(solution)/shard_map/all_to_all | solution.py:629
  139.7 14.1 %copy-start.21 = (bf16[96,128]{1,0:T(8,128)(2,1)S(1)}, bf16[96,128]{1,0:T(8,128)(2,1)}, u32[]{:S(2)}) copy-start(bf16[96,128]{1,0:T(8,128)(2,1)} %constant.25.clone.inverse_ref) | copy-start | bytes 73732
  (25 other events, 22.4 us)

commit v5 on v4

--- a/solution.py
+++ b/solution.py
@@ -107,7 +107,7 @@
 def z_inverse(in_ref, table, x, nx):
     per = 2 * MZ // nx
     rows = jnp.concatenate(
-        [in_ref[owner, x * per : (x + 1) * per, :] for owner in range(nx)], axis=0
+        [in_ref[owner].astype(F32)[x * per : (x + 1) * per] for owner in range(nx)], axis=0
     )
     return lax.dot_general(
         pieces(rows), table, (((0,), (0,)), ((), ())), preferred_element_type=F32
@@ -233,12 +233,25 @@
         z_forward(grad.reshape(cy * c, z), forward_ref[...], back_ref, x, nx)
 
 
-def finish_kernel(nx, stencil_ref, slab_ref, inverse_ref, out_ref):
+def finish_kernel(
+    nx,
+    scale,
+    stencil_ref,
+    message_ref,
+    inverse_ref,
+    out_ref,
+    taps_ref,
+    point_ref,
+    packed_ref,
+    turned_ref,
+):
     c, cx, cy, z = out_ref.shape
     for x in range(cx):
-        spectral = z_inverse(slab_ref, inverse_ref[...], x, nx).reshape(cy, c, z)
+        spectral = z_inverse(message_ref, inverse_ref[...], x, nx).reshape(cy, c, z)
         stencil = jnp.stack([stencil_ref[x, :, y * z : (y + 1) * z] for y in range(cy)])
         out_ref[:, x] = jnp.swapaxes(spectral + stencil, 0, 1)
+    skip = 2 * MZ * cx // nx
+    unpack(scale, skip, message_ref, taps_ref, point_ref, packed_ref, turned_ref)
 
 
 def x_kernel(table_ref, data_ref, out_ref):
@@ -252,6 +265,7 @@
         out_ref[owner, :count] = got[owner * count : (owner + 1) * count]
     if data.shape[1] > rows:
         extra = data[:, rows:].sum(0)
+        extra = extra.astype(out_ref.dtype)
         for owner in range(out_ref.shape[0]):
             out_ref[owner, count:] = extra
 
@@ -271,13 +285,14 @@
     back_ref[4 * C : 5 * C, 3 * C :] = point.T.astype(BF16)
 
 
-def unpack_kernel(scale, skip, message_ref, taps_ref, point_ref, packed_ref, turned_ref):
+def unpack(scale, skip, message_ref, taps_ref, point_ref, packed_ref, turned_ref):
     devices, rows, lanes = message_ref.shape
     per, tiles_in = rows - skip, lanes // 128
     for owner in range(devices):
+        message = message_ref[owner].astype(F32)
         for tile in range(tiles_in):
             row = (owner * tiles_in + tile) * per
-            packed_ref[row : row + per] = message_ref[owner, skip:, tile * 128 : (tile + 1) * 128]
+            packed_ref[row : row + per] = message[skip:, tile * 128 : (tile + 1) * 128]
     for tap in range(27):
         group, e = tap // 3, tap % 3
         if e < 2:
@@ -372,17 +387,18 @@
             yield piece, tile, slice(start, start + 2 * C)
 
 
-def spread_modes(modes, table_ref):
+def spread_modes(modes, table_ref, spread_refs):
     count = C * C // SPAN
-    made = {}
+    made = set()
 
     def get(piece):
         for p in range(piece, min(piece + 2, count)):
             if p not in made:
-                made[p] = jnp.dot(
+                made.add(p)
+                spread_refs[p % 2][...] = jnp.dot(
                     modes, table_ref[:, p * SPAN : (p + 1) * SPAN], preferred_element_type=F32
                 )
-        return made[piece]
+        return spread_refs[piece % 2]
 
     return get
 
@@ -399,6 +415,9 @@
     sum_ref,
     rows_ref,
     block_ref,
+    even_ref,
+    odd_ref,
+    total_ref,
 ):
     step = pl.program_id(0)
 
@@ -411,22 +430,29 @@
 
         y_forward(mz, data_ref, forward_ref, rows_ref, store)
 
-    spread = spread_modes(modes_ref[step], table_ref)
-    real = [jnp.zeros((MY, 2 * C), F32)] * QUAD
-    imag = [jnp.zeros((MY, 2 * C), F32)] * QUAD
-    for piece, tile, columns in tiles():
+    spread = spread_modes(modes_ref[step], table_ref, (even_ref, odd_ref))
+    for piece in range(C * C // SPAN):
         modes = spread(piece)
-        inside = slice(tile * 2 * C, (tile + 1) * 2 * C)
         for pair in range(QUAD):
-            mode_re = modes[place(0, pair), inside]
-            mode_im = modes[place(1, pair), inside]
-            weight_re = weight_ref[0, 0, pair, :, columns].astype(F32)
-            weight_im = weight_ref[1, 0, pair, :, columns].astype(F32)
-            real[pair] += mode_re * weight_re - mode_im * weight_im
-            imag[pair] += mode_re * weight_im + mode_im * weight_re
-    for pair in range(QUAD):
-        sum_ref[step, place(0, pair), :] = real[pair][:, :C] + real[pair][:, C:]
-        sum_ref[step, place(1, pair), :] = imag[pair][:, :C] + imag[pair][:, C:]
+            real = imag = None
+            for tile in range(SPAN // (2 * C)):
+                inside = slice(tile * 2 * C, (tile + 1) * 2 * C)
+                columns = slice(piece * SPAN + inside.start, piece * SPAN + inside.stop)
+                mode_re = modes[place(0, pair), inside]
+                mode_im = modes[place(1, pair), inside]
+                weight_re = weight_ref[0, 0, pair, :, columns].astype(F32)
+                weight_im = weight_ref[1, 0, pair, :, columns].astype(F32)
+                term_re = mode_re * weight_re - mode_im * weight_im
+                term_im = mode_re * weight_im + mode_im * weight_re
+                real = term_re if real is None else real + term_re
+                imag = term_im if imag is None else imag + term_im
+            if piece:
+                real += total_ref[place(0, pair), :]
+                imag += total_ref[place(1, pair), :]
+            total_ref[place(0, pair), :] = real
+            total_ref[place(1, pair), :] = imag
+    total = total_ref[...]
+    sum_ref[step] = total[:, :C] + total[:, C:]
 
     @pl.when(step == pl.num_programs(0) - 1)
     def _():
@@ -486,18 +512,24 @@
         y_inverse(mz, sum_ref, inverse_ref, out_ref, block_ref)
 
 
-def outer_kernel(alpha, modes_ref, back_ref, table_ref, out_ref):
-    spread = spread_modes(modes_ref[0], table_ref)
-    for piece, tile, columns in tiles():
+def outer_kernel(alpha, modes_ref, back_ref, table_ref, out_ref, even_ref, odd_ref):
+    spread = spread_modes(modes_ref[0], table_ref, (even_ref, odd_ref))
+    for piece in range(C * C // SPAN):
         modes = spread(piece)
-        inside = slice(tile * 2 * C, (tile + 1) * 2 * C)
         for pair in range(QUAD):
             back_re = back_ref[0, place(0, pair), :] * alpha
             back_im = back_ref[0, place(1, pair), :] * alpha
-            mode_re = modes[place(0, pair), inside]
-            mode_im = modes[place(1, pair), inside]
-            out_ref[0, 0, pair, :, columns] = mode_re * back_re + mode_im * back_im
-            out_ref[1, 0, pair, :, columns] = mode_re * back_im - mode_im * back_re
+            for tile in range(SPAN // (2 * C)):
+                inside = slice(tile * 2 * C, (tile + 1) * 2 * C)
+                columns = slice(piece * SPAN + inside.start, piece * SPAN + inside.stop)
+                mode_re = modes[place(0, pair), inside]
+                mode_im = modes[place(1, pair), inside]
+                out_ref[0, 0, pair, :, columns] = mode_re * back_re + mode_im * back_im
+                out_ref[1, 0, pair, :, columns] = mode_re * back_im - mode_im * back_re
+
+
+def in_hbm(value):
+    return pltpu.with_memory_space_constraint(value, pltpu.HBM)
 
 
 def whole():
@@ -556,14 +588,14 @@
             pltpu.VMEM(data.shape, F32),
             *scratch,
         ],
-        compiler_params=params(48),
+        compiler_params=params(20),
         cost_estimate=cost(weight.size * 8, weight.size * 2),
-    )(data, weight, *tables)
+    )(data, in_hbm(weight), *map(in_hbm, tables))
 
 
 def outer(modes, back, table, shape, alpha, start, count, prior=None):
     def kernel(*refs):
-        outer_kernel(alpha, *refs[:3], refs[-1])
+        outer_kernel(alpha, *refs[:3], *refs[-3:])
 
     group = lambda ref: pl.BlockSpec((1,) + ref.shape[1:], lambda step: (step + start, 0, 0))
     given = () if prior is None else (prior,)
@@ -575,9 +607,10 @@
         out_specs=group_block(shape, start),
         out_shape=jax.ShapeDtypeStruct(shape, F32),
         input_output_aliases={3: 0} if given else {},
-        compiler_params=params(24),
+        scratch_shapes=[pltpu.VMEM((2 * QUAD * MY, SPAN), F32)] * 2,
+        compiler_params=params(20),
         cost_estimate=cost(math.prod(shape) * 4, math.prod(shape) * 4),
-    )(modes, back, table, *given)
+    )(modes, back, in_hbm(table), *given)
 
 
 def shift(block, axis, step):
@@ -657,7 +690,7 @@
         return call(
             x_kernel,
             [((lead, rows, lanes), kind)],
-            (table, block),
+            (in_hbm(table), block),
             mib=16,
             flops=2 * table.size * lanes,
             moved=8 * block.size,
@@ -669,19 +702,21 @@
     conv_table, back_table = call(
         taps_kernel,
         [((9 * c, 4 * c), BF16)] * 2,
-        (stencil_weight, pointwise_weight),
+        (in_hbm(stencil_weight), in_hbm(pointwise_weight)),
         [pltpu.VMEM((27 * c, c), F32)],
         moved=stencil_weight.size * 6,
     )
     turned, slab = call(
         functools.partial(prep_kernel, nx),
         [turned_shape, slab_shape],
-        (state, z_state),
+        (in_hbm(state), in_hbm(z_state)),
         flops=2 * 96 * state.size,
         moved=state.size * 5,
     )
     block = x_stage(x_fwd, swap(slab, "gx"), ny)
-    block, *faces = together(block, *x_halos(turned))
+    block, conv_table, back_table, *faces = together(
+        block, conv_table, back_table, *x_halos(turned)
+    )
     modes_in, block = per_mode(
         mix_kernel,
         swap(block, "gy"),
@@ -689,6 +724,7 @@
         (spread, y_fwd, y_inv),
         (2 * c, BF16),
         F32,
+        [pltpu.VMEM((2 * QUAD * MY, SPAN), F32)] * 2 + [pltpu.VMEM((2 * QUAD * MY, 2 * c), F32)],
     )
     block, *faces = together(block, *faces)
     edges = y_halos(turned, *faces)
@@ -699,7 +735,7 @@
     output, grad, slab = call(
         functools.partial(gelu_kernel, nx),
         [((c, cx, cy, z), BF16), turned_shape, slab_shape],
-        (stencil, swap(block, "gx"), cotangent, z_spectral, z_grad),
+        (stencil, swap(block, "gx"), cotangent, in_hbm(z_spectral), in_hbm(z_grad)),
         flops=2 * 192 * state.size,
         moved=state.size * 12,
     )
@@ -723,7 +759,7 @@
     extra = packed.shape[0]
     packed = jnp.broadcast_to(packed[None], (ny, extra, lanes))
     block = x_stage(
-        x_inv, swap(jnp.concatenate([block, packed], axis=1), "gy"), nx, F32, extra
+        x_inv, swap(jnp.concatenate([block, packed], axis=1), "gy"), nx, BF16, extra
     )
     stencil_back = conv(grad, (*faces, *edges), back_table, True)
     shape = spectral_weight.shape
@@ -737,19 +773,13 @@
     grad_modes = outer(
         modes_in, back_modes, spread, shape, alpha, early, groups - early, grad_modes
     )
-    grad_state = call(
-        functools.partial(finish_kernel, nx),
-        [((c, cx, cy, z), F32)],
-        (stencil_back, message, z_back),
+    grad_state, grad_stencil, grad_point = call(
+        functools.partial(finish_kernel, nx, alpha),
+        [((c, cx, cy, z), F32), ((c, 27 * c), F32), ((c, c), F32)],
+        (stencil_back, message, in_hbm(z_back)),
+        [pltpu.VMEM(grad_taps.shape, F32), pltpu.VMEM((27 * c, c), F32)],
         flops=2 * 96 * state.size,
         moved=state.size * 10,
-    )[0]
-    grad_stencil, grad_point = call(
-        functools.partial(unpack_kernel, alpha, x_rows),
-        [((c, 27 * c), F32), ((c, c), F32)],
-        (message,),
-        [pltpu.VMEM(grad_taps.shape, F32), pltpu.VMEM((27 * c, c), F32)],
-        moved=grad_taps.size * 8,
     )
     return (output, grad_state, grad_modes, grad_stencil, grad_point)
 

time: 159 us -> 148 us (0.931)
  local copies, waits for them, and re-layouts: 24.4 us -> 6.85 us
  Pallas kernels: 44.3 us -> 52.8 us
  starting transfers between devices: 60.6 us -> 55.3 us
  waiting for transfers between devices: 24.4 us -> 29.7 us
    unnamed x80 -> x30, local copies, waits for them, and re-layouts: 22.5 us -> 6.77 us
    all_to_all x9, waiting for transfers between devices: 22.7 us -> 29.6 us  [swap(): return lax.all_to_all(block, axis, split_axis=0, concat_axis=0, tiled=True)]
    pallas_call x12 -> x11, Pallas kernels: 17.7 us -> 23.5 us  [call(): pl.pallas_call(kernel, out_shape=[jax.ShapeDtypeStruct(*out) for out in o...]
    all_to_all x9, starting transfers between devices: 41.6 us -> 37.9 us  [swap(): return lax.all_to_all(block, axis, split_axis=0, concat_axis=0, tiled=True)]
    pallas_call x2, Pallas kernels: 9 us -> 11.4 us  [outer(): pl.pallas_call(kernel, grid=(count,), in_specs=[group(modes), group(back)...]
    ppermute x8, starting transfers between devices: 19.1 us -> 17.4 us  [shift(): return lax.ppermute(block, axis, pairs)]
    ppermute x8, waiting for transfers between devices: 1.66 us -> 0.02 us  [shift(): return lax.ppermute(block, axis, pairs)]
  transfers between devices with their start and end apart: 17 -> 17, of which waited for: 7 -> 7; matrix products, arithmetic and copies ran while one was open for 1% -> 0% of each run, Pallas kernels for 18% -> 23%
where the time goes in v5:
time: 148 us; the launch traced here: 146 us
  starting transfers between devices  55.3 us (37%)
  Pallas kernels  52.8 us (36%)
  waiting for transfers between devices  29.7 us (20%)
  local copies, waits for them, and re-layouts  6.85 us (5%)
    all_to_all x9, starting transfers between devices, swap(): return lax.all_to_all(block, axis, split_axis=0, concat_axis=0, tiled=True)  37.9 us
    all_to_all x9, waiting for transfers between devices, swap(): return lax.all_to_all(block, axis, split_axis=0, concat_axis=0, tiled=True)  29.6 us
    pallas_call x11, Pallas kernels, call(): pl.pallas_call(kernel, out_shape=[jax.ShapeDtypeStruct(*out) for out in o...  23.5 us
    pallas_call x2, Pallas kernels, per_mode(): pl.pallas_call(functools.partial(kernel, mz), grid=(groups,), in_specs=[f...  17.8 us
    ppermute x8, starting transfers between devices, shift(): return lax.ppermute(block, axis, pairs)  17.4 us
    pallas_call x2, Pallas kernels, outer(): pl.pallas_call(kernel, grid=(count,), in_specs=[group(modes), group(back)...  11.4 us
    unnamed x30, local copies, waits for them, and re-layouts  6.77 us
  transfers between devices with their start and end apart: 17, of which 7 were waited for; matrix products, arithmetic and copies ran while one was open for 0% of the time, Pallas kernels for 23%

profile of v5, /device:TPU:0, one launch (start us, length us, event | category | flops | bytes accessed | tf_op | source)
XLA Modules:
  0.0 146.3 jit_solution(12377196720725452127)
XLA Ops:
  0.6 2.2 %shard_map.182 = (bf16[4,8,64,128]{3,2,1,0:T(8,128)(2,1)S(1)}, f32[8,16,512]{2,1,0:T(8,128)}) custom-call(bf16[64,4,8,128]{3,2,1,0:T(8,128)(2,1)} %field_ref.1, bf16[96,128]{1,0:T(8,128)(2,1)} %constant.22.clone.table_ref), custom_call_target="tpu_custom_call" | custom-call | flops 50331648 | bytes 1310720 | tf_op jit(solution)/shard_map/pallas_call | solution.py:548
  2.9 5.2 %all-to-all-start = ((f32[8,16,512]{2,1,0:T(8,128)}), f32[8,16,512]{2,1,0:T(8,128)S(1)}, u32[]{:S(2)}, u32[]{:S(2)}) async-start(f32[8,16,512]{2,1,0:T(8,128)} %get-tuple-element.41), calls=%async_computation | async-start | bytes 524288 | tf_op jit(solution)/shard_map/all_to_all | solution.py:662
  8.1 2.4 %collective-permute-start = (bf16[8,64,128]{2,1,0:T(8,128)(2,1)S(1)}, bf16[8,64,128]{2,1,0:T(8,128)(2,1)S(1)}, u32[]{:S(2)}, u32[]{:S(2)}) collective-permute-start(bf16[8,64,128]{2,1,0:T(8,128)(2,1)S(1)} %get-tuple-element.82), channel_id=1, source_target_pairs={{0,4},{4,8},{8,12},{12,16},{16,20},{20,24},{24,28},{1,5},{5,9},{9,... | collective-permute-start | bytes 393224 | tf_op jit(solution)/shard_map/ppermute | solution.py:619
  13.3 1.6 %all-to-all-done.data_ref = f32[8,16,512]{2,1,0:T(8,128)S(1)} async-done(((f32[8,16,512]{2,1,0:T(8,128)}), f32[8,16,512]{2,1,0:T(8,128)S(1)}, u32[]{:S(2)}, u32[]{:S(2)}) %all-to-all-start) | async-done | bytes 262176 | tf_op jit(solution)/shard_map/all_to_all | solution.py:662
  15.0 1.8 %shard_map.183 = f32[4,32,512]{2,1,0:T(8,128)} custom-call(bf16[128,384]{1,0:T(8,128)(2,1)} %constant.26.clone.table_ref, f32[8,16,512]{2,1,0:T(8,128)S(1)} %all-to-all-done.data_ref), custom_call_target="tpu_custom_call" | custom-call | flops 50331648 | bytes 524288 | tf_op jit(solution)/shard_map/pallas_call | solution.py:548
  16.8 4.9 %all-to-all-start.1 = ((f32[4,32,512]{2,1,0:T(8,128)}), f32[4,32,512]{2,1,0:T(8,128)S(1)}, u32[]{:S(2)}, u32[]{:S(2)}) async-start(f32[4,32,512]{2,1,0:T(8,128)} %shard_map.183), calls=%async_computation.1 | async-start | bytes 524288 | tf_op jit(solution)/shard_map/all_to_all | solution.py:662
  21.7 9.9 %all-to-all-done.1.data_ref = f32[4,32,512]{2,1,0:T(8,128)S(1)} async-done(((f32[4,32,512]{2,1,0:T(8,128)}), f32[4,32,512]{2,1,0:T(8,128)S(1)}, u32[]{:S(2)}, u32[]{:S(2)}) %all-to-all-start.1) | async-done | bytes 262176 | tf_op jit(solution)/shard_map/all_to_all | solution.py:662
  31.7 9.3 %shard_map.185 = (bf16[4,256,128]{2,1,0:T(8,128)(2,1)S(1)}, f32[4,32,512]{2,1,0:T(8,128)}) custom-call(f32[4,32,512]{2,1,0:T(8,128)S(1)} %all-to-all-done.1.data_ref, bf16[2,2,8,32,4096]{4,3,2,1,0:T(8,128)(2,1)} %weight_ref.3, bf16[128,4096]{1,0:T(8,128)(2,1)} %constant.30.clone.table_ref.refs_2_, bf16[64,192]{1,0:T(8,128)(2,1)} %constant.28.clone.forward_ref, ...), custom_call_target="tpu_custom_call" | custom-call | flops 33554432 | bytes 8388608 | tf_op jit(solution)/shard_map/pallas_call | solution.py:576
  41.0 3.4 %all-to-all-start.2 = ((f32[4,32,512]{2,1,0:T(8,128)}), f32[4,32,512]{2,1,0:T(8,128)S(1)}, u32[]{:S(2)}, u32[]{:S(2)}) async-start(f32[4,32,512]{2,1,0:T(8,128)} %get-tuple-element.50), calls=%async_computation.2 | async-start | bytes 524288 | tf_op jit(solution)/shard_map/all_to_all | solution.py:662
  45.8 4.6 %collective-permute-start.2 = (bf16[6,64,128]{2,1,0:T(8,128)(2,1)S(1)}, bf16[6,64,128]{2,1,0:T(8,128)(2,1)S(1)}, u32[]{:S(2)}, u32[]{:S(2)}) collective-permute-start(bf16[6,64,128]{2,1,0:T(8,128)(2,1)S(1)} %pad_maximum_fusion.1), channel_id=1, source_target_pairs={{0,1},{1,2},{2,3},{4,5},{5,6},{6,7},{8,9},{9,10},{10,11},{12,13},{... | collective-permute-start | bytes 294920 | tf_op jit(solution)/shard_map/ppermute | solution.py:619
  50.4 4.3 %all-to-all-done.2.data_ref = f32[4,32,512]{2,1,0:T(8,128)S(1)} async-done(((f32[4,32,512]{2,1,0:T(8,128)}), f32[4,32,512]{2,1,0:T(8,128)S(1)}, u32[]{:S(2)}, u32[]{:S(2)}) %all-to-all-start.2) | async-done | bytes 262176 | tf_op jit(solution)/shard_map/all_to_all | solution.py:662
  54.7 1.8 %shard_map.186 = f32[8,16,512]{2,1,0:T(8,128)} custom-call(bf16[128,384]{1,0:T(8,128)(2,1)} %constant.27.clone.table_ref, f32[4,32,512]{2,1,0:T(8,128)S(1)} %all-to-all-done.2.data_ref), custom_call_target="tpu_custom_call" | custom-call | flops 50331648 | bytes 524288 | tf_op jit(solution)/shard_map/pallas_call | solution.py:548
  57.2 3.6 %all-to-all-start.3 = ((f32[8,16,512]{2,1,0:T(8,128)}), f32[8,16,512]{2,1,0:T(8,128)S(1)}, u32[]{:S(2)}, u32[]{:S(2)}) async-start(f32[8,16,512]{2,1,0:T(8,128)} %shard_map.186), calls=%async_computation.3 | async-start | bytes 524288 | tf_op jit(solution)/shard_map/all_to_all | solution.py:662
  62.6 1.9 %shard_map.187.stencil_ref = f32[4,64,1024]{2,1,0:T(8,128)S(1)} custom-call(bf16[4,8,64,128]{3,2,1,0:T(8,128)(2,1)S(1)} %get-tuple-element.40.body_ref, bf16[8,64,128]{2,1,0:T(8,128)(2,1)S(1)} %collective-permute-done.xlo_ref, bf16[8,64,128]{2,1,0:T(8,128)(2,1)S(1)} %collective-permute-done.1.xhi_ref, bf16[6,64,128]{2,1,0:T(8,128)(2,1)S(1)} %copy-done.9, ...), custom_call_target="tpu_custom_call" | custom-call | flops 905969664 | bytes 2097152 | tf_op jit(solution)/shard_map/pallas_call | solution.py:548
  64.5 3.3 %all-to-all-done.3.slab_ref = f32[8,16,512]{2,1,0:T(8,128)S(1)} async-done(((f32[8,16,512]{2,1,0:T(8,128)}), f32[8,16,512]{2,1,0:T(8,128)S(1)}, u32[]{:S(2)}, u32[]{:S(2)}) %all-to-all-start.3) | async-done | bytes 262176 | tf_op jit(solution)/shard_map/all_to_all | solution.py:662
  67.7 3.1 %shard_map.188 = (bf16[64,4,8,128]{3,2,1,0:T(8,128)(2,1)}, bf16[4,8,64,128]{3,2,1,0:T(8,128)(2,1)S(1)}, f32[8,16,512]{2,1,0:T(8,128)}) custom-call(f32[4,64,1024]{2,1,0:T(8,128)S(1)} %shard_map.187.stencil_ref, f32[8,16,512]{2,1,0:T(8,128)S(1)} %all-to-all-done.3.slab_ref, bf16[64,4,8,128]{3,2,1,0:T(8,128)(2,1)S(1)} %copy-done, ...), custom_call_target="tpu_custom_call" | custom-call | flops 100663296 | bytes 3145728 | tf_op jit(solution)/shard_map/pallas_call | solution.py:548
  73.4 5.7 %all-to-all-start.4 = ((f32[8,16,512]{2,1,0:T(8,128)}), f32[8,16,512]{2,1,0:T(8,128)S(1)}, u32[]{:S(2)}, u32[]{:S(2)}) async-start(f32[8,16,512]{2,1,0:T(8,128)} %get-tuple-element.56), calls=%async_computation.4 | async-start | bytes 524288 | tf_op jit(solution)/shard_map/all_to_all | solution.py:662
  79.2 6.9 %all-to-all-done.4.data_ref = f32[8,16,512]{2,1,0:T(8,128)S(1)} async-done(((f32[8,16,512]{2,1,0:T(8,128)}), f32[8,16,512]{2,1,0:T(8,128)S(1)}, u32[]{:S(2)}, u32[]{:S(2)}) %all-to-all-start.4) | async-done | bytes 262176 | tf_op jit(solution)/shard_map/all_to_all | solution.py:662
  86.1 1.8 %shard_map.189 = bf16[4,32,512]{2,1,0:T(8,128)(2,1)} custom-call(bf16[128,384]{1,0:T(8,128)(2,1)} %constant.26.clone.table_ref, f32[8,16,512]{2,1,0:T(8,128)S(1)} %all-to-all-done.4.data_ref), custom_call_target="tpu_custom_call" | custom-call | flops 50331648 | bytes 524288 | tf_op jit(solution)/shard_map/pallas_call | solution.py:548
  89.2 3.9 %all-to-all-start.5 = ((bf16[4,32,512]{2,1,0:T(8,128)(2,1)}), bf16[4,32,512]{2,1,0:T(8,128)(2,1)S(1)}, u32[]{:S(2)}, u32[]{:S(2)}) async-start(bf16[4,32,512]{2,1,0:T(8,128)(2,1)} %shard_map.189), calls=%async_computation.5 | async-start | bytes 262144 | tf_op jit(solution)/shard_map/all_to_all | solution.py:662
  93.1 4.0 %collective-permute-start.6 = (bf16[6,64,128]{2,1,0:T(8,128)(2,1)S(1)}, bf16[6,64,128]{2,1,0:T(8,128)(2,1)S(1)}, u32[]{:S(2)}, u32[]{:S(2)}) collective-permute-start(bf16[6,64,128]{2,1,0:T(8,128)(2,1)S(1)} %pad_maximum_fusion.3), channel_id=1, source_target_pairs={{0,1},{1,2},{2,3},{4,5},{5,6},{6,7},{8,9},{9,10},{10,11},{12,13},{... | collective-permute-start | bytes 294920 | tf_op jit(solution)/shard_map/ppermute | solution.py:619
  99.8 3.1 %shard_map.190 = f32[1024,128]{1,0:T(8,128)} custom-call(bf16[4,8,64,128]{3,2,1,0:T(8,128)(2,1)S(1)} %get-tuple-element.57.grad_ref.body_ref, bf16[4,8,64,128]{3,2,1,0:T(8,128)(2,1)S(1)} %get-tuple-element.40.body_ref, bf16[8,64,128]{2,1,0:T(8,128)(2,1)S(1)} %collective-permute-done.xlo_ref, bf16[8,64,128]{2,1,0:T(8,128)(2,1)S(1)} %copy-done.2, ...), custom_call_target="tpu_custom_call" | custom-call | flops 905969664 | bytes 2097152 | tf_op jit(solution)/shard_map/pallas_call | solution.py:548
  103.6 3.8 %all-to-all-start.6 = ((f32[8,128,128]{2,1,0:T(8,128)}), f32[8,128,128]{2,1,0:T(8,128)S(1)}, u32[]{:S(2)}, u32[]{:S(2)}) async-start(f32[8,128,128]{2,1,0:T(8,128)} %bitcast.8), calls=%async_computation.6 | async-start | bytes 1048576 | tf_op jit(solution)/shard_map/all_to_all | solution.py:662
  107.4 8.5 %shard_map.191 = (f32[4,256,128]{2,1,0:T(8,128)S(1)}, bf16[4,32,512]{2,1,0:T(8,128)(2,1)S(1)}) custom-call(bf16[4,32,512]{2,1,0:T(8,128)(2,1)S(1)} %all-to-all-done.5.data_ref, bf16[2,2,8,32,4096]{4,3,2,1,0:T(8,128)(2,1)} %weight_ref.3, bf16[8,512]{1,0:T(8,128)(2,1)} %constant.31.clone.table_ref, bf16[64,192]{1,0:T(8,128)(2,1)} %constant.28.clone.forward_ref, ...), custom_call_target="tpu_custom_call" | custom-call | flops 33554432 | bytes 8388608 | tf_op jit(solution)/shard_map/pallas_call | solution.py:576
  117.7 3.6 %all-to-all-start.7 = ((bf16[4,64,512]{2,1,0:T(8,128)(2,1)}), bf16[4,64,512]{2,1,0:T(8,128)(2,1)S(1)}, u32[]{:S(2)}, u32[]{:S(2)}) async-start(bf16[4,64,512]{2,1,0:T(8,128)(2,1)} %pad_maximum_fusion), calls=%async_computation.7 | async-start | bytes 524288 | tf_op jit(solution)/shard_map/all_to_all | solution.py:662
  121.3 5.7 %shard_map.194.refs_3_ = f32[2,2,8,32,4096]{4,3,2,1,0:T(8,128)} custom-call(bf16[4,256,128]{2,1,0:T(8,128)(2,1)S(1)} %get-tuple-element.67.refs_0_, f32[4,256,128]{2,1,0:T(8,128)S(1)} %get-tuple-element.68.refs_1_, bf16[128,4096]{1,0:T(8,128)(2,1)} %constant.30.clone.table_ref.refs_2_), custom_call_target="tpu_custom_call" | custom-call | flops 16777216 | bytes 16777216 | tf_op jit(solution)/shard_map/pallas_call | solution.py:602
  128.0 1.9 %shard_map.193.stencil_ref = f32[4,64,1024]{2,1,0:T(8,128)S(1)} custom-call(bf16[4,8,64,128]{3,2,1,0:T(8,128)(2,1)S(1)} %get-tuple-element.57.grad_ref.body_ref, bf16[8,64,128]{2,1,0:T(8,128)(2,1)S(1)} %collective-permute-done.4.xlo_ref, bf16[8,64,128]{2,1,0:T(8,128)(2,1)S(1)} %collective-permute-done.5.xhi_ref, bf16[6,64,128]{2,1,0:T(8,128)(2,1)S(1)} %copy-done.14, ...), custom_call_target="tpu_custom_call" | custom-call | flops 905969664 | bytes 2097152 | tf_op jit(solution)/shard_map/pallas_call | solution.py:548
  129.8 1.9 %shard_map.192 = bf16[8,48,512]{2,1,0:T(8,128)(2,1)} custom-call(bf16[128,384]{1,0:T(8,128)(2,1)} %constant.27.clone.table_ref, bf16[4,64,512]{2,1,0:T(8,128)(2,1)S(1)} %all-to-all-done.7.data_ref), custom_call_target="tpu_custom_call" | custom-call | flops 50331648 | bytes 1048576 | tf_op jit(solution)/shard_map/pallas_call | solution.py:548
  131.7 3.7 %all-to-all-start.8 = ((bf16[8,48,512]{2,1,0:T(8,128)(2,1)}), bf16[8,48,512]{2,1,0:T(8,128)(2,1)S(1)}, u32[]{:S(2)}, u32[]{:S(2)}) async-start(bf16[8,48,512]{2,1,0:T(8,128)(2,1)} %shard_map.192), calls=%async_computation.8 | async-start | bytes 786432 | tf_op jit(solution)/shard_map/all_to_all | solution.py:662
  135.4 5.7 %shard_map.196 = f32[2,2,8,32,4096]{4,3,2,1,0:T(8,128)} custom-call(bf16[4,256,128]{2,1,0:T(8,128)(2,1)S(1)} %get-tuple-element.67.refs_0_, f32[4,256,128]{2,1,0:T(8,128)S(1)} %get-tuple-element.68.refs_1_, bf16[128,4096]{1,0:T(8,128)(2,1)} %constant.30.clone.table_ref.refs_2_, f32[2,2,8,32,4096]{4,3,2,1,0:T(8,128)} %shard_map.194.refs_3_), custom_call_target="tpu_custom_call", output_to_operand_aliasing={{}: (3, {})} | custom-call | flops 16777216 | bytes 16777216 | tf_op jit(solution)/shard_map/pallas_call | solution.py:602
  141.2 2.6 %all-to-all-done.8.message_ref = bf16[8,48,512]{2,1,0:T(8,128)(2,1)S(1)} async-done(((bf16[8,48,512]{2,1,0:T(8,128)(2,1)}), bf16[8,48,512]{2,1,0:T(8,128)(2,1)S(1)}, u32[]{:S(2)}, u32[]{:S(2)}) %all-to-all-start.8) | async-done | bytes 393248 | tf_op jit(solution)/shard_map/all_to_all | solution.py:662
  143.8 2.5 %shard_map.195 = (f32[64,4,8,128]{3,2,1,0:T(8,128)}, f32[64,1728]{1,0:T(8,128)}, f32[64,64]{1,0:T(8,128)}) custom-call(f32[4,64,1024]{2,1,0:T(8,128)S(1)} %shard_map.193.stencil_ref, bf16[8,48,512]{2,1,0:T(8,128)(2,1)S(1)} %all-to-all-done.8.message_ref, bf16[96,128]{1,0:T(8,128)(2,1)} %constant.25.clone.inverse_ref), custom_call_target="tpu_custom_call" | custom-call | flops 50331648 | bytes 2621440 | tf_op jit(solution)/shard_map/pallas_call | solution.py:548
  (63 shorter events, 16.7 us)
Async XLA Ops:
  0.6 67.1 %copy-start = (bf16[64,4,8,128]{3,2,1,0:T(8,128)(2,1)S(1)}, bf16[64,4,8,128]{3,2,1,0:T(8,128)(2,1)}, u32[]{:S(2)}) copy-start(bf16[64,4,8,128]{3,2,1,0:T(8,128)(2,1)} %cot_ref.1) | copy-start | bytes 1572868
  2.9 12.1 %all-to-all-start = ((f32[8,16,512]{2,1,0:T(8,128)}), f32[8,16,512]{2,1,0:T(8,128)S(1)}, u32[]{:S(2)}, u32[]{:S(2)}) async-start(f32[8,16,512]{2,1,0:T(8,128)} %get-tuple-element.41), calls=%async_computation | async-start | bytes 524288 | tf_op jit(solution)/shard_map/all_to_all | solution.py:662
  8.1 8.7 %collective-permute-start = (bf16[8,64,128]{2,1,0:T(8,128)(2,1)S(1)}, bf16[8,64,128]{2,1,0:T(8,128)(2,1)S(1)}, u32[]{:S(2)}, u32[]{:S(2)}) collective-permute-start(bf16[8,64,128]{2,1,0:T(8,128)(2,1)S(1)} %get-tuple-element.82), channel_id=1, source_target_pairs={{0,4},{4,8},{8,12},{12,16},{16,20},{20,24},{24,28},{1,5},{5,9},{9,... | collective-permute-start | bytes 393224 | tf_op jit(solution)/shard_map/ppermute | solution.py:619
  10.5 6.3 %collective-permute-start.1 = (bf16[8,64,128]{2,1,0:T(8,128)(2,1)S(1)}, bf16[8,64,128]{2,1,0:T(8,128)(2,1)S(1)}, u32[]{:S(2)}, u32[]{:S(2)}) collective-permute-start(bf16[8,64,128]{2,1,0:T(8,128)(2,1)S(1)} %get-tuple-element.81), channel_id=1, source_target_pairs={{4,0},{8,4},{12,8},{16,12},{20,16},{24,20},{28,24},{5,1},{9,5},{13... | collective-permute-start | bytes 393224 | tf_op jit(solution)/shard_map/ppermute | solution.py:619
  13.3 51.1 %copy-start.3 = (bf16[576,256]{1,0:T(8,128)(2,1)}, bf16[576,256]{1,0:T(8,128)(2,1)S(1)}, u32[]{:S(2)}) copy-start(bf16[576,256]{1,0:T(8,128)(2,1)S(1)} %get-tuple-element.66.weight_ref) | copy-start | bytes 884740
  16.8 54.0 %copy-start.1 = (bf16[8,64,128]{2,1,0:T(8,128)(2,1)}, bf16[8,64,128]{2,1,0:T(8,128)(2,1)S(1)}, u32[]{:S(2)}) copy-start(bf16[8,64,128]{2,1,0:T(8,128)(2,1)S(1)} %collective-permute-done.1.xhi_ref) | copy-start | bytes 393220
  16.8 14.8 %all-to-all-start.1 = ((f32[4,32,512]{2,1,0:T(8,128)}), f32[4,32,512]{2,1,0:T(8,128)S(1)}, u32[]{:S(2)}, u32[]{:S(2)}) async-start(f32[4,32,512]{2,1,0:T(8,128)} %shard_map.183), calls=%async_computation.1 | async-start | bytes 524288 | tf_op jit(solution)/shard_map/all_to_all | solution.py:662
  41.0 13.6 %all-to-all-start.2 = ((f32[4,32,512]{2,1,0:T(8,128)}), f32[4,32,512]{2,1,0:T(8,128)S(1)}, u32[]{:S(2)}, u32[]{:S(2)}) async-start(f32[4,32,512]{2,1,0:T(8,128)} %get-tuple-element.50), calls=%async_computation.2 | async-start | bytes 524288 | tf_op jit(solution)/shard_map/all_to_all | solution.py:662
  44.5 12.0 %collective-permute-start.3 = (bf16[6,64,128]{2,1,0:T(8,128)(2,1)S(1)}, bf16[6,64,128]{2,1,0:T(8,128)(2,1)S(1)}, u32[]{:S(2)}, u32[]{:S(2)}) collective-permute-start(bf16[6,64,128]{2,1,0:T(8,128)(2,1)S(1)} %pad_maximum_fusion.2), channel_id=1, source_target_pairs={{1,0},{2,1},{3,2},{5,4},{6,5},{7,6},{9,8},{10,9},{11,10},{13,12},{... | collective-permute-start | bytes 294920 | tf_op jit(solution)/shard_map/ppermute | solution.py:619
  45.8 10.7 %collective-permute-start.2 = (bf16[6,64,128]{2,1,0:T(8,128)(2,1)S(1)}, bf16[6,64,128]{2,1,0:T(8,128)(2,1)S(1)}, u32[]{:S(2)}, u32[]{:S(2)}) collective-permute-start(bf16[6,64,128]{2,1,0:T(8,128)(2,1)S(1)} %pad_maximum_fusion.1), channel_id=1, source_target_pairs={{0,1},{1,2},{2,3},{4,5},{5,6},{6,7},{8,9},{9,10},{10,11},{12,13},{... | collective-permute-start | bytes 294920 | tf_op jit(solution)/shard_map/ppermute | solution.py:619
  56.5 0.6 copy-start.5
  56.5 0.7 copy-start.8
  57.2 10.6 %all-to-all-start.3 = ((f32[8,16,512]{2,1,0:T(8,128)}), f32[8,16,512]{2,1,0:T(8,128)S(1)}, u32[]{:S(2)}, u32[]{:S(2)}) async-start(f32[8,16,512]{2,1,0:T(8,128)} %shard_map.186), calls=%async_computation.3 | async-start | bytes 524288 | tf_op jit(solution)/shard_map/all_to_all | solution.py:662
  60.8 0.9 copy-start.6
  61.7 0.9 copy-start.9
  70.8 17.0 %collective-permute-start.4 = (bf16[8,64,128]{2,1,0:T(8,128)(2,1)S(1)}, bf16[8,64,128]{2,1,0:T(8,128)(2,1)S(1)}, u32[]{:S(2)}, u32[]{:S(2)}) collective-permute-start(bf16[8,64,128]{2,1,0:T(8,128)(2,1)S(1)} %get-tuple-element.78), channel_id=1, source_target_pairs={{0,4},{4,8},{8,12},{12,16},{16,20},{20,24},{24,28},{1,5},{5,9},{9,... | collective-permute-start | bytes 393224 | tf_op jit(solution)/shard_map/ppermute | solution.py:619
  72.1 15.7 %collective-permute-start.5 = (bf16[8,64,128]{2,1,0:T(8,128)(2,1)S(1)}, bf16[8,64,128]{2,1,0:T(8,128)(2,1)S(1)}, u32[]{:S(2)}, u32[]{:S(2)}) collective-permute-start(bf16[8,64,128]{2,1,0:T(8,128)(2,1)S(1)} %get-tuple-element.77), channel_id=1, source_target_pairs={{4,0},{8,4},{12,8},{16,12},{20,16},{24,20},{28,24},{5,1},{9,5},{13... | collective-permute-start | bytes 393224 | tf_op jit(solution)/shard_map/ppermute | solution.py:619
  73.4 12.7 %all-to-all-start.4 = ((f32[8,16,512]{2,1,0:T(8,128)}), f32[8,16,512]{2,1,0:T(8,128)S(1)}, u32[]{:S(2)}, u32[]{:S(2)}) async-start(f32[8,16,512]{2,1,0:T(8,128)} %get-tuple-element.56), calls=%async_computation.4 | async-start | bytes 524288 | tf_op jit(solution)/shard_map/all_to_all | solution.py:662
  87.9 15.0 %collective-permute-start.7 = (bf16[6,64,128]{2,1,0:T(8,128)(2,1)S(1)}, bf16[6,64,128]{2,1,0:T(8,128)(2,1)S(1)}, u32[]{:S(2)}, u32[]{:S(2)}) collective-permute-start(bf16[6,64,128]{2,1,0:T(8,128)(2,1)S(1)} %pad_maximum_fusion.4), channel_id=1, source_target_pairs={{1,0},{2,1},{3,2},{5,4},{6,5},{7,6},{9,8},{10,9},{11,10},{13,12},{... | collective-permute-start | bytes 294920 | tf_op jit(solution)/shard_map/ppermute | solution.py:619
  89.2 14.4 %all-to-all-start.5 = ((bf16[4,32,512]{2,1,0:T(8,128)(2,1)}), bf16[4,32,512]{2,1,0:T(8,128)(2,1)S(1)}, u32[]{:S(2)}, u32[]{:S(2)}) async-start(bf16[4,32,512]{2,1,0:T(8,128)(2,1)} %shard_map.189), calls=%async_computation.5 | async-start | bytes 262144 | tf_op jit(solution)/shard_map/all_to_all | solution.py:662
  93.1 9.7 %collective-permute-start.6 = (bf16[6,64,128]{2,1,0:T(8,128)(2,1)S(1)}, bf16[6,64,128]{2,1,0:T(8,128)(2,1)S(1)}, u32[]{:S(2)}, u32[]{:S(2)}) collective-permute-start(bf16[6,64,128]{2,1,0:T(8,128)(2,1)S(1)} %pad_maximum_fusion.3), channel_id=1, source_target_pairs={{0,1},{1,2},{2,3},{4,5},{5,6},{6,7},{8,9},{9,10},{10,11},{12,13},{... | collective-permute-start | bytes 294920 | tf_op jit(solution)/shard_map/ppermute | solution.py:619
  97.1 0.9 copy-start.2
  98.0 0.9 copy-start.7
  98.9 0.9 copy-start.10
  102.9 0.7 copy-start.11
  102.9 0.7 copy-start.13
  103.6 23.4 %copy-start.14 = (bf16[6,64,128]{2,1,0:T(8,128)(2,1)S(1)}, bf16[6,64,128]{2,1,0:T(8,128)(2,1)}, u32[]{:S(2)}) copy-start(bf16[6,64,128]{2,1,0:T(8,128)(2,1)} %copy-done.13) | copy-start | bytes 294916
  103.6 13.3 %all-to-all-start.6 = ((f32[8,128,128]{2,1,0:T(8,128)}), f32[8,128,128]{2,1,0:T(8,128)S(1)}, u32[]{:S(2)}, u32[]{:S(2)}) async-start(f32[8,128,128]{2,1,0:T(8,128)} %bitcast.8), calls=%async_computation.6 | async-start | bytes 1048576 | tf_op jit(solution)/shard_map/all_to_all | solution.py:662
  107.4 19.6 %copy-start.12 = (bf16[6,64,128]{2,1,0:T(8,128)(2,1)S(1)}, bf16[6,64,128]{2,1,0:T(8,128)(2,1)}, u32[]{:S(2)}) copy-start(bf16[6,64,128]{2,1,0:T(8,128)(2,1)} %copy-done.11) | copy-start | bytes 294916
  117.7 12.1 %all-to-all-start.7 = ((bf16[4,64,512]{2,1,0:T(8,128)(2,1)}), bf16[4,64,512]{2,1,0:T(8,128)(2,1)S(1)}, u32[]{:S(2)}, u32[]{:S(2)}) async-start(bf16[4,64,512]{2,1,0:T(8,128)(2,1)} %pad_maximum_fusion), calls=%async_computation.7 | async-start | bytes 524288 | tf_op jit(solution)/shard_map/all_to_all | solution.py:662
  127.0 1.0 copy-start.4
  131.7 12.1 %all-to-all-start.8 = ((bf16[8,48,512]{2,1,0:T(8,128)(2,1)}), bf16[8,48,512]{2,1,0:T(8,128)(2,1)S(1)}, u32[]{:S(2)}, u32[]{:S(2)}) async-start(bf16[8,48,512]{2,1,0:T(8,128)(2,1)} %shard_map.192), calls=%async_computation.8 | async-start | bytes 786432 | tf_op jit(solution)/shard_map/all_to_all | solution.py:662

commit v6 on v5

--- a/solution.py
+++ b/solution.py
@@ -123,15 +123,12 @@
         z_forward(turned.reshape(cy * c, z), table_ref[...], slab_ref, x, nx)
 
 
-def plane_rows(p, cx, body_ref, xlo_ref, xhi_ref, ylo_ref, yhi_ref):
+def plane_rows(p, cx, body_ref, ylo_ref, yhi_ref, xlo_ref, xhi_ref):
     cy = body_ref.shape[1]
-    if p == 0:
-        middle = [xlo_ref[y] for y in range(cy)]
-    elif p == cx + 1:
-        middle = [xhi_ref[y] for y in range(cy)]
-    else:
-        middle = [body_ref[p - 1, y] for y in range(cy)]
-    return [ylo_ref[p]] + middle + [yhi_ref[p]]
+    if p in (0, cx + 1):
+        face_ref = xhi_ref if p else xlo_ref
+        return [face_ref[y] for y in range(cy + 2)]
+    return [ylo_ref[p - 1]] + [body_ref[p - 1, y] for y in range(cy)] + [yhi_ref[p - 1]]
 
 
 def fill_shifts(blocks, rim_ref, flip=False):
@@ -151,11 +148,11 @@
 
 
 def conv_kernel(
-    flip, body_ref, xlo_ref, xhi_ref, ylo_ref, yhi_ref, weight_ref, out_ref, rim_ref
+    flip, body_ref, ylo_ref, yhi_ref, xlo_ref, xhi_ref, weight_ref, out_ref, rim_ref
 ):
     cx, cy, c, z = body_ref.shape
     for p in range(cx + 2):
-        blocks = plane_rows(p, cx, body_ref, xlo_ref, xhi_ref, ylo_ref, yhi_ref)
+        blocks = plane_rows(p, cx, body_ref, ylo_ref, yhi_ref, xlo_ref, xhi_ref)
         fill_shifts(blocks, rim_ref, flip)
         places = [a for a in range(3) if 0 <= p - (2 - a if flip else a) < cx]
         first = places[0]
@@ -179,7 +176,7 @@
 
 
 def weight_grad_kernel(
-    grad_ref, body_ref, xlo_ref, xhi_ref, ylo_ref, yhi_ref, out_ref, rim_ref, wide_ref, sum_ref
+    grad_ref, body_ref, ylo_ref, yhi_ref, xlo_ref, xhi_ref, out_ref, rim_ref, wide_ref, sum_ref
 ):
     cx, cy, c, z = body_ref.shape
     group = 3 * c
@@ -191,7 +188,7 @@
                 wide_ref[row : row + c, (y + b) * z : (y + b + 1) * z] = grad_ref[x, y]
     sum_ref[...] = jnp.zeros_like(sum_ref)
     for p in range(cx + 2):
-        fill_shifts(plane_rows(p, cx, body_ref, xlo_ref, xhi_ref, ylo_ref, yhi_ref), rim_ref)
+        fill_shifts(plane_rows(p, cx, body_ref, ylo_ref, yhi_ref, xlo_ref, xhi_ref), rim_ref)
         first, last = max(0, p - 2), min(cx - 1, p)
         got = lax.dot_general(
             wide_ref[first * group : (last + 1) * group, :],
@@ -512,20 +509,17 @@
         y_inverse(mz, sum_ref, inverse_ref, out_ref, block_ref)
 
 
-def outer_kernel(alpha, modes_ref, back_ref, table_ref, out_ref, even_ref, odd_ref):
-    spread = spread_modes(modes_ref[0], table_ref, (even_ref, odd_ref))
-    for piece in range(C * C // SPAN):
-        modes = spread(piece)
-        for pair in range(QUAD):
-            back_re = back_ref[0, place(0, pair), :] * alpha
-            back_im = back_ref[0, place(1, pair), :] * alpha
-            for tile in range(SPAN // (2 * C)):
-                inside = slice(tile * 2 * C, (tile + 1) * 2 * C)
-                columns = slice(piece * SPAN + inside.start, piece * SPAN + inside.stop)
-                mode_re = modes[place(0, pair), inside]
-                mode_im = modes[place(1, pair), inside]
-                out_ref[0, 0, pair, :, columns] = mode_re * back_re + mode_im * back_im
-                out_ref[1, 0, pair, :, columns] = mode_re * back_im - mode_im * back_re
+def outer_kernel(alpha, modes_ref, back_ref, table_ref, out_ref):
+    spread = jnp.dot(modes_ref[0], table_ref[...], preferred_element_type=F32)
+    for pair in range(QUAD):
+        back_re = back_ref[0, place(0, pair), :] * alpha
+        back_im = back_ref[0, place(1, pair), :] * alpha
+        for tile in range(out_ref.shape[4] // (2 * C)):
+            columns = slice(tile * 2 * C, (tile + 1) * 2 * C)
+            mode_re = spread[place(0, pair), columns]
+            mode_im = spread[place(1, pair), columns]
+            out_ref[0, 0, pair, :, columns] = mode_re * back_re + mode_im * back_im
+            out_ref[1, 0, pair, :, columns] = mode_re * back_im - mode_im * back_re
 
 
 def in_hbm(value):
@@ -560,11 +554,10 @@
     return pl.BlockSpec(shape, lambda step: (0,) * len(shape))
 
 
-def group_block(shape, start=0):
+def group_block(shape):
     per = shape[2] // QUAD
     return pl.BlockSpec(
-        (2, 1, QUAD) + shape[3:],
-        lambda step: (0, (step + start) // per, (step + start) % per, 0, 0),
+        (2, 1, QUAD) + shape[3:], lambda step: (0, step // per, step % per, 0, 0)
     )
 
 
@@ -595,20 +588,28 @@
 
 def outer(modes, back, table, shape, alpha, start, count, prior=None):
     def kernel(*refs):
-        outer_kernel(alpha, *refs[:3], *refs[-3:])
-
-    group = lambda ref: pl.BlockSpec((1,) + ref.shape[1:], lambda step: (step + start, 0, 0))
+        outer_kernel(alpha, *refs[:3], refs[-1])
+
+    per = shape[2] // QUAD
+    width = 2 * SPAN
+    group = lambda ref: pl.BlockSpec((1,) + ref.shape[1:], lambda q, piece: (q + start, 0, 0))
     given = () if prior is None else (prior,)
     return pl.pallas_call(
         kernel,
-        grid=(count,),
-        in_specs=[group(modes), group(back), full(table.shape)]
+        grid=(count, shape[4] // width),
+        in_specs=[
+            group(modes),
+            group(back),
+            pl.BlockSpec((table.shape[0], width), lambda q, piece: (0, piece)),
+        ]
         + [pl.BlockSpec(memory_space=pl.ANY)] * len(given),
-        out_specs=group_block(shape, start),
+        out_specs=pl.BlockSpec(
+            (2, 1, QUAD, shape[3], width),
+            lambda q, piece: (0, (q + start) // per, (q + start) % per, 0, piece),
+        ),
         out_shape=jax.ShapeDtypeStruct(shape, F32),
         input_output_aliases={3: 0} if given else {},
-        scratch_shapes=[pltpu.VMEM((2 * QUAD * MY, SPAN), F32)] * 2,
-        compiler_params=params(20),
+        compiler_params=params(16),
         cost_estimate=cost(math.prod(shape) * 4, math.prod(shape) * 4),
     )(modes, back, in_hbm(table), *given)
 
@@ -619,13 +620,13 @@
     return lax.ppermute(block, axis, pairs)
 
 
-def x_halos(turned):
-    return shift(turned[-1], "gx", 1), shift(turned[0], "gx", -1)
-
-
-def y_halos(turned, xlo, xhi):
-    edge = lambda y: jnp.concatenate([xlo[None, y], turned[:, y], xhi[None, y]], axis=0)
-    return shift(edge(-1), "gy", 1), shift(edge(0), "gy", -1)
+def y_halos(turned):
+    return shift(turned[:, -1], "gy", 1), shift(turned[:, 0], "gy", -1)
+
+
+def x_halos(turned, ylo, yhi):
+    edge = lambda x: jnp.concatenate([ylo[x][None], turned[x], yhi[x][None]], axis=0)
+    return shift(edge(-1), "gx", 1), shift(edge(0), "gx", -1)
 
 
 def conv(turned, rim, weight, flip):
@@ -633,7 +634,7 @@
     return call(
         functools.partial(conv_kernel, flip),
         [((cx, c, cy * z), F32)],
-        (turned, *rim, weight),
+        (turned, *map(in_hbm, rim), in_hbm(weight)),
         [pltpu.VMEM((4 * c, (cy + 2) * z), BF16)],
         mib=32,
         flops=2 * 27 * c * c * cx * cy * z,
@@ -646,7 +647,7 @@
     return call(
         weight_grad_kernel,
         [((16 * c, 2 * c), F32)],
-        (grad, turned, *rim),
+        (grad, turned, *map(in_hbm, rim)),
         [
             pltpu.VMEM((4 * c, (cy + 2) * z), BF16),
             pltpu.VMEM((cx * 3 * c, (cy + 2) * z), BF16),
@@ -690,7 +691,7 @@
         return call(
             x_kernel,
             [((lead, rows, lanes), kind)],
-            (in_hbm(table), block),
+            (table, block),
             mib=16,
             flops=2 * table.size * lanes,
             moved=8 * block.size,
@@ -715,7 +716,7 @@
     )
     block = x_stage(x_fwd, swap(slab, "gx"), ny)
     block, conv_table, back_table, *faces = together(
-        block, conv_table, back_table, *x_halos(turned)
+        block, conv_table, back_table, *y_halos(turned)
     )
     modes_in, block = per_mode(
         mix_kernel,
@@ -726,24 +727,24 @@
         F32,
         [pltpu.VMEM((2 * QUAD * MY, SPAN), F32)] * 2 + [pltpu.VMEM((2 * QUAD * MY, 2 * c), F32)],
     )
-    block, *faces = together(block, *faces)
-    edges = y_halos(turned, *faces)
+    block, *edges = together(block, *x_halos(turned, *faces))
+    rim = (*faces, *edges)
     block = x_stage(x_inv, swap(block, "gy"), nx)
-    block, *edges = together(block, *edges)
-    rim = (*faces, *edges)
     stencil = conv(turned, rim, conv_table, False)
     output, grad, slab = call(
         functools.partial(gelu_kernel, nx),
         [((c, cx, cy, z), BF16), turned_shape, slab_shape],
-        (stencil, swap(block, "gx"), cotangent, in_hbm(z_spectral), in_hbm(z_grad)),
+        (stencil, swap(block, "gx"), cotangent, z_spectral, z_grad),
         flops=2 * 192 * state.size,
         moved=state.size * 12,
     )
 
     grad_taps = weight_grad(grad, turned, rim)
     block = x_stage(x_fwd, swap(slab, "gx"), ny, BF16)
-    block, *faces = together(block, *x_halos(grad))
-    edges = y_halos(grad, *faces)
+    grad, grad_taps = together(grad, grad_taps)
+    faces = y_halos(grad)
+    block, grad_taps = together(block, grad_taps)
+    edges = x_halos(grad, *faces)
     block, grad_taps, *edges = together(swap(block, "gy"), grad_taps, *edges)
     mine = swap(grad_taps.reshape(nx, -1, 2 * c), "gx").sum(0)
     back_modes, block = per_mode(
@@ -776,7 +777,7 @@
     grad_state, grad_stencil, grad_point = call(
         functools.partial(finish_kernel, nx, alpha),
         [((c, cx, cy, z), F32), ((c, 27 * c), F32), ((c, c), F32)],
-        (stencil_back, message, in_hbm(z_back)),
+        (stencil_back, message, z_back),
         [pltpu.VMEM(grad_taps.shape, F32), pltpu.VMEM((27 * c, c), F32)],
         flops=2 * 96 * state.size,
         moved=state.size * 10,

time: 148 us -> 146 us (0.986)
  blocking collectives: 0 us -> 10.6 us
  waiting for transfers between devices: 29.7 us -> 24.3 us
  local copies, waits for them, and re-layouts: 6.85 us -> 1.95 us
  starting transfers between devices: 55.3 us -> 50.6 us
  Pallas kernels: 52.8 us -> 54.8 us
    all_to_all x0 -> x1, blocking collectives: none -> 10.6 us  [swap(): return lax.all_to_all(block, axis, split_axis=0, concat_axis=0, tiled=True)]
    all_to_all x9 -> x8, waiting for transfers between devices: 29.6 us -> 21.9 us  [swap(): return lax.all_to_all(block, axis, split_axis=0, concat_axis=0, tiled=True)]
    unnamed x30 -> x36, local copies, waits for them, and re-layouts: 6.77 us -> 1.87 us
    pallas_call x2, Pallas kernels: 11.4 us -> 15.9 us  [outer(): pl.pallas_call(kernel, grid=(count, shape[4] // width), in_specs=[group(m...]
    all_to_all x9 -> x8, starting transfers between devices: 37.9 us -> 33.9 us  [swap(): return lax.all_to_all(block, axis, split_axis=0, concat_axis=0, tiled=True)]
    ppermute x8, waiting for transfers between devices: 0.02 us -> 2.39 us  [shift(): return lax.ppermute(block, axis, pairs)]
    pallas_call x11, Pallas kernels: 23.5 us -> 21.9 us  [call(): pl.pallas_call(kernel, out_shape=[jax.ShapeDtypeStruct(*out) for out in o...]
  transfers between devices with their start and end apart: 17 -> 16, of which waited for: 7 -> 9; matrix products, arithmetic and copies ran while one was open for 0% -> 0% of each run, Pallas kernels for 23% -> 29%
where the time goes in v6:
time: 146 us; the launch traced here: 144 us
  Pallas kernels  54.8 us (38%)
  starting transfers between devices  50.6 us (35%)
  waiting for transfers between devices  24.3 us (17%)
  blocking collectives  10.6 us (7%)
  local copies, waits for them, and re-layouts  1.95 us (1%)
    all_to_all x8, starting transfers between devices, swap(): return lax.all_to_all(block, axis, split_axis=0, concat_axis=0, tiled=True)  33.9 us
    all_to_all x8, waiting for transfers between devices, swap(): return lax.all_to_all(block, axis, split_axis=0, concat_axis=0, tiled=True)  21.9 us
    pallas_call x11, Pallas kernels, call(): pl.pallas_call(kernel, out_shape=[jax.ShapeDtypeStruct(*out) for out in o...  21.9 us
    pallas_call x2, Pallas kernels, per_mode(): pl.pallas_call(functools.partial(kernel, mz), grid=(groups,), in_specs=[f...  17.1 us
    ppermute x8, starting transfers between devices, shift(): return lax.ppermute(block, axis, pairs)  16.7 us
    pallas_call x2, Pallas kernels, outer(): pl.pallas_call(kernel, grid=(count, shape[4] // width), in_specs=[group(m...  15.9 us
    all_to_all x1, blocking collectives, swap(): return lax.all_to_all(block, axis, split_axis=0, concat_axis=0, tiled=True)  10.6 us
  transfers between devices with their start and end apart: 16, of which 9 were waited for; matrix products, arithmetic and copies ran while one was open for 0% of the time, Pallas kernels for 29%

profile of v6, /device:TPU:0, one launch (start us, length us, event | category | flops | bytes accessed | tf_op | source)
XLA Modules:
  0.0 144.3 jit_solution(1472935054046406039)
XLA Ops:
  0.7 2.2 %shard_map.182 = (bf16[4,8,64,128]{3,2,1,0:T(8,128)(2,1)S(1)}, f32[8,16,512]{2,1,0:T(8,128)}) custom-call(bf16[64,4,8,128]{3,2,1,0:T(8,128)(2,1)} %field_ref.1, bf16[96,128]{1,0:T(8,128)(2,1)} %constant.22.clone.table_ref), custom_call_target="tpu_custom_call" | custom-call | flops 50331648 | bytes 1310720 | tf_op jit(solution)/shard_map/pallas_call | solution.py:542
  2.9 4.9 %collective-permute-start = (bf16[4,64,128]{2,1,0:T(8,128)(2,1)S(1)}, bf16[4,64,128]{2,1,0:T(8,128)(2,1)S(1)}, u32[]{:S(2)}, u32[]{:S(2)}) collective-permute-start(bf16[4,64,128]{2,1,0:T(8,128)(2,1)S(1)} %get-tuple-element.78), channel_id=1, source_target_pairs={{0,1},{1,2},{2,3},{4,5},{5,6},{6,7},{8,9},{9,10},{10,11},{12,13},{... | collective-permute-start | bytes 196616 | tf_op jit(solution)/shard_map/ppermute | solution.py:620
  7.9 1.3 collective-permute-start.1
  9.2 3.7 %all-to-all-start = ((f32[8,16,512]{2,1,0:T(8,128)}), f32[8,16,512]{2,1,0:T(8,128)S(1)}, u32[]{:S(2)}, u32[]{:S(2)}) async-start(f32[8,16,512]{2,1,0:T(8,128)} %get-tuple-element.39), calls=%async_computation | async-start | bytes 524288 | tf_op jit(solution)/shard_map/all_to_all | solution.py:663
  12.9 1.5 %shard_map.184 = (bf16[576,256]{1,0:T(8,128)(2,1)S(1)}, bf16[576,256]{1,0:T(8,128)(2,1)S(1)}) custom-call(bf16[64,1728]{1,0:T(8,128)(2,1)} %taps_ref.1, bf16[64,64]{1,0:T(8,128)(2,1)} %point_ref.1), custom_call_target="tpu_custom_call" | custom-call | bytes 663552 | tf_op jit(solution)/shard_map/pallas_call | solution.py:542
  14.5 5.4 %all-to-all-done.data_ref = f32[8,16,512]{2,1,0:T(8,128)S(1)} async-done(((f32[8,16,512]{2,1,0:T(8,128)}), f32[8,16,512]{2,1,0:T(8,128)S(1)}, u32[]{:S(2)}, u32[]{:S(2)}) %all-to-all-start) | async-done | bytes 262176 | tf_op jit(solution)/shard_map/all_to_all | solution.py:663
  21.7 5.9 %all-to-all-start.1 = ((f32[4,32,512]{2,1,0:T(8,128)}), f32[4,32,512]{2,1,0:T(8,128)S(1)}, u32[]{:S(2)}, u32[]{:S(2)}) async-start(f32[4,32,512]{2,1,0:T(8,128)} %shard_map.183), calls=%async_computation.1 | async-start | bytes 524288 | tf_op jit(solution)/shard_map/all_to_all | solution.py:663
  27.7 1.3 collective-permute-start.3
  29.0 3.0 %collective-permute-start.2 = (bf16[10,64,128]{2,1,0:T(8,128)(2,1)S(1)}, bf16[10,64,128]{2,1,0:T(8,128)(2,1)S(1)}, u32[]{:S(2)}, u32[]{:S(2)}) collective-permute-start(bf16[10,64,128]{2,1,0:T(8,128)(2,1)S(1)} %pad_maximum_fusion.1), channel_id=1, source_target_pairs={{0,4},{4,8},{8,12},{12,16},{16,20},{20,24},{24,28},{1,5},{5,9},{9,... | collective-permute-start | bytes 491528 | tf_op jit(solution)/shard_map/ppermute | solution.py:620
  32.1 3.8 %all-to-all-done.1.data_ref = f32[4,32,512]{2,1,0:T(8,128)S(1)} async-done(((f32[4,32,512]{2,1,0:T(8,128)}), f32[4,32,512]{2,1,0:T(8,128)S(1)}, u32[]{:S(2)}, u32[]{:S(2)}) %all-to-all-start.1) | async-done | bytes 262176 | tf_op jit(solution)/shard_map/all_to_all | solution.py:663
  35.9 8.7 %shard_map.185 = (bf16[4,256,128]{2,1,0:T(8,128)(2,1)S(1)}, f32[4,32,512]{2,1,0:T(8,128)S(1)}) custom-call(f32[4,32,512]{2,1,0:T(8,128)S(1)} %all-to-all-done.1.data_ref, bf16[2,2,8,32,4096]{4,3,2,1,0:T(8,128)(2,1)} %weight_ref.3, bf16[128,4096]{1,0:T(8,128)(2,1)} %constant.30.clone.table_ref.refs_2_, bf16[64,192]{1,0:T(8,128)(2,1)} %constant.28.clone.forward_ref, ...), custom_call_target="tpu_custom_call" | custom-call | flops 33554432 | bytes 8388608 | tf_op jit(solution)/shard_map/pallas_call | solution.py:569
  44.6 10.6 %all_to_all.45.data_ref = f32[4,32,512]{2,1,0:T(8,128)S(1)} all-to-all(f32[4,32,512]{2,1,0:T(8,128)S(1)} %get-tuple-element.49), channel_id=1, replica_groups=mesh['gx'=8,'gy'=4] {'gy'}, dimensions={0} | all-to-all | bytes 524288 | tf_op jit(solution)/shard_map/all_to_all | solution.py:663
  57.0 3.4 %all-to-all-start.3 = ((f32[8,16,512]{2,1,0:T(8,128)}), f32[8,16,512]{2,1,0:T(8,128)S(1)}, u32[]{:S(2)}, u32[]{:S(2)}) async-start(f32[8,16,512]{2,1,0:T(8,128)} %shard_map.187), calls=%async_computation.3 | async-start | bytes 524288 | tf_op jit(solution)/shard_map/all_to_all | solution.py:663
  60.5 3.1 %shard_map.186.stencil_ref = f32[4,64,1024]{2,1,0:T(8,128)S(1)} custom-call(bf16[4,8,64,128]{3,2,1,0:T(8,128)(2,1)S(1)} %get-tuple-element.38.body_ref, bf16[4,64,128]{2,1,0:T(8,128)(2,1)} %copy-done.12, bf16[4,64,128]{2,1,0:T(8,128)(2,1)} %copy-done.13, bf16[10,64,128]{2,1,0:T(8,128)(2,1)} %copy-done.17, bf16[10,64,128]{2,1,0:T(8,128)(2,1)} %copy-done.16, ...), custom_call_target="tpu_custom_call" | custom-call | flops 905969664 | bytes 2097152 | tf_op jit(solution)/shard_map/pallas_call | solution.py:542
  63.6 3.8 %all-to-all-done.3.slab_ref = f32[8,16,512]{2,1,0:T(8,128)S(1)} async-done(((f32[8,16,512]{2,1,0:T(8,128)}), f32[8,16,512]{2,1,0:T(8,128)S(1)}, u32[]{:S(2)}, u32[]{:S(2)}) %all-to-all-start.3) | async-done | bytes 262176 | tf_op jit(solution)/shard_map/all_to_all | solution.py:663
  67.3 2.3 %shard_map.188 = (bf16[64,4,8,128]{3,2,1,0:T(8,128)(2,1)}, bf16[4,8,64,128]{3,2,1,0:T(8,128)(2,1)S(1)}, f32[8,16,512]{2,1,0:T(8,128)}) custom-call(f32[4,64,1024]{2,1,0:T(8,128)S(1)} %shard_map.186.stencil_ref, f32[8,16,512]{2,1,0:T(8,128)S(1)} %all-to-all-done.3.slab_ref, bf16[64,4,8,128]{3,2,1,0:T(8,128)(2,1)S(1)} %copy-done, ...), custom_call_target="tpu_custom_call" | custom-call | flops 100663296 | bytes 3145728 | tf_op jit(solution)/shard_map/pallas_call | solution.py:542
  69.6 4.1 %shard_map.190 = f32[1024,128]{1,0:T(8,128)} custom-call(bf16[4,8,64,128]{3,2,1,0:T(8,128)(2,1)S(1)} %get-tuple-element.56.grad_ref.body_ref, bf16[4,8,64,128]{3,2,1,0:T(8,128)(2,1)S(1)} %get-tuple-element.38.body_ref, bf16[4,64,128]{2,1,0:T(8,128)(2,1)} %copy-done.12, bf16[4,64,128]{2,1,0:T(8,128)(2,1)} %copy-done.13, bf16[10,64,128]{2,1,0:T(8,128)(2,1)} %copy-done.17, ...), custom_call_target="tpu_custom_call" | custom-call | flops 905969664 | bytes 2097152 | tf_op jit(solution)/shard_map/pallas_call | solution.py:542
  73.8 2.1 %collective-permute-start.4 = (bf16[4,64,128]{2,1,0:T(8,128)(2,1)S(1)}, bf16[4,64,128]{2,1,0:T(8,128)(2,1)S(1)}, u32[]{:S(2)}, u32[]{:S(2)}) collective-permute-start(bf16[4,64,128]{2,1,0:T(8,128)(2,1)S(1)} %get-tuple-element.73), channel_id=1, source_target_pairs={{0,1},{1,2},{2,3},{4,5},{5,6},{6,7},{8,9},{9,10},{10,11},{12,13},{... | collective-permute-start | bytes 196616 | tf_op jit(solution)/shard_map/ppermute | solution.py:620
  77.2 3.4 %all-to-all-start.4 = ((f32[8,16,512]{2,1,0:T(8,128)}), f32[8,16,512]{2,1,0:T(8,128)S(1)}, u32[]{:S(2)}, u32[]{:S(2)}) async-start(f32[8,16,512]{2,1,0:T(8,128)} %get-tuple-element.51), calls=%async_computation.4 | async-start | bytes 524288 | tf_op jit(solution)/shard_map/all_to_all | solution.py:663
  80.7 1.4 collective-permute-done.5.yhi_ref
  83.4 4.1 %all-to-all-done.4.data_ref = f32[8,16,512]{2,1,0:T(8,128)S(1)} async-done(((f32[8,16,512]{2,1,0:T(8,128)}), f32[8,16,512]{2,1,0:T(8,128)S(1)}, u32[]{:S(2)}, u32[]{:S(2)}) %all-to-all-start.4) | async-done | bytes 262176 | tf_op jit(solution)/shard_map/all_to_all | solution.py:663
  88.4 5.2 %all-to-all-start.5 = ((bf16[4,32,512]{2,1,0:T(8,128)(2,1)}), bf16[4,32,512]{2,1,0:T(8,128)(2,1)S(1)}, u32[]{:S(2)}, u32[]{:S(2)}) async-start(bf16[4,32,512]{2,1,0:T(8,128)(2,1)} %shard_map.189), calls=%async_computation.5 | async-start | bytes 262144 | tf_op jit(solution)/shard_map/all_to_all | solution.py:663
  93.6 1.4 collective-permute-start.6
  96.1 3.4 %all-to-all-done.5.data_ref = bf16[4,32,512]{2,1,0:T(8,128)(2,1)S(1)} async-done(((bf16[4,32,512]{2,1,0:T(8,128)(2,1)}), bf16[4,32,512]{2,1,0:T(8,128)(2,1)S(1)}, u32[]{:S(2)}, u32[]{:S(2)}) %all-to-all-start.5) | async-done | bytes 131104 | tf_op jit(solution)/shard_map/all_to_all | solution.py:663
  99.5 3.7 %all-to-all-start.6 = ((f32[8,128,128]{2,1,0:T(8,128)}), f32[8,128,128]{2,1,0:T(8,128)S(1)}, u32[]{:S(2)}, u32[]{:S(2)}) async-start(f32[8,128,128]{2,1,0:T(8,128)} %bitcast.8), calls=%async_computation.6 | async-start | bytes 1048576 | tf_op jit(solution)/shard_map/all_to_all | solution.py:663
  103.2 8.5 %shard_map.191 = (f32[4,256,128]{2,1,0:T(8,128)S(1)}, bf16[4,32,512]{2,1,0:T(8,128)(2,1)S(1)}) custom-call(bf16[4,32,512]{2,1,0:T(8,128)(2,1)S(1)} %all-to-all-done.5.data_ref, bf16[2,2,8,32,4096]{4,3,2,1,0:T(8,128)(2,1)} %weight_ref.3, bf16[8,512]{1,0:T(8,128)(2,1)} %constant.31.clone.table_ref, bf16[64,192]{1,0:T(8,128)(2,1)} %constant.28.clone.forward_ref, ...), custom_call_target="tpu_custom_call" | custom-call | flops 33554432 | bytes 8388608 | tf_op jit(solution)/shard_map/pallas_call | solution.py:569
  113.6 5.1 %all-to-all-start.7 = ((bf16[4,64,512]{2,1,0:T(8,128)(2,1)}), bf16[4,64,512]{2,1,0:T(8,128)(2,1)S(1)}, u32[]{:S(2)}, u32[]{:S(2)}) async-start(bf16[4,64,512]{2,1,0:T(8,128)(2,1)} %pad_maximum_fusion), calls=%async_computation.7 | async-start | bytes 524288 | tf_op jit(solution)/shard_map/all_to_all | solution.py:663
  118.7 7.9 %shard_map.194.refs_3_ = f32[2,2,8,32,4096]{4,3,2,1,0:T(8,128)} custom-call(bf16[4,256,128]{2,1,0:T(8,128)(2,1)S(1)} %get-tuple-element.63.refs_0_, f32[4,256,128]{2,1,0:T(8,128)S(1)} %get-tuple-element.64.refs_1_, bf16[128,4096]{1,0:T(8,128)(2,1)} %constant.30.clone.table_ref.refs_2_), custom_call_target="tpu_custom_call" | custom-call | flops 16777216 | bytes 16777216 | tf_op jit(solution)/shard_map/pallas_call | solution.py:597
  126.7 3.0 %shard_map.193.stencil_ref = f32[4,64,1024]{2,1,0:T(8,128)S(1)} custom-call(bf16[4,8,64,128]{3,2,1,0:T(8,128)(2,1)S(1)} %get-tuple-element.56.grad_ref.body_ref, bf16[4,64,128]{2,1,0:T(8,128)(2,1)} %copy-done.10, bf16[4,64,128]{2,1,0:T(8,128)(2,1)} %copy-done.11, bf16[10,64,128]{2,1,0:T(8,128)(2,1)} %copy-done.15, bf16[10,64,128]{2,1,0:T(8,128)(2,1)} %copy-done.14, ...), custom_call_target="tpu_custom_call" | custom-call | flops 905969664 | bytes 2097152 | tf_op jit(solution)/shard_map/pallas_call | solution.py:542
  130.7 3.5 %all-to-all-start.8 = ((bf16[8,48,512]{2,1,0:T(8,128)(2,1)}), bf16[8,48,512]{2,1,0:T(8,128)(2,1)S(1)}, u32[]{:S(2)}, u32[]{:S(2)}) async-start(bf16[8,48,512]{2,1,0:T(8,128)(2,1)} %shard_map.192), calls=%async_computation.8 | async-start | bytes 786432 | tf_op jit(solution)/shard_map/all_to_all | solution.py:663
  134.2 7.9 %shard_map.196 = f32[2,2,8,32,4096]{4,3,2,1,0:T(8,128)} custom-call(bf16[4,256,128]{2,1,0:T(8,128)(2,1)S(1)} %get-tuple-element.63.refs_0_, f32[4,256,128]{2,1,0:T(8,128)S(1)} %get-tuple-element.64.refs_1_, bf16[128,4096]{1,0:T(8,128)(2,1)} %constant.30.clone.table_ref.refs_2_, f32[2,2,8,32,4096]{4,3,2,1,0:T(8,128)} %shard_map.194.refs_3_), custom_call_target="tpu_custom_call", output_to_operand_aliasing={{}: (3, {})} | custom-call | flops 16777216 | bytes 16777216 | tf_op jit(solution)/shard_map/pallas_call | solution.py:597
  142.5 1.8 %shard_map.195 = (f32[64,4,8,128]{3,2,1,0:T(8,128)}, f32[64,1728]{1,0:T(8,128)}, f32[64,64]{1,0:T(8,128)}) custom-call(f32[4,64,1024]{2,1,0:T(8,128)S(1)} %shard_map.193.stencil_ref, bf16[8,48,512]{2,1,0:T(8,128)(2,1)S(1)} %all-to-all-done.8.message_ref, bf16[96,128]{1,0:T(8,128)(2,1)S(1)} %copy-done.7), custom_call_target="tpu_custom_call" | custom-call | flops 50331648 | bytes 2621440 | tf_op jit(solution)/shard_map/pallas_call | solution.py:542
  (68 shorter events, 11.7 us)
Async XLA Ops:
  0.6 86.9 %copy-start.4 = (bf16[128,384]{1,0:T(8,128)(2,1)S(1)}, bf16[128,384]{1,0:T(8,128)(2,1)}, u32[]{:S(2)}) copy-start(bf16[128,384]{1,0:T(8,128)(2,1)} %constant.26.clone.table_ref) | copy-start | bytes 294916
  0.6 66.7 %copy-start.5 = (bf16[96,128]{1,0:T(8,128)(2,1)S(1)}, bf16[96,128]{1,0:T(8,128)(2,1)}, u32[]{:S(2)}) copy-start(bf16[96,128]{1,0:T(8,128)(2,1)} %constant.23.clone.forward_ref) | copy-start | bytes 73732
  0.7 66.7 %copy-start.6 = (bf16[96,128]{1,0:T(8,128)(2,1)S(1)}, bf16[96,128]{1,0:T(8,128)(2,1)}, u32[]{:S(2)}) copy-start(bf16[96,128]{1,0:T(8,128)(2,1)} %constant.24.clone.inverse_ref) | copy-start | bytes 73732
  0.7 66.7 %copy-start = (bf16[64,4,8,128]{3,2,1,0:T(8,128)(2,1)S(1)}, bf16[64,4,8,128]{3,2,1,0:T(8,128)(2,1)}, u32[]{:S(2)}) copy-start(bf16[64,4,8,128]{3,2,1,0:T(8,128)(2,1)} %cot_ref.1) | copy-start | bytes 1572868
  2.9 18.7 %collective-permute-start = (bf16[4,64,128]{2,1,0:T(8,128)(2,1)S(1)}, bf16[4,64,128]{2,1,0:T(8,128)(2,1)S(1)}, u32[]{:S(2)}, u32[]{:S(2)}) collective-permute-start(bf16[4,64,128]{2,1,0:T(8,128)(2,1)S(1)} %get-tuple-element.78), channel_id=1, source_target_pairs={{0,1},{1,2},{2,3},{4,5},{5,6},{6,7},{8,9},{9,10},{10,11},{12,13},{... | collective-permute-start | bytes 196616 | tf_op jit(solution)/shard_map/ppermute | solution.py:620
  7.9 13.8 %collective-permute-start.1 = (bf16[4,64,128]{2,1,0:T(8,128)(2,1)S(1)}, bf16[4,64,128]{2,1,0:T(8,128)(2,1)S(1)}, u32[]{:S(2)}, u32[]{:S(2)}) collective-permute-start(bf16[4,64,128]{2,1,0:T(8,128)(2,1)S(1)} %get-tuple-element.77), channel_id=1, source_target_pairs={{1,0},{2,1},{3,2},{5,4},{6,5},{7,6},{9,8},{10,9},{11,10},{13,12},{... | collective-permute-start | bytes 196616 | tf_op jit(solution)/shard_map/ppermute | solution.py:620
  9.2 10.7 %all-to-all-start = ((f32[8,16,512]{2,1,0:T(8,128)}), f32[8,16,512]{2,1,0:T(8,128)S(1)}, u32[]{:S(2)}, u32[]{:S(2)}) async-start(f32[8,16,512]{2,1,0:T(8,128)} %get-tuple-element.39), calls=%async_computation | async-start | bytes 524288 | tf_op jit(solution)/shard_map/all_to_all | solution.py:663
  14.5 17.6 %copy-start.8 = (bf16[576,256]{1,0:T(8,128)(2,1)}, bf16[576,256]{1,0:T(8,128)(2,1)S(1)}, u32[]{:S(2)}) copy-start(bf16[576,256]{1,0:T(8,128)(2,1)S(1)} %get-tuple-element.62.weight_ref) | copy-start | bytes 884740
  14.5 17.6 %copy-start.9 = (bf16[576,256]{1,0:T(8,128)(2,1)}, bf16[576,256]{1,0:T(8,128)(2,1)S(1)}, u32[]{:S(2)}) copy-start(bf16[576,256]{1,0:T(8,128)(2,1)S(1)} %get-tuple-element.48.weight_ref) | copy-start | bytes 884740
  21.7 38.8 %copy-start.12 = (bf16[4,64,128]{2,1,0:T(8,128)(2,1)}, bf16[4,64,128]{2,1,0:T(8,128)(2,1)S(1)}, u32[]{:S(2)}) copy-start(bf16[4,64,128]{2,1,0:T(8,128)(2,1)S(1)} %collective-permute-done.ylo_ref) | copy-start | bytes 196612
  21.7 38.8 %copy-start.13 = (bf16[4,64,128]{2,1,0:T(8,128)(2,1)}, bf16[4,64,128]{2,1,0:T(8,128)(2,1)S(1)}, u32[]{:S(2)}) copy-start(bf16[4,64,128]{2,1,0:T(8,128)(2,1)S(1)} %collective-permute-done.1.yhi_ref) | copy-start | bytes 196612
  21.7 14.2 %all-to-all-start.1 = ((f32[4,32,512]{2,1,0:T(8,128)}), f32[4,32,512]{2,1,0:T(8,128)S(1)}, u32[]{:S(2)}, u32[]{:S(2)}) async-start(f32[4,32,512]{2,1,0:T(8,128)} %shard_map.183), calls=%async_computation.1 | async-start | bytes 524288 | tf_op jit(solution)/shard_map/all_to_all | solution.py:663
  27.7 16.9 %collective-permute-start.3 = (bf16[10,64,128]{2,1,0:T(8,128)(2,1)S(1)}, bf16[10,64,128]{2,1,0:T(8,128)(2,1)S(1)}, u32[]{:S(2)}, u32[]{:S(2)}) collective-permute-start(bf16[10,64,128]{2,1,0:T(8,128)(2,1)S(1)} %pad_maximum_fusion.2), channel_id=1, source_target_pairs={{4,0},{8,4},{12,8},{16,12},{20,16},{24,20},{28,24},{5,1},{9,5},{13... | collective-permute-start | bytes 491528 | tf_op jit(solution)/shard_map/ppermute | solution.py:620
  29.0 15.5 %collective-permute-start.2 = (bf16[10,64,128]{2,1,0:T(8,128)(2,1)S(1)}, bf16[10,64,128]{2,1,0:T(8,128)(2,1)S(1)}, u32[]{:S(2)}, u32[]{:S(2)}) collective-permute-start(bf16[10,64,128]{2,1,0:T(8,128)(2,1)S(1)} %pad_maximum_fusion.1), channel_id=1, source_target_pairs={{0,4},{4,8},{8,12},{12,16},{16,20},{20,24},{24,28},{1,5},{5,9},{9,... | collective-permute-start | bytes 491528 | tf_op jit(solution)/shard_map/ppermute | solution.py:620
  44.6 15.9 %copy-start.16 = (bf16[10,64,128]{2,1,0:T(8,128)(2,1)}, bf16[10,64,128]{2,1,0:T(8,128)(2,1)S(1)}, u32[]{:S(2)}) copy-start(bf16[10,64,128]{2,1,0:T(8,128)(2,1)S(1)} %collective-permute-done.3.xhi_ref) | copy-start | bytes 491524
  44.6 15.9 %copy-start.17 = (bf16[10,64,128]{2,1,0:T(8,128)(2,1)}, bf16[10,64,128]{2,1,0:T(8,128)(2,1)S(1)}, u32[]{:S(2)}) copy-start(bf16[10,64,128]{2,1,0:T(8,128)(2,1)S(1)} %collective-permute-done.2.xlo_ref) | copy-start | bytes 491524
  57.0 10.3 %all-to-all-start.3 = ((f32[8,16,512]{2,1,0:T(8,128)}), f32[8,16,512]{2,1,0:T(8,128)S(1)}, u32[]{:S(2)}, u32[]{:S(2)}) async-start(f32[8,16,512]{2,1,0:T(8,128)} %shard_map.187), calls=%async_computation.3 | async-start | bytes 524288 | tf_op jit(solution)/shard_map/all_to_all | solution.py:663
  73.8 6.9 %collective-permute-start.4 = (bf16[4,64,128]{2,1,0:T(8,128)(2,1)S(1)}, bf16[4,64,128]{2,1,0:T(8,128)(2,1)S(1)}, u32[]{:S(2)}, u32[]{:S(2)}) collective-permute-start(bf16[4,64,128]{2,1,0:T(8,128)(2,1)S(1)} %get-tuple-element.73), channel_id=1, source_target_pairs={{0,1},{1,2},{2,3},{4,5},{5,6},{6,7},{8,9},{9,10},{10,11},{12,13},{... | collective-permute-start | bytes 196616 | tf_op jit(solution)/shard_map/ppermute | solution.py:620
  75.9 6.2 %collective-permute-start.5 = (bf16[4,64,128]{2,1,0:T(8,128)(2,1)S(1)}, bf16[4,64,128]{2,1,0:T(8,128)(2,1)S(1)}, u32[]{:S(2)}, u32[]{:S(2)}) collective-permute-start(bf16[4,64,128]{2,1,0:T(8,128)(2,1)S(1)} %get-tuple-element.74), channel_id=1, source_target_pairs={{1,0},{2,1},{3,2},{5,4},{6,5},{7,6},{9,8},{10,9},{11,10},{13,12},{... | collective-permute-start | bytes 196616 | tf_op jit(solution)/shard_map/ppermute | solution.py:620
  77.2 10.3 %all-to-all-start.4 = ((f32[8,16,512]{2,1,0:T(8,128)}), f32[8,16,512]{2,1,0:T(8,128)S(1)}, u32[]{:S(2)}, u32[]{:S(2)}) async-start(f32[8,16,512]{2,1,0:T(8,128)} %get-tuple-element.51), calls=%async_computation.4 | async-start | bytes 524288 | tf_op jit(solution)/shard_map/all_to_all | solution.py:663
  80.7 46.0 %copy-start.10 = (bf16[4,64,128]{2,1,0:T(8,128)(2,1)}, bf16[4,64,128]{2,1,0:T(8,128)(2,1)S(1)}, u32[]{:S(2)}) copy-start(bf16[4,64,128]{2,1,0:T(8,128)(2,1)S(1)} %collective-permute-done.4.ylo_ref) | copy-start | bytes 196612
  82.1 44.6 %copy-start.11 = (bf16[4,64,128]{2,1,0:T(8,128)(2,1)}, bf16[4,64,128]{2,1,0:T(8,128)(2,1)S(1)}, u32[]{:S(2)}) copy-start(bf16[4,64,128]{2,1,0:T(8,128)(2,1)S(1)} %collective-permute-done.5.yhi_ref) | copy-start | bytes 196612
  82.1 12.9 %collective-permute-start.7 = (bf16[10,64,128]{2,1,0:T(8,128)(2,1)S(1)}, bf16[10,64,128]{2,1,0:T(8,128)(2,1)S(1)}, u32[]{:S(2)}, u32[]{:S(2)}) collective-permute-start(bf16[10,64,128]{2,1,0:T(8,128)(2,1)S(1)} %pad_maximum_fusion.4), channel_id=1, source_target_pairs={{4,0},{8,4},{12,8},{16,12},{20,16},{24,20},{28,24},{5,1},{9,5},{13... | collective-permute-start | bytes 491528 | tf_op jit(solution)/shard_map/ppermute | solution.py:620
  88.4 11.1 %all-to-all-start.5 = ((bf16[4,32,512]{2,1,0:T(8,128)(2,1)}), bf16[4,32,512]{2,1,0:T(8,128)(2,1)S(1)}, u32[]{:S(2)}, u32[]{:S(2)}) async-start(bf16[4,32,512]{2,1,0:T(8,128)(2,1)} %shard_map.189), calls=%async_computation.5 | async-start | bytes 262144 | tf_op jit(solution)/shard_map/all_to_all | solution.py:663
  93.6 36.1 %copy-start.2 = (bf16[128,384]{1,0:T(8,128)(2,1)S(1)}, bf16[128,384]{1,0:T(8,128)(2,1)}, u32[]{:S(2)}) copy-start(bf16[128,384]{1,0:T(8,128)(2,1)} %constant.27.clone.table_ref) | copy-start | bytes 294916
  93.6 2.4 %collective-permute-start.6 = (bf16[10,64,128]{2,1,0:T(8,128)(2,1)S(1)}, bf16[10,64,128]{2,1,0:T(8,128)(2,1)S(1)}, u32[]{:S(2)}, u32[]{:S(2)}) collective-permute-start(bf16[10,64,128]{2,1,0:T(8,128)(2,1)S(1)} %pad_maximum_fusion.3), channel_id=1, source_target_pairs={{0,4},{4,8},{8,12},{12,16},{16,20},{20,24},{24,28},{1,5},{5,9},{9,... | collective-permute-start | bytes 491528 | tf_op jit(solution)/shard_map/ppermute | solution.py:620
  95.1 31.6 %copy-start.14 = (bf16[10,64,128]{2,1,0:T(8,128)(2,1)}, bf16[10,64,128]{2,1,0:T(8,128)(2,1)S(1)}, u32[]{:S(2)}) copy-start(bf16[10,64,128]{2,1,0:T(8,128)(2,1)S(1)} %collective-permute-done.7.xhi_ref) | copy-start | bytes 491524
  96.0 30.6 %copy-start.15 = (bf16[10,64,128]{2,1,0:T(8,128)(2,1)}, bf16[10,64,128]{2,1,0:T(8,128)(2,1)S(1)}, u32[]{:S(2)}) copy-start(bf16[10,64,128]{2,1,0:T(8,128)(2,1)S(1)} %collective-permute-done.6.xlo_ref) | copy-start | bytes 491524
  99.5 13.4 %all-to-all-start.6 = ((f32[8,128,128]{2,1,0:T(8,128)}), f32[8,128,128]{2,1,0:T(8,128)S(1)}, u32[]{:S(2)}, u32[]{:S(2)}) async-start(f32[8,128,128]{2,1,0:T(8,128)} %bitcast.8), calls=%async_computation.6 | async-start | bytes 1048576 | tf_op jit(solution)/shard_map/all_to_all | solution.py:663
  113.6 16.1 %all-to-all-start.7 = ((bf16[4,64,512]{2,1,0:T(8,128)(2,1)}), bf16[4,64,512]{2,1,0:T(8,128)(2,1)S(1)}, u32[]{:S(2)}, u32[]{:S(2)}) async-start(bf16[4,64,512]{2,1,0:T(8,128)(2,1)} %pad_maximum_fusion), calls=%async_computation.7 | async-start | bytes 524288 | tf_op jit(solution)/shard_map/all_to_all | solution.py:663
  130.7 11.7 %all-to-all-start.8 = ((bf16[8,48,512]{2,1,0:T(8,128)(2,1)}), bf16[8,48,512]{2,1,0:T(8,128)(2,1)S(1)}, u32[]{:S(2)}, u32[]{:S(2)}) async-start(bf16[8,48,512]{2,1,0:T(8,128)(2,1)} %shard_map.192), calls=%async_computation.8 | async-start | bytes 786432 | tf_op jit(solution)/shard_map/all_to_all | solution.py:663
  134.2 8.3 %copy-start.7 = (bf16[96,128]{1,0:T(8,128)(2,1)S(1)}, bf16[96,128]{1,0:T(8,128)(2,1)}, u32[]{:S(2)}) copy-start(bf16[96,128]{1,0:T(8,128)(2,1)} %constant.25.clone.inverse_ref) | copy-start | bytes 73732
  (2 other events, 1.8 us)

commit v7 on v5

--- a/solution.py
+++ b/solution.py
@@ -380,13 +380,6 @@
     return np.kron(np.eye(SPAN // C), np.ones((1, C))).astype(jnp.bfloat16)
 
 
-def tiles():
-    for piece in range(C * C // SPAN):
-        for tile in range(SPAN // (2 * C)):
-            start = piece * SPAN + tile * 2 * C
-            yield piece, tile, slice(start, start + 2 * C)
-
-
 def spread_modes(modes, table_ref, spread_refs):
     count = C * C // SPAN
     made = set()
@@ -401,6 +394,18 @@
         return spread_refs[piece % 2]
 
     return get
+
+
+def weight_copies(weight_ref, held_ref, sem_ref):
+    per = weight_ref.shape[2] // QUAD
+    return [
+        pltpu.make_async_copy(
+            weight_ref.at[:, g // per, g % per * QUAD : (g % per + 1) * QUAD],
+            held_ref.at[g],
+            sem_ref.at[g],
+        )
+        for g in range(held_ref.shape[0])
+    ]
 
 
 def mix_kernel(
@@ -415,48 +420,53 @@
     sum_ref,
     rows_ref,
     block_ref,
+    held_ref,
+    sem_ref,
+    spread_ref,
+    spread_sem_ref,
     even_ref,
     odd_ref,
     total_ref,
 ):
-    step = pl.program_id(0)
-
-    @pl.when(step == 0)
-    def _():
-        def store(group, part, pair, values):
-            high = values.astype(BF16)
-            low = (values - high.astype(F32)).astype(BF16)
-            modes_ref[group, place(part, pair), :] = jnp.concatenate([high, low], axis=1)
-
-        y_forward(mz, data_ref, forward_ref, rows_ref, store)
-
-    spread = spread_modes(modes_ref[step], table_ref, (even_ref, odd_ref))
-    for piece in range(C * C // SPAN):
-        modes = spread(piece)
-        for pair in range(QUAD):
-            real = imag = None
-            for tile in range(SPAN // (2 * C)):
-                inside = slice(tile * 2 * C, (tile + 1) * 2 * C)
-                columns = slice(piece * SPAN + inside.start, piece * SPAN + inside.stop)
-                mode_re = modes[place(0, pair), inside]
-                mode_im = modes[place(1, pair), inside]
-                weight_re = weight_ref[0, 0, pair, :, columns].astype(F32)
-                weight_im = weight_ref[1, 0, pair, :, columns].astype(F32)
-                term_re = mode_re * weight_re - mode_im * weight_im
-                term_im = mode_re * weight_im + mode_im * weight_re
-                real = term_re if real is None else real + term_re
-                imag = term_im if imag is None else imag + term_im
-            if piece:
-                real += total_ref[place(0, pair), :]
-                imag += total_ref[place(1, pair), :]
-            total_ref[place(0, pair), :] = real
-            total_ref[place(1, pair), :] = imag
-    total = total_ref[...]
-    sum_ref[step] = total[:, :C] + total[:, C:]
-
-    @pl.when(step == pl.num_programs(0) - 1)
-    def _():
-        y_inverse(mz, sum_ref, inverse_ref, out_ref, block_ref)
+    copies = weight_copies(weight_ref, held_ref, sem_ref)
+    table_copy = pltpu.make_async_copy(table_ref, spread_ref, spread_sem_ref)
+    table_copy.start()
+    for copy in copies:
+        copy.start()
+
+    def store(group, part, pair, values):
+        high = values.astype(BF16)
+        low = (values - high.astype(F32)).astype(BF16)
+        modes_ref[group, place(part, pair), :] = jnp.concatenate([high, low], axis=1)
+
+    y_forward(mz, data_ref, forward_ref, rows_ref, store)
+    table_copy.wait()
+    for group, copy in enumerate(copies):
+        copy.wait()
+        spread = spread_modes(modes_ref[group], spread_ref, (even_ref, odd_ref))
+        for piece in range(C * C // SPAN):
+            modes = spread(piece)
+            for pair in range(QUAD):
+                real = imag = None
+                for tile in range(SPAN // (2 * C)):
+                    inside = slice(tile * 2 * C, (tile + 1) * 2 * C)
+                    columns = slice(piece * SPAN + inside.start, piece * SPAN + inside.stop)
+                    mode_re = modes[place(0, pair), inside]
+                    mode_im = modes[place(1, pair), inside]
+                    weight_re = held_ref[group, 0, pair, :, columns].astype(F32)
+                    weight_im = held_ref[group, 1, pair, :, columns].astype(F32)
+                    term_re = mode_re * weight_re - mode_im * weight_im
+                    term_im = mode_re * weight_im + mode_im * weight_re
+                    real = term_re if real is None else real + term_re
+                    imag = term_im if imag is None else imag + term_im
+                if piece:
+                    real += total_ref[place(0, pair), :]
+                    imag += total_ref[place(1, pair), :]
+                total_ref[place(0, pair), :] = real
+                total_ref[place(1, pair), :] = imag
+        total = total_ref[...]
+        sum_ref[group] = total[:, :C] + total[:, C:]
+    y_inverse(mz, sum_ref, inverse_ref, out_ref, block_ref)
 
 
 def mix_back_kernel(
@@ -471,51 +481,60 @@
     sum_ref,
     rows_ref,
     block_ref,
+    held_ref,
+    sem_ref,
     term_ref,
 ):
-    step = pl.program_id(0)
-
-    @pl.when(step == 0)
-    def _():
-        def store(group, part, pair, values):
-            modes_ref[group, place(part, pair), :] = jnp.concatenate([values, values], axis=1)
-
-        y_forward(mz, data_ref, forward_ref, rows_ref, store)
-
-    total = []
-    for piece, tile, columns in tiles():
-        for pair in range(QUAD):
-            mode_re = modes_ref[step, place(0, pair), :]
-            mode_im = modes_ref[step, place(1, pair), :]
-            weight_re = weight_ref[0, 0, pair, :, columns].astype(F32)
-            weight_im = weight_ref[1, 0, pair, :, columns].astype(F32)
-            term_ref[place(0, pair), columns] = (
-                weight_re * mode_re + weight_im * mode_im
-            ).astype(BF16)
-            term_ref[place(1, pair), columns] = (
-                weight_re * mode_im - weight_im * mode_re
-            ).astype(BF16)
-        if columns.stop % SPAN == 0:
-            whole_piece = slice(piece * SPAN, (piece + 1) * SPAN)
+    copies = weight_copies(weight_ref, held_ref, sem_ref)
+    for copy in copies:
+        copy.start()
+
+    def store(group, part, pair, values):
+        modes_ref[group, place(part, pair), :] = jnp.concatenate([values, values], axis=1)
+
+    y_forward(mz, data_ref, forward_ref, rows_ref, store)
+    for group, copy in enumerate(copies):
+        copy.wait()
+        total = []
+        for piece in range(C * C // SPAN):
+            for pair in range(QUAD):
+                mode_re = modes_ref[group, place(0, pair), :]
+                mode_im = modes_ref[group, place(1, pair), :]
+                for tile in range(SPAN // (2 * C)):
+                    start = piece * SPAN + tile * 2 * C
+                    columns = slice(start, start + 2 * C)
+                    weight_re = held_ref[group, 0, pair, :, columns].astype(F32)
+                    weight_im = held_ref[group, 1, pair, :, columns].astype(F32)
+                    term_ref[place(0, pair), columns] = (
+                        weight_re * mode_re + weight_im * mode_im
+                    ).astype(BF16)
+                    term_ref[place(1, pair), columns] = (
+                        weight_re * mode_im - weight_im * mode_re
+                    ).astype(BF16)
             total.append(
                 lax.dot_general(
                     table_ref[...],
-                    term_ref[:, whole_piece],
+                    term_ref[:, piece * SPAN : (piece + 1) * SPAN],
                     (((1,), (1,)), ((), ())),
                     preferred_element_type=F32,
                 )
             )
-    sum_ref[step] = jnp.concatenate(total, axis=0).T
-
-    @pl.when(step == pl.num_programs(0) - 1)
-    def _():
-        y_inverse(mz, sum_ref, inverse_ref, out_ref, block_ref)
-
-
-def outer_kernel(alpha, modes_ref, back_ref, table_ref, out_ref, even_ref, odd_ref):
-    spread = spread_modes(modes_ref[0], table_ref, (even_ref, odd_ref))
-    for piece in range(C * C // SPAN):
-        modes = spread(piece)
+        sum_ref[group] = jnp.concatenate(total, axis=0).T
+    y_inverse(mz, sum_ref, inverse_ref, out_ref, block_ref)
+
+
+def outer_kernel(alpha, modes_ref, back_ref, table_ref, out_ref):
+    count = C * C // SPAN
+    made = lambda piece: jnp.dot(
+        modes_ref[0],
+        table_ref[:, piece * SPAN : (piece + 1) * SPAN],
+        preferred_element_type=F32,
+    )
+    ahead = made(0)
+    for piece in range(count):
+        modes = ahead
+        if piece + 1 < count:
+            ahead = made(piece + 1)
         for pair in range(QUAD):
             back_re = back_ref[0, place(0, pair), :] * alpha
             back_im = back_ref[0, place(1, pair), :] * alpha
@@ -556,28 +575,21 @@
     )(*args)
 
 
-def full(shape):
-    return pl.BlockSpec(shape, lambda step: (0,) * len(shape))
-
-
-def group_block(shape, start=0):
-    per = shape[2] // QUAD
-    return pl.BlockSpec(
-        (2, 1, QUAD) + shape[3:],
-        lambda step: (0, (step + start) // per, (step + start) % per, 0, 0),
-    )
-
-
-def per_mode(kernel, data, weight, tables, modes, kind, scratch=()):
-    _, mz, mx, _, _ = weight.shape
+def per_mode(kernel, data, weight, table, tables, modes, kind, scratch=()):
+    _, mz, mx, my, wide = weight.shape
     groups = mz * mx // QUAD
     rows = 2 * QUAD * MY
     modes_shape = (groups, rows, modes[0])
     return pl.pallas_call(
         functools.partial(kernel, mz),
-        grid=(groups,),
-        in_specs=[full(data.shape), group_block(weight.shape)] + [full(t.shape) for t in tables],
-        out_specs=[full(modes_shape), full(data.shape)],
+        in_specs=[
+            whole(),
+            pl.BlockSpec(memory_space=pl.ANY),
+            pl.BlockSpec(memory_space=pl.ANY) if table.size > weight.size // 16 else whole(),
+            whole(),
+            whole(),
+        ],
+        out_specs=[whole(), whole()],
         out_shape=[
             jax.ShapeDtypeStruct(modes_shape, modes[1]),
             jax.ShapeDtypeStruct(data.shape, kind),
@@ -586,31 +598,29 @@
             pltpu.VMEM((groups, rows, C), F32),
             pltpu.VMEM((tables[-1].shape[0], mz * mx * C), F32),
             pltpu.VMEM(data.shape, F32),
+            pltpu.VMEM((groups, 2, QUAD, my, wide), BF16),
+            pltpu.SemaphoreType.DMA((groups,)),
             *scratch,
         ],
-        compiler_params=params(20),
+        compiler_params=params(24),
         cost_estimate=cost(weight.size * 8, weight.size * 2),
-    )(data, in_hbm(weight), *map(in_hbm, tables))
-
-
-def outer(modes, back, table, shape, alpha, start, count, prior=None):
-    def kernel(*refs):
-        outer_kernel(alpha, *refs[:3], *refs[-3:])
-
-    group = lambda ref: pl.BlockSpec((1,) + ref.shape[1:], lambda step: (step + start, 0, 0))
-    given = () if prior is None else (prior,)
+    )(data, in_hbm(weight), in_hbm(table), *tables)
+
+
+def outer(modes, back, table, shape, alpha):
+    per = shape[2] // QUAD
+    group = lambda ref: pl.BlockSpec((1,) + ref.shape[1:], lambda step: (step, 0, 0))
     return pl.pallas_call(
-        kernel,
-        grid=(count,),
-        in_specs=[group(modes), group(back), full(table.shape)]
-        + [pl.BlockSpec(memory_space=pl.ANY)] * len(given),
-        out_specs=group_block(shape, start),
+        functools.partial(outer_kernel, alpha),
+        grid=(modes.shape[0],),
+        in_specs=[group(modes), group(back), pl.BlockSpec(table.shape, lambda step: (0, 0))],
+        out_specs=pl.BlockSpec(
+            (2, 1, QUAD) + shape[3:], lambda step: (0, step // per, step % per, 0, 0)
+        ),
         out_shape=jax.ShapeDtypeStruct(shape, F32),
-        input_output_aliases={3: 0} if given else {},
-        scratch_shapes=[pltpu.VMEM((2 * QUAD * MY, SPAN), F32)] * 2,
         compiler_params=params(20),
         cost_estimate=cost(math.prod(shape) * 4, math.prod(shape) * 4),
-    )(modes, back, in_hbm(table), *given)
+    )(modes, back, in_hbm(table))
 
 
 def shift(block, axis, step):
@@ -633,7 +643,7 @@
     return call(
         functools.partial(conv_kernel, flip),
         [((cx, c, cy * z), F32)],
-        (turned, *rim, weight),
+        (turned, *map(in_hbm, rim), in_hbm(weight)),
         [pltpu.VMEM((4 * c, (cy + 2) * z), BF16)],
         mib=32,
         flops=2 * 27 * c * c * cx * cy * z,
@@ -646,7 +656,7 @@
     return call(
         weight_grad_kernel,
         [((16 * c, 2 * c), F32)],
-        (grad, turned, *rim),
+        (grad, turned, *map(in_hbm, rim)),
         [
             pltpu.VMEM((4 * c, (cy + 2) * z), BF16),
             pltpu.VMEM((cx * 3 * c, (cy + 2) * z), BF16),
@@ -690,7 +700,7 @@
         return call(
             x_kernel,
             [((lead, rows, lanes), kind)],
-            (in_hbm(table), block),
+            (table, block),
             mib=16,
             flops=2 * table.size * lanes,
             moved=8 * block.size,
@@ -721,28 +731,29 @@
         mix_kernel,
         swap(block, "gy"),
         spectral_weight,
-        (spread, y_fwd, y_inv),
+        spread,
+        (y_fwd, y_inv),
         (2 * c, BF16),
         F32,
-        [pltpu.VMEM((2 * QUAD * MY, SPAN), F32)] * 2 + [pltpu.VMEM((2 * QUAD * MY, 2 * c), F32)],
-    )
-    block, *faces = together(block, *faces)
-    edges = y_halos(turned, *faces)
+        [pltpu.VMEM(spread.shape, BF16), pltpu.SemaphoreType.DMA]
+        + [pltpu.VMEM((2 * QUAD * MY, SPAN), F32)] * 2
+        + [pltpu.VMEM((2 * QUAD * MY, 2 * c), F32)],
+    )
+    block, *edges = together(block, *y_halos(turned, *faces))
+    rim = (*faces, *edges)
     block = x_stage(x_inv, swap(block, "gy"), nx)
-    block, *edges = together(block, *edges)
-    rim = (*faces, *edges)
     stencil = conv(turned, rim, conv_table, False)
     output, grad, slab = call(
         functools.partial(gelu_kernel, nx),
         [((c, cx, cy, z), BF16), turned_shape, slab_shape],
-        (stencil, swap(block, "gx"), cotangent, in_hbm(z_spectral), in_hbm(z_grad)),
+        (stencil, swap(block, "gx"), cotangent, z_spectral, z_grad),
         flops=2 * 192 * state.size,
         moved=state.size * 12,
     )
 
     grad_taps = weight_grad(grad, turned, rim)
     block = x_stage(x_fwd, swap(slab, "gx"), ny, BF16)
-    block, *faces = together(block, *x_halos(grad))
+    block, grad_taps, *faces = together(block, grad_taps, *x_halos(grad))
     edges = y_halos(grad, *faces)
     block, grad_taps, *edges = together(swap(block, "gy"), grad_taps, *edges)
     mine = swap(grad_taps.reshape(nx, -1, 2 * c), "gx").sum(0)
@@ -750,7 +761,8 @@
         mix_back_kernel,
         block,
         spectral_weight,
-        (gather, y_fwd, y_inv),
+        gather,
+        (y_fwd, y_inv),
         (2 * c, F32),
         BF16,
         [pltpu.VMEM((2 * QUAD * MY, c * c), BF16)],
@@ -762,21 +774,13 @@
         x_inv, swap(jnp.concatenate([block, packed], axis=1), "gy"), nx, BF16, extra
     )
     stencil_back = conv(grad, (*faces, *edges), back_table, True)
-    shape = spectral_weight.shape
-    groups = modes_in.shape[0]
-    early = groups // 2
-    grad_modes = None
-    if early:
-        grad_modes = outer(modes_in, back_modes, spread, shape, alpha, 0, early)
-        block, stencil_back, grad_modes = together(block, stencil_back, grad_modes)
+    block, stencil_back = together(block, stencil_back)
     message = swap(block, "gx")
-    grad_modes = outer(
-        modes_in, back_modes, spread, shape, alpha, early, groups - early, grad_modes
-    )
+    grad_modes = outer(modes_in, back_modes, spread, spectral_weight.shape, alpha)
     grad_state, grad_stencil, grad_point = call(
         functools.partial(finish_kernel, nx, alpha),
         [((c, cx, cy, z), F32), ((c, 27 * c), F32), ((c, c), F32)],
-        (stencil_back, message, in_hbm(z_back)),
+        (stencil_back, message, z_back),
         [pltpu.VMEM(grad_taps.shape, F32), pltpu.VMEM((27 * c, c), F32)],
         flops=2 * 96 * state.size,
         moved=state.size * 10,

time: 148 us -> 139 us (0.939)
  blocking collectives: 0 us -> 11.9 us
  waiting for transfers between devices: 29.7 us -> 21.5 us
  Pallas kernels: 52.8 us -> 46.5 us
  starting transfers between devices: 55.3 us -> 50.5 us
  local copies, waits for them, and re-layouts: 6.85 us -> 4.89 us
    all_to_all x9 -> x8, waiting for transfers between devices: 29.6 us -> 15.3 us  [swap(): return lax.all_to_all(block, axis, split_axis=0, concat_axis=0, tiled=True)]
    all_to_all x0 -> x1, blocking collectives: none -> 11.9 us  [swap(): return lax.all_to_all(block, axis, split_axis=0, concat_axis=0, tiled=True)]
    all_to_all x9 -> x8, starting transfers between devices: 37.9 us -> 31.1 us  [swap(): return lax.all_to_all(block, axis, split_axis=0, concat_axis=0, tiled=True)]
    ppermute x8, waiting for transfers between devices: 0.02 us -> 6.18 us  [shift(): return lax.ppermute(block, axis, pairs)]
    pallas_call x4 -> x3, Pallas kernels: 29.3 us -> 24.7 us  [the longest x2 15.9 us: per_mode(): pl.pallas_call(functools.partial(kernel, mz), in_specs=[whole(), pl.Block...]
    ppermute x8, starting transfers between devices: 17.4 us -> 19.4 us  [shift(): return lax.ppermute(block, axis, pairs)]
    unnamed x30 -> x46, local copies, waits for them, and re-layouts: 6.77 us -> 4.8 us
    pallas_call x11, Pallas kernels: 23.5 us -> 21.7 us  [call(): pl.pallas_call(kernel, out_shape=[jax.ShapeDtypeStruct(*out) for out in o...]
  transfers between devices with their start and end apart: 17 -> 16, of which waited for: 7 -> 7; matrix products, arithmetic and copies ran while one was open for 0% -> 0% of each run, Pallas kernels for 23% -> 28%
where the time goes in v7:
time: 139 us; the launch traced here: 137 us
  starting transfers between devices  50.5 us (36%)
  Pallas kernels  46.5 us (33%)
  waiting for transfers between devices  21.5 us (15%)
  blocking collectives  11.9 us (9%)
  local copies, waits for them, and re-layouts  4.89 us (4%)
    all_to_all x8, starting transfers between devices, swap(): return lax.all_to_all(block, axis, split_axis=0, concat_axis=0, tiled=True)  31.1 us
    pallas_call x11, Pallas kernels, call(): pl.pallas_call(kernel, out_shape=[jax.ShapeDtypeStruct(*out) for out in o...  21.7 us
    ppermute x8, starting transfers between devices, shift(): return lax.ppermute(block, axis, pairs)  19.4 us
    pallas_call x2, Pallas kernels, per_mode(): pl.pallas_call(functools.partial(kernel, mz), in_specs=[whole(), pl.Block...  15.9 us
    all_to_all x8, waiting for transfers between devices, swap(): return lax.all_to_all(block, axis, split_axis=0, concat_axis=0, tiled=True)  15.3 us
    all_to_all x1, blocking collectives, swap(): return lax.all_to_all(block, axis, split_axis=0, concat_axis=0, tiled=True)  11.9 us
    pallas_call x1, Pallas kernels, outer(): pl.pallas_call(functools.partial(outer_kernel, alpha), grid=(modes.shape[...  8.85 us
    ppermute x8, waiting for transfers between devices, shift(): return lax.ppermute(block, axis, pairs)  6.18 us
  transfers between devices with their start and end apart: 16, of which 7 were waited for; matrix products, arithmetic and copies ran while one was open for 0% of the time, Pallas kernels for 28%

profile of v7, /device:TPU:0, one launch (start us, length us, event | category | flops | bytes accessed | tf_op | source)
XLA Modules:
  0.0 137.1 jit_solution(11513696849856562213)
XLA Ops:
  0.7 2.2 %shard_map.182 = (bf16[4,8,64,128]{3,2,1,0:T(8,128)(2,1)S(1)}, f32[8,16,512]{2,1,0:T(8,128)}) custom-call(bf16[64,4,8,128]{3,2,1,0:T(8,128)(2,1)} %field_ref.1, bf16[96,128]{1,0:T(8,128)(2,1)} %constant.22.clone.table_ref), custom_call_target="tpu_custom_call" | custom-call | flops 50331648 | bytes 1310720 | tf_op jit(solution)/shard_map/pallas_call | solution.py:567
  2.9 5.2 %all-to-all-start = ((f32[8,16,512]{2,1,0:T(8,128)}), f32[8,16,512]{2,1,0:T(8,128)S(1)}, u32[]{:S(2)}, u32[]{:S(2)}) async-start(f32[8,16,512]{2,1,0:T(8,128)} %get-tuple-element.38), calls=%async_computation | async-start | bytes 524288 | tf_op jit(solution)/shard_map/all_to_all | solution.py:672
  8.1 1.3 collective-permute-start.1
  9.4 3.0 %collective-permute-start = (bf16[8,64,128]{2,1,0:T(8,128)(2,1)S(1)}, bf16[8,64,128]{2,1,0:T(8,128)(2,1)S(1)}, u32[]{:S(2)}, u32[]{:S(2)}) collective-permute-start(bf16[8,64,128]{2,1,0:T(8,128)(2,1)S(1)} %get-tuple-element.76), channel_id=1, source_target_pairs={{0,4},{4,8},{8,12},{12,16},{16,20},{20,24},{24,28},{1,5},{5,9},{9,... | collective-permute-start | bytes 393224 | tf_op jit(solution)/shard_map/ppermute | solution.py:629
  12.5 1.5 %shard_map.184 = (bf16[576,256]{1,0:T(8,128)(2,1)S(1)}, bf16[576,256]{1,0:T(8,128)(2,1)S(1)}) custom-call(bf16[64,1728]{1,0:T(8,128)(2,1)} %taps_ref.1, bf16[64,64]{1,0:T(8,128)(2,1)} %point_ref.1), custom_call_target="tpu_custom_call" | custom-call | bytes 663552 | tf_op jit(solution)/shard_map/pallas_call | solution.py:567
  16.9 4.9 %all-to-all-start.1 = ((f32[4,32,512]{2,1,0:T(8,128)}), f32[4,32,512]{2,1,0:T(8,128)S(1)}, u32[]{:S(2)}, u32[]{:S(2)}) async-start(f32[4,32,512]{2,1,0:T(8,128)} %shard_map.183), calls=%async_computation.1 | async-start | bytes 524288 | tf_op jit(solution)/shard_map/all_to_all | solution.py:672
  21.8 3.9 %collective-permute-start.2 = (bf16[6,64,128]{2,1,0:T(8,128)(2,1)S(1)}, bf16[6,64,128]{2,1,0:T(8,128)(2,1)S(1)}, u32[]{:S(2)}, u32[]{:S(2)}) collective-permute-start(bf16[6,64,128]{2,1,0:T(8,128)(2,1)S(1)} %pad_maximum_fusion.1), channel_id=1, source_target_pairs={{0,1},{1,2},{2,3},{4,5},{5,6},{6,7},{8,9},{9,10},{10,11},{12,13},{... | collective-permute-start | bytes 294920 | tf_op jit(solution)/shard_map/ppermute | solution.py:629
  25.8 1.4 %collective-permute-start.3 = (bf16[6,64,128]{2,1,0:T(8,128)(2,1)S(1)}, bf16[6,64,128]{2,1,0:T(8,128)(2,1)S(1)}, u32[]{:S(2)}, u32[]{:S(2)}) collective-permute-start(bf16[6,64,128]{2,1,0:T(8,128)(2,1)S(1)} %pad_maximum_fusion.2), channel_id=1, source_target_pairs={{1,0},{2,1},{3,2},{5,4},{6,5},{7,6},{9,8},{10,9},{11,10},{13,12},{... | collective-permute-start | bytes 294920 | tf_op jit(solution)/shard_map/ppermute | solution.py:629
  27.2 4.6 %all-to-all-done.1.data_ref = f32[4,32,512]{2,1,0:T(8,128)S(1)} async-done(((f32[4,32,512]{2,1,0:T(8,128)}), f32[4,32,512]{2,1,0:T(8,128)S(1)}, u32[]{:S(2)}, u32[]{:S(2)}) %all-to-all-start.1) | async-done | bytes 262176 | tf_op jit(solution)/shard_map/all_to_all | solution.py:672
  33.4 7.9 %shard_map.185 = (bf16[4,256,128]{2,1,0:T(8,128)(2,1)S(1)}, f32[4,32,512]{2,1,0:T(8,128)S(1)}) custom-call(f32[4,32,512]{2,1,0:T(8,128)S(1)} %all-to-all-done.1.data_ref, bf16[2,2,8,32,4096]{4,3,2,1,0:T(8,128)(2,1)} %weight_ref.3, bf16[128,4096]{1,0:T(8,128)(2,1)} %constant.30.clone.table_ref, bf16[64,192]{1,0:T(8,128)(2,1)S(1)} %copy-done.8, ...), custom_call_target="tpu_custom_call" | custom-call | flops 33554432 | bytes 8388608 | tf_op jit(solution)/shard_map/pallas_call | solution.py:583
  41.3 11.9 %all_to_all.45.data_ref = f32[4,32,512]{2,1,0:T(8,128)S(1)} all-to-all(f32[4,32,512]{2,1,0:T(8,128)S(1)} %get-tuple-element.48), channel_id=1, replica_groups=mesh['gx'=8,'gy'=4] {'gy'}, dimensions={0} | all-to-all | bytes 524288 | tf_op jit(solution)/shard_map/all_to_all | solution.py:672
  55.1 3.4 %all-to-all-start.3 = ((f32[8,16,512]{2,1,0:T(8,128)}), f32[8,16,512]{2,1,0:T(8,128)S(1)}, u32[]{:S(2)}, u32[]{:S(2)}) async-start(f32[8,16,512]{2,1,0:T(8,128)} %shard_map.187), calls=%async_computation.3 | async-start | bytes 524288 | tf_op jit(solution)/shard_map/all_to_all | solution.py:672
  58.5 3.1 %shard_map.186.stencil_ref = f32[4,64,1024]{2,1,0:T(8,128)S(1)} custom-call(bf16[4,8,64,128]{3,2,1,0:T(8,128)(2,1)S(1)} %get-tuple-element.37.body_ref, bf16[8,64,128]{2,1,0:T(8,128)(2,1)} %copy-done.18, bf16[8,64,128]{2,1,0:T(8,128)(2,1)} %copy-done.17, bf16[6,64,128]{2,1,0:T(8,128)(2,1)} %copy-done.19, bf16[6,64,128]{2,1,0:T(8,128)(2,1)} %copy-done.21, ...), custom_call_target="tpu_custom_call" | custom-call | flops 905969664 | bytes 2097152 | tf_op jit(solution)/shard_map/pallas_call | solution.py:567
  61.6 3.8 %all-to-all-done.3.slab_ref = f32[8,16,512]{2,1,0:T(8,128)S(1)} async-done(((f32[8,16,512]{2,1,0:T(8,128)}), f32[8,16,512]{2,1,0:T(8,128)S(1)}, u32[]{:S(2)}, u32[]{:S(2)}) %all-to-all-start.3) | async-done | bytes 262176 | tf_op jit(solution)/shard_map/all_to_all | solution.py:672
  65.4 2.2 %shard_map.188 = (bf16[64,4,8,128]{3,2,1,0:T(8,128)(2,1)}, bf16[4,8,64,128]{3,2,1,0:T(8,128)(2,1)S(1)}, f32[8,16,512]{2,1,0:T(8,128)S(1)}) custom-call(f32[4,64,1024]{2,1,0:T(8,128)S(1)} %shard_map.186.stencil_ref, f32[8,16,512]{2,1,0:T(8,128)S(1)} %all-to-all-done.3.slab_ref, bf16[64,4,8,128]{3,2,1,0:T(8,128)(2,1)S(1)} %copy-done, ...), custom_call_target="tpu_custom_call" | custom-call | flops 100663296 | bytes 3145728 | tf_op jit(solution)/shard_map/pallas_call | solution.py:567
  68.2 3.4 %all-to-all-start.4 = ((f32[8,16,512]{2,1,0:T(8,128)}), f32[8,16,512]{2,1,0:T(8,128)S(1)}, u32[]{:S(2)}, u32[]{:S(2)}) async-start(f32[8,16,512]{2,1,0:T(8,128)} %copy-done.5), calls=%async_computation.4 | async-start | bytes 524288 | tf_op jit(solution)/shard_map/all_to_all | solution.py:672
  71.7 1.3 collective-permute-start.5
  73.0 3.2 %collective-permute-start.4 = (bf16[8,64,128]{2,1,0:T(8,128)(2,1)S(1)}, bf16[8,64,128]{2,1,0:T(8,128)(2,1)S(1)}, u32[]{:S(2)}, u32[]{:S(2)}) collective-permute-start(bf16[8,64,128]{2,1,0:T(8,128)(2,1)S(1)} %get-tuple-element.72), channel_id=1, source_target_pairs={{0,4},{4,8},{8,12},{12,16},{16,20},{20,24},{24,28},{1,5},{5,9},{9,... | collective-permute-start | bytes 393224 | tf_op jit(solution)/shard_map/ppermute | solution.py:629
  76.2 4.1 %shard_map.190 = f32[1024,128]{1,0:T(8,128)} custom-call(bf16[4,8,64,128]{3,2,1,0:T(8,128)(2,1)S(1)} %get-tuple-element.51.grad_ref.body_ref, bf16[4,8,64,128]{3,2,1,0:T(8,128)(2,1)S(1)} %get-tuple-element.37.body_ref, bf16[8,64,128]{2,1,0:T(8,128)(2,1)} %copy-done.18, bf16[8,64,128]{2,1,0:T(8,128)(2,1)} %copy-done.17, bf16[6,64,128]{2,1,0:T(8,128)(2,1)} %copy-done.19, ...), custom_call_target="tpu_custom_call" | custom-call | flops 905969664 | bytes 2097152 | tf_op jit(solution)/shard_map/pallas_call | solution.py:567
  81.3 3.3 %all-to-all-start.5 = ((bf16[4,32,512]{2,1,0:T(8,128)(2,1)}), bf16[4,32,512]{2,1,0:T(8,128)(2,1)S(1)}, u32[]{:S(2)}, u32[]{:S(2)}) async-start(bf16[4,32,512]{2,1,0:T(8,128)(2,1)} %shard_map.189), calls=%async_computation.5 | async-start | bytes 262144 | tf_op jit(solution)/shard_map/all_to_all | solution.py:672
  84.7 3.9 %collective-permute-start.6 = (bf16[6,64,128]{2,1,0:T(8,128)(2,1)S(1)}, bf16[6,64,128]{2,1,0:T(8,128)(2,1)S(1)}, u32[]{:S(2)}, u32[]{:S(2)}) collective-permute-start(bf16[6,64,128]{2,1,0:T(8,128)(2,1)S(1)} %pad_maximum_fusion.3), channel_id=1, source_target_pairs={{0,1},{1,2},{2,3},{4,5},{5,6},{6,7},{8,9},{9,10},{10,11},{12,13},{... | collective-permute-start | bytes 294920 | tf_op jit(solution)/shard_map/ppermute | solution.py:629
  89.9 1.6 %collective-permute-done.6.ylo_ref = bf16[6,64,128]{2,1,0:T(8,128)(2,1)S(1)} collective-permute-done((bf16[6,64,128]{2,1,0:T(8,128)(2,1)S(1)}, bf16[6,64,128]{2,1,0:T(8,128)(2,1)S(1)}, u32[]{:S(2)}, u32[]{:S(2)}) %collective-permute-start.6) | collective-permute-done | bytes 98336 | tf_op jit(solution)/shard_map/ppermute | solution.py:629
  91.4 4.6 %collective-permute-done.7.yhi_ref = bf16[6,64,128]{2,1,0:T(8,128)(2,1)S(1)} collective-permute-done((bf16[6,64,128]{2,1,0:T(8,128)(2,1)S(1)}, bf16[6,64,128]{2,1,0:T(8,128)(2,1)S(1)}, u32[]{:S(2)}, u32[]{:S(2)}) %collective-permute-start.7) | collective-permute-done | bytes 98336 | tf_op jit(solution)/shard_map/ppermute | solution.py:629
  96.1 3.5 %all-to-all-start.6 = ((f32[8,128,128]{2,1,0:T(8,128)}), f32[8,128,128]{2,1,0:T(8,128)S(1)}, u32[]{:S(2)}, u32[]{:S(2)}) async-start(f32[8,128,128]{2,1,0:T(8,128)} %bitcast.8), calls=%async_computation.6 | async-start | bytes 1048576 | tf_op jit(solution)/shard_map/all_to_all | solution.py:672
  99.6 8.0 %shard_map.191 = (f32[4,256,128]{2,1,0:T(8,128)S(1)}, bf16[4,32,512]{2,1,0:T(8,128)(2,1)S(1)}) custom-call(bf16[4,32,512]{2,1,0:T(8,128)(2,1)S(1)} %all-to-all-done.5.data_ref, bf16[2,2,8,32,4096]{4,3,2,1,0:T(8,128)(2,1)} %weight_ref.3, bf16[8,512]{1,0:T(8,128)(2,1)} %constant.31.clone.table_ref, bf16[64,192]{1,0:T(8,128)(2,1)S(1)} %copy-done.9, ...), custom_call_target="tpu_custom_call" | custom-call | flops 33554432 | bytes 8388608 | tf_op jit(solution)/shard_map/pallas_call | solution.py:583
  107.6 1.6 %all-to-all-done.6 = f32[8,128,128]{2,1,0:T(8,128)S(1)} async-done(((f32[8,128,128]{2,1,0:T(8,128)}), f32[8,128,128]{2,1,0:T(8,128)S(1)}, u32[]{:S(2)}, u32[]{:S(2)}) %all-to-all-start.6) | async-done | bytes 524320 | tf_op jit(solution)/shard_map/all_to_all | solution.py:672
  110.0 3.6 %all-to-all-start.7 = ((bf16[4,64,512]{2,1,0:T(8,128)(2,1)}), bf16[4,64,512]{2,1,0:T(8,128)(2,1)S(1)}, u32[]{:S(2)}, u32[]{:S(2)}) async-start(bf16[4,64,512]{2,1,0:T(8,128)(2,1)} %pad_maximum_fusion), calls=%async_computation.7 | async-start | bytes 524288 | tf_op jit(solution)/shard_map/all_to_all | solution.py:672
  113.7 3.0 %shard_map.193.stencil_ref = f32[4,64,1024]{2,1,0:T(8,128)S(1)} custom-call(bf16[4,8,64,128]{3,2,1,0:T(8,128)(2,1)S(1)} %get-tuple-element.51.grad_ref.body_ref, bf16[8,64,128]{2,1,0:T(8,128)(2,1)} %copy-done.16, bf16[8,64,128]{2,1,0:T(8,128)(2,1)} %copy-done.15, bf16[6,64,128]{2,1,0:T(8,128)(2,1)} %copy-done.20, bf16[6,64,128]{2,1,0:T(8,128)(2,1)} %copy-done.22, ...), custom_call_target="tpu_custom_call" | custom-call | flops 905969664 | bytes 2097152 | tf_op jit(solution)/shard_map/pallas_call | solution.py:567
  116.8 5.0 %all-to-all-done.7.data_ref = bf16[4,64,512]{2,1,0:T(8,128)(2,1)S(1)} async-done(((bf16[4,64,512]{2,1,0:T(8,128)(2,1)}), bf16[4,64,512]{2,1,0:T(8,128)(2,1)S(1)}, u32[]{:S(2)}, u32[]{:S(2)}) %all-to-all-start.7) | async-done | bytes 262176 | tf_op jit(solution)/shard_map/all_to_all | solution.py:672
  122.7 3.7 %all-to-all-start.8 = ((bf16[8,48,512]{2,1,0:T(8,128)(2,1)}), bf16[8,48,512]{2,1,0:T(8,128)(2,1)S(1)}, u32[]{:S(2)}, u32[]{:S(2)}) async-start(bf16[8,48,512]{2,1,0:T(8,128)(2,1)} %shard_map.192), calls=%async_computation.8 | async-start | bytes 786432 | tf_op jit(solution)/shard_map/all_to_all | solution.py:672
  126.4 8.9 %shard_map.195 = f32[2,2,8,32,4096]{4,3,2,1,0:T(8,128)} custom-call(bf16[4,256,128]{2,1,0:T(8,128)(2,1)S(1)} %get-tuple-element.65.modes_ref, f32[4,256,128]{2,1,0:T(8,128)S(1)} %get-tuple-element.66.back_ref, bf16[128,4096]{1,0:T(8,128)(2,1)} %constant.30.clone.table_ref), custom_call_target="tpu_custom_call" | custom-call | flops 16777216 | bytes 16777216 | tf_op jit(solution)/shard_map/pallas_call | solution.py:613
  135.3 1.8 %shard_map.194 = (f32[64,4,8,128]{3,2,1,0:T(8,128)}, f32[64,1728]{1,0:T(8,128)}, f32[64,64]{1,0:T(8,128)}) custom-call(f32[4,64,1024]{2,1,0:T(8,128)S(1)} %shard_map.193.stencil_ref, bf16[8,48,512]{2,1,0:T(8,128)(2,1)S(1)} %all-to-all-done.8.message_ref, bf16[96,128]{1,0:T(8,128)(2,1)S(1)} %copy-done.12), custom_call_target="tpu_custom_call" | custom-call | flops 50331648 | bytes 2621440 | tf_op jit(solution)/shard_map/pallas_call | solution.py:567
  (77 shorter events, 11.1 us)
Async XLA Ops:
  0.6 79.7 %copy-start.4 = (bf16[128,384]{1,0:T(8,128)(2,1)S(1)}, bf16[128,384]{1,0:T(8,128)(2,1)}, u32[]{:S(2)}) copy-start(bf16[128,384]{1,0:T(8,128)(2,1)} %constant.26.clone.table_ref) | copy-start | bytes 294916
  0.6 98.9 %copy-start.7 = (bf16[64,192]{1,0:T(8,128)(2,1)S(1)}, bf16[64,192]{1,0:T(8,128)(2,1)}, u32[]{:S(2)}) copy-start(bf16[64,192]{1,0:T(8,128)(2,1)} %constant.29.clone.inverse_ref) | copy-start | bytes 73732
  0.7 98.9 %copy-start.9 = (bf16[64,192]{1,0:T(8,128)(2,1)S(1)}, bf16[64,192]{1,0:T(8,128)(2,1)}, u32[]{:S(2)}) copy-start(bf16[64,192]{1,0:T(8,128)(2,1)} %constant.28.clone.forward_ref) | copy-start | bytes 73732
  0.7 64.7 %copy-start.10 = (bf16[96,128]{1,0:T(8,128)(2,1)S(1)}, bf16[96,128]{1,0:T(8,128)(2,1)}, u32[]{:S(2)}) copy-start(bf16[96,128]{1,0:T(8,128)(2,1)} %constant.24.clone.inverse_ref) | copy-start | bytes 73732
  0.7 64.7 %copy-start.11 = (bf16[96,128]{1,0:T(8,128)(2,1)S(1)}, bf16[96,128]{1,0:T(8,128)(2,1)}, u32[]{:S(2)}) copy-start(bf16[96,128]{1,0:T(8,128)(2,1)} %constant.23.clone.forward_ref) | copy-start | bytes 73732
  0.7 64.7 %copy-start = (bf16[64,4,8,128]{3,2,1,0:T(8,128)(2,1)S(1)}, bf16[64,4,8,128]{3,2,1,0:T(8,128)(2,1)}, u32[]{:S(2)}) copy-start(bf16[64,4,8,128]{3,2,1,0:T(8,128)(2,1)} %cot_ref.1) | copy-start | bytes 1572868
  2.9 12.1 %all-to-all-start = ((f32[8,16,512]{2,1,0:T(8,128)}), f32[8,16,512]{2,1,0:T(8,128)S(1)}, u32[]{:S(2)}, u32[]{:S(2)}) async-start(f32[8,16,512]{2,1,0:T(8,128)} %get-tuple-element.38), calls=%async_computation | async-start | bytes 524288 | tf_op jit(solution)/shard_map/all_to_all | solution.py:672
  8.1 8.7 %collective-permute-start.1 = (bf16[8,64,128]{2,1,0:T(8,128)(2,1)S(1)}, bf16[8,64,128]{2,1,0:T(8,128)(2,1)S(1)}, u32[]{:S(2)}, u32[]{:S(2)}) collective-permute-start(bf16[8,64,128]{2,1,0:T(8,128)(2,1)S(1)} %get-tuple-element.75), channel_id=1, source_target_pairs={{4,0},{8,4},{12,8},{16,12},{20,16},{24,20},{28,24},{5,1},{9,5},{13... | collective-permute-start | bytes 393224 | tf_op jit(solution)/shard_map/ppermute | solution.py:629
  9.4 7.5 %collective-permute-start = (bf16[8,64,128]{2,1,0:T(8,128)(2,1)S(1)}, bf16[8,64,128]{2,1,0:T(8,128)(2,1)S(1)}, u32[]{:S(2)}, u32[]{:S(2)}) collective-permute-start(bf16[8,64,128]{2,1,0:T(8,128)(2,1)S(1)} %get-tuple-element.76), channel_id=1, source_target_pairs={{0,4},{4,8},{8,12},{12,16},{16,20},{20,24},{24,28},{1,5},{5,9},{9,... | collective-permute-start | bytes 393224 | tf_op jit(solution)/shard_map/ppermute | solution.py:629
  14.8 40.3 %copy-start.13 = (bf16[576,256]{1,0:T(8,128)(2,1)}, bf16[576,256]{1,0:T(8,128)(2,1)S(1)}, u32[]{:S(2)}) copy-start(bf16[576,256]{1,0:T(8,128)(2,1)S(1)} %get-tuple-element.61.weight_ref) | copy-start | bytes 884740
  16.9 38.2 %copy-start.18 = (bf16[8,64,128]{2,1,0:T(8,128)(2,1)}, bf16[8,64,128]{2,1,0:T(8,128)(2,1)S(1)}, u32[]{:S(2)}) copy-start(bf16[8,64,128]{2,1,0:T(8,128)(2,1)S(1)} %collective-permute-done.xlo_ref) | copy-start | bytes 393220
  16.9 15.0 %all-to-all-start.1 = ((f32[4,32,512]{2,1,0:T(8,128)}), f32[4,32,512]{2,1,0:T(8,128)S(1)}, u32[]{:S(2)}, u32[]{:S(2)}) async-start(f32[4,32,512]{2,1,0:T(8,128)} %shard_map.183), calls=%async_computation.1 | async-start | bytes 524288 | tf_op jit(solution)/shard_map/all_to_all | solution.py:672
  21.8 19.5 %collective-permute-start.2 = (bf16[6,64,128]{2,1,0:T(8,128)(2,1)S(1)}, bf16[6,64,128]{2,1,0:T(8,128)(2,1)S(1)}, u32[]{:S(2)}, u32[]{:S(2)}) collective-permute-start(bf16[6,64,128]{2,1,0:T(8,128)(2,1)S(1)} %pad_maximum_fusion.1), channel_id=1, source_target_pairs={{0,1},{1,2},{2,3},{4,5},{5,6},{6,7},{8,9},{9,10},{10,11},{12,13},{... | collective-permute-start | bytes 294920 | tf_op jit(solution)/shard_map/ppermute | solution.py:629
  25.8 95.9 %copy-start.2 = (bf16[128,384]{1,0:T(8,128)(2,1)S(1)}, bf16[128,384]{1,0:T(8,128)(2,1)}, u32[]{:S(2)}) copy-start(bf16[128,384]{1,0:T(8,128)(2,1)} %constant.27.clone.table_ref) | copy-start | bytes 294916
  25.8 15.5 %collective-permute-start.3 = (bf16[6,64,128]{2,1,0:T(8,128)(2,1)S(1)}, bf16[6,64,128]{2,1,0:T(8,128)(2,1)S(1)}, u32[]{:S(2)}, u32[]{:S(2)}) collective-permute-start(bf16[6,64,128]{2,1,0:T(8,128)(2,1)S(1)} %pad_maximum_fusion.2), channel_id=1, source_target_pairs={{1,0},{2,1},{3,2},{5,4},{6,5},{7,6},{9,8},{10,9},{11,10},{13,12},{... | collective-permute-start | bytes 294920 | tf_op jit(solution)/shard_map/ppermute | solution.py:629
  41.3 17.2 %copy-start.19 = (bf16[6,64,128]{2,1,0:T(8,128)(2,1)}, bf16[6,64,128]{2,1,0:T(8,128)(2,1)S(1)}, u32[]{:S(2)}) copy-start(bf16[6,64,128]{2,1,0:T(8,128)(2,1)S(1)} %collective-permute-done.2.ylo_ref) | copy-start | bytes 294916
  41.3 13.7 %copy-start.21 = (bf16[6,64,128]{2,1,0:T(8,128)(2,1)}, bf16[6,64,128]{2,1,0:T(8,128)(2,1)S(1)}, u32[]{:S(2)}) copy-start(bf16[6,64,128]{2,1,0:T(8,128)(2,1)S(1)} %collective-permute-done.3.yhi_ref) | copy-start | bytes 294916
  55.1 10.3 %all-to-all-start.3 = ((f32[8,16,512]{2,1,0:T(8,128)}), f32[8,16,512]{2,1,0:T(8,128)S(1)}, u32[]{:S(2)}, u32[]{:S(2)}) async-start(f32[8,16,512]{2,1,0:T(8,128)} %shard_map.187), calls=%async_computation.3 | async-start | bytes 524288 | tf_op jit(solution)/shard_map/all_to_all | solution.py:672
  68.2 12.1 %all-to-all-start.4 = ((f32[8,16,512]{2,1,0:T(8,128)}), f32[8,16,512]{2,1,0:T(8,128)S(1)}, u32[]{:S(2)}, u32[]{:S(2)}) async-start(f32[8,16,512]{2,1,0:T(8,128)} %copy-done.5), calls=%async_computation.4 | async-start | bytes 524288 | tf_op jit(solution)/shard_map/all_to_all | solution.py:672
  71.7 9.6 %collective-permute-start.5 = (bf16[8,64,128]{2,1,0:T(8,128)(2,1)S(1)}, bf16[8,64,128]{2,1,0:T(8,128)(2,1)S(1)}, u32[]{:S(2)}, u32[]{:S(2)}) collective-permute-start(bf16[8,64,128]{2,1,0:T(8,128)(2,1)S(1)} %get-tuple-element.71), channel_id=1, source_target_pairs={{4,0},{8,4},{12,8},{16,12},{20,16},{24,20},{28,24},{5,1},{9,5},{13... | collective-permute-start | bytes 393224 | tf_op jit(solution)/shard_map/ppermute | solution.py:629
  73.0 8.3 %collective-permute-start.4 = (bf16[8,64,128]{2,1,0:T(8,128)(2,1)S(1)}, bf16[8,64,128]{2,1,0:T(8,128)(2,1)S(1)}, u32[]{:S(2)}, u32[]{:S(2)}) collective-permute-start(bf16[8,64,128]{2,1,0:T(8,128)(2,1)S(1)} %get-tuple-element.72), channel_id=1, source_target_pairs={{0,4},{4,8},{8,12},{12,16},{16,20},{20,24},{24,28},{1,5},{5,9},{9,... | collective-permute-start | bytes 393224 | tf_op jit(solution)/shard_map/ppermute | solution.py:629
  81.3 32.4 %copy-start.15 = (bf16[8,64,128]{2,1,0:T(8,128)(2,1)}, bf16[8,64,128]{2,1,0:T(8,128)(2,1)S(1)}, u32[]{:S(2)}) copy-start(bf16[8,64,128]{2,1,0:T(8,128)(2,1)S(1)} %collective-permute-done.5.xhi_ref) | copy-start | bytes 393220
  81.3 32.4 %copy-start.16 = (bf16[8,64,128]{2,1,0:T(8,128)(2,1)}, bf16[8,64,128]{2,1,0:T(8,128)(2,1)S(1)}, u32[]{:S(2)}) copy-start(bf16[8,64,128]{2,1,0:T(8,128)(2,1)S(1)} %collective-permute-done.4.xlo_ref) | copy-start | bytes 393220
  81.3 14.8 %all-to-all-start.5 = ((bf16[4,32,512]{2,1,0:T(8,128)(2,1)}), bf16[4,32,512]{2,1,0:T(8,128)(2,1)S(1)}, u32[]{:S(2)}, u32[]{:S(2)}) async-start(bf16[4,32,512]{2,1,0:T(8,128)(2,1)} %shard_map.189), calls=%async_computation.5 | async-start | bytes 262144 | tf_op jit(solution)/shard_map/all_to_all | solution.py:672
  84.7 6.8 %collective-permute-start.6 = (bf16[6,64,128]{2,1,0:T(8,128)(2,1)S(1)}, bf16[6,64,128]{2,1,0:T(8,128)(2,1)S(1)}, u32[]{:S(2)}, u32[]{:S(2)}) collective-permute-start(bf16[6,64,128]{2,1,0:T(8,128)(2,1)S(1)} %pad_maximum_fusion.3), channel_id=1, source_target_pairs={{0,1},{1,2},{2,3},{4,5},{5,6},{6,7},{8,9},{9,10},{10,11},{12,13},{... | collective-permute-start | bytes 294920 | tf_op jit(solution)/shard_map/ppermute | solution.py:629
  88.6 7.5 %collective-permute-start.7 = (bf16[6,64,128]{2,1,0:T(8,128)(2,1)S(1)}, bf16[6,64,128]{2,1,0:T(8,128)(2,1)S(1)}, u32[]{:S(2)}, u32[]{:S(2)}) collective-permute-start(bf16[6,64,128]{2,1,0:T(8,128)(2,1)S(1)} %pad_maximum_fusion.4), channel_id=1, source_target_pairs={{1,0},{2,1},{3,2},{5,4},{6,5},{7,6},{9,8},{10,9},{11,10},{13,12},{... | collective-permute-start | bytes 294920 | tf_op jit(solution)/shard_map/ppermute | solution.py:629
  91.4 22.2 %copy-start.20 = (bf16[6,64,128]{2,1,0:T(8,128)(2,1)}, bf16[6,64,128]{2,1,0:T(8,128)(2,1)S(1)}, u32[]{:S(2)}) copy-start(bf16[6,64,128]{2,1,0:T(8,128)(2,1)S(1)} %collective-permute-done.6.ylo_ref) | copy-start | bytes 294916
  96.1 17.6 %copy-start.22 = (bf16[6,64,128]{2,1,0:T(8,128)(2,1)}, bf16[6,64,128]{2,1,0:T(8,128)(2,1)S(1)}, u32[]{:S(2)}) copy-start(bf16[6,64,128]{2,1,0:T(8,128)(2,1)S(1)} %collective-permute-done.7.yhi_ref) | copy-start | bytes 294916
  96.1 13.2 %all-to-all-start.6 = ((f32[8,128,128]{2,1,0:T(8,128)}), f32[8,128,128]{2,1,0:T(8,128)S(1)}, u32[]{:S(2)}, u32[]{:S(2)}) async-start(f32[8,128,128]{2,1,0:T(8,128)} %bitcast.8), calls=%async_computation.6 | async-start | bytes 1048576 | tf_op jit(solution)/shard_map/all_to_all | solution.py:672
  99.6 35.7 %copy-start.12 = (bf16[96,128]{1,0:T(8,128)(2,1)S(1)}, bf16[96,128]{1,0:T(8,128)(2,1)}, u32[]{:S(2)}) copy-start(bf16[96,128]{1,0:T(8,128)(2,1)} %constant.25.clone.inverse_ref) | copy-start | bytes 73732
  110.0 11.7 %all-to-all-start.7 = ((bf16[4,64,512]{2,1,0:T(8,128)(2,1)}), bf16[4,64,512]{2,1,0:T(8,128)(2,1)S(1)}, u32[]{:S(2)}, u32[]{:S(2)}) async-start(bf16[4,64,512]{2,1,0:T(8,128)(2,1)} %pad_maximum_fusion), calls=%async_computation.7 | async-start | bytes 524288 | tf_op jit(solution)/shard_map/all_to_all | solution.py:672
  122.7 12.6 %all-to-all-start.8 = ((bf16[8,48,512]{2,1,0:T(8,128)(2,1)}), bf16[8,48,512]{2,1,0:T(8,128)(2,1)S(1)}, u32[]{:S(2)}, u32[]{:S(2)}) async-start(bf16[8,48,512]{2,1,0:T(8,128)(2,1)} %shard_map.192), calls=%async_computation.8 | async-start | bytes 786432 | tf_op jit(solution)/shard_map/all_to_all | solution.py:672
  (7 other events, 13.6 us)

commit v8 on v7

--- a/solution.py
+++ b/solution.py
@@ -82,11 +82,13 @@
     return against_pieces(forward.reshape(size_k, size_x), inverse.reshape(size_x, size_k))
 
 
-def y_tables(wide):
+def y_table(wide):
     theta = angles(centred(MY), np.arange(wide), wide)
     forward = rotation(theta, -1.0).reshape(2 * MY, 2 * wide)
     inverse = rotation(theta.T, 1.0).reshape(2 * wide, 2 * MY)
-    return against_pieces(forward, inverse)
+    forward, inverse = against_pieces(forward, inverse)
+    inverse = np.pad(inverse, ((0, 0), (0, forward.shape[1] - inverse.shape[1])))
+    return np.concatenate([forward, inverse], axis=0)
 
 
 def pieces(values):
@@ -179,10 +181,31 @@
 
 
 def weight_grad_kernel(
-    grad_ref, body_ref, xlo_ref, xhi_ref, ylo_ref, yhi_ref, out_ref, rim_ref, wide_ref, sum_ref
+    grad_ref,
+    body_ref,
+    xlo_any,
+    xhi_any,
+    ylo_any,
+    yhi_any,
+    out_ref,
+    rim_ref,
+    wide_ref,
+    sum_ref,
+    xlo_ref,
+    xhi_ref,
+    ylo_ref,
+    yhi_ref,
+    sem_ref,
 ):
     cx, cy, c, z = body_ref.shape
     group = 3 * c
+    held = (xlo_ref, xhi_ref, ylo_ref, yhi_ref)
+    copies = [
+        pltpu.make_async_copy(given, ref, sem_ref.at[i])
+        for i, (given, ref) in enumerate(zip((xlo_any, xhi_any, ylo_any, yhi_any), held))
+    ]
+    for copy in copies:
+        copy.start()
     wide_ref[...] = jnp.zeros_like(wide_ref)
     for x in range(cx):
         for b in range(3):
@@ -190,6 +213,8 @@
                 row = x * group + b * c
                 wide_ref[row : row + c, (y + b) * z : (y + b + 1) * z] = grad_ref[x, y]
     sum_ref[...] = jnp.zeros_like(sum_ref)
+    for copy in copies:
+        copy.wait()
     for p in range(cx + 2):
         fill_shifts(plane_rows(p, cx, body_ref, xlo_ref, xhi_ref, ylo_ref, yhi_ref), rim_ref)
         first, last = max(0, p - 2), min(cx - 1, p)
@@ -328,7 +353,7 @@
                 for kx in range(mx):
                     column = (kz * mx + kx) * C
                     rows_ref[row : row + cy, column : column + C] = block[kx]
-    got = jnp.dot(table_ref[...], pieces(rows_ref[...]), preferred_element_type=F32)
+    got = jnp.dot(table_ref[: 2 * MY], pieces(rows_ref[...]), preferred_element_type=F32)
     for q in range(count):
         block = got[:, q * C : (q + 1) * C]
         for part in range(2):
@@ -348,7 +373,9 @@
         for part in range(2)
     ]
     got = jnp.dot(
-        table_ref[...], pieces(jnp.concatenate(rows, axis=0)), preferred_element_type=F32
+        table_ref[2 * MY :, : 6 * MY],
+        pieces(jnp.concatenate(rows, axis=0)),
+        preferred_element_type=F32,
     )
     ny, _, lanes = out_ref.shape
     cy = lanes // C
@@ -413,8 +440,7 @@
     data_ref,
     weight_ref,
     table_ref,
-    forward_ref,
-    inverse_ref,
+    turn_ref,
     modes_ref,
     out_ref,
     sum_ref,
@@ -439,7 +465,7 @@
         low = (values - high.astype(F32)).astype(BF16)
         modes_ref[group, place(part, pair), :] = jnp.concatenate([high, low], axis=1)
 
-    y_forward(mz, data_ref, forward_ref, rows_ref, store)
+    y_forward(mz, data_ref, turn_ref, rows_ref, store)
     table_copy.wait()
     for group, copy in enumerate(copies):
         copy.wait()
@@ -466,7 +492,7 @@
                 total_ref[place(1, pair), :] = imag
         total = total_ref[...]
         sum_ref[group] = total[:, :C] + total[:, C:]
-    y_inverse(mz, sum_ref, inverse_ref, out_ref, block_ref)
+    y_inverse(mz, sum_ref, turn_ref, out_ref, block_ref)
 
 
 def mix_back_kernel(
@@ -474,8 +500,7 @@
     data_ref,
     weight_ref,
     table_ref,
-    forward_ref,
-    inverse_ref,
+    turn_ref,
     modes_ref,
     out_ref,
     sum_ref,
@@ -492,7 +517,7 @@
     def store(group, part, pair, values):
         modes_ref[group, place(part, pair), :] = jnp.concatenate([values, values], axis=1)
 
-    y_forward(mz, data_ref, forward_ref, rows_ref, store)
+    y_forward(mz, data_ref, turn_ref, rows_ref, store)
     for group, copy in enumerate(copies):
         copy.wait()
         total = []
@@ -520,7 +545,7 @@
                 )
             )
         sum_ref[group] = jnp.concatenate(total, axis=0).T
-    y_inverse(mz, sum_ref, inverse_ref, out_ref, block_ref)
+    y_inverse(mz, sum_ref, turn_ref, out_ref, block_ref)
 
 
 def outer_kernel(alpha, modes_ref, back_ref, table_ref, out_ref):
@@ -563,11 +588,14 @@
     return pl.CostEstimate(flops=int(flops), bytes_accessed=int(moved), transcendentals=0)
 
 
-def call(kernel, outs, args, scratch=(), mib=24, flops=0, moved=0):
+def call(kernel, outs, args, scratch=(), mib=24, flops=0, moved=0, anywhere=()):
     return pl.pallas_call(
         kernel,
         out_shape=[jax.ShapeDtypeStruct(*out) for out in outs],
-        in_specs=[whole() for _ in args],
+        in_specs=[
+            pl.BlockSpec(memory_space=pl.ANY) if i in anywhere else whole()
+            for i in range(len(args))
+        ],
         out_specs=[whole() for _ in outs],
         scratch_shapes=list(scratch),
         compiler_params=params(mib),
@@ -575,7 +603,7 @@
     )(*args)
 
 
-def per_mode(kernel, data, weight, table, tables, modes, kind, scratch=()):
+def per_mode(kernel, data, weight, table, turn, modes, kind, scratch=()):
     _, mz, mx, my, wide = weight.shape
     groups = mz * mx // QUAD
     rows = 2 * QUAD * MY
@@ -585,8 +613,7 @@
         in_specs=[
             whole(),
             pl.BlockSpec(memory_space=pl.ANY),
-            pl.BlockSpec(memory_space=pl.ANY) if table.size > weight.size // 16 else whole(),
-            whole(),
+            pl.BlockSpec(memory_space=pl.ANY) if kernel is mix_kernel else whole(),
             whole(),
         ],
         out_specs=[whole(), whole()],
@@ -596,7 +623,7 @@
         ],
         scratch_shapes=[
             pltpu.VMEM((groups, rows, C), F32),
-            pltpu.VMEM((tables[-1].shape[0], mz * mx * C), F32),
+            pltpu.VMEM((turn.shape[0] - 2 * MY, mz * mx * C), F32),
             pltpu.VMEM(data.shape, F32),
             pltpu.VMEM((groups, 2, QUAD, my, wide), BF16),
             pltpu.SemaphoreType.DMA((groups,)),
@@ -604,7 +631,7 @@
         ],
         compiler_params=params(24),
         cost_estimate=cost(weight.size * 8, weight.size * 2),
-    )(data, in_hbm(weight), in_hbm(table), *tables)
+    )(data, in_hbm(weight), in_hbm(table), turn)
 
 
 def outer(modes, back, table, shape, alpha):
@@ -620,7 +647,7 @@
         out_shape=jax.ShapeDtypeStruct(shape, F32),
         compiler_params=params(20),
         cost_estimate=cost(math.prod(shape) * 4, math.prod(shape) * 4),
-    )(modes, back, in_hbm(table))
+    )(modes, back, table)
 
 
 def shift(block, axis, step):
@@ -661,7 +688,10 @@
             pltpu.VMEM((4 * c, (cy + 2) * z), BF16),
             pltpu.VMEM((cx * 3 * c, (cy + 2) * z), BF16),
             pltpu.VMEM((9 * c, 4 * c), F32),
+            *(pltpu.VMEM(halo.shape, BF16) for halo in rim),
+            pltpu.SemaphoreType.DMA((len(rim),)),
         ],
+        anywhere=(2, 3, 4, 5),
         mib=32,
         flops=2 * 27 * c * c * cx * cy * z,
         moved=turned.size * 8,
@@ -690,7 +720,7 @@
     z_spectral = jnp.asarray(z_inverse_table(nx, mz, beta * double))
     z_back = jnp.asarray(z_inverse_table(nx, mz, alpha * beta * ones))
     x_fwd, x_inv = (jnp.asarray(t) for t in x_tables(wide_x, mz, mx))
-    y_fwd, y_inv = (jnp.asarray(t) for t in y_tables(wide_y))
+    y_turn = jnp.asarray(y_table(wide_y))
     spread, gather = jnp.asarray(spread_table()), jnp.asarray(gather_table())
     lanes = cy * c
     x_rows = cx * 2 * mz
@@ -732,7 +762,7 @@
         swap(block, "gy"),
         spectral_weight,
         spread,
-        (y_fwd, y_inv),
+        y_turn,
         (2 * c, BF16),
         F32,
         [pltpu.VMEM(spread.shape, BF16), pltpu.SemaphoreType.DMA]
@@ -755,14 +785,15 @@
     block = x_stage(x_fwd, swap(slab, "gx"), ny, BF16)
     block, grad_taps, *faces = together(block, grad_taps, *x_halos(grad))
     edges = y_halos(grad, *faces)
-    block, grad_taps, *edges = together(swap(block, "gy"), grad_taps, *edges)
+    block, grad_taps, ylo = together(swap(block, "gy"), grad_taps, edges[0])
+    edges = (ylo, edges[1])
     mine = swap(grad_taps.reshape(nx, -1, 2 * c), "gx").sum(0)
     back_modes, block = per_mode(
         mix_back_kernel,
         block,
         spectral_weight,
         gather,
-        (y_fwd, y_inv),
+        y_turn,
         (2 * c, F32),
         BF16,
         [pltpu.VMEM((2 * QUAD * MY, c * c), BF16)],

time: 139 us -> 144 us (1.036)
  local copies, waits for them, and re-layouts: 4.89 us -> 11.6 us
  waiting for transfers between devices: 21.5 us -> 19.7 us
  starting transfers between devices: 50.5 us -> 52.3 us
    all_to_all x8, waiting for transfers between devices: 15.3 us -> 10 us  [swap(): return lax.all_to_all(block, axis, split_axis=0, concat_axis=0, tiled=True)]
    unnamed x46 -> x56, local copies, waits for them, and re-layouts: 4.8 us -> 9.71 us
    ppermute x8, waiting for transfers between devices: 6.18 us -> 9.7 us  [shift(): return lax.ppermute(block, axis, pairs)]
    all_to_all x8, starting transfers between devices: 31.1 us -> 32.9 us  [swap(): return lax.all_to_all(block, axis, split_axis=0, concat_axis=0, tiled=True)]
  transfers between devices with their start and end apart: 16 -> 16, of which waited for: 7 -> 7; matrix products, arithmetic and copies ran while one was open for 0% -> 1% of each run, Pallas kernels for 28% -> 26%
where the time goes in v8:
time: 144 us; the launch traced here: 143 us
  starting transfers between devices  52.3 us (36%)
  Pallas kernels  45.1 us (31%)
  waiting for transfers between devices  19.7 us (14%)
  blocking collectives  12 us (8%)
  local copies, waits for them, and re-layouts  11.6 us (8%)
    all_to_all x8, starting transfers between devices, swap(): return lax.all_to_all(block, axis, split_axis=0, concat_axis=0, tiled=True)  32.9 us
    pallas_call x11, Pallas kernels, call(): pl.pallas_call(kernel, out_shape=[jax.ShapeDtypeStruct(*out) for out in o...  21.6 us
    ppermute x8, starting transfers between devices, shift(): return lax.ppermute(block, axis, pairs)  19.4 us
    pallas_call x2, Pallas kernels, per_mode(): pl.pallas_call(functools.partial(kernel, mz), in_specs=[whole(), pl.Block...  15.9 us
    all_to_all x1, blocking collectives, swap(): return lax.all_to_all(block, axis, split_axis=0, concat_axis=0, tiled=True)  12 us
    all_to_all x8, waiting for transfers between devices, swap(): return lax.all_to_all(block, axis, split_axis=0, concat_axis=0, tiled=True)  10 us
    unnamed x56, local copies, waits for them, and re-layouts  9.71 us
    ppermute x8, waiting for transfers between devices, shift(): return lax.ppermute(block, axis, pairs)  9.7 us
  transfers between devices with their start and end apart: 16, of which 7 were waited for; matrix products, arithmetic and copies ran while one was open for 1% of the time, Pallas kernels for 26%

profile of v8, /device:TPU:0, one launch (start us, length us, event | category | flops | bytes accessed | tf_op | source)
XLA Modules:
  0.0 142.7 jit_solution(646775885488209395)
XLA Ops:
  0.7 2.2 %shard_map.173 = (bf16[4,8,64,128]{3,2,1,0:T(8,128)(2,1)S(1)}, f32[8,16,512]{2,1,0:T(8,128)}) custom-call(bf16[64,4,8,128]{3,2,1,0:T(8,128)(2,1)} %field_ref.1, bf16[96,128]{1,0:T(8,128)(2,1)} %constant.20.clone.table_ref), custom_call_target="tpu_custom_call" | custom-call | flops 50331648 | bytes 1310720 | tf_op jit(solution)/shard_map/pallas_call | solution.py:592
  2.9 5.2 %all-to-all-start = ((f32[8,16,512]{2,1,0:T(8,128)}), f32[8,16,512]{2,1,0:T(8,128)S(1)}, u32[]{:S(2)}, u32[]{:S(2)}) async-start(f32[8,16,512]{2,1,0:T(8,128)} %get-tuple-element.37), calls=%async_computation | async-start | bytes 524288 | tf_op jit(solution)/shard_map/all_to_all | solution.py:702
  8.1 1.3 collective-permute-start.1
  9.4 3.0 %collective-permute-start = (bf16[8,64,128]{2,1,0:T(8,128)(2,1)S(1)}, bf16[8,64,128]{2,1,0:T(8,128)(2,1)S(1)}, u32[]{:S(2)}, u32[]{:S(2)}) collective-permute-start(bf16[8,64,128]{2,1,0:T(8,128)(2,1)S(1)} %get-tuple-element.74), channel_id=1, source_target_pairs={{0,4},{4,8},{8,12},{12,16},{16,20},{20,24},{24,28},{1,5},{5,9},{9,... | collective-permute-start | bytes 393224 | tf_op jit(solution)/shard_map/ppermute | solution.py:656
  12.5 1.5 %shard_map.175 = (bf16[576,256]{1,0:T(8,128)(2,1)S(1)}, bf16[576,256]{1,0:T(8,128)(2,1)S(1)}) custom-call(bf16[64,1728]{1,0:T(8,128)(2,1)} %taps_ref.1, bf16[64,64]{1,0:T(8,128)(2,1)} %point_ref.1), custom_call_target="tpu_custom_call" | custom-call | bytes 663552 | tf_op jit(solution)/shard_map/pallas_call | solution.py:592
  16.9 4.9 %all-to-all-start.1 = ((f32[4,32,512]{2,1,0:T(8,128)}), f32[4,32,512]{2,1,0:T(8,128)S(1)}, u32[]{:S(2)}, u32[]{:S(2)}) async-start(f32[4,32,512]{2,1,0:T(8,128)} %shard_map.174), calls=%async_computation.1 | async-start | bytes 524288 | tf_op jit(solution)/shard_map/all_to_all | solution.py:702
  21.8 3.9 %collective-permute-start.2 = (bf16[6,64,128]{2,1,0:T(8,128)(2,1)S(1)}, bf16[6,64,128]{2,1,0:T(8,128)(2,1)S(1)}, u32[]{:S(2)}, u32[]{:S(2)}) collective-permute-start(bf16[6,64,128]{2,1,0:T(8,128)(2,1)S(1)} %pad_maximum_fusion.1), channel_id=1, source_target_pairs={{0,1},{1,2},{2,3},{4,5},{5,6},{6,7},{8,9},{9,10},{10,11},{12,13},{... | collective-permute-start | bytes 294920 | tf_op jit(solution)/shard_map/ppermute | solution.py:656
  25.8 1.4 collective-permute-start.3
  27.2 4.6 %all-to-all-done.1.data_ref = f32[4,32,512]{2,1,0:T(8,128)S(1)} async-done(((f32[4,32,512]{2,1,0:T(8,128)}), f32[4,32,512]{2,1,0:T(8,128)S(1)}, u32[]{:S(2)}, u32[]{:S(2)}) %all-to-all-start.1) | async-done | bytes 262176 | tf_op jit(solution)/shard_map/all_to_all | solution.py:702
  32.7 7.9 %shard_map.176 = (bf16[4,256,128]{2,1,0:T(8,128)(2,1)S(1)}, f32[4,32,512]{2,1,0:T(8,128)S(1)}) custom-call(f32[4,32,512]{2,1,0:T(8,128)S(1)} %all-to-all-done.1.data_ref, bf16[2,2,8,32,4096]{4,3,2,1,0:T(8,128)(2,1)} %weight_ref.3, bf16[128,4096]{1,0:T(8,128)(2,1)} %constant.27.clone.table_ref, bf16[128,192]{1,0:T(8,128)(2,1)S(1)} %copy-done.12), custom_call_target="tpu_custom_call" | custom-call | flops 33554432 | bytes 8388608 | tf_op jit(solution)/shard_map/pallas_call | solution.py:611
  40.6 12.0 %all_to_all.45.data_ref = f32[4,32,512]{2,1,0:T(8,128)S(1)} all-to-all(f32[4,32,512]{2,1,0:T(8,128)S(1)} %get-tuple-element.47), channel_id=1, replica_groups=mesh['gx'=8,'gy'=4] {'gy'}, dimensions={0} | all-to-all | bytes 524288 | tf_op jit(solution)/shard_map/all_to_all | solution.py:702
  54.5 3.4 %all-to-all-start.3 = ((f32[8,16,512]{2,1,0:T(8,128)}), f32[8,16,512]{2,1,0:T(8,128)S(1)}, u32[]{:S(2)}, u32[]{:S(2)}) async-start(f32[8,16,512]{2,1,0:T(8,128)} %shard_map.178), calls=%async_computation.3 | async-start | bytes 524288 | tf_op jit(solution)/shard_map/all_to_all | solution.py:702
  59.0 3.1 %shard_map.177.stencil_ref = f32[4,64,1024]{2,1,0:T(8,128)S(1)} custom-call(bf16[4,8,64,128]{3,2,1,0:T(8,128)(2,1)S(1)} %copy-done.10, bf16[8,64,128]{2,1,0:T(8,128)(2,1)} %copy-done.23, bf16[8,64,128]{2,1,0:T(8,128)(2,1)} %copy-done.22, bf16[6,64,128]{2,1,0:T(8,128)(2,1)} %copy-done.24, bf16[6,64,128]{2,1,0:T(8,128)(2,1)} %copy-done.26, ...), custom_call_target="tpu_custom_call" | custom-call | flops 905969664 | bytes 2097152 | tf_op jit(solution)/shard_map/pallas_call | solution.py:592
  62.1 2.7 %all-to-all-done.3.slab_ref = f32[8,16,512]{2,1,0:T(8,128)S(1)} async-done(((f32[8,16,512]{2,1,0:T(8,128)}), f32[8,16,512]{2,1,0:T(8,128)S(1)}, u32[]{:S(2)}, u32[]{:S(2)}) %all-to-all-start.3) | async-done | bytes 262176 | tf_op jit(solution)/shard_map/all_to_all | solution.py:702
  64.8 2.2 %shard_map.179 = (bf16[64,4,8,128]{3,2,1,0:T(8,128)(2,1)}, bf16[4,8,64,128]{3,2,1,0:T(8,128)(2,1)S(1)}, f32[8,16,512]{2,1,0:T(8,128)S(1)}) custom-call(f32[4,64,1024]{2,1,0:T(8,128)S(1)} %shard_map.177.stencil_ref, f32[8,16,512]{2,1,0:T(8,128)S(1)} %all-to-all-done.3.slab_ref, bf16[64,4,8,128]{3,2,1,0:T(8,128)(2,1)S(1)} %copy-done.1, ...), custom_call_target="tpu_custom_call" | custom-call | flops 100663296 | bytes 3145728 | tf_op jit(solution)/shard_map/pallas_call | solution.py:592
  68.5 3.4 %all-to-all-start.4 = ((f32[8,16,512]{2,1,0:T(8,128)}), f32[8,16,512]{2,1,0:T(8,128)S(1)}, u32[]{:S(2)}, u32[]{:S(2)}) async-start(f32[8,16,512]{2,1,0:T(8,128)} %copy-done.14), calls=%async_computation.4 | async-start | bytes 524288 | tf_op jit(solution)/shard_map/all_to_all | solution.py:702
  72.9 1.3 collective-permute-start.5
  74.2 3.2 %collective-permute-start.4 = (bf16[8,64,128]{2,1,0:T(8,128)(2,1)S(1)}, bf16[8,64,128]{2,1,0:T(8,128)(2,1)S(1)}, u32[]{:S(2)}, u32[]{:S(2)}) collective-permute-start(bf16[8,64,128]{2,1,0:T(8,128)(2,1)S(1)} %get-tuple-element.70), channel_id=1, source_target_pairs={{0,4},{4,8},{8,12},{12,16},{16,20},{20,24},{24,28},{1,5},{5,9},{9,... | collective-permute-start | bytes 393224 | tf_op jit(solution)/shard_map/ppermute | solution.py:656
  80.4 4.0 %shard_map.181 = f32[1024,128]{1,0:T(8,128)} custom-call(bf16[4,8,64,128]{3,2,1,0:T(8,128)(2,1)S(1)} %copy-done.7, bf16[4,8,64,128]{3,2,1,0:T(8,128)(2,1)S(1)} %copy-done.11, bf16[8,64,128]{2,1,0:T(8,128)(2,1)} %copy-done.23, bf16[8,64,128]{2,1,0:T(8,128)(2,1)} %copy-done.22, bf16[6,64,128]{2,1,0:T(8,128)(2,1)} %copy-done.24, bf16[6,64,128]{2,1,0:T(8,128)(2,1)} %copy-done.26), custom_call_target="tpu_custom_call" | custom-call | flops 905969664 | bytes 2097152 | tf_op jit(solution)/shard_map/pallas_call | solution.py:592
  85.4 3.3 %all-to-all-start.5 = ((bf16[4,32,512]{2,1,0:T(8,128)(2,1)}), bf16[4,32,512]{2,1,0:T(8,128)(2,1)S(1)}, u32[]{:S(2)}, u32[]{:S(2)}) async-start(bf16[4,32,512]{2,1,0:T(8,128)(2,1)} %shard_map.180), calls=%async_computation.5 | async-start | bytes 262144 | tf_op jit(solution)/shard_map/all_to_all | solution.py:702
  88.8 3.9 %collective-permute-start.6 = (bf16[6,64,128]{2,1,0:T(8,128)(2,1)S(1)}, bf16[6,64,128]{2,1,0:T(8,128)(2,1)S(1)}, u32[]{:S(2)}, u32[]{:S(2)}) collective-permute-start(bf16[6,64,128]{2,1,0:T(8,128)(2,1)S(1)} %pad_maximum_fusion.3), channel_id=1, source_target_pairs={{0,1},{1,2},{2,3},{4,5},{5,6},{6,7},{8,9},{9,10},{10,11},{12,13},{... | collective-permute-start | bytes 294920 | tf_op jit(solution)/shard_map/ppermute | solution.py:656
  92.7 2.9 %collective-permute-done.6.ylo_ref = bf16[6,64,128]{2,1,0:T(8,128)(2,1)S(1)} collective-permute-done((bf16[6,64,128]{2,1,0:T(8,128)(2,1)S(1)}, bf16[6,64,128]{2,1,0:T(8,128)(2,1)S(1)}, u32[]{:S(2)}, u32[]{:S(2)}) %collective-permute-start.6) | collective-permute-done | bytes 98336 | tf_op jit(solution)/shard_map/ppermute | solution.py:656
  95.5 3.7 %all-to-all-start.6 = ((f32[8,128,128]{2,1,0:T(8,128)}), f32[8,128,128]{2,1,0:T(8,128)S(1)}, u32[]{:S(2)}, u32[]{:S(2)}) async-start(f32[8,128,128]{2,1,0:T(8,128)} %bitcast.7), calls=%async_computation.6 | async-start | bytes 1048576 | tf_op jit(solution)/shard_map/all_to_all | solution.py:702
  99.2 8.0 %shard_map.182 = (f32[4,256,128]{2,1,0:T(8,128)S(1)}, bf16[4,32,512]{2,1,0:T(8,128)(2,1)S(1)}) custom-call(bf16[4,32,512]{2,1,0:T(8,128)(2,1)S(1)} %all-to-all-done.5.data_ref, bf16[2,2,8,32,4096]{4,3,2,1,0:T(8,128)(2,1)} %weight_ref.3, bf16[8,512]{1,0:T(8,128)(2,1)} %constant.28.clone.table_ref, bf16[128,192]{1,0:T(8,128)(2,1)S(1)} %copy-done.13), custom_call_target="tpu_custom_call" | custom-call | flops 33554432 | bytes 8388608 | tf_op jit(solution)/shard_map/pallas_call | solution.py:611
  107.2 1.7 %all-to-all-done.6 = f32[8,128,128]{2,1,0:T(8,128)S(1)} async-done(((f32[8,128,128]{2,1,0:T(8,128)}), f32[8,128,128]{2,1,0:T(8,128)S(1)}, u32[]{:S(2)}, u32[]{:S(2)}) %all-to-all-start.6) | async-done | bytes 524320 | tf_op jit(solution)/shard_map/all_to_all | solution.py:702
  109.8 5.6 %all-to-all-start.7 = ((bf16[4,64,512]{2,1,0:T(8,128)(2,1)}), bf16[4,64,512]{2,1,0:T(8,128)(2,1)S(1)}, u32[]{:S(2)}, u32[]{:S(2)}) async-start(bf16[4,64,512]{2,1,0:T(8,128)(2,1)} %pad_maximum_fusion), calls=%async_computation.7 | async-start | bytes 524288 | tf_op jit(solution)/shard_map/all_to_all | solution.py:702
  115.3 1.3 collective-permute-start.7
  116.6 6.8 %collective-permute-done.7.yhi_ref = bf16[6,64,128]{2,1,0:T(8,128)(2,1)S(1)} collective-permute-done((bf16[6,64,128]{2,1,0:T(8,128)(2,1)S(1)}, bf16[6,64,128]{2,1,0:T(8,128)(2,1)S(1)}, u32[]{:S(2)}, u32[]{:S(2)}) %collective-permute-start.7) | collective-permute-done | bytes 98336 | tf_op jit(solution)/shard_map/ppermute | solution.py:656
  125.1 3.0 %shard_map.184.stencil_ref = f32[4,64,1024]{2,1,0:T(8,128)S(1)} custom-call(bf16[4,8,64,128]{3,2,1,0:T(8,128)(2,1)S(1)} %copy-done.8, bf16[8,64,128]{2,1,0:T(8,128)(2,1)} %copy-done.21, bf16[8,64,128]{2,1,0:T(8,128)(2,1)} %copy-done.20, bf16[6,64,128]{2,1,0:T(8,128)(2,1)} %copy-done.25, bf16[6,64,128]{2,1,0:T(8,128)(2,1)} %copy-done.27, ...), custom_call_target="tpu_custom_call" | custom-call | flops 905969664 | bytes 2097152 | tf_op jit(solution)/shard_map/pallas_call | solution.py:592
  129.2 3.5 %all-to-all-start.8 = ((bf16[8,48,512]{2,1,0:T(8,128)(2,1)}), bf16[8,48,512]{2,1,0:T(8,128)(2,1)S(1)}, u32[]{:S(2)}, u32[]{:S(2)}) async-start(bf16[8,48,512]{2,1,0:T(8,128)(2,1)} %shard_map.183), calls=%async_computation.8 | async-start | bytes 786432 | tf_op jit(solution)/shard_map/all_to_all | solution.py:702
  132.7 7.6 %shard_map.186 = f32[2,2,8,32,4096]{4,3,2,1,0:T(8,128)} custom-call(bf16[4,256,128]{2,1,0:T(8,128)(2,1)S(1)} %get-tuple-element.63.modes_ref, f32[4,256,128]{2,1,0:T(8,128)S(1)} %get-tuple-element.64.back_ref, bf16[128,4096]{1,0:T(8,128)(2,1)S(1)} %copy-done), custom_call_target="tpu_custom_call" | custom-call | flops 16777216 | bytes 16777216 | tf_op jit(solution)/shard_map/pallas_call | solution.py:640
  140.9 1.8 %shard_map.185 = (f32[64,4,8,128]{3,2,1,0:T(8,128)}, f32[64,1728]{1,0:T(8,128)}, f32[64,64]{1,0:T(8,128)}) custom-call(f32[4,64,1024]{2,1,0:T(8,128)S(1)} %shard_map.184.stencil_ref, bf16[8,48,512]{2,1,0:T(8,128)(2,1)S(1)} %all-to-all-done.8.message_ref, bf16[96,128]{1,0:T(8,128)(2,1)S(1)} %copy-done.17), custom_call_target="tpu_custom_call" | custom-call | flops 50331648 | bytes 2621440 | tf_op jit(solution)/shard_map/pallas_call | solution.py:592
  (87 shorter events, 17.2 us)
Async XLA Ops:
  0.6 83.8 %copy-start.5 = (bf16[128,384]{1,0:T(8,128)(2,1)S(1)}, bf16[128,384]{1,0:T(8,128)(2,1)}, u32[]{:S(2)}) copy-start(bf16[128,384]{1,0:T(8,128)(2,1)} %constant.24.clone.table_ref) | copy-start | bytes 294916
  0.6 98.6 %copy-start.13 = (bf16[128,192]{1,0:T(8,128)(2,1)S(1)}, bf16[128,192]{1,0:T(8,128)(2,1)}, u32[]{:S(2)}) copy-start(bf16[128,192]{1,0:T(8,128)(2,1)} %constant.26.clone.turn_ref) | copy-start | bytes 147460
  0.7 64.2 %copy-start.15 = (bf16[96,128]{1,0:T(8,128)(2,1)S(1)}, bf16[96,128]{1,0:T(8,128)(2,1)}, u32[]{:S(2)}) copy-start(bf16[96,128]{1,0:T(8,128)(2,1)} %constant.22.clone.inverse_ref) | copy-start | bytes 73732
  0.7 64.1 %copy-start.16 = (bf16[96,128]{1,0:T(8,128)(2,1)S(1)}, bf16[96,128]{1,0:T(8,128)(2,1)}, u32[]{:S(2)}) copy-start(bf16[96,128]{1,0:T(8,128)(2,1)} %constant.21.clone.forward_ref) | copy-start | bytes 73732
  0.7 64.1 %copy-start.1 = (bf16[64,4,8,128]{3,2,1,0:T(8,128)(2,1)S(1)}, bf16[64,4,8,128]{3,2,1,0:T(8,128)(2,1)}, u32[]{:S(2)}) copy-start(bf16[64,4,8,128]{3,2,1,0:T(8,128)(2,1)} %cot_ref.1) | copy-start | bytes 1572868
  2.9 28.9 %copy-start.9 = (bf16[4,8,64,128]{3,2,1,0:T(8,128)(2,1)}, bf16[4,8,64,128]{3,2,1,0:T(8,128)(2,1)S(1)}, u32[]{:S(2)}) copy-start(bf16[4,8,64,128]{3,2,1,0:T(8,128)(2,1)S(1)} %get-tuple-element.36.body_ref) | copy-start | bytes 1572868
  2.9 12.1 %all-to-all-start = ((f32[8,16,512]{2,1,0:T(8,128)}), f32[8,16,512]{2,1,0:T(8,128)S(1)}, u32[]{:S(2)}, u32[]{:S(2)}) async-start(f32[8,16,512]{2,1,0:T(8,128)} %get-tuple-element.37), calls=%async_computation | async-start | bytes 524288 | tf_op jit(solution)/shard_map/all_to_all | solution.py:702
  8.1 8.7 %collective-permute-start.1 = (bf16[8,64,128]{2,1,0:T(8,128)(2,1)S(1)}, bf16[8,64,128]{2,1,0:T(8,128)(2,1)S(1)}, u32[]{:S(2)}, u32[]{:S(2)}) collective-permute-start(bf16[8,64,128]{2,1,0:T(8,128)(2,1)S(1)} %get-tuple-element.73), channel_id=1, source_target_pairs={{4,0},{8,4},{12,8},{16,12},{20,16},{24,20},{28,24},{5,1},{9,5},{13... | collective-permute-start | bytes 393224 | tf_op jit(solution)/shard_map/ppermute | solution.py:656
  9.4 7.5 %collective-permute-start = (bf16[8,64,128]{2,1,0:T(8,128)(2,1)S(1)}, bf16[8,64,128]{2,1,0:T(8,128)(2,1)S(1)}, u32[]{:S(2)}, u32[]{:S(2)}) collective-permute-start(bf16[8,64,128]{2,1,0:T(8,128)(2,1)S(1)} %get-tuple-element.74), channel_id=1, source_target_pairs={{0,4},{4,8},{8,12},{12,16},{16,20},{20,24},{24,28},{1,5},{5,9},{9,... | collective-permute-start | bytes 393224 | tf_op jit(solution)/shard_map/ppermute | solution.py:656
  14.7 39.8 %copy-start.18 = (bf16[576,256]{1,0:T(8,128)(2,1)}, bf16[576,256]{1,0:T(8,128)(2,1)S(1)}, u32[]{:S(2)}) copy-start(bf16[576,256]{1,0:T(8,128)(2,1)S(1)} %get-tuple-element.59.weight_ref) | copy-start | bytes 884740
  16.9 8.9 %copy-start.22 = (bf16[8,64,128]{2,1,0:T(8,128)(2,1)}, bf16[8,64,128]{2,1,0:T(8,128)(2,1)S(1)}, u32[]{:S(2)}) copy-start(bf16[8,64,128]{2,1,0:T(8,128)(2,1)S(1)} %collective-permute-done.1.xhi_ref.xhi_any) | copy-start | bytes 393220
  16.9 37.6 %copy-start.23 = (bf16[8,64,128]{2,1,0:T(8,128)(2,1)}, bf16[8,64,128]{2,1,0:T(8,128)(2,1)S(1)}, u32[]{:S(2)}) copy-start(bf16[8,64,128]{2,1,0:T(8,128)(2,1)S(1)} %collective-permute-done.xlo_ref.xlo_any) | copy-start | bytes 393220
  16.9 15.0 %all-to-all-start.1 = ((f32[4,32,512]{2,1,0:T(8,128)}), f32[4,32,512]{2,1,0:T(8,128)S(1)}, u32[]{:S(2)}, u32[]{:S(2)}) async-start(f32[4,32,512]{2,1,0:T(8,128)} %shard_map.174), calls=%async_computation.1 | async-start | bytes 524288 | tf_op jit(solution)/shard_map/all_to_all | solution.py:702
  21.8 18.8 %collective-permute-start.2 = (bf16[6,64,128]{2,1,0:T(8,128)(2,1)S(1)}, bf16[6,64,128]{2,1,0:T(8,128)(2,1)S(1)}, u32[]{:S(2)}, u32[]{:S(2)}) collective-permute-start(bf16[6,64,128]{2,1,0:T(8,128)(2,1)S(1)} %pad_maximum_fusion.1), channel_id=1, source_target_pairs={{0,1},{1,2},{2,3},{4,5},{5,6},{6,7},{8,9},{9,10},{10,11},{12,13},{... | collective-permute-start | bytes 294920 | tf_op jit(solution)/shard_map/ppermute | solution.py:656
  25.8 102.4 %copy-start.3 = (bf16[128,384]{1,0:T(8,128)(2,1)S(1)}, bf16[128,384]{1,0:T(8,128)(2,1)}, u32[]{:S(2)}) copy-start(bf16[128,384]{1,0:T(8,128)(2,1)} %constant.25.clone.table_ref) | copy-start | bytes 294916
  25.8 14.8 %collective-permute-start.3 = (bf16[6,64,128]{2,1,0:T(8,128)(2,1)S(1)}, bf16[6,64,128]{2,1,0:T(8,128)(2,1)S(1)}, u32[]{:S(2)}, u32[]{:S(2)}) collective-permute-start(bf16[6,64,128]{2,1,0:T(8,128)(2,1)S(1)} %pad_maximum_fusion.2), channel_id=1, source_target_pairs={{1,0},{2,1},{3,2},{5,4},{6,5},{7,6},{9,8},{10,9},{11,10},{13,12},{... | collective-permute-start | bytes 294920 | tf_op jit(solution)/shard_map/ppermute | solution.py:656
  40.6 92.1 %copy-start = (bf16[128,4096]{1,0:T(8,128)(2,1)S(1)}, bf16[128,4096]{1,0:T(8,128)(2,1)}, u32[]{:S(2)}) copy-start(bf16[128,4096]{1,0:T(8,128)(2,1)} %constant.27.clone.table_ref) | copy-start | bytes 3145732
  40.6 17.3 %copy-start.24 = (bf16[6,64,128]{2,1,0:T(8,128)(2,1)}, bf16[6,64,128]{2,1,0:T(8,128)(2,1)S(1)}, u32[]{:S(2)}) copy-start(bf16[6,64,128]{2,1,0:T(8,128)(2,1)S(1)} %collective-permute-done.2.ylo_ref.ylo_any) | copy-start | bytes 294916
  40.6 13.9 %copy-start.26 = (bf16[6,64,128]{2,1,0:T(8,128)(2,1)}, bf16[6,64,128]{2,1,0:T(8,128)(2,1)S(1)}, u32[]{:S(2)}) copy-start(bf16[6,64,128]{2,1,0:T(8,128)(2,1)S(1)} %collective-permute-done.3.yhi_ref.yhi_any) | copy-start | bytes 294916
  54.5 10.3 %all-to-all-start.3 = ((f32[8,16,512]{2,1,0:T(8,128)}), f32[8,16,512]{2,1,0:T(8,128)S(1)}, u32[]{:S(2)}, u32[]{:S(2)}) async-start(f32[8,16,512]{2,1,0:T(8,128)} %shard_map.178), calls=%async_computation.3 | async-start | bytes 524288 | tf_op jit(solution)/shard_map/all_to_all | solution.py:702
  68.5 15.9 %all-to-all-start.4 = ((f32[8,16,512]{2,1,0:T(8,128)}), f32[8,16,512]{2,1,0:T(8,128)S(1)}, u32[]{:S(2)}, u32[]{:S(2)}) async-start(f32[8,16,512]{2,1,0:T(8,128)} %copy-done.14), calls=%async_computation.4 | async-start | bytes 524288 | tf_op jit(solution)/shard_map/all_to_all | solution.py:702
  72.9 12.4 %collective-permute-start.5 = (bf16[8,64,128]{2,1,0:T(8,128)(2,1)S(1)}, bf16[8,64,128]{2,1,0:T(8,128)(2,1)S(1)}, u32[]{:S(2)}, u32[]{:S(2)}) collective-permute-start(bf16[8,64,128]{2,1,0:T(8,128)(2,1)S(1)} %get-tuple-element.69), channel_id=1, source_target_pairs={{4,0},{8,4},{12,8},{16,12},{20,16},{24,20},{28,24},{5,1},{9,5},{13... | collective-permute-start | bytes 393224 | tf_op jit(solution)/shard_map/ppermute | solution.py:656
  74.2 11.2 %collective-permute-start.4 = (bf16[8,64,128]{2,1,0:T(8,128)(2,1)S(1)}, bf16[8,64,128]{2,1,0:T(8,128)(2,1)S(1)}, u32[]{:S(2)}, u32[]{:S(2)}) collective-permute-start(bf16[8,64,128]{2,1,0:T(8,128)(2,1)S(1)} %get-tuple-element.70), channel_id=1, source_target_pairs={{0,4},{4,8},{8,12},{12,16},{16,20},{20,24},{24,28},{1,5},{5,9},{9,... | collective-permute-start | bytes 393224 | tf_op jit(solution)/shard_map/ppermute | solution.py:656
  85.4 38.1 %copy-start.20 = (bf16[8,64,128]{2,1,0:T(8,128)(2,1)}, bf16[8,64,128]{2,1,0:T(8,128)(2,1)S(1)}, u32[]{:S(2)}) copy-start(bf16[8,64,128]{2,1,0:T(8,128)(2,1)S(1)} %collective-permute-done.5.xhi_ref) | copy-start | bytes 393220
  85.4 10.2 %all-to-all-start.5 = ((bf16[4,32,512]{2,1,0:T(8,128)(2,1)}), bf16[4,32,512]{2,1,0:T(8,128)(2,1)S(1)}, u32[]{:S(2)}, u32[]{:S(2)}) async-start(bf16[4,32,512]{2,1,0:T(8,128)(2,1)} %shard_map.180), calls=%async_computation.5 | async-start | bytes 262144 | tf_op jit(solution)/shard_map/all_to_all | solution.py:702
  88.8 6.7 %collective-permute-start.6 = (bf16[6,64,128]{2,1,0:T(8,128)(2,1)S(1)}, bf16[6,64,128]{2,1,0:T(8,128)(2,1)S(1)}, u32[]{:S(2)}, u32[]{:S(2)}) collective-permute-start(bf16[6,64,128]{2,1,0:T(8,128)(2,1)S(1)} %pad_maximum_fusion.3), channel_id=1, source_target_pairs={{0,1},{1,2},{2,3},{4,5},{5,6},{6,7},{8,9},{9,10},{10,11},{12,13},{... | collective-permute-start | bytes 294920 | tf_op jit(solution)/shard_map/ppermute | solution.py:656
  95.5 19.8 %copy-start.25 = (bf16[6,64,128]{2,1,0:T(8,128)(2,1)}, bf16[6,64,128]{2,1,0:T(8,128)(2,1)S(1)}, u32[]{:S(2)}) copy-start(bf16[6,64,128]{2,1,0:T(8,128)(2,1)S(1)} %collective-permute-done.6.ylo_ref) | copy-start | bytes 294916
  95.5 13.4 %all-to-all-start.6 = ((f32[8,128,128]{2,1,0:T(8,128)}), f32[8,128,128]{2,1,0:T(8,128)S(1)}, u32[]{:S(2)}, u32[]{:S(2)}) async-start(f32[8,128,128]{2,1,0:T(8,128)} %bitcast.7), calls=%async_computation.6 | async-start | bytes 1048576 | tf_op jit(solution)/shard_map/all_to_all | solution.py:702
  99.2 41.7 %copy-start.17 = (bf16[96,128]{1,0:T(8,128)(2,1)S(1)}, bf16[96,128]{1,0:T(8,128)(2,1)}, u32[]{:S(2)}) copy-start(bf16[96,128]{1,0:T(8,128)(2,1)} %constant.23.clone.inverse_ref) | copy-start | bytes 73732
  109.8 18.4 %all-to-all-start.7 = ((bf16[4,64,512]{2,1,0:T(8,128)(2,1)}), bf16[4,64,512]{2,1,0:T(8,128)(2,1)S(1)}, u32[]{:S(2)}, u32[]{:S(2)}) async-start(bf16[4,64,512]{2,1,0:T(8,128)(2,1)} %pad_maximum_fusion), calls=%async_computation.7 | async-start | bytes 524288 | tf_op jit(solution)/shard_map/all_to_all | solution.py:702
  115.3 8.1 %collective-permute-start.7 = (bf16[6,64,128]{2,1,0:T(8,128)(2,1)S(1)}, bf16[6,64,128]{2,1,0:T(8,128)(2,1)S(1)}, u32[]{:S(2)}, u32[]{:S(2)}) collective-permute-start(bf16[6,64,128]{2,1,0:T(8,128)(2,1)S(1)} %pad_maximum_fusion.4), channel_id=1, source_target_pairs={{1,0},{2,1},{3,2},{5,4},{6,5},{7,6},{9,8},{10,9},{11,10},{13,12},{... | collective-permute-start | bytes 294920 | tf_op jit(solution)/shard_map/ppermute | solution.py:656
  129.2 11.7 %all-to-all-start.8 = ((bf16[8,48,512]{2,1,0:T(8,128)(2,1)}), bf16[8,48,512]{2,1,0:T(8,128)(2,1)S(1)}, u32[]{:S(2)}, u32[]{:S(2)}) async-start(bf16[8,48,512]{2,1,0:T(8,128)(2,1)} %shard_map.183), calls=%async_computation.8 | async-start | bytes 786432 | tf_op jit(solution)/shard_map/all_to_all | solution.py:702
  (12 other events, 13.0 us)

commit v9 on v8

--- a/solution.py
+++ b/solution.py
@@ -239,7 +239,16 @@
 
 
 def gelu_kernel(
-    nx, stencil_ref, slab_ref, cot_ref, inverse_ref, forward_ref, out_ref, turned_ref, back_ref
+    nx,
+    stencil_ref,
+    slab_ref,
+    cot_ref,
+    inverse_ref,
+    forward_ref,
+    out_ref,
+    turned_ref,
+    message_ref,
+    back_ref,
 ):
     c, cx, cy, z = cot_ref.shape
     root = math.sqrt(2.0 / math.pi)
@@ -256,6 +265,11 @@
         grad = (cot * slope).astype(BF16)
         turned_ref[x] = grad
         z_forward(grad.reshape(cy * c, z), forward_ref[...], back_ref, x, nx)
+    ny = message_ref.shape[0] // nx
+    for owner in range(nx):
+        block = back_ref[owner].astype(BF16)
+        for copy in range(ny):
+            message_ref[owner * ny + copy] = block
 
 
 def finish_kernel(
@@ -336,12 +350,11 @@
 SPAN = 8 * C
 
 
-def y_forward(mz, data_ref, table_ref, rows_ref, store):
-    ny, _, lanes = data_ref.shape
-    cy = lanes // C
+def y_forward(mz, blocks, table_ref, rows_ref, store):
+    ny, cy = len(blocks), blocks[0].shape[1] // C
     count = rows_ref.shape[1] // C
     for owner in range(ny):
-        data = data_ref[owner].astype(F32)
+        data = blocks[owner]
         for part in range(2):
             for kz in range(mz):
                 mx = count // mz
@@ -465,7 +478,8 @@
         low = (values - high.astype(F32)).astype(BF16)
         modes_ref[group, place(part, pair), :] = jnp.concatenate([high, low], axis=1)
 
-    y_forward(mz, data_ref, turn_ref, rows_ref, store)
+    blocks = [data_ref[owner] for owner in range(data_ref.shape[0])]
+    y_forward(mz, blocks, turn_ref, rows_ref, store)
     table_copy.wait()
     for group, copy in enumerate(copies):
         copy.wait()
@@ -501,6 +515,7 @@
     weight_ref,
     table_ref,
     turn_ref,
+    x_ref,
     modes_ref,
     out_ref,
     sum_ref,
@@ -517,7 +532,18 @@
     def store(group, part, pair, values):
         modes_ref[group, place(part, pair), :] = jnp.concatenate([values, values], axis=1)
 
-    y_forward(mz, data_ref, turn_ref, rows_ref, store)
+    ny = block_ref.shape[0]
+    size = x_ref.shape[1] // 3
+    blocks = []
+    for owner in range(ny):
+        rows = jnp.concatenate(
+            [data_ref[i].astype(F32) for i in range(owner, data_ref.shape[0], ny)], axis=0
+        ).astype(BF16)
+        blocks.append(
+            jnp.dot(x_ref[:, :size], rows, preferred_element_type=F32)
+            + jnp.dot(x_ref[:, 2 * size :], rows, preferred_element_type=F32)
+        )
+    y_forward(mz, blocks, turn_ref, rows_ref, store)
     for group, copy in enumerate(copies):
         copy.wait()
         total = []
@@ -603,35 +629,36 @@
     )(*args)
 
 
-def per_mode(kernel, data, weight, table, turn, modes, kind, scratch=()):
+def per_mode(kernel, data, weight, table, tables, modes, kind, scratch=()):
     _, mz, mx, my, wide = weight.shape
     groups = mz * mx // QUAD
     rows = 2 * QUAD * MY
     modes_shape = (groups, rows, modes[0])
+    block = (MX // mx, 2 * mz * mx, data.shape[2])
     return pl.pallas_call(
         functools.partial(kernel, mz),
         in_specs=[
             whole(),
             pl.BlockSpec(memory_space=pl.ANY),
             pl.BlockSpec(memory_space=pl.ANY) if kernel is mix_kernel else whole(),
-            whole(),
-        ],
+        ]
+        + [whole() for _ in tables],
         out_specs=[whole(), whole()],
         out_shape=[
             jax.ShapeDtypeStruct(modes_shape, modes[1]),
-            jax.ShapeDtypeStruct(data.shape, kind),
+            jax.ShapeDtypeStruct(block, kind),
         ],
         scratch_shapes=[
             pltpu.VMEM((groups, rows, C), F32),
-            pltpu.VMEM((turn.shape[0] - 2 * MY, mz * mx * C), F32),
-            pltpu.VMEM(data.shape, F32),
+            pltpu.VMEM((tables[0].shape[0] - 2 * MY, mz * mx * C), F32),
+            pltpu.VMEM(block, F32),
             pltpu.VMEM((groups, 2, QUAD, my, wide), BF16),
             pltpu.SemaphoreType.DMA((groups,)),
             *scratch,
         ],
         compiler_params=params(24),
         cost_estimate=cost(weight.size * 8, weight.size * 2),
-    )(data, in_hbm(weight), in_hbm(table), turn)
+    )(data, in_hbm(weight), in_hbm(table), *tables)
 
 
 def outer(modes, back, table, shape, alpha):
@@ -647,7 +674,7 @@
         out_shape=jax.ShapeDtypeStruct(shape, F32),
         compiler_params=params(20),
         cost_estimate=cost(math.prod(shape) * 4, math.prod(shape) * 4),
-    )(modes, back, table)
+    )(modes, back, in_hbm(table))
 
 
 def shift(block, axis, step):
@@ -762,7 +789,7 @@
         swap(block, "gy"),
         spectral_weight,
         spread,
-        y_turn,
+        (y_turn,),
         (2 * c, BF16),
         F32,
         [pltpu.VMEM(spread.shape, BF16), pltpu.SemaphoreType.DMA]
@@ -775,25 +802,27 @@
     stencil = conv(turned, rim, conv_table, False)
     output, grad, slab = call(
         functools.partial(gelu_kernel, nx),
-        [((c, cx, cy, z), BF16), turned_shape, slab_shape],
+        [((c, cx, cy, z), BF16), turned_shape, ((nx * ny, x_rows, lanes), BF16)],
         (stencil, swap(block, "gx"), cotangent, z_spectral, z_grad),
+        [pltpu.VMEM(slab_shape[0], F32)],
         flops=2 * 192 * state.size,
         moved=state.size * 12,
     )
 
     grad_taps = weight_grad(grad, turned, rim)
-    block = x_stage(x_fwd, swap(slab, "gx"), ny, BF16)
-    block, grad_taps, *faces = together(block, grad_taps, *x_halos(grad))
+    faces = x_halos(grad)
     edges = y_halos(grad, *faces)
-    block, grad_taps, ylo = together(swap(block, "gy"), grad_taps, edges[0])
-    edges = (ylo, edges[1])
+    x_mine = x_fwd.reshape(ny, -1, x_fwd.shape[1])
+    x_mine = lax.dynamic_index_in_dim(x_mine, lax.axis_index("gy"), 0, keepdims=False)
+    block = swap(slab, ("gx", "gy"))
+    block, grad_taps, *edges = together(block, grad_taps, *edges)
     mine = swap(grad_taps.reshape(nx, -1, 2 * c), "gx").sum(0)
     back_modes, block = per_mode(
         mix_back_kernel,
         block,
         spectral_weight,
         gather,
-        y_turn,
+        (y_turn, x_mine),
         (2 * c, F32),
         BF16,
         [pltpu.VMEM((2 * QUAD * MY, c * c), BF16)],

time: 144 us -> 133 us (0.924)
  local copies, waits for them, and re-layouts: 11.6 us -> 3.53 us
  starting transfers between devices: 52.3 us -> 49.3 us
    unnamed x56 -> x38, local copies, waits for them, and re-layouts: 9.71 us -> 2.7 us
    all_to_all x8 -> x7, waiting for transfers between devices: 10 us -> 16.2 us  [swap(): return lax.all_to_all(block, axis, split_axis=0, concat_axis=0, tiled=True)]
    ppermute x8, waiting for transfers between devices: 9.7 us -> 4.02 us  [shift(): return lax.ppermute(block, axis, pairs)]
    all_to_all x8 -> x7, starting transfers between devices: 32.9 us -> 31.4 us  [swap(): return lax.all_to_all(block, axis, split_axis=0, concat_axis=0, tiled=True)]
    ppermute x8, starting transfers between devices: 19.4 us -> 17.9 us  [shift(): return lax.ppermute(block, axis, pairs)]
    pallas_call x11 -> x10, Pallas kernels: 21.6 us -> 21 us  [call(): pl.pallas_call(kernel, out_shape=[jax.ShapeDtypeStruct(*out) for out in o...]
  transfers between devices with their start and end apart: 16 -> 15, of which waited for: 7 -> 7; matrix products, arithmetic and copies ran while one was open for 1% -> 1% of each run, Pallas kernels for 26% -> 28%
where the time goes in v9:
time: 133 us; the launch traced here: 132 us
  starting transfers between devices  49.3 us (37%)
  Pallas kernels  45.7 us (34%)
  waiting for transfers between devices  20.2 us (15%)
  blocking collectives  11.2 us (8%)
  local copies, waits for them, and re-layouts  3.53 us (3%)
    all_to_all x7, starting transfers between devices, swap(): return lax.all_to_all(block, axis, split_axis=0, concat_axis=0, tiled=True)  31.4 us
    pallas_call x10, Pallas kernels, call(): pl.pallas_call(kernel, out_shape=[jax.ShapeDtypeStruct(*out) for out in o...  21 us
    ppermute x8, starting transfers between devices, shift(): return lax.ppermute(block, axis, pairs)  17.9 us
    all_to_all x7, waiting for transfers between devices, swap(): return lax.all_to_all(block, axis, split_axis=0, concat_axis=0, tiled=True)  16.2 us
    pallas_call x2, Pallas kernels, per_mode(): pl.pallas_call(functools.partial(kernel, mz), in_specs=[whole(), pl.Block...  15.9 us
    all_to_all x1, blocking collectives, swap(): return lax.all_to_all(block, axis, split_axis=0, concat_axis=0, tiled=True)  11.2 us
    pallas_call x1, Pallas kernels, outer(): pl.pallas_call(functools.partial(outer_kernel, alpha), grid=(modes.shape[...  8.85 us
    ppermute x8, waiting for transfers between devices, shift(): return lax.ppermute(block, axis, pairs)  4.02 us
  transfers between devices with their start and end apart: 15, of which 7 were waited for; matrix products, arithmetic and copies ran while one was open for 1% of the time, Pallas kernels for 28%

profile of v9, /device:TPU:0, one launch (start us, length us, event | category | flops | bytes accessed | tf_op | source)
XLA Modules:
  0.0 131.9 jit_solution(3894931079556660552)
XLA Ops:
  0.7 2.2 %shard_map.173 = (bf16[4,8,64,128]{3,2,1,0:T(8,128)(2,1)S(1)}, f32[8,16,512]{2,1,0:T(8,128)}) custom-call(bf16[64,4,8,128]{3,2,1,0:T(8,128)(2,1)} %field_ref.1, bf16[96,128]{1,0:T(8,128)(2,1)} %constant.30.clone.table_ref), custom_call_target="tpu_custom_call" | custom-call | flops 50331648 | bytes 1310720 | tf_op jit(solution)/shard_map/pallas_call | solution.py:618
  2.9 5.2 %all-to-all-start = ((f32[8,16,512]{2,1,0:T(8,128)}), f32[8,16,512]{2,1,0:T(8,128)S(1)}, u32[]{:S(2)}, u32[]{:S(2)}) async-start(f32[8,16,512]{2,1,0:T(8,128)} %get-tuple-element.34), calls=%async_computation | async-start | bytes 524288 | tf_op jit(solution)/shard_map/all_to_all | solution.py:729
  8.1 1.3 collective-permute-start.1
  9.4 3.0 %collective-permute-start = (bf16[8,64,128]{2,1,0:T(8,128)(2,1)S(1)}, bf16[8,64,128]{2,1,0:T(8,128)(2,1)S(1)}, u32[]{:S(2)}, u32[]{:S(2)}) collective-permute-start(bf16[8,64,128]{2,1,0:T(8,128)(2,1)S(1)} %get-tuple-element.68), channel_id=1, source_target_pairs={{0,4},{4,8},{8,12},{12,16},{16,20},{20,24},{24,28},{1,5},{5,9},{9,... | collective-permute-start | bytes 393224 | tf_op jit(solution)/shard_map/ppermute | solution.py:683
  12.5 1.5 %shard_map.175 = (bf16[576,256]{1,0:T(8,128)(2,1)S(1)}, bf16[576,256]{1,0:T(8,128)(2,1)S(1)}) custom-call(bf16[64,1728]{1,0:T(8,128)(2,1)} %taps_ref.1, bf16[64,64]{1,0:T(8,128)(2,1)} %point_ref.1), custom_call_target="tpu_custom_call" | custom-call | bytes 663552 | tf_op jit(solution)/shard_map/pallas_call | solution.py:618
  16.9 4.9 %all-to-all-start.1 = ((f32[4,32,512]{2,1,0:T(8,128)}), f32[4,32,512]{2,1,0:T(8,128)S(1)}, u32[]{:S(2)}, u32[]{:S(2)}) async-start(f32[4,32,512]{2,1,0:T(8,128)} %shard_map.174), calls=%async_computation.1 | async-start | bytes 524288 | tf_op jit(solution)/shard_map/all_to_all | solution.py:729
  21.8 3.9 %collective-permute-start.2 = (bf16[6,64,128]{2,1,0:T(8,128)(2,1)S(1)}, bf16[6,64,128]{2,1,0:T(8,128)(2,1)S(1)}, u32[]{:S(2)}, u32[]{:S(2)}) collective-permute-start(bf16[6,64,128]{2,1,0:T(8,128)(2,1)S(1)} %pad_maximum_fusion.1), channel_id=1, source_target_pairs={{0,1},{1,2},{2,3},{4,5},{5,6},{6,7},{8,9},{9,10},{10,11},{12,13},{... | collective-permute-start | bytes 294920 | tf_op jit(solution)/shard_map/ppermute | solution.py:683
  25.8 1.4 %collective-permute-start.3 = (bf16[6,64,128]{2,1,0:T(8,128)(2,1)S(1)}, bf16[6,64,128]{2,1,0:T(8,128)(2,1)S(1)}, u32[]{:S(2)}, u32[]{:S(2)}) collective-permute-start(bf16[6,64,128]{2,1,0:T(8,128)(2,1)S(1)} %pad_maximum_fusion.2), channel_id=1, source_target_pairs={{1,0},{2,1},{3,2},{5,4},{6,5},{7,6},{9,8},{10,9},{11,10},{13,12},{... | collective-permute-start | bytes 294920 | tf_op jit(solution)/shard_map/ppermute | solution.py:683
  27.2 4.7 %all-to-all-done.1.data_ref = f32[4,32,512]{2,1,0:T(8,128)S(1)} async-done(((f32[4,32,512]{2,1,0:T(8,128)}), f32[4,32,512]{2,1,0:T(8,128)S(1)}, u32[]{:S(2)}, u32[]{:S(2)}) %all-to-all-start.1) | async-done | bytes 262176 | tf_op jit(solution)/shard_map/all_to_all | solution.py:729
  32.8 7.9 %shard_map.176 = (bf16[4,256,128]{2,1,0:T(8,128)(2,1)S(1)}, f32[4,32,512]{2,1,0:T(8,128)S(1)}) custom-call(f32[4,32,512]{2,1,0:T(8,128)S(1)} %all-to-all-done.1.data_ref, bf16[2,2,8,32,4096]{4,3,2,1,0:T(8,128)(2,1)} %weight_ref.3, bf16[128,4096]{1,0:T(8,128)(2,1)} %constant.37.clone.table_ref, bf16[128,192]{1,0:T(8,128)(2,1)S(1)} %copy-done.3), custom_call_target="tpu_custom_call" | custom-call | flops 33554432 | bytes 8388608 | tf_op jit(solution)/shard_map/pallas_call | solution.py:638
  40.7 11.2 %all_to_all.40.data_ref = f32[4,32,512]{2,1,0:T(8,128)S(1)} all-to-all(f32[4,32,512]{2,1,0:T(8,128)S(1)} %get-tuple-element.44), channel_id=1, replica_groups=mesh['gx'=8,'gy'=4] {'gy'}, dimensions={0} | all-to-all | bytes 524288 | tf_op jit(solution)/shard_map/all_to_all | solution.py:729
  53.8 3.4 %all-to-all-start.3 = ((f32[8,16,512]{2,1,0:T(8,128)}), f32[8,16,512]{2,1,0:T(8,128)S(1)}, u32[]{:S(2)}, u32[]{:S(2)}) async-start(f32[8,16,512]{2,1,0:T(8,128)} %shard_map.178), calls=%async_computation.3 | async-start | bytes 524288 | tf_op jit(solution)/shard_map/all_to_all | solution.py:729
  57.2 3.1 %shard_map.177.stencil_ref = f32[4,64,1024]{2,1,0:T(8,128)S(1)} custom-call(bf16[4,8,64,128]{3,2,1,0:T(8,128)(2,1)S(1)} %get-tuple-element.33.body_ref, bf16[8,64,128]{2,1,0:T(8,128)(2,1)} %copy-done.14, bf16[8,64,128]{2,1,0:T(8,128)(2,1)} %copy-done.13, bf16[6,64,128]{2,1,0:T(8,128)(2,1)} %copy-done.15, bf16[6,64,128]{2,1,0:T(8,128)(2,1)} %copy-done.16, ...), custom_call_target="tpu_custom_call" | custom-call | flops 905969664 | bytes 2097152 | tf_op jit(solution)/shard_map/pallas_call | solution.py:618
  60.3 3.8 %all-to-all-done.3.slab_ref = f32[8,16,512]{2,1,0:T(8,128)S(1)} async-done(((f32[8,16,512]{2,1,0:T(8,128)}), f32[8,16,512]{2,1,0:T(8,128)S(1)}, u32[]{:S(2)}, u32[]{:S(2)}) %all-to-all-start.3) | async-done | bytes 262176 | tf_op jit(solution)/shard_map/all_to_all | solution.py:729
  64.1 2.4 %shard_map.179 = (bf16[64,4,8,128]{3,2,1,0:T(8,128)(2,1)}, bf16[4,8,64,128]{3,2,1,0:T(8,128)(2,1)S(1)}, bf16[32,16,512]{2,1,0:T(8,128)(2,1)}) custom-call(f32[4,64,1024]{2,1,0:T(8,128)S(1)} %shard_map.177.stencil_ref, f32[8,16,512]{2,1,0:T(8,128)S(1)} %all-to-all-done.3.slab_ref, bf16[64,4,8,128]{3,2,1,0:T(8,128)(2,1)S(1)} %copy-done, ...), custom_call_target="tpu_custom_call" | custom-call | flops 100663296 | bytes 3145728 | tf_op jit(solution)/shard_map/pallas_call | solution.py:618
  66.5 2.6 %all-to-all-start.4 = ((bf16[32,16,512]{2,1,0:T(8,128)(2,1)}), bf16[32,16,512]{2,1,0:T(8,128)(2,1)S(1)}, u32[]{:S(2)}, u32[]{:S(2)}) async-start(bf16[32,16,512]{2,1,0:T(8,128)(2,1)} %get-tuple-element.46), calls=%async_computation.4 | async-start | bytes 1048576 | tf_op jit(solution)/shard_map/all_to_all | solution.py:729
  69.2 2.0 %collective-permute-start.4 = (bf16[8,64,128]{2,1,0:T(8,128)(2,1)S(1)}, bf16[8,64,128]{2,1,0:T(8,128)(2,1)S(1)}, u32[]{:S(2)}, u32[]{:S(2)}) collective-permute-start(bf16[8,64,128]{2,1,0:T(8,128)(2,1)S(1)} %get-tuple-element.63), channel_id=1, source_target_pairs={{0,4},{4,8},{8,12},{12,16},{16,20},{20,24},{24,28},{1,5},{5,9},{9,... | collective-permute-start | bytes 393224 | tf_op jit(solution)/shard_map/ppermute | solution.py:683
  71.2 1.3 collective-permute-start.5
  72.6 3.0 %collective-permute-done.5.xhi_ref = bf16[8,64,128]{2,1,0:T(8,128)(2,1)S(1)} collective-permute-done((bf16[8,64,128]{2,1,0:T(8,128)(2,1)S(1)}, bf16[8,64,128]{2,1,0:T(8,128)(2,1)S(1)}, u32[]{:S(2)}, u32[]{:S(2)}) %collective-permute-start.5) | collective-permute-done | bytes 131104 | tf_op jit(solution)/shard_map/ppermute | solution.py:683
  75.6 3.4 %collective-permute-start.6 = (bf16[6,64,128]{2,1,0:T(8,128)(2,1)S(1)}, bf16[6,64,128]{2,1,0:T(8,128)(2,1)S(1)}, u32[]{:S(2)}, u32[]{:S(2)}) collective-permute-start(bf16[6,64,128]{2,1,0:T(8,128)(2,1)S(1)} %pad_maximum_fusion.3), channel_id=1, source_target_pairs={{0,1},{1,2},{2,3},{4,5},{5,6},{6,7},{8,9},{9,10},{10,11},{12,13},{... | collective-permute-start | bytes 294920 | tf_op jit(solution)/shard_map/ppermute | solution.py:683
  79.1 1.5 %collective-permute-start.7 = (bf16[6,64,128]{2,1,0:T(8,128)(2,1)S(1)}, bf16[6,64,128]{2,1,0:T(8,128)(2,1)S(1)}, u32[]{:S(2)}, u32[]{:S(2)}) collective-permute-start(bf16[6,64,128]{2,1,0:T(8,128)(2,1)S(1)} %pad_maximum_fusion.4), channel_id=1, source_target_pairs={{1,0},{2,1},{3,2},{5,4},{6,5},{7,6},{9,8},{10,9},{11,10},{13,12},{... | collective-permute-start | bytes 294920 | tf_op jit(solution)/shard_map/ppermute | solution.py:683
  80.6 4.0 %shard_map.180 = f32[1024,128]{1,0:T(8,128)} custom-call(bf16[4,8,64,128]{3,2,1,0:T(8,128)(2,1)S(1)} %get-tuple-element.47.grad_ref.body_ref, bf16[4,8,64,128]{3,2,1,0:T(8,128)(2,1)S(1)} %get-tuple-element.33.body_ref, bf16[8,64,128]{2,1,0:T(8,128)(2,1)} %copy-done.14, bf16[8,64,128]{2,1,0:T(8,128)(2,1)} %copy-done.13, bf16[6,64,128]{2,1,0:T(8,128)(2,1)} %copy-done.15, ...), custom_call_target="tpu_custom_call" | custom-call | flops 905969664 | bytes 2097152 | tf_op jit(solution)/shard_map/pallas_call | solution.py:618
  84.6 1.0 collective-permute-done.7.yhi_ref
  85.6 7.4 %all-to-all-start.5 = ((f32[8,128,128]{2,1,0:T(8,128)}), f32[8,128,128]{2,1,0:T(8,128)S(1)}, u32[]{:S(2)}, u32[]{:S(2)}) async-start(f32[8,128,128]{2,1,0:T(8,128)} %bitcast.9), calls=%async_computation.5 | async-start | bytes 1048576 | tf_op jit(solution)/shard_map/all_to_all | solution.py:729
  93.8 8.0 %shard_map.181 = (f32[4,256,128]{2,1,0:T(8,128)S(1)}, bf16[4,32,512]{2,1,0:T(8,128)(2,1)S(1)}) custom-call(bf16[32,16,512]{2,1,0:T(8,128)(2,1)S(1)} %all-to-all-done.4.data_ref, bf16[2,2,8,32,4096]{4,3,2,1,0:T(8,128)(2,1)} %weight_ref.3, bf16[8,512]{1,0:T(8,128)(2,1)} %constant.38.clone.table_ref, bf16[128,192]{1,0:T(8,128)(2,1)S(1)} %copy-done.4, ...), custom_call_target="tpu_custom_call" | custom-call | flops 33554432 | bytes 8388608 | tf_op jit(solution)/shard_map/pallas_call | solution.py:638
  103.6 4.2 %all-to-all-start.6 = ((bf16[4,64,512]{2,1,0:T(8,128)(2,1)}), bf16[4,64,512]{2,1,0:T(8,128)(2,1)S(1)}, u32[]{:S(2)}, u32[]{:S(2)}) async-start(bf16[4,64,512]{2,1,0:T(8,128)(2,1)} %pad_maximum_fusion), calls=%async_computation.6 | async-start | bytes 524288 | tf_op jit(solution)/shard_map/all_to_all | solution.py:729
  107.8 3.0 %shard_map.183.stencil_ref = f32[4,64,1024]{2,1,0:T(8,128)S(1)} custom-call(bf16[4,8,64,128]{3,2,1,0:T(8,128)(2,1)S(1)} %get-tuple-element.47.grad_ref.body_ref, bf16[8,64,128]{2,1,0:T(8,128)(2,1)} %copy-done.11, bf16[8,64,128]{2,1,0:T(8,128)(2,1)} %copy-done.12, bf16[6,64,128]{2,1,0:T(8,128)(2,1)} %copy-done.17, bf16[6,64,128]{2,1,0:T(8,128)(2,1)} %copy-done.18, ...), custom_call_target="tpu_custom_call" | custom-call | flops 905969664 | bytes 2097152 | tf_op jit(solution)/shard_map/pallas_call | solution.py:618
  110.8 5.7 %all-to-all-done.6.data_ref = bf16[4,64,512]{2,1,0:T(8,128)(2,1)S(1)} async-done(((bf16[4,64,512]{2,1,0:T(8,128)(2,1)}), bf16[4,64,512]{2,1,0:T(8,128)(2,1)S(1)}, u32[]{:S(2)}, u32[]{:S(2)}) %all-to-all-start.6) | async-done | bytes 262176 | tf_op jit(solution)/shard_map/all_to_all | solution.py:729
  116.5 1.0 shard_map.182
  117.5 3.7 %all-to-all-start.7 = ((bf16[8,48,512]{2,1,0:T(8,128)(2,1)}), bf16[8,48,512]{2,1,0:T(8,128)(2,1)S(1)}, u32[]{:S(2)}, u32[]{:S(2)}) async-start(bf16[8,48,512]{2,1,0:T(8,128)(2,1)} %shard_map.182), calls=%async_computation.7 | async-start | bytes 786432 | tf_op jit(solution)/shard_map/all_to_all | solution.py:729
  121.2 8.8 %shard_map.185 = f32[2,2,8,32,4096]{4,3,2,1,0:T(8,128)} custom-call(bf16[4,256,128]{2,1,0:T(8,128)(2,1)S(1)} %get-tuple-element.57.modes_ref, f32[4,256,128]{2,1,0:T(8,128)S(1)} %get-tuple-element.58.back_ref, bf16[128,4096]{1,0:T(8,128)(2,1)} %constant.37.clone.table_ref), custom_call_target="tpu_custom_call" | custom-call | flops 16777216 | bytes 16777216 | tf_op jit(solution)/shard_map/pallas_call | solution.py:667
  130.1 1.8 %shard_map.184 = (f32[64,4,8,128]{3,2,1,0:T(8,128)}, f32[64,1728]{1,0:T(8,128)}, f32[64,64]{1,0:T(8,128)}) custom-call(f32[4,64,1024]{2,1,0:T(8,128)S(1)} %shard_map.183.stencil_ref, bf16[8,48,512]{2,1,0:T(8,128)(2,1)S(1)} %all-to-all-done.7.message_ref, bf16[96,128]{1,0:T(8,128)(2,1)S(1)} %copy-done.8), custom_call_target="tpu_custom_call" | custom-call | flops 50331648 | bytes 2621440 | tf_op jit(solution)/shard_map/pallas_call | solution.py:618
  (67 shorter events, 8.2 us)
Async XLA Ops:
  0.6 93.1 %copy-start.4 = (bf16[128,192]{1,0:T(8,128)(2,1)S(1)}, bf16[128,192]{1,0:T(8,128)(2,1)}, u32[]{:S(2)}) copy-start(bf16[128,192]{1,0:T(8,128)(2,1)} %constant.36.clone.turn_ref) | copy-start | bytes 147460
  0.6 63.5 %copy-start.6 = (bf16[96,128]{1,0:T(8,128)(2,1)S(1)}, bf16[96,128]{1,0:T(8,128)(2,1)}, u32[]{:S(2)}) copy-start(bf16[96,128]{1,0:T(8,128)(2,1)} %constant.32.clone.inverse_ref) | copy-start | bytes 73732
  0.7 63.5 %copy-start.7 = (bf16[96,128]{1,0:T(8,128)(2,1)S(1)}, bf16[96,128]{1,0:T(8,128)(2,1)}, u32[]{:S(2)}) copy-start(bf16[96,128]{1,0:T(8,128)(2,1)} %constant.31.clone.forward_ref) | copy-start | bytes 73732
  0.7 63.4 %copy-start = (bf16[64,4,8,128]{3,2,1,0:T(8,128)(2,1)S(1)}, bf16[64,4,8,128]{3,2,1,0:T(8,128)(2,1)}, u32[]{:S(2)}) copy-start(bf16[64,4,8,128]{3,2,1,0:T(8,128)(2,1)} %cot_ref.1) | copy-start | bytes 1572868
  2.9 12.1 %all-to-all-start = ((f32[8,16,512]{2,1,0:T(8,128)}), f32[8,16,512]{2,1,0:T(8,128)S(1)}, u32[]{:S(2)}, u32[]{:S(2)}) async-start(f32[8,16,512]{2,1,0:T(8,128)} %get-tuple-element.34), calls=%async_computation | async-start | bytes 524288 | tf_op jit(solution)/shard_map/all_to_all | solution.py:729
  8.1 8.7 %collective-permute-start.1 = (bf16[8,64,128]{2,1,0:T(8,128)(2,1)S(1)}, bf16[8,64,128]{2,1,0:T(8,128)(2,1)S(1)}, u32[]{:S(2)}, u32[]{:S(2)}) collective-permute-start(bf16[8,64,128]{2,1,0:T(8,128)(2,1)S(1)} %get-tuple-element.67), channel_id=1, source_target_pairs={{4,0},{8,4},{12,8},{16,12},{20,16},{24,20},{28,24},{5,1},{9,5},{13... | collective-permute-start | bytes 393224 | tf_op jit(solution)/shard_map/ppermute | solution.py:683
  9.4 7.5 %collective-permute-start = (bf16[8,64,128]{2,1,0:T(8,128)(2,1)S(1)}, bf16[8,64,128]{2,1,0:T(8,128)(2,1)S(1)}, u32[]{:S(2)}, u32[]{:S(2)}) collective-permute-start(bf16[8,64,128]{2,1,0:T(8,128)(2,1)S(1)} %get-tuple-element.68), channel_id=1, source_target_pairs={{0,4},{4,8},{8,12},{12,16},{16,20},{20,24},{24,28},{1,5},{5,9},{9,... | collective-permute-start | bytes 393224 | tf_op jit(solution)/shard_map/ppermute | solution.py:683
  14.0 13.2 %copy-start.9 = (bf16[576,256]{1,0:T(8,128)(2,1)}, bf16[576,256]{1,0:T(8,128)(2,1)S(1)}, u32[]{:S(2)}) copy-start(bf16[576,256]{1,0:T(8,128)(2,1)S(1)} %get-tuple-element.53.weight_ref) | copy-start | bytes 884740
  14.0 13.2 %copy-start.10 = (bf16[576,256]{1,0:T(8,128)(2,1)}, bf16[576,256]{1,0:T(8,128)(2,1)S(1)}, u32[]{:S(2)}) copy-start(bf16[576,256]{1,0:T(8,128)(2,1)S(1)} %get-tuple-element.43.weight_ref) | copy-start | bytes 884740
  15.0 0.9 copy-start.5
  16.9 8.9 %copy-start.13 = (bf16[8,64,128]{2,1,0:T(8,128)(2,1)}, bf16[8,64,128]{2,1,0:T(8,128)(2,1)S(1)}, u32[]{:S(2)}) copy-start(bf16[8,64,128]{2,1,0:T(8,128)(2,1)S(1)} %collective-permute-done.1.xhi_ref.xhi_any) | copy-start | bytes 393220
  16.9 36.9 %copy-start.14 = (bf16[8,64,128]{2,1,0:T(8,128)(2,1)}, bf16[8,64,128]{2,1,0:T(8,128)(2,1)S(1)}, u32[]{:S(2)}) copy-start(bf16[8,64,128]{2,1,0:T(8,128)(2,1)S(1)} %collective-permute-done.xlo_ref.xlo_any) | copy-start | bytes 393220
  16.9 15.1 %all-to-all-start.1 = ((f32[4,32,512]{2,1,0:T(8,128)}), f32[4,32,512]{2,1,0:T(8,128)S(1)}, u32[]{:S(2)}, u32[]{:S(2)}) async-start(f32[4,32,512]{2,1,0:T(8,128)} %shard_map.174), calls=%async_computation.1 | async-start | bytes 524288 | tf_op jit(solution)/shard_map/all_to_all | solution.py:729
  21.8 18.9 %collective-permute-start.2 = (bf16[6,64,128]{2,1,0:T(8,128)(2,1)S(1)}, bf16[6,64,128]{2,1,0:T(8,128)(2,1)S(1)}, u32[]{:S(2)}, u32[]{:S(2)}) collective-permute-start(bf16[6,64,128]{2,1,0:T(8,128)(2,1)S(1)} %pad_maximum_fusion.1), channel_id=1, source_target_pairs={{0,1},{1,2},{2,3},{4,5},{5,6},{6,7},{8,9},{9,10},{10,11},{12,13},{... | collective-permute-start | bytes 294920 | tf_op jit(solution)/shard_map/ppermute | solution.py:683
  25.8 90.7 %copy-start.2 = (bf16[128,384]{1,0:T(8,128)(2,1)S(1)}, bf16[128,384]{1,0:T(8,128)(2,1)}, u32[]{:S(2)}) copy-start(bf16[128,384]{1,0:T(8,128)(2,1)} %constant.35.clone.table_ref) | copy-start | bytes 294916
  25.8 14.9 %collective-permute-start.3 = (bf16[6,64,128]{2,1,0:T(8,128)(2,1)S(1)}, bf16[6,64,128]{2,1,0:T(8,128)(2,1)S(1)}, u32[]{:S(2)}, u32[]{:S(2)}) collective-permute-start(bf16[6,64,128]{2,1,0:T(8,128)(2,1)S(1)} %pad_maximum_fusion.2), channel_id=1, source_target_pairs={{1,0},{2,1},{3,2},{5,4},{6,5},{7,6},{9,8},{10,9},{11,10},{13,12},{... | collective-permute-start | bytes 294920 | tf_op jit(solution)/shard_map/ppermute | solution.py:683
  40.7 16.5 %copy-start.15 = (bf16[6,64,128]{2,1,0:T(8,128)(2,1)}, bf16[6,64,128]{2,1,0:T(8,128)(2,1)S(1)}, u32[]{:S(2)}) copy-start(bf16[6,64,128]{2,1,0:T(8,128)(2,1)S(1)} %collective-permute-done.2.ylo_ref.ylo_any) | copy-start | bytes 294916
  40.7 16.5 %copy-start.16 = (bf16[6,64,128]{2,1,0:T(8,128)(2,1)}, bf16[6,64,128]{2,1,0:T(8,128)(2,1)S(1)}, u32[]{:S(2)}) copy-start(bf16[6,64,128]{2,1,0:T(8,128)(2,1)S(1)} %collective-permute-done.3.yhi_ref.yhi_any) | copy-start | bytes 294916
  53.8 10.3 %all-to-all-start.3 = ((f32[8,16,512]{2,1,0:T(8,128)}), f32[8,16,512]{2,1,0:T(8,128)S(1)}, u32[]{:S(2)}, u32[]{:S(2)}) async-start(f32[8,16,512]{2,1,0:T(8,128)} %shard_map.178), calls=%async_computation.3 | async-start | bytes 524288 | tf_op jit(solution)/shard_map/all_to_all | solution.py:729
  66.5 19.1 %all-to-all-start.4 = ((bf16[32,16,512]{2,1,0:T(8,128)(2,1)}), bf16[32,16,512]{2,1,0:T(8,128)(2,1)S(1)}, u32[]{:S(2)}, u32[]{:S(2)}) async-start(bf16[32,16,512]{2,1,0:T(8,128)(2,1)} %get-tuple-element.46), calls=%async_computation.4 | async-start | bytes 1048576 | tf_op jit(solution)/shard_map/all_to_all | solution.py:729
  69.2 3.4 %collective-permute-start.4 = (bf16[8,64,128]{2,1,0:T(8,128)(2,1)S(1)}, bf16[8,64,128]{2,1,0:T(8,128)(2,1)S(1)}, u32[]{:S(2)}, u32[]{:S(2)}) collective-permute-start(bf16[8,64,128]{2,1,0:T(8,128)(2,1)S(1)} %get-tuple-element.63), channel_id=1, source_target_pairs={{0,4},{4,8},{8,12},{12,16},{16,20},{20,24},{24,28},{1,5},{5,9},{9,... | collective-permute-start | bytes 393224 | tf_op jit(solution)/shard_map/ppermute | solution.py:683
  71.2 4.4 %collective-permute-start.5 = (bf16[8,64,128]{2,1,0:T(8,128)(2,1)S(1)}, bf16[8,64,128]{2,1,0:T(8,128)(2,1)S(1)}, u32[]{:S(2)}, u32[]{:S(2)}) collective-permute-start(bf16[8,64,128]{2,1,0:T(8,128)(2,1)S(1)} %get-tuple-element.64), channel_id=1, source_target_pairs={{4,0},{8,4},{12,8},{16,12},{20,16},{24,20},{28,24},{5,1},{9,5},{13... | collective-permute-start | bytes 393224 | tf_op jit(solution)/shard_map/ppermute | solution.py:683
  72.5 13.1 %copy-start.11 = (bf16[8,64,128]{2,1,0:T(8,128)(2,1)}, bf16[8,64,128]{2,1,0:T(8,128)(2,1)S(1)}, u32[]{:S(2)}) copy-start(bf16[8,64,128]{2,1,0:T(8,128)(2,1)S(1)} %collective-permute-done.4.xlo_ref) | copy-start | bytes 393220
  75.6 28.0 %copy-start.12 = (bf16[8,64,128]{2,1,0:T(8,128)(2,1)}, bf16[8,64,128]{2,1,0:T(8,128)(2,1)S(1)}, u32[]{:S(2)}) copy-start(bf16[8,64,128]{2,1,0:T(8,128)(2,1)S(1)} %collective-permute-done.5.xhi_ref) | copy-start | bytes 393220
  75.6 9.0 %collective-permute-start.6 = (bf16[6,64,128]{2,1,0:T(8,128)(2,1)S(1)}, bf16[6,64,128]{2,1,0:T(8,128)(2,1)S(1)}, u32[]{:S(2)}, u32[]{:S(2)}) collective-permute-start(bf16[6,64,128]{2,1,0:T(8,128)(2,1)S(1)} %pad_maximum_fusion.3), channel_id=1, source_target_pairs={{0,1},{1,2},{2,3},{4,5},{5,6},{6,7},{8,9},{9,10},{10,11},{12,13},{... | collective-permute-start | bytes 294920 | tf_op jit(solution)/shard_map/ppermute | solution.py:683
  79.1 6.5 %collective-permute-start.7 = (bf16[6,64,128]{2,1,0:T(8,128)(2,1)S(1)}, bf16[6,64,128]{2,1,0:T(8,128)(2,1)S(1)}, u32[]{:S(2)}, u32[]{:S(2)}) collective-permute-start(bf16[6,64,128]{2,1,0:T(8,128)(2,1)S(1)} %pad_maximum_fusion.4), channel_id=1, source_target_pairs={{1,0},{2,1},{3,2},{5,4},{6,5},{7,6},{9,8},{10,9},{11,10},{13,12},{... | collective-permute-start | bytes 294920 | tf_op jit(solution)/shard_map/ppermute | solution.py:683
  84.6 23.2 %copy-start.17 = (bf16[6,64,128]{2,1,0:T(8,128)(2,1)}, bf16[6,64,128]{2,1,0:T(8,128)(2,1)S(1)}, u32[]{:S(2)}) copy-start(bf16[6,64,128]{2,1,0:T(8,128)(2,1)S(1)} %collective-permute-done.6.ylo_ref) | copy-start | bytes 294916
  85.6 22.2 %copy-start.18 = (bf16[6,64,128]{2,1,0:T(8,128)(2,1)}, bf16[6,64,128]{2,1,0:T(8,128)(2,1)S(1)}, u32[]{:S(2)}) copy-start(bf16[6,64,128]{2,1,0:T(8,128)(2,1)S(1)} %collective-permute-done.7.yhi_ref) | copy-start | bytes 294916
  85.6 17.2 %all-to-all-start.5 = ((f32[8,128,128]{2,1,0:T(8,128)}), f32[8,128,128]{2,1,0:T(8,128)S(1)}, u32[]{:S(2)}, u32[]{:S(2)}) async-start(f32[8,128,128]{2,1,0:T(8,128)} %bitcast.9), calls=%async_computation.5 | async-start | bytes 1048576 | tf_op jit(solution)/shard_map/all_to_all | solution.py:729
  93.8 36.3 %copy-start.8 = (bf16[96,128]{1,0:T(8,128)(2,1)S(1)}, bf16[96,128]{1,0:T(8,128)(2,1)}, u32[]{:S(2)}) copy-start(bf16[96,128]{1,0:T(8,128)(2,1)} %constant.33.clone.inverse_ref) | copy-start | bytes 73732
  103.6 12.9 %all-to-all-start.6 = ((bf16[4,64,512]{2,1,0:T(8,128)(2,1)}), bf16[4,64,512]{2,1,0:T(8,128)(2,1)S(1)}, u32[]{:S(2)}, u32[]{:S(2)}) async-start(bf16[4,64,512]{2,1,0:T(8,128)(2,1)} %pad_maximum_fusion), calls=%async_computation.6 | async-start | bytes 524288 | tf_op jit(solution)/shard_map/all_to_all | solution.py:729
  117.5 12.6 %all-to-all-start.7 = ((bf16[8,48,512]{2,1,0:T(8,128)(2,1)}), bf16[8,48,512]{2,1,0:T(8,128)(2,1)S(1)}, u32[]{:S(2)}, u32[]{:S(2)}) async-start(bf16[8,48,512]{2,1,0:T(8,128)(2,1)} %shard_map.182), calls=%async_computation.7 | async-start | bytes 786432 | tf_op jit(solution)/shard_map/all_to_all | solution.py:729
  (2 other events, 1.7 us)

commit v10 on v9

--- a/solution.py
+++ b/solution.py
@@ -187,6 +187,8 @@
     xhi_any,
     ylo_any,
     yhi_any,
+    slab_ref,
+    message_ref,
     out_ref,
     rim_ref,
     wide_ref,
@@ -236,6 +238,15 @@
         row = (9 + k) * c
         out_ref[row : row + c] = jnp.concatenate(last[2 * k : 2 * k + 2], axis=1)
     out_ref[14 * c :] = jnp.zeros((2 * c, 2 * c), F32)
+    devices, rows, lanes = message_ref.shape
+    nx, skip, _ = slab_ref.shape
+    per, tiles_in = rows - skip, lanes // (2 * c)
+    for device in range(devices):
+        start = device * per * tiles_in
+        share = [out_ref[start + t * per : start + (t + 1) * per] for t in range(tiles_in)]
+        message_ref[device] = jnp.concatenate(
+            [slab_ref[device // (devices // nx)], jnp.concatenate(share, axis=1)], axis=0
+        ).astype(BF16)
 
 
 def gelu_kernel(
@@ -247,7 +258,6 @@
     forward_ref,
     out_ref,
     turned_ref,
-    message_ref,
     back_ref,
 ):
     c, cx, cy, z = cot_ref.shape
@@ -265,11 +275,6 @@
         grad = (cot * slope).astype(BF16)
         turned_ref[x] = grad
         z_forward(grad.reshape(cy * c, z), forward_ref[...], back_ref, x, nx)
-    ny = message_ref.shape[0] // nx
-    for owner in range(nx):
-        block = back_ref[owner].astype(BF16)
-        for copy in range(ny):
-            message_ref[owner * ny + copy] = block
 
 
 def finish_kernel(
@@ -283,30 +288,27 @@
     point_ref,
     packed_ref,
     turned_ref,
+    slab_ref,
 ):
     c, cx, cy, z = out_ref.shape
+    ny = message_ref.shape[0] // nx
+    for owner in range(nx):
+        parts = [message_ref[owner * ny + j].astype(F32) for j in range(ny)]
+        slab_ref[owner] = sum(parts[1:], parts[0])[: slab_ref.shape[1]]
     for x in range(cx):
-        spectral = z_inverse(message_ref, inverse_ref[...], x, nx).reshape(cy, c, z)
+        spectral = z_inverse(slab_ref, inverse_ref[...], x, nx).reshape(cy, c, z)
         stencil = jnp.stack([stencil_ref[x, :, y * z : (y + 1) * z] for y in range(cy)])
         out_ref[:, x] = jnp.swapaxes(spectral + stencil, 0, 1)
-    skip = 2 * MZ * cx // nx
+    skip = slab_ref.shape[1]
     unpack(scale, skip, message_ref, taps_ref, point_ref, packed_ref, turned_ref)
 
 
 def x_kernel(table_ref, data_ref, out_ref):
-    data = data_ref[...].astype(F32)
-    lanes = data.shape[2]
-    rows = table_ref.shape[1] // (3 * data.shape[0])
-    flat = pieces(data[:, :rows].reshape(-1, lanes))
-    got = jnp.dot(table_ref[...], flat, preferred_element_type=F32).astype(out_ref.dtype)
+    flat = pieces(data_ref[...].reshape(-1, data_ref.shape[2]))
+    got = jnp.dot(table_ref[...], flat, preferred_element_type=F32)
     count = got.shape[0] // out_ref.shape[0]
     for owner in range(out_ref.shape[0]):
-        out_ref[owner, :count] = got[owner * count : (owner + 1) * count]
-    if data.shape[1] > rows:
-        extra = data[:, rows:].sum(0)
-        extra = extra.astype(out_ref.dtype)
-        for owner in range(out_ref.shape[0]):
-            out_ref[owner, count:] = extra
+        out_ref[owner] = got[owner * count : (owner + 1) * count]
 
 
 def taps_kernel(taps_ref, point_ref, forward_ref, back_ref, turned_ref):
@@ -328,10 +330,10 @@
     devices, rows, lanes = message_ref.shape
     per, tiles_in = rows - skip, lanes // 128
     for owner in range(devices):
-        message = message_ref[owner].astype(F32)
+        message = message_ref[owner].astype(F32)[skip:]
         for tile in range(tiles_in):
             row = (owner * tiles_in + tile) * per
-            packed_ref[row : row + per] = message[skip:, tile * 128 : (tile + 1) * 128]
+            packed_ref[row : row + per] = message[:, tile * 128 : (tile + 1) * 128]
     for tap in range(27):
         group, e = tap // 3, tap % 3
         if e < 2:
@@ -373,7 +375,7 @@
             store(q // QUAD, part, q % QUAD, block[part * MY : (part + 1) * MY])
 
 
-def y_inverse(mz, sum_ref, table_ref, out_ref, block_ref):
+def y_inverse(mz, sum_ref, table_ref, block_ref):
     rows = [
         jnp.concatenate(
             [
@@ -390,7 +392,7 @@
         pieces(jnp.concatenate(rows, axis=0)),
         preferred_element_type=F32,
     )
-    ny, _, lanes = out_ref.shape
+    ny, _, lanes = block_ref.shape
     cy = lanes // C
     count = got.shape[1] // C
     mx = count // mz
@@ -404,7 +406,6 @@
                 start = (part * mz + kz) * mx
                 for y in range(cy):
                     block_ref[owner, start : start + mx, y * C : (y + 1) * C] = block[y]
-    out_ref[...] = block_ref[...].astype(out_ref.dtype)
 
 
 def place(part, pair):
@@ -458,7 +459,6 @@
     out_ref,
     sum_ref,
     rows_ref,
-    block_ref,
     held_ref,
     sem_ref,
     spread_ref,
@@ -506,7 +506,7 @@
                 total_ref[place(1, pair), :] = imag
         total = total_ref[...]
         sum_ref[group] = total[:, :C] + total[:, C:]
-    y_inverse(mz, sum_ref, turn_ref, out_ref, block_ref)
+    y_inverse(mz, sum_ref, turn_ref, out_ref)
 
 
 def mix_back_kernel(
@@ -516,14 +516,15 @@
     table_ref,
     turn_ref,
     x_ref,
+    x_back_ref,
     modes_ref,
     out_ref,
     sum_ref,
     rows_ref,
-    block_ref,
     held_ref,
     sem_ref,
     term_ref,
+    block_ref,
 ):
     copies = weight_copies(weight_ref, held_ref, sem_ref)
     for copy in copies:
@@ -532,12 +533,16 @@
     def store(group, part, pair, values):
         modes_ref[group, place(part, pair), :] = jnp.concatenate([values, values], axis=1)
 
-    ny = block_ref.shape[0]
+    devices, ny = data_ref.shape[0], block_ref.shape[0]
     size = x_ref.shape[1] // 3
+    skip = size * ny // devices
+    share = data_ref[0].astype(F32)[skip:]
+    for device in range(1, devices):
+        share += data_ref[device].astype(F32)[skip:]
     blocks = []
     for owner in range(ny):
         rows = jnp.concatenate(
-            [data_ref[i].astype(F32) for i in range(owner, data_ref.shape[0], ny)], axis=0
+            [data_ref[i].astype(F32)[:skip] for i in range(owner, devices, ny)], axis=0
         ).astype(BF16)
         blocks.append(
             jnp.dot(x_ref[:, :size], rows, preferred_element_type=F32)
@@ -571,7 +576,12 @@
                 )
             )
         sum_ref[group] = jnp.concatenate(total, axis=0).T
-    y_inverse(mz, sum_ref, turn_ref, out_ref, block_ref)
+    y_inverse(mz, sum_ref, turn_ref, block_ref)
+    for owner in range(ny):
+        got = jnp.dot(x_back_ref[...], pieces(block_ref[owner]), preferred_element_type=F32)
+        for i in range(devices // ny):
+            rows = got[i * skip : (i + 1) * skip]
+            out_ref[i * ny + owner] = jnp.concatenate([rows, share], axis=0).astype(BF16)
 
 
 def outer_kernel(alpha, modes_ref, back_ref, table_ref, out_ref):
@@ -629,12 +639,11 @@
     )(*args)
 
 
-def per_mode(kernel, data, weight, table, tables, modes, kind, scratch=()):
+def per_mode(kernel, data, weight, table, tables, modes, scratch=()):
     _, mz, mx, my, wide = weight.shape
     groups = mz * mx // QUAD
     rows = 2 * QUAD * MY
     modes_shape = (groups, rows, modes[0])
-    block = (MX // mx, 2 * mz * mx, data.shape[2])
     return pl.pallas_call(
         functools.partial(kernel, mz),
         in_specs=[
@@ -646,12 +655,11 @@
         out_specs=[whole(), whole()],
         out_shape=[
             jax.ShapeDtypeStruct(modes_shape, modes[1]),
-            jax.ShapeDtypeStruct(block, kind),
+            jax.ShapeDtypeStruct(data.shape, data.dtype),
         ],
         scratch_shapes=[
             pltpu.VMEM((groups, rows, C), F32),
             pltpu.VMEM((tables[0].shape[0] - 2 * MY, mz * mx * C), F32),
-            pltpu.VMEM(block, F32),
             pltpu.VMEM((groups, 2, QUAD, my, wide), BF16),
             pltpu.SemaphoreType.DMA((groups,)),
             *scratch,
@@ -705,23 +713,26 @@
     )[0]
 
 
-def weight_grad(grad, turned, rim):
+def weight_grad(grad, turned, rim, slab, devices):
     cx, cy, c, z = turned.shape
+    _, skip, lanes = slab.shape
+    extra = 16 * c * 2 * c // (devices * lanes)
     return call(
         weight_grad_kernel,
-        [((16 * c, 2 * c), F32)],
-        (grad, turned, *map(in_hbm, rim)),
+        [((devices, skip + extra, lanes), BF16)],
+        (grad, turned, *map(in_hbm, rim), slab),
         [
+            pltpu.VMEM((16 * c, 2 * c), F32),
             pltpu.VMEM((4 * c, (cy + 2) * z), BF16),
             pltpu.VMEM((cx * 3 * c, (cy + 2) * z), BF16),
             pltpu.VMEM((9 * c, 4 * c), F32),
             *(pltpu.VMEM(halo.shape, BF16) for halo in rim),
             pltpu.SemaphoreType.DMA((len(rim),)),
         ],
-        anywhere=(2, 3, 4, 5),
         mib=32,
         flops=2 * 27 * c * c * cx * cy * z,
         moved=turned.size * 8,
+        anywhere=(2, 3, 4, 5),
     )[0]
 
 
@@ -752,11 +763,10 @@
     lanes = cy * c
     x_rows = cx * 2 * mz
 
-    def x_stage(table, block, lead, kind=F32, extra=0):
-        rows = table.shape[0] // lead + extra
+    def x_stage(table, block, lead):
         return call(
             x_kernel,
-            [((lead, rows, lanes), kind)],
+            [((lead, table.shape[0] // lead, lanes), F32)],
             (table, block),
             mib=16,
             flops=2 * table.size * lanes,
@@ -780,9 +790,16 @@
         flops=2 * 96 * state.size,
         moved=state.size * 5,
     )
+    here = lax.axis_index("gy")
+    x_mine = x_fwd.reshape(ny, -1, x_fwd.shape[1])
+    x_mine = lax.dynamic_index_in_dim(x_mine, here, 0, keepdims=False)
+    x_back = x_inv.reshape(x_inv.shape[0], 3, ny, -1)
+    x_back = lax.dynamic_index_in_dim(x_back, here, 2, keepdims=False)
+    x_back = x_back.reshape(x_inv.shape[0], -1)
+
     block = x_stage(x_fwd, swap(slab, "gx"), ny)
-    block, conv_table, back_table, *faces = together(
-        block, conv_table, back_table, *x_halos(turned)
+    block, conv_table, back_table, x_mine, x_back, *faces = together(
+        block, conv_table, back_table, x_mine, x_back, *x_halos(turned)
     )
     modes_in, block = per_mode(
         mix_kernel,
@@ -791,7 +808,6 @@
         spread,
         (y_turn,),
         (2 * c, BF16),
-        F32,
         [pltpu.VMEM(spread.shape, BF16), pltpu.SemaphoreType.DMA]
         + [pltpu.VMEM((2 * QUAD * MY, SPAN), F32)] * 2
         + [pltpu.VMEM((2 * QUAD * MY, 2 * c), F32)],
@@ -802,46 +818,40 @@
     stencil = conv(turned, rim, conv_table, False)
     output, grad, slab = call(
         functools.partial(gelu_kernel, nx),
-        [((c, cx, cy, z), BF16), turned_shape, ((nx * ny, x_rows, lanes), BF16)],
+        [((c, cx, cy, z), BF16), turned_shape, slab_shape],
         (stencil, swap(block, "gx"), cotangent, z_spectral, z_grad),
-        [pltpu.VMEM(slab_shape[0], F32)],
         flops=2 * 192 * state.size,
         moved=state.size * 12,
     )
 
-    grad_taps = weight_grad(grad, turned, rim)
+    message = weight_grad(grad, turned, rim, slab, nx * ny)
     faces = x_halos(grad)
     edges = y_halos(grad, *faces)
-    x_mine = x_fwd.reshape(ny, -1, x_fwd.shape[1])
-    x_mine = lax.dynamic_index_in_dim(x_mine, lax.axis_index("gy"), 0, keepdims=False)
-    block = swap(slab, ("gx", "gy"))
-    block, grad_taps, *edges = together(block, grad_taps, *edges)
-    mine = swap(grad_taps.reshape(nx, -1, 2 * c), "gx").sum(0)
-    back_modes, block = per_mode(
+    message, *edges = together(swap(message, ("gx", "gy")), *edges)
+    back_modes, message = per_mode(
         mix_back_kernel,
-        block,
+        message,
         spectral_weight,
         gather,
-        (y_turn, x_mine),
+        (y_turn, x_mine, x_back),
         (2 * c, F32),
-        BF16,
-        [pltpu.VMEM((2 * QUAD * MY, c * c), BF16)],
-    )
-    packed = jnp.concatenate(jnp.split(mine, lanes // (2 * c)), axis=1).astype(BF16)
-    extra = packed.shape[0]
-    packed = jnp.broadcast_to(packed[None], (ny, extra, lanes))
-    block = x_stage(
-        x_inv, swap(jnp.concatenate([block, packed], axis=1), "gy"), nx, BF16, extra
-    )
+        [
+            pltpu.VMEM((2 * QUAD * MY, c * c), BF16),
+            pltpu.VMEM((ny, 2 * mz * mx, lanes), F32),
+        ],
+    )
+    message = swap(message, ("gx", "gy"))
     stencil_back = conv(grad, (*faces, *edges), back_table, True)
-    block, stencil_back = together(block, stencil_back)
-    message = swap(block, "gx")
     grad_modes = outer(modes_in, back_modes, spread, spectral_weight.shape, alpha)
     grad_state, grad_stencil, grad_point = call(
         functools.partial(finish_kernel, nx, alpha),
         [((c, cx, cy, z), F32), ((c, 27 * c), F32), ((c, c), F32)],
         (stencil_back, message, z_back),
-        [pltpu.VMEM(grad_taps.shape, F32), pltpu.VMEM((27 * c, c), F32)],
+        [
+            pltpu.VMEM((16 * c, 2 * c), F32),
+            pltpu.VMEM((27 * c, c), F32),
+            pltpu.VMEM(slab_shape[0], F32),
+        ],
         flops=2 * 96 * state.size,
         moved=state.size * 10,
     )

time: 133 us -> 133 us (level)
  starting transfers between devices: 49.3 us -> 42 us
  waiting for transfers between devices: 20.2 us -> 24.7 us
  blocking collectives: 11.2 us -> 13.1 us
    all_to_all x7 -> x5, starting transfers between devices: 31.4 us -> 23.3 us  [swap(): return lax.all_to_all(block, axis, split_axis=0, concat_axis=0, tiled=True)]
    ppermute x8, waiting for transfers between devices: 4.02 us -> 6.92 us  [shift(): return lax.ppermute(block, axis, pairs)]
    all_to_all x1, blocking collectives: 11.2 us -> 13.1 us  [swap(): return lax.all_to_all(block, axis, split_axis=0, concat_axis=0, tiled=True)]
    all_to_all x7 -> x5, waiting for transfers between devices: 16.2 us -> 17.8 us  [swap(): return lax.all_to_all(block, axis, split_axis=0, concat_axis=0, tiled=True)]
    pallas_call x10 -> x9, Pallas kernels: 21 us -> 19.8 us  [call(): pl.pallas_call(kernel, out_shape=[jax.ShapeDtypeStruct(*out) for out in o...]
    unnamed x38 -> x36, local copies, waits for them, and re-layouts: 2.7 us -> 2.7 us
  transfers between devices with their start and end apart: 15 -> 13, of which waited for: 7 -> 7; matrix products, arithmetic and copies ran while one was open for 1% -> 1% of each run, Pallas kernels for 28% -> 19%
where the time goes in v10:
time: 133 us; the launch traced here: 131 us
  Pallas kernels  45.6 us (34%)
  starting transfers between devices  42 us (32%)
  waiting for transfers between devices  24.7 us (19%)
  blocking collectives  13.1 us (10%)
  local copies, waits for them, and re-layouts  4.42 us (3%)
    all_to_all x5, starting transfers between devices, swap(): return lax.all_to_all(block, axis, split_axis=0, concat_axis=0, tiled=True)  23.3 us
    pallas_call x9, Pallas kernels, call(): pl.pallas_call(kernel, out_shape=[jax.ShapeDtypeStruct(*out) for out in o...  19.8 us
    ppermute x8, starting transfers between devices, shift(): return lax.ppermute(block, axis, pairs)  18.8 us
    all_to_all x5, waiting for transfers between devices, swap(): return lax.all_to_all(block, axis, split_axis=0, concat_axis=0, tiled=True)  17.8 us
    pallas_call x2, Pallas kernels, per_mode(): pl.pallas_call(functools.partial(kernel, mz), in_specs=[whole(), pl.Block...  16.9 us
    all_to_all x1, blocking collectives, swap(): return lax.all_to_all(block, axis, split_axis=0, concat_axis=0, tiled=True)  13.1 us
    pallas_call x1, Pallas kernels, outer(): pl.pallas_call(functools.partial(outer_kernel, alpha), grid=(modes.shape[...  8.86 us
    ppermute x8, waiting for transfers between devices, shift(): return lax.ppermute(block, axis, pairs)  6.92 us
  transfers between devices with their start and end apart: 13, of which 7 were waited for; matrix products, arithmetic and copies ran while one was open for 1% of the time, Pallas kernels for 19%

profile of v10, /device:TPU:0, one launch (start us, length us, event | category | flops | bytes accessed | tf_op | source)
XLA Modules:
  0.0 131.0 jit_solution(18324517545055096758)
XLA Ops:
  0.7 2.2 %shard_map.173 = (bf16[4,8,64,128]{3,2,1,0:T(8,128)(2,1)S(1)}, f32[8,16,512]{2,1,0:T(8,128)}) custom-call(bf16[64,4,8,128]{3,2,1,0:T(8,128)(2,1)} %field_ref.1, bf16[96,128]{1,0:T(8,128)(2,1)} %constant.32.clone.table_ref), custom_call_target="tpu_custom_call" | custom-call | flops 50331648 | bytes 1310720 | tf_op jit(solution)/shard_map/pallas_call | solution.py:628
  2.9 5.2 %all-to-all-start = ((f32[8,16,512]{2,1,0:T(8,128)}), f32[8,16,512]{2,1,0:T(8,128)S(1)}, u32[]{:S(2)}, u32[]{:S(2)}) async-start(f32[8,16,512]{2,1,0:T(8,128)} %get-tuple-element.33), calls=%async_computation | async-start | bytes 524288 | tf_op jit(solution)/shard_map/all_to_all | solution.py:740
  8.1 1.3 collective-permute-start.1
  9.4 3.0 %collective-permute-start = (bf16[8,64,128]{2,1,0:T(8,128)(2,1)S(1)}, bf16[8,64,128]{2,1,0:T(8,128)(2,1)S(1)}, u32[]{:S(2)}, u32[]{:S(2)}) collective-permute-start(bf16[8,64,128]{2,1,0:T(8,128)(2,1)S(1)} %get-tuple-element.66), channel_id=1, source_target_pairs={{0,4},{4,8},{8,12},{12,16},{16,20},{20,24},{24,28},{1,5},{5,9},{9,... | collective-permute-start | bytes 393224 | tf_op jit(solution)/shard_map/ppermute | solution.py:691
  13.2 1.5 %shard_map.175 = (bf16[576,256]{1,0:T(8,128)(2,1)S(1)}, bf16[576,256]{1,0:T(8,128)(2,1)S(1)}) custom-call(bf16[64,1728]{1,0:T(8,128)(2,1)} %taps_ref.1, bf16[64,64]{1,0:T(8,128)(2,1)} %point_ref.1), custom_call_target="tpu_custom_call" | custom-call | bytes 663552 | tf_op jit(solution)/shard_map/pallas_call | solution.py:628
  16.5 0.9 shard_map.174
  17.4 4.9 %all-to-all-start.1 = ((f32[4,32,512]{2,1,0:T(8,128)}), f32[4,32,512]{2,1,0:T(8,128)S(1)}, u32[]{:S(2)}, u32[]{:S(2)}) async-start(f32[4,32,512]{2,1,0:T(8,128)} %shard_map.174), calls=%async_computation.1 | async-start | bytes 524288 | tf_op jit(solution)/shard_map/all_to_all | solution.py:740
  22.4 3.9 %collective-permute-start.2 = (bf16[6,64,128]{2,1,0:T(8,128)(2,1)S(1)}, bf16[6,64,128]{2,1,0:T(8,128)(2,1)S(1)}, u32[]{:S(2)}, u32[]{:S(2)}) collective-permute-start(bf16[6,64,128]{2,1,0:T(8,128)(2,1)S(1)} %pad_maximum_fusion), channel_id=1, source_target_pairs={{0,1},{1,2},{2,3},{4,5},{5,6},{6,7},{8,9},{9,10},{10,11},{12,13},{... | collective-permute-start | bytes 294920 | tf_op jit(solution)/shard_map/ppermute | solution.py:691
  26.3 1.3 collective-permute-start.3
  27.6 3.6 %all-to-all-done.1.data_ref = f32[4,32,512]{2,1,0:T(8,128)S(1)} async-done(((f32[4,32,512]{2,1,0:T(8,128)}), f32[4,32,512]{2,1,0:T(8,128)S(1)}, u32[]{:S(2)}, u32[]{:S(2)}) %all-to-all-start.1) | async-done | bytes 262176 | tf_op jit(solution)/shard_map/all_to_all | solution.py:740
  32.1 7.8 %shard_map.176 = (bf16[4,256,128]{2,1,0:T(8,128)(2,1)S(1)}, f32[4,32,512]{2,1,0:T(8,128)S(1)}) custom-call(f32[4,32,512]{2,1,0:T(8,128)S(1)} %all-to-all-done.1.data_ref, bf16[2,2,8,32,4096]{4,3,2,1,0:T(8,128)(2,1)} %weight_ref.3, bf16[128,4096]{1,0:T(8,128)(2,1)} %constant.39.clone.table_ref, bf16[128,192]{1,0:T(8,128)(2,1)S(1)} %copy-done.1), custom_call_target="tpu_custom_call" | custom-call | flops 33554432 | bytes 8388608 | tf_op jit(solution)/shard_map/pallas_call | solution.py:647
  40.0 13.1 %all_to_all.30.data_ref = f32[4,32,512]{2,1,0:T(8,128)S(1)} all-to-all(f32[4,32,512]{2,1,0:T(8,128)S(1)} %get-tuple-element.43), channel_id=1, replica_groups=mesh['gx'=8,'gy'=4] {'gy'}, dimensions={0} | all-to-all | bytes 524288 | tf_op jit(solution)/shard_map/all_to_all | solution.py:740
  53.9 0.9 shard_map.178
  54.9 3.6 %all-to-all-start.3 = ((f32[8,16,512]{2,1,0:T(8,128)}), f32[8,16,512]{2,1,0:T(8,128)S(1)}, u32[]{:S(2)}, u32[]{:S(2)}) async-start(f32[8,16,512]{2,1,0:T(8,128)} %shard_map.178), calls=%async_computation.3 | async-start | bytes 524288 | tf_op jit(solution)/shard_map/all_to_all | solution.py:740
  58.5 3.1 %shard_map.177.stencil_ref = f32[4,64,1024]{2,1,0:T(8,128)S(1)} custom-call(bf16[4,8,64,128]{3,2,1,0:T(8,128)(2,1)S(1)} %get-tuple-element.32.body_ref, bf16[8,64,128]{2,1,0:T(8,128)(2,1)} %copy-done.13, bf16[8,64,128]{2,1,0:T(8,128)(2,1)} %copy-done.12, bf16[6,64,128]{2,1,0:T(8,128)(2,1)} %copy-done.14, bf16[6,64,128]{2,1,0:T(8,128)(2,1)} %copy-done.16, ...), custom_call_target="tpu_custom_call" | custom-call | flops 905969664 | bytes 2097152 | tf_op jit(solution)/shard_map/pallas_call | solution.py:628
  61.6 3.6 %all-to-all-done.3.slab_ref = f32[8,16,512]{2,1,0:T(8,128)S(1)} async-done(((f32[8,16,512]{2,1,0:T(8,128)}), f32[8,16,512]{2,1,0:T(8,128)S(1)}, u32[]{:S(2)}, u32[]{:S(2)}) %all-to-all-start.3) | async-done | bytes 262176 | tf_op jit(solution)/shard_map/all_to_all | solution.py:740
  65.2 2.2 %shard_map.179 = (bf16[64,4,8,128]{3,2,1,0:T(8,128)(2,1)}, bf16[4,8,64,128]{3,2,1,0:T(8,128)(2,1)S(1)}, f32[8,16,512]{2,1,0:T(8,128)S(1)}) custom-call(f32[4,64,1024]{2,1,0:T(8,128)S(1)} %shard_map.177.stencil_ref, f32[8,16,512]{2,1,0:T(8,128)S(1)} %all-to-all-done.3.slab_ref, bf16[64,4,8,128]{3,2,1,0:T(8,128)(2,1)S(1)} %copy-done, ...), custom_call_target="tpu_custom_call" | custom-call | flops 100663296 | bytes 3145728 | tf_op jit(solution)/shard_map/pallas_call | solution.py:628
  67.3 4.1 %shard_map.180 = bf16[32,24,512]{2,1,0:T(8,128)(2,1)} custom-call(bf16[4,8,64,128]{3,2,1,0:T(8,128)(2,1)S(1)} %get-tuple-element.45.grad_ref.body_ref, bf16[4,8,64,128]{3,2,1,0:T(8,128)(2,1)S(1)} %get-tuple-element.32.body_ref, bf16[8,64,128]{2,1,0:T(8,128)(2,1)} %copy-done.13, bf16[8,64,128]{2,1,0:T(8,128)(2,1)} %copy-done.12, ...), custom_call_target="tpu_custom_call" | custom-call | flops 905969664 | bytes 2097152 | tf_op jit(solution)/shard_map/pallas_call | solution.py:628
  71.5 2.6 %all-to-all-start.4 = ((bf16[32,24,512]{2,1,0:T(8,128)(2,1)}), bf16[32,24,512]{2,1,0:T(8,128)(2,1)S(1)}, u32[]{:S(2)}, u32[]{:S(2)}) async-start(bf16[32,24,512]{2,1,0:T(8,128)(2,1)} %shard_map.180), calls=%async_computation.4 | async-start | bytes 1572864 | tf_op jit(solution)/shard_map/all_to_all | solution.py:740
  74.1 1.3 collective-permute-start.5
  75.4 3.0 %collective-permute-start.4 = (bf16[8,64,128]{2,1,0:T(8,128)(2,1)S(1)}, bf16[8,64,128]{2,1,0:T(8,128)(2,1)S(1)}, u32[]{:S(2)}, u32[]{:S(2)}) collective-permute-start(bf16[8,64,128]{2,1,0:T(8,128)(2,1)S(1)} %get-tuple-element.62), channel_id=1, source_target_pairs={{0,4},{4,8},{8,12},{12,16},{16,20},{20,24},{24,28},{1,5},{5,9},{9,... | collective-permute-start | bytes 393224 | tf_op jit(solution)/shard_map/ppermute | solution.py:691
  79.5 3.6 %collective-permute-start.6 = (bf16[6,64,128]{2,1,0:T(8,128)(2,1)S(1)}, bf16[6,64,128]{2,1,0:T(8,128)(2,1)S(1)}, u32[]{:S(2)}, u32[]{:S(2)}) collective-permute-start(bf16[6,64,128]{2,1,0:T(8,128)(2,1)S(1)} %pad_maximum_fusion.2), channel_id=1, source_target_pairs={{0,1},{1,2},{2,3},{4,5},{5,6},{6,7},{8,9},{9,10},{10,11},{12,13},{... | collective-permute-start | bytes 294920 | tf_op jit(solution)/shard_map/ppermute | solution.py:691
  83.1 1.3 collective-permute-start.7
  84.5 4.9 %collective-permute-done.6.ylo_ref = bf16[6,64,128]{2,1,0:T(8,128)(2,1)S(1)} collective-permute-done((bf16[6,64,128]{2,1,0:T(8,128)(2,1)S(1)}, bf16[6,64,128]{2,1,0:T(8,128)(2,1)S(1)}, u32[]{:S(2)}, u32[]{:S(2)}) %collective-permute-start.6) | collective-permute-done | bytes 98336 | tf_op jit(solution)/shard_map/ppermute | solution.py:691
  89.5 1.1 collective-permute-done.7.yhi_ref
  90.5 3.2 %all-to-all-done.4.data_ref = bf16[32,24,512]{2,1,0:T(8,128)(2,1)S(1)} async-done(((bf16[32,24,512]{2,1,0:T(8,128)(2,1)}), bf16[32,24,512]{2,1,0:T(8,128)(2,1)S(1)}, u32[]{:S(2)}, u32[]{:S(2)}) %all-to-all-start.4) | async-done | bytes 786464 | tf_op jit(solution)/shard_map/all_to_all | solution.py:740
  93.7 9.1 %shard_map.182 = (f32[4,256,128]{2,1,0:T(8,128)S(1)}, bf16[32,24,512]{2,1,0:T(8,128)(2,1)}) custom-call(bf16[32,24,512]{2,1,0:T(8,128)(2,1)S(1)} %all-to-all-done.4.data_ref, bf16[2,2,8,32,4096]{4,3,2,1,0:T(8,128)(2,1)} %weight_ref.3, bf16[8,512]{1,0:T(8,128)(2,1)} %constant.40.clone.table_ref, bf16[128,192]{1,0:T(8,128)(2,1)S(1)} %copy-done.2, ...), custom_call_target="tpu_custom_call" | custom-call | flops 33554432 | bytes 8388608 | tf_op jit(solution)/shard_map/pallas_call | solution.py:647
  102.8 7.0 %all-to-all-start.5 = ((bf16[32,24,512]{2,1,0:T(8,128)(2,1)}), bf16[32,24,512]{2,1,0:T(8,128)(2,1)S(1)}, u32[]{:S(2)}, u32[]{:S(2)}) async-start(bf16[32,24,512]{2,1,0:T(8,128)(2,1)} %get-tuple-element.53), calls=%async_computation.5 | async-start | bytes 1572864 | tf_op jit(solution)/shard_map/all_to_all | solution.py:740
  109.8 8.9 %shard_map.184 = f32[2,2,8,32,4096]{4,3,2,1,0:T(8,128)} custom-call(bf16[4,256,128]{2,1,0:T(8,128)(2,1)S(1)} %get-tuple-element.55.modes_ref, f32[4,256,128]{2,1,0:T(8,128)S(1)} %get-tuple-element.56.back_ref, bf16[128,4096]{1,0:T(8,128)(2,1)} %constant.39.clone.table_ref), custom_call_target="tpu_custom_call" | custom-call | flops 16777216 | bytes 16777216 | tf_op jit(solution)/shard_map/pallas_call | solution.py:675
  118.7 3.0 %shard_map.181.stencil_ref = f32[4,64,1024]{2,1,0:T(8,128)S(1)} custom-call(bf16[4,8,64,128]{3,2,1,0:T(8,128)(2,1)S(1)} %get-tuple-element.45.grad_ref.body_ref, bf16[8,64,128]{2,1,0:T(8,128)(2,1)} %copy-done.11, bf16[8,64,128]{2,1,0:T(8,128)(2,1)} %copy-done.10, bf16[6,64,128]{2,1,0:T(8,128)(2,1)} %copy-done.15, bf16[6,64,128]{2,1,0:T(8,128)(2,1)} %copy-done.17, ...), custom_call_target="tpu_custom_call" | custom-call | flops 905969664 | bytes 2097152 | tf_op jit(solution)/shard_map/pallas_call | solution.py:628
  121.7 7.5 %all-to-all-done.5.message_ref = bf16[32,24,512]{2,1,0:T(8,128)(2,1)S(1)} async-done(((bf16[32,24,512]{2,1,0:T(8,128)(2,1)}), bf16[32,24,512]{2,1,0:T(8,128)(2,1)S(1)}, u32[]{:S(2)}, u32[]{:S(2)}) %all-to-all-start.5) | async-done | bytes 786464 | tf_op jit(solution)/shard_map/all_to_all | solution.py:740
  129.2 1.8 %shard_map.183 = (f32[64,4,8,128]{3,2,1,0:T(8,128)}, f32[64,1728]{1,0:T(8,128)}, f32[64,64]{1,0:T(8,128)}) custom-call(f32[4,64,1024]{2,1,0:T(8,128)S(1)} %shard_map.181.stencil_ref, bf16[32,24,512]{2,1,0:T(8,128)(2,1)S(1)} %all-to-all-done.5.message_ref, bf16[96,128]{1,0:T(8,128)(2,1)S(1)} %copy-done.5), custom_call_target="tpu_custom_call" | custom-call | flops 50331648 | bytes 2621440 | tf_op jit(solution)/shard_map/pallas_call | solution.py:628
  (57 shorter events, 5.4 us)
Async XLA Ops:
  0.6 93.1 %copy-start.2 = (bf16[128,192]{1,0:T(8,128)(2,1)S(1)}, bf16[128,192]{1,0:T(8,128)(2,1)}, u32[]{:S(2)}) copy-start(bf16[128,192]{1,0:T(8,128)(2,1)} %constant.38.clone.turn_ref) | copy-start | bytes 147460
  0.6 64.5 %copy-start.6 = (bf16[96,128]{1,0:T(8,128)(2,1)S(1)}, bf16[96,128]{1,0:T(8,128)(2,1)}, u32[]{:S(2)}) copy-start(bf16[96,128]{1,0:T(8,128)(2,1)} %constant.34.clone.inverse_ref) | copy-start | bytes 73732
  0.7 64.5 %copy-start.7 = (bf16[96,128]{1,0:T(8,128)(2,1)S(1)}, bf16[96,128]{1,0:T(8,128)(2,1)}, u32[]{:S(2)}) copy-start(bf16[96,128]{1,0:T(8,128)(2,1)} %constant.33.clone.forward_ref) | copy-start | bytes 73732
  0.7 64.5 %copy-start = (bf16[64,4,8,128]{3,2,1,0:T(8,128)(2,1)S(1)}, bf16[64,4,8,128]{3,2,1,0:T(8,128)(2,1)}, u32[]{:S(2)}) copy-start(bf16[64,4,8,128]{3,2,1,0:T(8,128)(2,1)} %cot_ref.1) | copy-start | bytes 1572868
  2.9 12.7 %all-to-all-start = ((f32[8,16,512]{2,1,0:T(8,128)}), f32[8,16,512]{2,1,0:T(8,128)S(1)}, u32[]{:S(2)}, u32[]{:S(2)}) async-start(f32[8,16,512]{2,1,0:T(8,128)} %get-tuple-element.33), calls=%async_computation | async-start | bytes 524288 | tf_op jit(solution)/shard_map/all_to_all | solution.py:740
  8.1 9.3 %collective-permute-start.1 = (bf16[8,64,128]{2,1,0:T(8,128)(2,1)S(1)}, bf16[8,64,128]{2,1,0:T(8,128)(2,1)S(1)}, u32[]{:S(2)}, u32[]{:S(2)}) collective-permute-start(bf16[8,64,128]{2,1,0:T(8,128)(2,1)S(1)} %get-tuple-element.65), channel_id=1, source_target_pairs={{4,0},{8,4},{12,8},{16,12},{20,16},{24,20},{28,24},{5,1},{9,5},{13... | collective-permute-start | bytes 393224 | tf_op jit(solution)/shard_map/ppermute | solution.py:691
  9.4 8.0 %collective-permute-start = (bf16[8,64,128]{2,1,0:T(8,128)(2,1)S(1)}, bf16[8,64,128]{2,1,0:T(8,128)(2,1)S(1)}, u32[]{:S(2)}, u32[]{:S(2)}) collective-permute-start(bf16[8,64,128]{2,1,0:T(8,128)(2,1)S(1)} %get-tuple-element.66), channel_id=1, source_target_pairs={{0,4},{4,8},{8,12},{12,16},{16,20},{20,24},{24,28},{1,5},{5,9},{9,... | collective-permute-start | bytes 393224 | tf_op jit(solution)/shard_map/ppermute | solution.py:691
  14.8 12.8 %copy-start.8 = (bf16[576,256]{1,0:T(8,128)(2,1)}, bf16[576,256]{1,0:T(8,128)(2,1)S(1)}, u32[]{:S(2)}) copy-start(bf16[576,256]{1,0:T(8,128)(2,1)S(1)} %get-tuple-element.49.weight_ref) | copy-start | bytes 884740
  14.8 12.8 %copy-start.9 = (bf16[576,256]{1,0:T(8,128)(2,1)}, bf16[576,256]{1,0:T(8,128)(2,1)S(1)}, u32[]{:S(2)}) copy-start(bf16[576,256]{1,0:T(8,128)(2,1)S(1)} %get-tuple-element.42.weight_ref) | copy-start | bytes 884740
  15.6 0.9 copy-start.4
  17.4 41.1 %copy-start.12 = (bf16[8,64,128]{2,1,0:T(8,128)(2,1)}, bf16[8,64,128]{2,1,0:T(8,128)(2,1)S(1)}, u32[]{:S(2)}) copy-start(bf16[8,64,128]{2,1,0:T(8,128)(2,1)S(1)} %collective-permute-done.1.xhi_ref.xhi_any) | copy-start | bytes 393220
  17.4 37.4 %copy-start.13 = (bf16[8,64,128]{2,1,0:T(8,128)(2,1)}, bf16[8,64,128]{2,1,0:T(8,128)(2,1)S(1)}, u32[]{:S(2)}) copy-start(bf16[8,64,128]{2,1,0:T(8,128)(2,1)S(1)} %collective-permute-done.xlo_ref.xlo_any) | copy-start | bytes 393220
  17.4 13.8 %all-to-all-start.1 = ((f32[4,32,512]{2,1,0:T(8,128)}), f32[4,32,512]{2,1,0:T(8,128)S(1)}, u32[]{:S(2)}, u32[]{:S(2)}) async-start(f32[4,32,512]{2,1,0:T(8,128)} %shard_map.174), calls=%async_computation.1 | async-start | bytes 524288 | tf_op jit(solution)/shard_map/all_to_all | solution.py:740
  22.4 17.6 %collective-permute-start.2 = (bf16[6,64,128]{2,1,0:T(8,128)(2,1)S(1)}, bf16[6,64,128]{2,1,0:T(8,128)(2,1)S(1)}, u32[]{:S(2)}, u32[]{:S(2)}) collective-permute-start(bf16[6,64,128]{2,1,0:T(8,128)(2,1)S(1)} %pad_maximum_fusion), channel_id=1, source_target_pairs={{0,1},{1,2},{2,3},{4,5},{5,6},{6,7},{8,9},{9,10},{10,11},{12,13},{... | collective-permute-start | bytes 294920 | tf_op jit(solution)/shard_map/ppermute | solution.py:691
  26.3 13.6 %collective-permute-start.3 = (bf16[6,64,128]{2,1,0:T(8,128)(2,1)S(1)}, bf16[6,64,128]{2,1,0:T(8,128)(2,1)S(1)}, u32[]{:S(2)}, u32[]{:S(2)}) collective-permute-start(bf16[6,64,128]{2,1,0:T(8,128)(2,1)S(1)} %pad_maximum_fusion.1), channel_id=1, source_target_pairs={{1,0},{2,1},{3,2},{5,4},{6,5},{7,6},{9,8},{10,9},{11,10},{13,12},{... | collective-permute-start | bytes 294920 | tf_op jit(solution)/shard_map/ppermute | solution.py:691
  31.2 0.8 copy-start.1
  39.9 18.6 %copy-start.14 = (bf16[6,64,128]{2,1,0:T(8,128)(2,1)}, bf16[6,64,128]{2,1,0:T(8,128)(2,1)S(1)}, u32[]{:S(2)}) copy-start(bf16[6,64,128]{2,1,0:T(8,128)(2,1)S(1)} %collective-permute-done.2.ylo_ref.ylo_any) | copy-start | bytes 294916
  39.9 14.9 %copy-start.16 = (bf16[6,64,128]{2,1,0:T(8,128)(2,1)}, bf16[6,64,128]{2,1,0:T(8,128)(2,1)S(1)}, u32[]{:S(2)}) copy-start(bf16[6,64,128]{2,1,0:T(8,128)(2,1)S(1)} %collective-permute-done.3.yhi_ref.yhi_any) | copy-start | bytes 294916
  53.0 0.9 copy-start.3
  54.9 10.3 %all-to-all-start.3 = ((f32[8,16,512]{2,1,0:T(8,128)}), f32[8,16,512]{2,1,0:T(8,128)S(1)}, u32[]{:S(2)}, u32[]{:S(2)}) async-start(f32[8,16,512]{2,1,0:T(8,128)} %shard_map.178), calls=%async_computation.3 | async-start | bytes 524288 | tf_op jit(solution)/shard_map/all_to_all | solution.py:740
  71.5 22.2 %all-to-all-start.4 = ((bf16[32,24,512]{2,1,0:T(8,128)(2,1)}), bf16[32,24,512]{2,1,0:T(8,128)(2,1)S(1)}, u32[]{:S(2)}, u32[]{:S(2)}) async-start(bf16[32,24,512]{2,1,0:T(8,128)(2,1)} %shard_map.180), calls=%async_computation.4 | async-start | bytes 1572864 | tf_op jit(solution)/shard_map/all_to_all | solution.py:740
  74.1 4.4 %collective-permute-start.5 = (bf16[8,64,128]{2,1,0:T(8,128)(2,1)S(1)}, bf16[8,64,128]{2,1,0:T(8,128)(2,1)S(1)}, u32[]{:S(2)}, u32[]{:S(2)}) collective-permute-start(bf16[8,64,128]{2,1,0:T(8,128)(2,1)S(1)} %get-tuple-element.61), channel_id=1, source_target_pairs={{4,0},{8,4},{12,8},{16,12},{20,16},{24,20},{28,24},{5,1},{9,5},{13... | collective-permute-start | bytes 393224 | tf_op jit(solution)/shard_map/ppermute | solution.py:691
  75.4 4.0 %collective-permute-start.4 = (bf16[8,64,128]{2,1,0:T(8,128)(2,1)S(1)}, bf16[8,64,128]{2,1,0:T(8,128)(2,1)S(1)}, u32[]{:S(2)}, u32[]{:S(2)}) collective-permute-start(bf16[8,64,128]{2,1,0:T(8,128)(2,1)S(1)} %get-tuple-element.62), channel_id=1, source_target_pairs={{0,4},{4,8},{8,12},{12,16},{16,20},{20,24},{24,28},{1,5},{5,9},{9,... | collective-permute-start | bytes 393224 | tf_op jit(solution)/shard_map/ppermute | solution.py:691
  78.5 50.7 %copy-start.5 = (bf16[96,128]{1,0:T(8,128)(2,1)S(1)}, bf16[96,128]{1,0:T(8,128)(2,1)}, u32[]{:S(2)}) copy-start(bf16[96,128]{1,0:T(8,128)(2,1)} %constant.35.clone.inverse_ref) | copy-start | bytes 73732
  78.5 40.1 %copy-start.10 = (bf16[8,64,128]{2,1,0:T(8,128)(2,1)}, bf16[8,64,128]{2,1,0:T(8,128)(2,1)S(1)}, u32[]{:S(2)}) copy-start(bf16[8,64,128]{2,1,0:T(8,128)(2,1)S(1)} %collective-permute-done.5.xhi_ref) | copy-start | bytes 393220
  79.5 11.1 %copy-start.11 = (bf16[8,64,128]{2,1,0:T(8,128)(2,1)}, bf16[8,64,128]{2,1,0:T(8,128)(2,1)S(1)}, u32[]{:S(2)}) copy-start(bf16[8,64,128]{2,1,0:T(8,128)(2,1)S(1)} %collective-permute-done.4.xlo_ref) | copy-start | bytes 393220
  79.5 10.0 %collective-permute-start.6 = (bf16[6,64,128]{2,1,0:T(8,128)(2,1)S(1)}, bf16[6,64,128]{2,1,0:T(8,128)(2,1)S(1)}, u32[]{:S(2)}, u32[]{:S(2)}) collective-permute-start(bf16[6,64,128]{2,1,0:T(8,128)(2,1)S(1)} %pad_maximum_fusion.2), channel_id=1, source_target_pairs={{0,1},{1,2},{2,3},{4,5},{5,6},{6,7},{8,9},{9,10},{10,11},{12,13},{... | collective-permute-start | bytes 294920 | tf_op jit(solution)/shard_map/ppermute | solution.py:691
  83.1 7.4 %collective-permute-start.7 = (bf16[6,64,128]{2,1,0:T(8,128)(2,1)S(1)}, bf16[6,64,128]{2,1,0:T(8,128)(2,1)S(1)}, u32[]{:S(2)}, u32[]{:S(2)}) collective-permute-start(bf16[6,64,128]{2,1,0:T(8,128)(2,1)S(1)} %pad_maximum_fusion.3), channel_id=1, source_target_pairs={{1,0},{2,1},{3,2},{5,4},{6,5},{7,6},{9,8},{10,9},{11,10},{13,12},{... | collective-permute-start | bytes 294920 | tf_op jit(solution)/shard_map/ppermute | solution.py:691
  89.5 29.2 %copy-start.15 = (bf16[6,64,128]{2,1,0:T(8,128)(2,1)}, bf16[6,64,128]{2,1,0:T(8,128)(2,1)S(1)}, u32[]{:S(2)}) copy-start(bf16[6,64,128]{2,1,0:T(8,128)(2,1)S(1)} %collective-permute-done.6.ylo_ref) | copy-start | bytes 294916
  90.5 28.1 %copy-start.17 = (bf16[6,64,128]{2,1,0:T(8,128)(2,1)}, bf16[6,64,128]{2,1,0:T(8,128)(2,1)S(1)}, u32[]{:S(2)}) copy-start(bf16[6,64,128]{2,1,0:T(8,128)(2,1)S(1)} %collective-permute-done.7.yhi_ref) | copy-start | bytes 294916
  102.8 26.4 %all-to-all-start.5 = ((bf16[32,24,512]{2,1,0:T(8,128)(2,1)}), bf16[32,24,512]{2,1,0:T(8,128)(2,1)S(1)}, u32[]{:S(2)}, u32[]{:S(2)}) async-start(bf16[32,24,512]{2,1,0:T(8,128)(2,1)} %get-tuple-element.53), calls=%async_computation.5 | async-start | bytes 1572864 | tf_op jit(solution)/shard_map/all_to_all | solution.py:740

commit v11 on v9

--- a/solution.py
+++ b/solution.py
@@ -780,9 +780,12 @@
         flops=2 * 96 * state.size,
         moved=state.size * 5,
     )
+    x_mine = x_fwd.reshape(ny, -1, x_fwd.shape[1])
+    x_mine = lax.dynamic_index_in_dim(x_mine, lax.axis_index("gy"), 0, keepdims=False)
+
     block = x_stage(x_fwd, swap(slab, "gx"), ny)
-    block, conv_table, back_table, *faces = together(
-        block, conv_table, back_table, *x_halos(turned)
+    block, conv_table, back_table, x_mine, *faces = together(
+        block, conv_table, back_table, x_mine, *x_halos(turned)
     )
     modes_in, block = per_mode(
         mix_kernel,
@@ -811,9 +814,8 @@
 
     grad_taps = weight_grad(grad, turned, rim)
     faces = x_halos(grad)
+    grad_taps, *faces = together(grad_taps, *faces)
     edges = y_halos(grad, *faces)
-    x_mine = x_fwd.reshape(ny, -1, x_fwd.shape[1])
-    x_mine = lax.dynamic_index_in_dim(x_mine, lax.axis_index("gy"), 0, keepdims=False)
     block = swap(slab, ("gx", "gy"))
     block, grad_taps, *edges = together(block, grad_taps, *edges)
     mine = swap(grad_taps.reshape(nx, -1, 2 * c), "gx").sum(0)
@@ -833,10 +835,10 @@
     block = x_stage(
         x_inv, swap(jnp.concatenate([block, packed], axis=1), "gy"), nx, BF16, extra
     )
+    grad_modes = outer(modes_in, back_modes, spread, spectral_weight.shape, alpha)
+    block, grad_modes = together(block, grad_modes)
+    message = swap(block, "gx")
     stencil_back = conv(grad, (*faces, *edges), back_table, True)
-    block, stencil_back = together(block, stencil_back)
-    message = swap(block, "gx")
-    grad_modes = outer(modes_in, back_modes, spread, spectral_weight.shape, alpha)
     grad_state, grad_stencil, grad_point = call(
         functools.partial(finish_kernel, nx, alpha),
         [((c, cx, cy, z), F32), ((c, 27 * c), F32), ((c, c), F32)],

time: 133 us -> 133 us (level)
  starting transfers between devices: 49.3 us -> 46.5 us
  waiting for transfers between devices: 20.2 us -> 21.8 us
    all_to_all x7, starting transfers between devices: 31.4 us -> 27.5 us  [swap(): return lax.all_to_all(block, axis, split_axis=0, concat_axis=0, tiled=True)]
    ppermute x8, waiting for transfers between devices: 4.02 us -> 6.15 us  [shift(): return lax.ppermute(block, axis, pairs)]
where the time goes in v11:
time: 133 us; the launch traced here: 131 us
  starting transfers between devices  46.5 us (35%)
  Pallas kernels  45.8 us (34%)
  waiting for transfers between devices  21.8 us (16%)
  blocking collectives  11.9 us (9%)
  local copies, waits for them, and re-layouts  3.59 us (3%)
    all_to_all x7, starting transfers between devices, swap(): return lax.all_to_all(block, axis, split_axis=0, concat_axis=0, tiled=True)  27.5 us
    pallas_call x10, Pallas kernels, call(): pl.pallas_call(kernel, out_shape=[jax.ShapeDtypeStruct(*out) for out in o...  21 us
    ppermute x8, starting transfers between devices, shift(): return lax.ppermute(block, axis, pairs)  19 us
    pallas_call x2, Pallas kernels, per_mode(): pl.pallas_call(functools.partial(kernel, mz), in_specs=[whole(), pl.Block...  15.9 us
    all_to_all x7, waiting for transfers between devices, swap(): return lax.all_to_all(block, axis, split_axis=0, concat_axis=0, tiled=True)  15.6 us
    all_to_all x1, blocking collectives, swap(): return lax.all_to_all(block, axis, split_axis=0, concat_axis=0, tiled=True)  11.9 us
    pallas_call x1, Pallas kernels, outer(): pl.pallas_call(functools.partial(outer_kernel, alpha), grid=(modes.shape[...  8.86 us
    ppermute x8, waiting for transfers between devices, shift(): return lax.ppermute(block, axis, pairs)  6.15 us
  transfers between devices with their start and end apart: 15, of which 7 were waited for; matrix products, arithmetic and copies ran while one was open for 1% of the time, Pallas kernels for 28%

profile of v11, /device:TPU:0, one launch (start us, length us, event | category | flops | bytes accessed | tf_op | source)
XLA Modules:
  0.0 131.4 jit_solution(11484000651654740803)
XLA Ops:
  0.7 2.2 %shard_map.173 = (bf16[4,8,64,128]{3,2,1,0:T(8,128)(2,1)S(1)}, f32[8,16,512]{2,1,0:T(8,128)}) custom-call(bf16[64,4,8,128]{3,2,1,0:T(8,128)(2,1)} %field_ref.1, bf16[96,128]{1,0:T(8,128)(2,1)} %constant.30.clone.table_ref), custom_call_target="tpu_custom_call" | custom-call | flops 50331648 | bytes 1310720 | tf_op jit(solution)/shard_map/pallas_call | solution.py:618
  2.9 5.2 %all-to-all-start = ((f32[8,16,512]{2,1,0:T(8,128)}), f32[8,16,512]{2,1,0:T(8,128)S(1)}, u32[]{:S(2)}, u32[]{:S(2)}) async-start(f32[8,16,512]{2,1,0:T(8,128)} %get-tuple-element.38), calls=%async_computation | async-start | bytes 524288 | tf_op jit(solution)/shard_map/all_to_all | solution.py:729
  8.1 1.3 collective-permute-start.1
  9.4 3.0 %collective-permute-start = (bf16[8,64,128]{2,1,0:T(8,128)(2,1)S(1)}, bf16[8,64,128]{2,1,0:T(8,128)(2,1)S(1)}, u32[]{:S(2)}, u32[]{:S(2)}) collective-permute-start(bf16[8,64,128]{2,1,0:T(8,128)(2,1)S(1)} %get-tuple-element.76), channel_id=1, source_target_pairs={{0,4},{4,8},{8,12},{12,16},{16,20},{20,24},{24,28},{1,5},{5,9},{9,... | collective-permute-start | bytes 393224 | tf_op jit(solution)/shard_map/ppermute | solution.py:683
  12.5 1.5 %shard_map.175 = (bf16[576,256]{1,0:T(8,128)(2,1)S(1)}, bf16[576,256]{1,0:T(8,128)(2,1)S(1)}) custom-call(bf16[64,1728]{1,0:T(8,128)(2,1)} %taps_ref.1, bf16[64,64]{1,0:T(8,128)(2,1)} %point_ref.1), custom_call_target="tpu_custom_call" | custom-call | bytes 663552 | tf_op jit(solution)/shard_map/pallas_call | solution.py:618
  16.9 4.9 %all-to-all-start.1 = ((f32[4,32,512]{2,1,0:T(8,128)}), f32[4,32,512]{2,1,0:T(8,128)S(1)}, u32[]{:S(2)}, u32[]{:S(2)}) async-start(f32[4,32,512]{2,1,0:T(8,128)} %shard_map.174), calls=%async_computation.1 | async-start | bytes 524288 | tf_op jit(solution)/shard_map/all_to_all | solution.py:729
  21.8 3.9 %collective-permute-start.2 = (bf16[6,64,128]{2,1,0:T(8,128)(2,1)S(1)}, bf16[6,64,128]{2,1,0:T(8,128)(2,1)S(1)}, u32[]{:S(2)}, u32[]{:S(2)}) collective-permute-start(bf16[6,64,128]{2,1,0:T(8,128)(2,1)S(1)} %pad_maximum_fusion.1), channel_id=1, source_target_pairs={{0,1},{1,2},{2,3},{4,5},{5,6},{6,7},{8,9},{9,10},{10,11},{12,13},{... | collective-permute-start | bytes 294920 | tf_op jit(solution)/shard_map/ppermute | solution.py:683
  25.8 1.3 collective-permute-start.3
  27.1 4.8 %all-to-all-done.1.data_ref = f32[4,32,512]{2,1,0:T(8,128)S(1)} async-done(((f32[4,32,512]{2,1,0:T(8,128)}), f32[4,32,512]{2,1,0:T(8,128)S(1)}, u32[]{:S(2)}, u32[]{:S(2)}) %all-to-all-start.1) | async-done | bytes 262176 | tf_op jit(solution)/shard_map/all_to_all | solution.py:729
  32.7 7.9 %shard_map.176 = (bf16[4,256,128]{2,1,0:T(8,128)(2,1)S(1)}, f32[4,32,512]{2,1,0:T(8,128)S(1)}) custom-call(f32[4,32,512]{2,1,0:T(8,128)S(1)} %all-to-all-done.1.data_ref, bf16[2,2,8,32,4096]{4,3,2,1,0:T(8,128)(2,1)} %weight_ref.3, bf16[128,4096]{1,0:T(8,128)(2,1)} %constant.37.clone.table_ref, bf16[128,192]{1,0:T(8,128)(2,1)S(1)} %copy-done.3), custom_call_target="tpu_custom_call" | custom-call | flops 33554432 | bytes 8388608 | tf_op jit(solution)/shard_map/pallas_call | solution.py:638
  40.6 11.9 %all_to_all.40.data_ref = f32[4,32,512]{2,1,0:T(8,128)S(1)} all-to-all(f32[4,32,512]{2,1,0:T(8,128)S(1)} %get-tuple-element.48), channel_id=1, replica_groups=mesh['gx'=8,'gy'=4] {'gy'}, dimensions={0} | all-to-all | bytes 524288 | tf_op jit(solution)/shard_map/all_to_all | solution.py:729
  54.3 3.4 %all-to-all-start.3 = ((f32[8,16,512]{2,1,0:T(8,128)}), f32[8,16,512]{2,1,0:T(8,128)S(1)}, u32[]{:S(2)}, u32[]{:S(2)}) async-start(f32[8,16,512]{2,1,0:T(8,128)} %shard_map.178), calls=%async_computation.3 | async-start | bytes 524288 | tf_op jit(solution)/shard_map/all_to_all | solution.py:729
  57.8 3.1 %shard_map.177.stencil_ref = f32[4,64,1024]{2,1,0:T(8,128)S(1)} custom-call(bf16[4,8,64,128]{3,2,1,0:T(8,128)(2,1)S(1)} %get-tuple-element.37.body_ref, bf16[8,64,128]{2,1,0:T(8,128)(2,1)} %copy-done.14, bf16[8,64,128]{2,1,0:T(8,128)(2,1)} %copy-done.13, bf16[6,64,128]{2,1,0:T(8,128)(2,1)} %copy-done.17, bf16[6,64,128]{2,1,0:T(8,128)(2,1)} %copy-done.18, ...), custom_call_target="tpu_custom_call" | custom-call | flops 905969664 | bytes 2097152 | tf_op jit(solution)/shard_map/pallas_call | solution.py:618
  60.9 3.8 %all-to-all-done.3.slab_ref = f32[8,16,512]{2,1,0:T(8,128)S(1)} async-done(((f32[8,16,512]{2,1,0:T(8,128)}), f32[8,16,512]{2,1,0:T(8,128)S(1)}, u32[]{:S(2)}, u32[]{:S(2)}) %all-to-all-start.3) | async-done | bytes 262176 | tf_op jit(solution)/shard_map/all_to_all | solution.py:729
  64.6 2.4 %shard_map.179 = (bf16[64,4,8,128]{3,2,1,0:T(8,128)(2,1)}, bf16[4,8,64,128]{3,2,1,0:T(8,128)(2,1)S(1)}, bf16[32,16,512]{2,1,0:T(8,128)(2,1)}) custom-call(f32[4,64,1024]{2,1,0:T(8,128)S(1)} %shard_map.177.stencil_ref, f32[8,16,512]{2,1,0:T(8,128)S(1)} %all-to-all-done.3.slab_ref, bf16[64,4,8,128]{3,2,1,0:T(8,128)(2,1)S(1)} %copy-done, ...), custom_call_target="tpu_custom_call" | custom-call | flops 100663296 | bytes 3145728 | tf_op jit(solution)/shard_map/pallas_call | solution.py:618
  67.1 2.6 %all-to-all-start.4 = ((bf16[32,16,512]{2,1,0:T(8,128)(2,1)}), bf16[32,16,512]{2,1,0:T(8,128)(2,1)S(1)}, u32[]{:S(2)}, u32[]{:S(2)}) async-start(bf16[32,16,512]{2,1,0:T(8,128)(2,1)} %get-tuple-element.53), calls=%async_computation.4 | async-start | bytes 1048576 | tf_op jit(solution)/shard_map/all_to_all | solution.py:729
  69.7 1.3 collective-permute-start.5
  71.0 3.2 %collective-permute-start.4 = (bf16[8,64,128]{2,1,0:T(8,128)(2,1)S(1)}, bf16[8,64,128]{2,1,0:T(8,128)(2,1)S(1)}, u32[]{:S(2)}, u32[]{:S(2)}) collective-permute-start(bf16[8,64,128]{2,1,0:T(8,128)(2,1)S(1)} %get-tuple-element.72), channel_id=1, source_target_pairs={{0,4},{4,8},{8,12},{12,16},{16,20},{20,24},{24,28},{1,5},{5,9},{9,... | collective-permute-start | bytes 393224 | tf_op jit(solution)/shard_map/ppermute | solution.py:683
  74.3 4.1 %shard_map.180 = f32[1024,128]{1,0:T(8,128)} custom-call(bf16[4,8,64,128]{3,2,1,0:T(8,128)(2,1)S(1)} %get-tuple-element.50.grad_ref.body_ref, bf16[4,8,64,128]{3,2,1,0:T(8,128)(2,1)S(1)} %get-tuple-element.37.body_ref, bf16[8,64,128]{2,1,0:T(8,128)(2,1)} %copy-done.14, bf16[8,64,128]{2,1,0:T(8,128)(2,1)} %copy-done.13, bf16[6,64,128]{2,1,0:T(8,128)(2,1)} %copy-done.17, ...), custom_call_target="tpu_custom_call" | custom-call | flops 905969664 | bytes 2097152 | tf_op jit(solution)/shard_map/pallas_call | solution.py:618
  78.4 3.6 %collective-permute-start.6 = (bf16[6,64,128]{2,1,0:T(8,128)(2,1)S(1)}, bf16[6,64,128]{2,1,0:T(8,128)(2,1)S(1)}, u32[]{:S(2)}, u32[]{:S(2)}) collective-permute-start(bf16[6,64,128]{2,1,0:T(8,128)(2,1)S(1)} %pad_maximum_fusion.3), channel_id=1, source_target_pairs={{0,1},{1,2},{2,3},{4,5},{5,6},{6,7},{8,9},{9,10},{10,11},{12,13},{... | collective-permute-start | bytes 294920 | tf_op jit(solution)/shard_map/ppermute | solution.py:683
  82.0 1.3 collective-permute-start.7
  83.3 1.5 %collective-permute-done.6.ylo_ref = bf16[6,64,128]{2,1,0:T(8,128)(2,1)S(1)} collective-permute-done((bf16[6,64,128]{2,1,0:T(8,128)(2,1)S(1)}, bf16[6,64,128]{2,1,0:T(8,128)(2,1)S(1)}, u32[]{:S(2)}, u32[]{:S(2)}) %collective-permute-start.6) | collective-permute-done | bytes 98336 | tf_op jit(solution)/shard_map/ppermute | solution.py:683
  84.9 4.6 %collective-permute-done.7.yhi_ref = bf16[6,64,128]{2,1,0:T(8,128)(2,1)S(1)} collective-permute-done((bf16[6,64,128]{2,1,0:T(8,128)(2,1)S(1)}, bf16[6,64,128]{2,1,0:T(8,128)(2,1)S(1)}, u32[]{:S(2)}, u32[]{:S(2)}) %collective-permute-start.7) | collective-permute-done | bytes 98336 | tf_op jit(solution)/shard_map/ppermute | solution.py:683
  89.5 4.6 %all-to-all-start.5 = ((f32[8,128,128]{2,1,0:T(8,128)}), f32[8,128,128]{2,1,0:T(8,128)S(1)}, u32[]{:S(2)}, u32[]{:S(2)}) async-start(f32[8,128,128]{2,1,0:T(8,128)} %bitcast.9), calls=%async_computation.5 | async-start | bytes 1048576 | tf_op jit(solution)/shard_map/all_to_all | solution.py:729
  94.1 8.0 %shard_map.182 = (f32[4,256,128]{2,1,0:T(8,128)S(1)}, bf16[4,32,512]{2,1,0:T(8,128)(2,1)S(1)}) custom-call(bf16[32,16,512]{2,1,0:T(8,128)(2,1)S(1)} %all-to-all-done.4.data_ref, bf16[2,2,8,32,4096]{4,3,2,1,0:T(8,128)(2,1)} %weight_ref.3, bf16[8,512]{1,0:T(8,128)(2,1)} %constant.38.clone.table_ref, bf16[128,192]{1,0:T(8,128)(2,1)S(1)} %copy-done.4, ...), custom_call_target="tpu_custom_call" | custom-call | flops 33554432 | bytes 8388608 | tf_op jit(solution)/shard_map/pallas_call | solution.py:638
  102.1 1.7 %all-to-all-done.5 = f32[8,128,128]{2,1,0:T(8,128)S(1)} async-done(((f32[8,128,128]{2,1,0:T(8,128)}), f32[8,128,128]{2,1,0:T(8,128)S(1)}, u32[]{:S(2)}, u32[]{:S(2)}) %all-to-all-start.5) | async-done | bytes 524320 | tf_op jit(solution)/shard_map/all_to_all | solution.py:729
  104.6 3.4 %all-to-all-start.6 = ((bf16[4,64,512]{2,1,0:T(8,128)(2,1)}), bf16[4,64,512]{2,1,0:T(8,128)(2,1)S(1)}, u32[]{:S(2)}, u32[]{:S(2)}) async-start(bf16[4,64,512]{2,1,0:T(8,128)(2,1)} %pad_maximum_fusion), calls=%async_computation.6 | async-start | bytes 524288 | tf_op jit(solution)/shard_map/all_to_all | solution.py:729
  108.0 8.9 %shard_map.184 = f32[2,2,8,32,4096]{4,3,2,1,0:T(8,128)} custom-call(bf16[4,256,128]{2,1,0:T(8,128)(2,1)S(1)} %get-tuple-element.62.modes_ref, f32[4,256,128]{2,1,0:T(8,128)S(1)} %get-tuple-element.63.back_ref, bf16[128,4096]{1,0:T(8,128)(2,1)} %constant.37.clone.table_ref), custom_call_target="tpu_custom_call" | custom-call | flops 16777216 | bytes 16777216 | tf_op jit(solution)/shard_map/pallas_call | solution.py:667
  117.9 3.5 %all-to-all-start.7 = ((bf16[8,48,512]{2,1,0:T(8,128)(2,1)}), bf16[8,48,512]{2,1,0:T(8,128)(2,1)S(1)}, u32[]{:S(2)}, u32[]{:S(2)}) async-start(bf16[8,48,512]{2,1,0:T(8,128)(2,1)} %shard_map.183), calls=%async_computation.7 | async-start | bytes 786432 | tf_op jit(solution)/shard_map/all_to_all | solution.py:729
  121.4 3.0 %shard_map.181.stencil_ref = f32[4,64,1024]{2,1,0:T(8,128)S(1)} custom-call(bf16[4,8,64,128]{3,2,1,0:T(8,128)(2,1)S(1)} %get-tuple-element.50.grad_ref.body_ref, bf16[8,64,128]{2,1,0:T(8,128)(2,1)} %copy-done.12, bf16[8,64,128]{2,1,0:T(8,128)(2,1)} %copy-done.11, bf16[6,64,128]{2,1,0:T(8,128)(2,1)} %copy-done.15, bf16[6,64,128]{2,1,0:T(8,128)(2,1)} %copy-done.16, ...), custom_call_target="tpu_custom_call" | custom-call | flops 905969664 | bytes 2097152 | tf_op jit(solution)/shard_map/pallas_call | solution.py:618
  124.4 5.2 %all-to-all-done.7.message_ref = bf16[8,48,512]{2,1,0:T(8,128)(2,1)S(1)} async-done(((bf16[8,48,512]{2,1,0:T(8,128)(2,1)}), bf16[8,48,512]{2,1,0:T(8,128)(2,1)S(1)}, u32[]{:S(2)}, u32[]{:S(2)}) %all-to-all-start.7) | async-done | bytes 393248 | tf_op jit(solution)/shard_map/all_to_all | solution.py:729
  129.6 1.8 %shard_map.185 = (f32[64,4,8,128]{3,2,1,0:T(8,128)}, f32[64,1728]{1,0:T(8,128)}, f32[64,64]{1,0:T(8,128)}) custom-call(f32[4,64,1024]{2,1,0:T(8,128)S(1)} %shard_map.181.stencil_ref, bf16[8,48,512]{2,1,0:T(8,128)(2,1)S(1)} %all-to-all-done.7.message_ref, bf16[96,128]{1,0:T(8,128)(2,1)S(1)} %copy-done.8), custom_call_target="tpu_custom_call" | custom-call | flops 50331648 | bytes 2621440 | tf_op jit(solution)/shard_map/pallas_call | solution.py:618
  (67 shorter events, 7.5 us)
Async XLA Ops:
  0.6 93.4 %copy-start.4 = (bf16[128,192]{1,0:T(8,128)(2,1)S(1)}, bf16[128,192]{1,0:T(8,128)(2,1)}, u32[]{:S(2)}) copy-start(bf16[128,192]{1,0:T(8,128)(2,1)} %constant.36.clone.turn_ref) | copy-start | bytes 147460
  0.6 64.0 %copy-start.6 = (bf16[96,128]{1,0:T(8,128)(2,1)S(1)}, bf16[96,128]{1,0:T(8,128)(2,1)}, u32[]{:S(2)}) copy-start(bf16[96,128]{1,0:T(8,128)(2,1)} %constant.32.clone.inverse_ref) | copy-start | bytes 73732
  0.7 64.0 %copy-start.7 = (bf16[96,128]{1,0:T(8,128)(2,1)S(1)}, bf16[96,128]{1,0:T(8,128)(2,1)}, u32[]{:S(2)}) copy-start(bf16[96,128]{1,0:T(8,128)(2,1)} %constant.31.clone.forward_ref) | copy-start | bytes 73732
  0.7 64.0 %copy-start = (bf16[64,4,8,128]{3,2,1,0:T(8,128)(2,1)S(1)}, bf16[64,4,8,128]{3,2,1,0:T(8,128)(2,1)}, u32[]{:S(2)}) copy-start(bf16[64,4,8,128]{3,2,1,0:T(8,128)(2,1)} %cot_ref.1) | copy-start | bytes 1572868
  2.9 12.1 %all-to-all-start = ((f32[8,16,512]{2,1,0:T(8,128)}), f32[8,16,512]{2,1,0:T(8,128)S(1)}, u32[]{:S(2)}, u32[]{:S(2)}) async-start(f32[8,16,512]{2,1,0:T(8,128)} %get-tuple-element.38), calls=%async_computation | async-start | bytes 524288 | tf_op jit(solution)/shard_map/all_to_all | solution.py:729
  8.1 8.7 %collective-permute-start.1 = (bf16[8,64,128]{2,1,0:T(8,128)(2,1)S(1)}, bf16[8,64,128]{2,1,0:T(8,128)(2,1)S(1)}, u32[]{:S(2)}, u32[]{:S(2)}) collective-permute-start(bf16[8,64,128]{2,1,0:T(8,128)(2,1)S(1)} %get-tuple-element.75), channel_id=1, source_target_pairs={{4,0},{8,4},{12,8},{16,12},{20,16},{24,20},{28,24},{5,1},{9,5},{13... | collective-permute-start | bytes 393224 | tf_op jit(solution)/shard_map/ppermute | solution.py:683
  9.4 7.5 %collective-permute-start = (bf16[8,64,128]{2,1,0:T(8,128)(2,1)S(1)}, bf16[8,64,128]{2,1,0:T(8,128)(2,1)S(1)}, u32[]{:S(2)}, u32[]{:S(2)}) collective-permute-start(bf16[8,64,128]{2,1,0:T(8,128)(2,1)S(1)} %get-tuple-element.76), channel_id=1, source_target_pairs={{0,4},{4,8},{8,12},{12,16},{16,20},{20,24},{24,28},{1,5},{5,9},{9,... | collective-permute-start | bytes 393224 | tf_op jit(solution)/shard_map/ppermute | solution.py:683
  14.0 13.0 %copy-start.9 = (bf16[576,256]{1,0:T(8,128)(2,1)}, bf16[576,256]{1,0:T(8,128)(2,1)S(1)}, u32[]{:S(2)}) copy-start(bf16[576,256]{1,0:T(8,128)(2,1)S(1)} %get-tuple-element.57.weight_ref) | copy-start | bytes 884740
  14.0 13.0 %copy-start.10 = (bf16[576,256]{1,0:T(8,128)(2,1)}, bf16[576,256]{1,0:T(8,128)(2,1)S(1)}, u32[]{:S(2)}) copy-start(bf16[576,256]{1,0:T(8,128)(2,1)S(1)} %get-tuple-element.47.weight_ref) | copy-start | bytes 884740
  15.0 0.9 copy-start.5
  16.9 40.9 %copy-start.13 = (bf16[8,64,128]{2,1,0:T(8,128)(2,1)}, bf16[8,64,128]{2,1,0:T(8,128)(2,1)S(1)}, u32[]{:S(2)}) copy-start(bf16[8,64,128]{2,1,0:T(8,128)(2,1)S(1)} %collective-permute-done.1.xhi_ref.xhi_any) | copy-start | bytes 393220
  16.9 40.9 %copy-start.14 = (bf16[8,64,128]{2,1,0:T(8,128)(2,1)}, bf16[8,64,128]{2,1,0:T(8,128)(2,1)S(1)}, u32[]{:S(2)}) copy-start(bf16[8,64,128]{2,1,0:T(8,128)(2,1)S(1)} %collective-permute-done.xlo_ref.xlo_any) | copy-start | bytes 393220
  16.9 15.0 %all-to-all-start.1 = ((f32[4,32,512]{2,1,0:T(8,128)}), f32[4,32,512]{2,1,0:T(8,128)S(1)}, u32[]{:S(2)}, u32[]{:S(2)}) async-start(f32[4,32,512]{2,1,0:T(8,128)} %shard_map.174), calls=%async_computation.1 | async-start | bytes 524288 | tf_op jit(solution)/shard_map/all_to_all | solution.py:729
  21.8 18.8 %collective-permute-start.2 = (bf16[6,64,128]{2,1,0:T(8,128)(2,1)S(1)}, bf16[6,64,128]{2,1,0:T(8,128)(2,1)S(1)}, u32[]{:S(2)}, u32[]{:S(2)}) collective-permute-start(bf16[6,64,128]{2,1,0:T(8,128)(2,1)S(1)} %pad_maximum_fusion.1), channel_id=1, source_target_pairs={{0,1},{1,2},{2,3},{4,5},{5,6},{6,7},{8,9},{9,10},{10,11},{12,13},{... | collective-permute-start | bytes 294920 | tf_op jit(solution)/shard_map/ppermute | solution.py:683
  25.8 14.8 %collective-permute-start.3 = (bf16[6,64,128]{2,1,0:T(8,128)(2,1)S(1)}, bf16[6,64,128]{2,1,0:T(8,128)(2,1)S(1)}, u32[]{:S(2)}, u32[]{:S(2)}) collective-permute-start(bf16[6,64,128]{2,1,0:T(8,128)(2,1)S(1)} %pad_maximum_fusion.2), channel_id=1, source_target_pairs={{1,0},{2,1},{3,2},{5,4},{6,5},{7,6},{9,8},{10,9},{11,10},{13,12},{... | collective-permute-start | bytes 294920 | tf_op jit(solution)/shard_map/ppermute | solution.py:683
  40.6 13.8 %copy-start.17 = (bf16[6,64,128]{2,1,0:T(8,128)(2,1)}, bf16[6,64,128]{2,1,0:T(8,128)(2,1)S(1)}, u32[]{:S(2)}) copy-start(bf16[6,64,128]{2,1,0:T(8,128)(2,1)S(1)} %collective-permute-done.2.ylo_ref.ylo_any) | copy-start | bytes 294916
  40.6 13.7 %copy-start.18 = (bf16[6,64,128]{2,1,0:T(8,128)(2,1)}, bf16[6,64,128]{2,1,0:T(8,128)(2,1)S(1)}, u32[]{:S(2)}) copy-start(bf16[6,64,128]{2,1,0:T(8,128)(2,1)S(1)} %collective-permute-done.3.yhi_ref.yhi_any) | copy-start | bytes 294916
  54.3 10.3 %all-to-all-start.3 = ((f32[8,16,512]{2,1,0:T(8,128)}), f32[8,16,512]{2,1,0:T(8,128)S(1)}, u32[]{:S(2)}, u32[]{:S(2)}) async-start(f32[8,16,512]{2,1,0:T(8,128)} %shard_map.178), calls=%async_computation.3 | async-start | bytes 524288 | tf_op jit(solution)/shard_map/all_to_all | solution.py:729
  67.1 22.4 %all-to-all-start.4 = ((bf16[32,16,512]{2,1,0:T(8,128)(2,1)}), bf16[32,16,512]{2,1,0:T(8,128)(2,1)S(1)}, u32[]{:S(2)}, u32[]{:S(2)}) async-start(bf16[32,16,512]{2,1,0:T(8,128)(2,1)} %get-tuple-element.53), calls=%async_computation.4 | async-start | bytes 1048576 | tf_op jit(solution)/shard_map/all_to_all | solution.py:729
  69.7 8.6 %collective-permute-start.5 = (bf16[8,64,128]{2,1,0:T(8,128)(2,1)S(1)}, bf16[8,64,128]{2,1,0:T(8,128)(2,1)S(1)}, u32[]{:S(2)}, u32[]{:S(2)}) collective-permute-start(bf16[8,64,128]{2,1,0:T(8,128)(2,1)S(1)} %get-tuple-element.71), channel_id=1, source_target_pairs={{4,0},{8,4},{12,8},{16,12},{20,16},{24,20},{28,24},{5,1},{9,5},{13... | collective-permute-start | bytes 393224 | tf_op jit(solution)/shard_map/ppermute | solution.py:683
  71.0 7.3 %collective-permute-start.4 = (bf16[8,64,128]{2,1,0:T(8,128)(2,1)S(1)}, bf16[8,64,128]{2,1,0:T(8,128)(2,1)S(1)}, u32[]{:S(2)}, u32[]{:S(2)}) collective-permute-start(bf16[8,64,128]{2,1,0:T(8,128)(2,1)S(1)} %get-tuple-element.72), channel_id=1, source_target_pairs={{0,4},{4,8},{8,12},{12,16},{16,20},{20,24},{24,28},{1,5},{5,9},{9,... | collective-permute-start | bytes 393224 | tf_op jit(solution)/shard_map/ppermute | solution.py:683
  74.2 42.6 %copy-start.2 = (bf16[128,384]{1,0:T(8,128)(2,1)S(1)}, bf16[128,384]{1,0:T(8,128)(2,1)}, u32[]{:S(2)}) copy-start(bf16[128,384]{1,0:T(8,128)(2,1)} %constant.35.clone.table_ref) | copy-start | bytes 294916
  78.3 43.0 %copy-start.11 = (bf16[8,64,128]{2,1,0:T(8,128)(2,1)}, bf16[8,64,128]{2,1,0:T(8,128)(2,1)S(1)}, u32[]{:S(2)}) copy-start(bf16[8,64,128]{2,1,0:T(8,128)(2,1)S(1)} %collective-permute-done.5.xhi_ref) | copy-start | bytes 393220
  78.4 43.0 %copy-start.12 = (bf16[8,64,128]{2,1,0:T(8,128)(2,1)}, bf16[8,64,128]{2,1,0:T(8,128)(2,1)S(1)}, u32[]{:S(2)}) copy-start(bf16[8,64,128]{2,1,0:T(8,128)(2,1)S(1)} %collective-permute-done.4.xlo_ref) | copy-start | bytes 393220
  78.4 6.4 %collective-permute-start.6 = (bf16[6,64,128]{2,1,0:T(8,128)(2,1)S(1)}, bf16[6,64,128]{2,1,0:T(8,128)(2,1)S(1)}, u32[]{:S(2)}, u32[]{:S(2)}) collective-permute-start(bf16[6,64,128]{2,1,0:T(8,128)(2,1)S(1)} %pad_maximum_fusion.3), channel_id=1, source_target_pairs={{0,1},{1,2},{2,3},{4,5},{5,6},{6,7},{8,9},{9,10},{10,11},{12,13},{... | collective-permute-start | bytes 294920 | tf_op jit(solution)/shard_map/ppermute | solution.py:683
  82.0 7.4 %collective-permute-start.7 = (bf16[6,64,128]{2,1,0:T(8,128)(2,1)S(1)}, bf16[6,64,128]{2,1,0:T(8,128)(2,1)S(1)}, u32[]{:S(2)}, u32[]{:S(2)}) collective-permute-start(bf16[6,64,128]{2,1,0:T(8,128)(2,1)S(1)} %pad_maximum_fusion.4), channel_id=1, source_target_pairs={{1,0},{2,1},{3,2},{5,4},{6,5},{7,6},{9,8},{10,9},{11,10},{13,12},{... | collective-permute-start | bytes 294920 | tf_op jit(solution)/shard_map/ppermute | solution.py:683
  84.9 36.5 %copy-start.15 = (bf16[6,64,128]{2,1,0:T(8,128)(2,1)}, bf16[6,64,128]{2,1,0:T(8,128)(2,1)S(1)}, u32[]{:S(2)}) copy-start(bf16[6,64,128]{2,1,0:T(8,128)(2,1)S(1)} %collective-permute-done.6.ylo_ref) | copy-start | bytes 294916
  89.5 31.9 %copy-start.16 = (bf16[6,64,128]{2,1,0:T(8,128)(2,1)}, bf16[6,64,128]{2,1,0:T(8,128)(2,1)S(1)}, u32[]{:S(2)}) copy-start(bf16[6,64,128]{2,1,0:T(8,128)(2,1)S(1)} %collective-permute-done.7.yhi_ref) | copy-start | bytes 294916
  89.5 14.3 %all-to-all-start.5 = ((f32[8,128,128]{2,1,0:T(8,128)}), f32[8,128,128]{2,1,0:T(8,128)S(1)}, u32[]{:S(2)}, u32[]{:S(2)}) async-start(f32[8,128,128]{2,1,0:T(8,128)} %bitcast.9), calls=%async_computation.5 | async-start | bytes 1048576 | tf_op jit(solution)/shard_map/all_to_all | solution.py:729
  94.1 35.5 %copy-start.8 = (bf16[96,128]{1,0:T(8,128)(2,1)S(1)}, bf16[96,128]{1,0:T(8,128)(2,1)}, u32[]{:S(2)}) copy-start(bf16[96,128]{1,0:T(8,128)(2,1)} %constant.33.clone.inverse_ref) | copy-start | bytes 73732
  104.6 12.3 %all-to-all-start.6 = ((bf16[4,64,512]{2,1,0:T(8,128)(2,1)}), bf16[4,64,512]{2,1,0:T(8,128)(2,1)S(1)}, u32[]{:S(2)}, u32[]{:S(2)}) async-start(bf16[4,64,512]{2,1,0:T(8,128)(2,1)} %pad_maximum_fusion), calls=%async_computation.6 | async-start | bytes 524288 | tf_op jit(solution)/shard_map/all_to_all | solution.py:729
  117.9 11.7 %all-to-all-start.7 = ((bf16[8,48,512]{2,1,0:T(8,128)(2,1)}), bf16[8,48,512]{2,1,0:T(8,128)(2,1)S(1)}, u32[]{:S(2)}, u32[]{:S(2)}) async-start(bf16[8,48,512]{2,1,0:T(8,128)(2,1)} %shard_map.183), calls=%async_computation.7 | async-start | bytes 786432 | tf_op jit(solution)/shard_map/all_to_all | solution.py:729
  (2 other events, 1.7 us)

commit v12 on v11

--- a/solution.py
+++ b/solution.py
@@ -116,7 +116,22 @@
     )
 
 
-def prep_kernel(nx, field_ref, table_ref, turned_ref, slab_ref):
+def prep_kernel(
+    nx,
+    field_ref,
+    table_ref,
+    forward_ref,
+    inverse_ref,
+    turn_ref,
+    turned_ref,
+    slab_ref,
+    forward_out_ref,
+    inverse_out_ref,
+    turn_out_ref,
+):
+    forward_out_ref[...] = forward_ref[...]
+    inverse_out_ref[...] = inverse_ref[...]
+    turn_out_ref[...] = turn_ref[...]
     c, cx, cy, z = field_ref.shape
     for x in range(cx):
         block = jnp.swapaxes(field_ref[:, x].astype(F32), 0, 1)
@@ -773,15 +788,17 @@
         [pltpu.VMEM((27 * c, c), F32)],
         moved=stencil_weight.size * 6,
     )
-    turned, slab = call(
+    tables = (x_fwd, x_inv, y_turn)
+    turned, slab, *held = call(
         functools.partial(prep_kernel, nx),
-        [turned_shape, slab_shape],
-        (in_hbm(state), in_hbm(z_state)),
+        [turned_shape, slab_shape] + [(t.shape, BF16) for t in tables],
+        (in_hbm(state), in_hbm(z_state), *map(in_hbm, tables)),
         flops=2 * 96 * state.size,
         moved=state.size * 5,
     )
     x_mine = x_fwd.reshape(ny, -1, x_fwd.shape[1])
     x_mine = lax.dynamic_index_in_dim(x_mine, lax.axis_index("gy"), 0, keepdims=False)
+    x_fwd, x_inv, y_turn = held
 
     block = x_stage(x_fwd, swap(slab, "gx"), ny)
     block, conv_table, back_table, x_mine, *faces = together(
@@ -814,10 +831,8 @@
 
     grad_taps = weight_grad(grad, turned, rim)
     faces = x_halos(grad)
-    grad_taps, *faces = together(grad_taps, *faces)
-    edges = y_halos(grad, *faces)
     block = swap(slab, ("gx", "gy"))
-    block, grad_taps, *edges = together(block, grad_taps, *edges)
+    block, grad_taps, *faces = together(block, grad_taps, *faces)
     mine = swap(grad_taps.reshape(nx, -1, 2 * c), "gx").sum(0)
     back_modes, block = per_mode(
         mix_back_kernel,
@@ -836,8 +851,9 @@
         x_inv, swap(jnp.concatenate([block, packed], axis=1), "gy"), nx, BF16, extra
     )
     grad_modes = outer(modes_in, back_modes, spread, spectral_weight.shape, alpha)
-    block, grad_modes = together(block, grad_modes)
+    block, grad_modes, *faces = together(block, grad_modes, *faces)
     message = swap(block, "gx")
+    edges = y_halos(grad, *faces)
     stencil_back = conv(grad, (*faces, *edges), back_table, True)
     grad_state, grad_stencil, grad_point = call(
         functools.partial(finish_kernel, nx, alpha),

time: 133 us -> 133 us (level)
  local copies, waits for them, and re-layouts: 3.59 us -> 1.57 us
    unnamed x38 -> x28, local copies, waits for them, and re-layouts: 2.71 us -> 0.69 us
where the time goes in v12:
time: 133 us; the launch traced here: 131 us
  starting transfers between devices  47.3 us (36%)
  Pallas kernels  45.8 us (34%)
  waiting for transfers between devices  21.7 us (16%)
  blocking collectives  11.9 us (9%)
  other arithmetic  1.87 us (1%)
  local copies, waits for them, and re-layouts  1.57 us (1%)
    all_to_all x7, starting transfers between devices, swap(): return lax.all_to_all(block, axis, split_axis=0, concat_axis=0, tiled=True)  28 us
    pallas_call x10, Pallas kernels, call(): pl.pallas_call(kernel, out_shape=[jax.ShapeDtypeStruct(*out) for out in o...  21.1 us
    ppermute x8, starting transfers between devices, shift(): return lax.ppermute(block, axis, pairs)  19.3 us
    all_to_all x7, waiting for transfers between devices, swap(): return lax.all_to_all(block, axis, split_axis=0, concat_axis=0, tiled=True)  16.3 us
    pallas_call x2, Pallas kernels, per_mode(): pl.pallas_call(functools.partial(kernel, mz), in_specs=[whole(), pl.Block...  15.9 us
    all_to_all x1, blocking collectives, swap(): return lax.all_to_all(block, axis, split_axis=0, concat_axis=0, tiled=True)  11.9 us
    pallas_call x1, Pallas kernels, outer(): pl.pallas_call(functools.partial(outer_kernel, alpha), grid=(modes.shape[...  8.86 us
    ppermute x8, waiting for transfers between devices, shift(): return lax.ppermute(block, axis, pairs)  5.39 us
  transfers between devices with their start and end apart: 15, of which 7 were waited for; matrix products, arithmetic and copies ran while one was open for 1% of the time, Pallas kernels for 28%

profile of v12, /device:TPU:0, one launch (start us, length us, event | category | flops | bytes accessed | tf_op | source)
XLA Modules:
  0.0 131.2 jit_solution(5431751147242997393)
XLA Ops:
  0.7 2.3 %shard_map.173 = (bf16[4,8,64,128]{3,2,1,0:T(8,128)(2,1)S(1)}, f32[8,16,512]{2,1,0:T(8,128)}, bf16[128,384]{1,0:T(8,128)(2,1)S(1)}, bf16[128,384]{1,0:T(8,128)(2,1)S(1)}, bf16[128,192]{1,0:T(8,128)(2,1)S(1)}) custom-call(bf16[64,4,8,128]{3,2,1,0:T(8,128)(2,1)} %field_ref.1, bf16[96,128]{1,0:T(8,128)(2,1)} %constant.30.clone.table_ref, ...), custom_call_target="tpu_custom_call" | custom-call | flops 50331648 | bytes 1310720 | tf_op jit(solution)/shard_map/pallas_call | solution.py:633
  3.0 5.2 %all-to-all-start = ((f32[8,16,512]{2,1,0:T(8,128)}), f32[8,16,512]{2,1,0:T(8,128)S(1)}, u32[]{:S(2)}, u32[]{:S(2)}) async-start(f32[8,16,512]{2,1,0:T(8,128)} %get-tuple-element.41), calls=%async_computation | async-start | bytes 524288 | tf_op jit(solution)/shard_map/all_to_all | solution.py:744
  8.2 1.3 collective-permute-start.1
  9.5 3.0 %collective-permute-start = (bf16[8,64,128]{2,1,0:T(8,128)(2,1)S(1)}, bf16[8,64,128]{2,1,0:T(8,128)(2,1)S(1)}, u32[]{:S(2)}, u32[]{:S(2)}) collective-permute-start(bf16[8,64,128]{2,1,0:T(8,128)(2,1)S(1)} %get-tuple-element.80), channel_id=1, source_target_pairs={{0,4},{4,8},{8,12},{12,16},{16,20},{20,24},{24,28},{1,5},{5,9},{9,... | collective-permute-start | bytes 393224 | tf_op jit(solution)/shard_map/ppermute | solution.py:698
  12.6 1.5 %shard_map.175 = (bf16[576,256]{1,0:T(8,128)(2,1)S(1)}, bf16[576,256]{1,0:T(8,128)(2,1)S(1)}) custom-call(bf16[64,1728]{1,0:T(8,128)(2,1)} %taps_ref.1, bf16[64,64]{1,0:T(8,128)(2,1)} %point_ref.1), custom_call_target="tpu_custom_call" | custom-call | bytes 663552 | tf_op jit(solution)/shard_map/pallas_call | solution.py:633
  16.1 4.9 %all-to-all-start.1 = ((f32[4,32,512]{2,1,0:T(8,128)}), f32[4,32,512]{2,1,0:T(8,128)S(1)}, u32[]{:S(2)}, u32[]{:S(2)}) async-start(f32[4,32,512]{2,1,0:T(8,128)} %shard_map.174), calls=%async_computation.1 | async-start | bytes 524288 | tf_op jit(solution)/shard_map/all_to_all | solution.py:744
  21.0 3.9 %collective-permute-start.2 = (bf16[6,64,128]{2,1,0:T(8,128)(2,1)S(1)}, bf16[6,64,128]{2,1,0:T(8,128)(2,1)S(1)}, u32[]{:S(2)}, u32[]{:S(2)}) collective-permute-start(bf16[6,64,128]{2,1,0:T(8,128)(2,1)S(1)} %pad_maximum_fusion.1), channel_id=1, source_target_pairs={{0,1},{1,2},{2,3},{4,5},{5,6},{6,7},{8,9},{9,10},{10,11},{12,13},{... | collective-permute-start | bytes 294920 | tf_op jit(solution)/shard_map/ppermute | solution.py:698
  24.9 1.3 collective-permute-start.3
  26.2 4.8 %all-to-all-done.1.data_ref = f32[4,32,512]{2,1,0:T(8,128)S(1)} async-done(((f32[4,32,512]{2,1,0:T(8,128)}), f32[4,32,512]{2,1,0:T(8,128)S(1)}, u32[]{:S(2)}, u32[]{:S(2)}) %all-to-all-start.1) | async-done | bytes 262176 | tf_op jit(solution)/shard_map/all_to_all | solution.py:744
  31.0 7.9 %shard_map.176 = (bf16[4,256,128]{2,1,0:T(8,128)(2,1)S(1)}, f32[4,32,512]{2,1,0:T(8,128)S(1)}) custom-call(f32[4,32,512]{2,1,0:T(8,128)S(1)} %all-to-all-done.1.data_ref, bf16[2,2,8,32,4096]{4,3,2,1,0:T(8,128)(2,1)} %weight_ref.3, bf16[128,4096]{1,0:T(8,128)(2,1)} %constant.37.clone.table_ref, bf16[128,192]{1,0:T(8,128)(2,1)S(1)} %get-tuple-element.47.turn_ref), custom_call_target="tpu_custom_call" | custom-call | flops 33554432 | bytes 8388608 | tf_op jit(solution)/shard_map/pallas_call | solution.py:653
  39.0 11.9 %all_to_all.40.data_ref = f32[4,32,512]{2,1,0:T(8,128)S(1)} all-to-all(f32[4,32,512]{2,1,0:T(8,128)S(1)} %get-tuple-element.53), channel_id=1, replica_groups=mesh['gx'=8,'gy'=4] {'gy'}, dimensions={0} | all-to-all | bytes 524288 | tf_op jit(solution)/shard_map/all_to_all | solution.py:744
  51.8 3.7 %all-to-all-start.3 = ((f32[8,16,512]{2,1,0:T(8,128)}), f32[8,16,512]{2,1,0:T(8,128)S(1)}, u32[]{:S(2)}, u32[]{:S(2)}) async-start(f32[8,16,512]{2,1,0:T(8,128)} %shard_map.178), calls=%async_computation.3 | async-start | bytes 524288 | tf_op jit(solution)/shard_map/all_to_all | solution.py:744
  55.6 3.1 %shard_map.177.stencil_ref = f32[4,64,1024]{2,1,0:T(8,128)S(1)} custom-call(bf16[4,8,64,128]{3,2,1,0:T(8,128)(2,1)S(1)} %get-tuple-element.39.body_ref, bf16[8,64,128]{2,1,0:T(8,128)(2,1)} %copy-done.9, bf16[8,64,128]{2,1,0:T(8,128)(2,1)} %copy-done.8, bf16[6,64,128]{2,1,0:T(8,128)(2,1)} %copy-done.10, bf16[6,64,128]{2,1,0:T(8,128)(2,1)} %copy-done.11, ...), custom_call_target="tpu_custom_call" | custom-call | flops 905969664 | bytes 2097152 | tf_op jit(solution)/shard_map/pallas_call | solution.py:633
  58.6 3.9 %all-to-all-done.3.slab_ref = f32[8,16,512]{2,1,0:T(8,128)S(1)} async-done(((f32[8,16,512]{2,1,0:T(8,128)}), f32[8,16,512]{2,1,0:T(8,128)S(1)}, u32[]{:S(2)}, u32[]{:S(2)}) %all-to-all-start.3) | async-done | bytes 262176 | tf_op jit(solution)/shard_map/all_to_all | solution.py:744
  62.5 2.4 %shard_map.179 = (bf16[64,4,8,128]{3,2,1,0:T(8,128)(2,1)}, bf16[4,8,64,128]{3,2,1,0:T(8,128)(2,1)S(1)}, bf16[32,16,512]{2,1,0:T(8,128)(2,1)}) custom-call(f32[4,64,1024]{2,1,0:T(8,128)S(1)} %shard_map.177.stencil_ref, f32[8,16,512]{2,1,0:T(8,128)S(1)} %all-to-all-done.3.slab_ref, bf16[64,4,8,128]{3,2,1,0:T(8,128)(2,1)S(1)} %copy-done, ...), custom_call_target="tpu_custom_call" | custom-call | flops 100663296 | bytes 3145728 | tf_op jit(solution)/shard_map/pallas_call | solution.py:633
  64.9 2.6 %all-to-all-start.4 = ((bf16[32,16,512]{2,1,0:T(8,128)(2,1)}), bf16[32,16,512]{2,1,0:T(8,128)(2,1)S(1)}, u32[]{:S(2)}, u32[]{:S(2)}) async-start(bf16[32,16,512]{2,1,0:T(8,128)(2,1)} %get-tuple-element.56), calls=%async_computation.4 | async-start | bytes 1048576 | tf_op jit(solution)/shard_map/all_to_all | solution.py:744
  67.6 1.3 collective-permute-start.5
  68.9 3.2 %collective-permute-start.4 = (bf16[8,64,128]{2,1,0:T(8,128)(2,1)S(1)}, bf16[8,64,128]{2,1,0:T(8,128)(2,1)S(1)}, u32[]{:S(2)}, u32[]{:S(2)}) collective-permute-start(bf16[8,64,128]{2,1,0:T(8,128)(2,1)S(1)} %get-tuple-element.76), channel_id=1, source_target_pairs={{0,4},{4,8},{8,12},{12,16},{16,20},{20,24},{24,28},{1,5},{5,9},{9,... | collective-permute-start | bytes 393224 | tf_op jit(solution)/shard_map/ppermute | solution.py:698
  72.1 4.0 %shard_map.180 = f32[1024,128]{1,0:T(8,128)} custom-call(bf16[4,8,64,128]{3,2,1,0:T(8,128)(2,1)S(1)} %get-tuple-element.55.grad_ref.body_ref, bf16[4,8,64,128]{3,2,1,0:T(8,128)(2,1)S(1)} %get-tuple-element.39.body_ref, bf16[8,64,128]{2,1,0:T(8,128)(2,1)} %copy-done.9, bf16[8,64,128]{2,1,0:T(8,128)(2,1)} %copy-done.8, bf16[6,64,128]{2,1,0:T(8,128)(2,1)} %copy-done.10, ...), custom_call_target="tpu_custom_call" | custom-call | flops 905969664 | bytes 2097152 | tf_op jit(solution)/shard_map/pallas_call | solution.py:633
  76.2 5.7 %all-to-all-done.4.data_ref = bf16[32,16,512]{2,1,0:T(8,128)(2,1)S(1)} async-done(((bf16[32,16,512]{2,1,0:T(8,128)(2,1)}), bf16[32,16,512]{2,1,0:T(8,128)(2,1)S(1)}, u32[]{:S(2)}, u32[]{:S(2)}) %all-to-all-start.4) | async-done | bytes 524320 | tf_op jit(solution)/shard_map/all_to_all | solution.py:744
  81.9 4.1 %all-to-all-start.5 = ((f32[8,128,128]{2,1,0:T(8,128)}), f32[8,128,128]{2,1,0:T(8,128)}, u32[]{:S(2)}, u32[]{:S(2)}) async-start(f32[8,128,128]{2,1,0:T(8,128)} %bitcast.7), calls=%async_computation.5 | async-start | bytes 1048576 | tf_op jit(solution)/shard_map/all_to_all | solution.py:744
  86.1 8.0 %shard_map.181 = (f32[4,256,128]{2,1,0:T(8,128)S(1)}, bf16[4,32,512]{2,1,0:T(8,128)(2,1)S(1)}) custom-call(bf16[32,16,512]{2,1,0:T(8,128)(2,1)S(1)} %all-to-all-done.4.data_ref, bf16[2,2,8,32,4096]{4,3,2,1,0:T(8,128)(2,1)} %weight_ref.3, bf16[8,512]{1,0:T(8,128)(2,1)} %constant.38.clone.table_ref, bf16[128,192]{1,0:T(8,128)(2,1)S(1)} %get-tuple-element.47.turn_ref, ...), custom_call_target="tpu_custom_call" | custom-call | flops 33554432 | bytes 8388608 | tf_op jit(solution)/shard_map/pallas_call | solution.py:653
  94.1 1.7 %all-to-all-done.5 = f32[8,128,128]{2,1,0:T(8,128)} async-done(((f32[8,128,128]{2,1,0:T(8,128)}), f32[8,128,128]{2,1,0:T(8,128)}, u32[]{:S(2)}, u32[]{:S(2)}) %all-to-all-start.5) | async-done | bytes 524320 | tf_op jit(solution)/shard_map/all_to_all | solution.py:744
  97.6 4.0 %all-to-all-start.6 = ((bf16[4,64,512]{2,1,0:T(8,128)(2,1)}), bf16[4,64,512]{2,1,0:T(8,128)(2,1)S(1)}, u32[]{:S(2)}, u32[]{:S(2)}) async-start(bf16[4,64,512]{2,1,0:T(8,128)(2,1)} %pad_maximum_fusion), calls=%async_computation.6 | async-start | bytes 524288 | tf_op jit(solution)/shard_map/all_to_all | solution.py:744
  101.7 8.9 %shard_map.183 = f32[2,2,8,32,4096]{4,3,2,1,0:T(8,128)} custom-call(bf16[4,256,128]{2,1,0:T(8,128)(2,1)S(1)} %get-tuple-element.61.modes_ref, f32[4,256,128]{2,1,0:T(8,128)S(1)} %get-tuple-element.62.back_ref, bf16[128,4096]{1,0:T(8,128)(2,1)} %constant.37.clone.table_ref), custom_call_target="tpu_custom_call" | custom-call | flops 16777216 | bytes 16777216 | tf_op jit(solution)/shard_map/pallas_call | solution.py:682
  111.5 3.5 %all-to-all-start.7 = ((bf16[8,48,512]{2,1,0:T(8,128)(2,1)}), bf16[8,48,512]{2,1,0:T(8,128)(2,1)S(1)}, u32[]{:S(2)}, u32[]{:S(2)}) async-start(bf16[8,48,512]{2,1,0:T(8,128)(2,1)} %shard_map.182), calls=%async_computation.7 | async-start | bytes 786432 | tf_op jit(solution)/shard_map/all_to_all | solution.py:744
  115.0 4.0 %collective-permute-start.6 = (bf16[6,64,128]{2,1,0:T(8,128)(2,1)S(1)}, bf16[6,64,128]{2,1,0:T(8,128)(2,1)S(1)}, u32[]{:S(2)}, u32[]{:S(2)}) collective-permute-start(bf16[6,64,128]{2,1,0:T(8,128)(2,1)S(1)} %pad_maximum_fusion.3), channel_id=1, source_target_pairs={{0,1},{1,2},{2,3},{4,5},{5,6},{6,7},{8,9},{9,10},{10,11},{12,13},{... | collective-permute-start | bytes 294920 | tf_op jit(solution)/shard_map/ppermute | solution.py:698
  119.0 1.3 collective-permute-start.7
  120.3 1.2 collective-permute-done.6.ylo_ref
  121.6 4.1 %collective-permute-done.7.yhi_ref = bf16[6,64,128]{2,1,0:T(8,128)(2,1)S(1)} collective-permute-done((bf16[6,64,128]{2,1,0:T(8,128)(2,1)S(1)}, bf16[6,64,128]{2,1,0:T(8,128)(2,1)S(1)}, u32[]{:S(2)}, u32[]{:S(2)}) %collective-permute-start.7) | collective-permute-done | bytes 98336 | tf_op jit(solution)/shard_map/ppermute | solution.py:698
  126.4 3.0 %shard_map.184.stencil_ref = f32[4,64,1024]{2,1,0:T(8,128)S(1)} custom-call(bf16[4,8,64,128]{3,2,1,0:T(8,128)(2,1)S(1)} %get-tuple-element.55.grad_ref.body_ref, bf16[8,64,128]{2,1,0:T(8,128)(2,1)} %copy-done.7, bf16[8,64,128]{2,1,0:T(8,128)(2,1)} %copy-done.6, bf16[6,64,128]{2,1,0:T(8,128)(2,1)} %copy-done.12, bf16[6,64,128]{2,1,0:T(8,128)(2,1)} %copy-done.13, ...), custom_call_target="tpu_custom_call" | custom-call | flops 905969664 | bytes 2097152 | tf_op jit(solution)/shard_map/pallas_call | solution.py:633
  129.4 1.8 %shard_map.185 = (f32[64,4,8,128]{3,2,1,0:T(8,128)}, f32[64,1728]{1,0:T(8,128)}, f32[64,64]{1,0:T(8,128)}) custom-call(f32[4,64,1024]{2,1,0:T(8,128)S(1)} %shard_map.184.stencil_ref, bf16[8,48,512]{2,1,0:T(8,128)(2,1)S(1)} %all-to-all-done.7.message_ref, bf16[96,128]{1,0:T(8,128)(2,1)S(1)} %copy-done.3), custom_call_target="tpu_custom_call" | custom-call | flops 50331648 | bytes 2621440 | tf_op jit(solution)/shard_map/pallas_call | solution.py:633
  (57 shorter events, 6.5 us)
Async XLA Ops:
  0.6 61.9 %copy-start.1 = (bf16[96,128]{1,0:T(8,128)(2,1)S(1)}, bf16[96,128]{1,0:T(8,128)(2,1)}, u32[]{:S(2)}) copy-start(bf16[96,128]{1,0:T(8,128)(2,1)} %constant.32.clone.inverse_ref) | copy-start | bytes 73732
  0.6 61.9 %copy-start.2 = (bf16[96,128]{1,0:T(8,128)(2,1)S(1)}, bf16[96,128]{1,0:T(8,128)(2,1)}, u32[]{:S(2)}) copy-start(bf16[96,128]{1,0:T(8,128)(2,1)} %constant.31.clone.forward_ref) | copy-start | bytes 73732
  0.7 61.8 %copy-start = (bf16[64,4,8,128]{3,2,1,0:T(8,128)(2,1)S(1)}, bf16[64,4,8,128]{3,2,1,0:T(8,128)(2,1)}, u32[]{:S(2)}) copy-start(bf16[64,4,8,128]{3,2,1,0:T(8,128)(2,1)} %cot_ref.1) | copy-start | bytes 1572868
  3.0 12.1 %all-to-all-start = ((f32[8,16,512]{2,1,0:T(8,128)}), f32[8,16,512]{2,1,0:T(8,128)S(1)}, u32[]{:S(2)}, u32[]{:S(2)}) async-start(f32[8,16,512]{2,1,0:T(8,128)} %get-tuple-element.41), calls=%async_computation | async-start | bytes 524288 | tf_op jit(solution)/shard_map/all_to_all | solution.py:744
  8.2 7.9 %collective-permute-start.1 = (bf16[8,64,128]{2,1,0:T(8,128)(2,1)S(1)}, bf16[8,64,128]{2,1,0:T(8,128)(2,1)S(1)}, u32[]{:S(2)}, u32[]{:S(2)}) collective-permute-start(bf16[8,64,128]{2,1,0:T(8,128)(2,1)S(1)} %get-tuple-element.79), channel_id=1, source_target_pairs={{4,0},{8,4},{12,8},{16,12},{20,16},{24,20},{28,24},{5,1},{9,5},{13... | collective-permute-start | bytes 393224 | tf_op jit(solution)/shard_map/ppermute | solution.py:698
  9.5 6.6 %collective-permute-start = (bf16[8,64,128]{2,1,0:T(8,128)(2,1)S(1)}, bf16[8,64,128]{2,1,0:T(8,128)(2,1)S(1)}, u32[]{:S(2)}, u32[]{:S(2)}) collective-permute-start(bf16[8,64,128]{2,1,0:T(8,128)(2,1)S(1)} %get-tuple-element.80), channel_id=1, source_target_pairs={{0,4},{4,8},{8,12},{12,16},{16,20},{20,24},{24,28},{1,5},{5,9},{9,... | collective-permute-start | bytes 393224 | tf_op jit(solution)/shard_map/ppermute | solution.py:698
  14.1 16.9 %copy-start.4 = (bf16[576,256]{1,0:T(8,128)(2,1)}, bf16[576,256]{1,0:T(8,128)(2,1)S(1)}, u32[]{:S(2)}) copy-start(bf16[576,256]{1,0:T(8,128)(2,1)S(1)} %get-tuple-element.67.weight_ref) | copy-start | bytes 884740
  14.1 16.9 %copy-start.5 = (bf16[576,256]{1,0:T(8,128)(2,1)}, bf16[576,256]{1,0:T(8,128)(2,1)S(1)}, u32[]{:S(2)}) copy-start(bf16[576,256]{1,0:T(8,128)(2,1)S(1)} %get-tuple-element.51.weight_ref) | copy-start | bytes 884740
  16.1 39.5 %copy-start.8 = (bf16[8,64,128]{2,1,0:T(8,128)(2,1)}, bf16[8,64,128]{2,1,0:T(8,128)(2,1)S(1)}, u32[]{:S(2)}) copy-start(bf16[8,64,128]{2,1,0:T(8,128)(2,1)S(1)} %collective-permute-done.1.xhi_ref.xhi_any) | copy-start | bytes 393220
  16.1 35.7 %copy-start.9 = (bf16[8,64,128]{2,1,0:T(8,128)(2,1)}, bf16[8,64,128]{2,1,0:T(8,128)(2,1)S(1)}, u32[]{:S(2)}) copy-start(bf16[8,64,128]{2,1,0:T(8,128)(2,1)S(1)} %collective-permute-done.xlo_ref.xlo_any) | copy-start | bytes 393220
  16.1 15.0 %all-to-all-start.1 = ((f32[4,32,512]{2,1,0:T(8,128)}), f32[4,32,512]{2,1,0:T(8,128)S(1)}, u32[]{:S(2)}, u32[]{:S(2)}) async-start(f32[4,32,512]{2,1,0:T(8,128)} %shard_map.174), calls=%async_computation.1 | async-start | bytes 524288 | tf_op jit(solution)/shard_map/all_to_all | solution.py:744
  21.0 17.9 %collective-permute-start.2 = (bf16[6,64,128]{2,1,0:T(8,128)(2,1)S(1)}, bf16[6,64,128]{2,1,0:T(8,128)(2,1)S(1)}, u32[]{:S(2)}, u32[]{:S(2)}) collective-permute-start(bf16[6,64,128]{2,1,0:T(8,128)(2,1)S(1)} %pad_maximum_fusion.1), channel_id=1, source_target_pairs={{0,1},{1,2},{2,3},{4,5},{5,6},{6,7},{8,9},{9,10},{10,11},{12,13},{... | collective-permute-start | bytes 294920 | tf_op jit(solution)/shard_map/ppermute | solution.py:698
  24.9 14.0 %collective-permute-start.3 = (bf16[6,64,128]{2,1,0:T(8,128)(2,1)S(1)}, bf16[6,64,128]{2,1,0:T(8,128)(2,1)S(1)}, u32[]{:S(2)}, u32[]{:S(2)}) collective-permute-start(bf16[6,64,128]{2,1,0:T(8,128)(2,1)S(1)} %pad_maximum_fusion.2), channel_id=1, source_target_pairs={{1,0},{2,1},{3,2},{5,4},{6,5},{7,6},{9,8},{10,9},{11,10},{13,12},{... | collective-permute-start | bytes 294920 | tf_op jit(solution)/shard_map/ppermute | solution.py:698
  38.9 12.9 %copy-start.10 = (bf16[6,64,128]{2,1,0:T(8,128)(2,1)}, bf16[6,64,128]{2,1,0:T(8,128)(2,1)S(1)}, u32[]{:S(2)}) copy-start(bf16[6,64,128]{2,1,0:T(8,128)(2,1)S(1)} %collective-permute-done.2.ylo_ref.ylo_any) | copy-start | bytes 294916
  39.0 12.8 %copy-start.11 = (bf16[6,64,128]{2,1,0:T(8,128)(2,1)}, bf16[6,64,128]{2,1,0:T(8,128)(2,1)S(1)}, u32[]{:S(2)}) copy-start(bf16[6,64,128]{2,1,0:T(8,128)(2,1)S(1)} %collective-permute-done.3.yhi_ref.yhi_any) | copy-start | bytes 294916
  51.8 10.7 %all-to-all-start.3 = ((f32[8,16,512]{2,1,0:T(8,128)}), f32[8,16,512]{2,1,0:T(8,128)S(1)}, u32[]{:S(2)}, u32[]{:S(2)}) async-start(f32[8,16,512]{2,1,0:T(8,128)} %shard_map.178), calls=%async_computation.3 | async-start | bytes 524288 | tf_op jit(solution)/shard_map/all_to_all | solution.py:744
  64.9 17.0 %all-to-all-start.4 = ((bf16[32,16,512]{2,1,0:T(8,128)(2,1)}), bf16[32,16,512]{2,1,0:T(8,128)(2,1)S(1)}, u32[]{:S(2)}, u32[]{:S(2)}) async-start(bf16[32,16,512]{2,1,0:T(8,128)(2,1)} %get-tuple-element.56), calls=%async_computation.4 | async-start | bytes 1048576 | tf_op jit(solution)/shard_map/all_to_all | solution.py:744
  67.6 8.6 %collective-permute-start.5 = (bf16[8,64,128]{2,1,0:T(8,128)(2,1)S(1)}, bf16[8,64,128]{2,1,0:T(8,128)(2,1)S(1)}, u32[]{:S(2)}, u32[]{:S(2)}) collective-permute-start(bf16[8,64,128]{2,1,0:T(8,128)(2,1)S(1)} %get-tuple-element.75), channel_id=1, source_target_pairs={{4,0},{8,4},{12,8},{16,12},{20,16},{24,20},{28,24},{5,1},{9,5},{13... | collective-permute-start | bytes 393224 | tf_op jit(solution)/shard_map/ppermute | solution.py:698
  68.9 7.3 %collective-permute-start.4 = (bf16[8,64,128]{2,1,0:T(8,128)(2,1)S(1)}, bf16[8,64,128]{2,1,0:T(8,128)(2,1)S(1)}, u32[]{:S(2)}, u32[]{:S(2)}) collective-permute-start(bf16[8,64,128]{2,1,0:T(8,128)(2,1)S(1)} %get-tuple-element.76), channel_id=1, source_target_pairs={{0,4},{4,8},{8,12},{12,16},{16,20},{20,24},{24,28},{1,5},{5,9},{9,... | collective-permute-start | bytes 393224 | tf_op jit(solution)/shard_map/ppermute | solution.py:698
  76.1 49.6 %copy-start.6 = (bf16[8,64,128]{2,1,0:T(8,128)(2,1)}, bf16[8,64,128]{2,1,0:T(8,128)(2,1)S(1)}, u32[]{:S(2)}) copy-start(bf16[8,64,128]{2,1,0:T(8,128)(2,1)S(1)} %collective-permute-done.5.xhi_ref) | copy-start | bytes 393220
  76.1 49.6 %copy-start.7 = (bf16[8,64,128]{2,1,0:T(8,128)(2,1)}, bf16[8,64,128]{2,1,0:T(8,128)(2,1)S(1)}, u32[]{:S(2)}) copy-start(bf16[8,64,128]{2,1,0:T(8,128)(2,1)S(1)} %collective-permute-done.4.xlo_ref) | copy-start | bytes 393220
  81.9 13.9 %all-to-all-start.5 = ((f32[8,128,128]{2,1,0:T(8,128)}), f32[8,128,128]{2,1,0:T(8,128)}, u32[]{:S(2)}, u32[]{:S(2)}) async-start(f32[8,128,128]{2,1,0:T(8,128)} %bitcast.7), calls=%async_computation.5 | async-start | bytes 1048576 | tf_op jit(solution)/shard_map/all_to_all | solution.py:744
  86.0 43.4 %copy-start.3 = (bf16[96,128]{1,0:T(8,128)(2,1)S(1)}, bf16[96,128]{1,0:T(8,128)(2,1)}, u32[]{:S(2)}) copy-start(bf16[96,128]{1,0:T(8,128)(2,1)} %constant.33.clone.inverse_ref) | copy-start | bytes 73732
  97.6 12.9 %all-to-all-start.6 = ((bf16[4,64,512]{2,1,0:T(8,128)(2,1)}), bf16[4,64,512]{2,1,0:T(8,128)(2,1)S(1)}, u32[]{:S(2)}, u32[]{:S(2)}) async-start(bf16[4,64,512]{2,1,0:T(8,128)(2,1)} %pad_maximum_fusion), calls=%async_computation.6 | async-start | bytes 524288 | tf_op jit(solution)/shard_map/all_to_all | solution.py:744
  111.5 17.9 %all-to-all-start.7 = ((bf16[8,48,512]{2,1,0:T(8,128)(2,1)}), bf16[8,48,512]{2,1,0:T(8,128)(2,1)S(1)}, u32[]{:S(2)}, u32[]{:S(2)}) async-start(bf16[8,48,512]{2,1,0:T(8,128)(2,1)} %shard_map.182), calls=%async_computation.7 | async-start | bytes 786432 | tf_op jit(solution)/shard_map/all_to_all | solution.py:744
  115.0 6.5 %collective-permute-start.6 = (bf16[6,64,128]{2,1,0:T(8,128)(2,1)S(1)}, bf16[6,64,128]{2,1,0:T(8,128)(2,1)S(1)}, u32[]{:S(2)}, u32[]{:S(2)}) collective-permute-start(bf16[6,64,128]{2,1,0:T(8,128)(2,1)S(1)} %pad_maximum_fusion.3), channel_id=1, source_target_pairs={{0,1},{1,2},{2,3},{4,5},{5,6},{6,7},{8,9},{9,10},{10,11},{12,13},{... | collective-permute-start | bytes 294920 | tf_op jit(solution)/shard_map/ppermute | solution.py:698
  119.0 6.7 %collective-permute-start.7 = (bf16[6,64,128]{2,1,0:T(8,128)(2,1)S(1)}, bf16[6,64,128]{2,1,0:T(8,128)(2,1)S(1)}, u32[]{:S(2)}, u32[]{:S(2)}) collective-permute-start(bf16[6,64,128]{2,1,0:T(8,128)(2,1)S(1)} %pad_maximum_fusion.4), channel_id=1, source_target_pairs={{1,0},{2,1},{3,2},{5,4},{6,5},{7,6},{9,8},{10,9},{11,10},{13,12},{... | collective-permute-start | bytes 294920 | tf_op jit(solution)/shard_map/ppermute | solution.py:698
  121.6 4.1 %copy-start.12 = (bf16[6,64,128]{2,1,0:T(8,128)(2,1)}, bf16[6,64,128]{2,1,0:T(8,128)(2,1)S(1)}, u32[]{:S(2)}) copy-start(bf16[6,64,128]{2,1,0:T(8,128)(2,1)S(1)} %collective-permute-done.6.ylo_ref) | copy-start | bytes 294916
  125.7 0.6 copy-start.13

commit v13 on v12

--- a/solution.py
+++ b/solution.py
@@ -676,20 +676,30 @@
     )(data, in_hbm(weight), in_hbm(table), *tables)
 
 
-def outer(modes, back, table, shape, alpha):
+def outer(modes, back, table, shape, alpha, start, count, prior=None):
+    def kernel(*refs):
+        outer_kernel(alpha, *refs[:3], refs[-1])
+
     per = shape[2] // QUAD
-    group = lambda ref: pl.BlockSpec((1,) + ref.shape[1:], lambda step: (step, 0, 0))
+    group = lambda ref: pl.BlockSpec((1,) + ref.shape[1:], lambda step: (step + start, 0, 0))
+    given = () if prior is None else (prior,)
     return pl.pallas_call(
-        functools.partial(outer_kernel, alpha),
-        grid=(modes.shape[0],),
-        in_specs=[group(modes), group(back), pl.BlockSpec(table.shape, lambda step: (0, 0))],
+        kernel,
+        grid=(count,),
+        in_specs=[group(modes), group(back), pl.BlockSpec(table.shape, lambda step: (0, 0))]
+        + [pl.BlockSpec(memory_space=pl.ANY)] * len(given),
         out_specs=pl.BlockSpec(
-            (2, 1, QUAD) + shape[3:], lambda step: (0, step // per, step % per, 0, 0)
+            (2, 1, QUAD) + shape[3:],
+            lambda step: (0, (step + start) // per, (step + start) % per, 0, 0),
         ),
         out_shape=jax.ShapeDtypeStruct(shape, F32),
+        input_output_aliases={3: 0} if given else {},
         compiler_params=params(20),
-        cost_estimate=cost(math.prod(shape) * 4, math.prod(shape) * 4),
-    )(modes, back, in_hbm(table))
+        cost_estimate=cost(
+            math.prod(shape) * 4 * count / modes.shape[0],
+            math.prod(shape) * 4 * count / modes.shape[0],
+        ),
+    )(modes, back, in_hbm(table), *given)
 
 
 def shift(block, axis, step):
@@ -832,7 +842,8 @@
     grad_taps = weight_grad(grad, turned, rim)
     faces = x_halos(grad)
     block = swap(slab, ("gx", "gy"))
-    block, grad_taps, *faces = together(block, grad_taps, *faces)
+    edges = y_halos(grad, *faces)
+    block, grad_taps, ylo, *faces = together(block, grad_taps, edges[0], *faces)
     mine = swap(grad_taps.reshape(nx, -1, 2 * c), "gx").sum(0)
     back_modes, block = per_mode(
         mix_back_kernel,
@@ -847,14 +858,20 @@
     packed = jnp.concatenate(jnp.split(mine, lanes // (2 * c)), axis=1).astype(BF16)
     extra = packed.shape[0]
     packed = jnp.broadcast_to(packed[None], (ny, extra, lanes))
-    block = x_stage(
-        x_inv, swap(jnp.concatenate([block, packed], axis=1), "gy"), nx, BF16, extra
-    )
-    grad_modes = outer(modes_in, back_modes, spread, spectral_weight.shape, alpha)
-    block, grad_modes, *faces = together(block, grad_modes, *faces)
+    block, yhi = together(jnp.concatenate([block, packed], axis=1), edges[1])
+    block = x_stage(x_inv, swap(block, "gy"), nx, BF16, extra)
+    shape = spectral_weight.shape
+    groups = modes_in.shape[0]
+    early = groups * 3 // 4
+    grad_modes = None
+    if early:
+        grad_modes = outer(modes_in, back_modes, spread, shape, alpha, 0, early)
+        block, grad_modes = together(block, grad_modes)
     message = swap(block, "gx")
-    edges = y_halos(grad, *faces)
-    stencil_back = conv(grad, (*faces, *edges), back_table, True)
+    stencil_back = conv(grad, (*faces, ylo, yhi), back_table, True)
+    grad_modes = outer(
+        modes_in, back_modes, spread, shape, alpha, early, groups - early, grad_modes
+    )
     grad_state, grad_stencil, grad_point = call(
         functools.partial(finish_kernel, nx, alpha),
         [((c, cx, cy, z), F32), ((c, 27 * c), F32), ((c, c), F32)],

time: 133 us -> 131 us (0.985)
  waiting for transfers between devices: 21.7 us -> 15.4 us
  starting transfers between devices: 47.3 us -> 50.4 us
  Pallas kernels: 45.8 us -> 48.7 us
    all_to_all x7, starting transfers between devices: 28 us -> 32.6 us  [swap(): return lax.all_to_all(block, axis, split_axis=0, concat_axis=0, tiled=True)]
    all_to_all x7, waiting for transfers between devices: 16.3 us -> 12.3 us  [swap(): return lax.all_to_all(block, axis, split_axis=0, concat_axis=0, tiled=True)]
    pallas_call x1 -> x2, Pallas kernels: 8.86 us -> 11.8 us  [outer(): pl.pallas_call(kernel, grid=(count,), in_specs=[group(modes), group(back)...]
    ppermute x8, waiting for transfers between devices: 5.39 us -> 3.05 us  [shift(): return lax.ppermute(block, axis, pairs)]
    ppermute x8, starting transfers between devices: 19.3 us -> 17.8 us  [shift(): return lax.ppermute(block, axis, pairs)]
  transfers between devices with their start and end apart: 15 -> 15, of which waited for: 7 -> 8; matrix products, arithmetic and copies ran while one was open for 1% -> 1% of each run, Pallas kernels for 28% -> 31%
where the time goes in v13:
time: 131 us; the launch traced here: 130 us
  starting transfers between devices  50.4 us (38%)
  Pallas kernels  48.7 us (37%)
  waiting for transfers between devices  15.4 us (12%)
  blocking collectives  11.9 us (9%)
  local copies, waits for them, and re-layouts  1.34 us (1%)
    all_to_all x7, starting transfers between devices, swap(): return lax.all_to_all(block, axis, split_axis=0, concat_axis=0, tiled=True)  32.6 us
    pallas_call x10, Pallas kernels, call(): pl.pallas_call(kernel, out_shape=[jax.ShapeDtypeStruct(*out) for out in o...  21.1 us
    ppermute x8, starting transfers between devices, shift(): return lax.ppermute(block, axis, pairs)  17.8 us
    pallas_call x2, Pallas kernels, per_mode(): pl.pallas_call(functools.partial(kernel, mz), in_specs=[whole(), pl.Block...  15.9 us
    all_to_all x7, waiting for transfers between devices, swap(): return lax.all_to_all(block, axis, split_axis=0, concat_axis=0, tiled=True)  12.3 us
    all_to_all x1, blocking collectives, swap(): return lax.all_to_all(block, axis, split_axis=0, concat_axis=0, tiled=True)  11.9 us
    pallas_call x2, Pallas kernels, outer(): pl.pallas_call(kernel, grid=(count,), in_specs=[group(modes), group(back)...  11.8 us
    ppermute x8, waiting for transfers between devices, shift(): return lax.ppermute(block, axis, pairs)  3.05 us
  transfers between devices with their start and end apart: 15, of which 8 were waited for; matrix products, arithmetic and copies ran while one was open for 1% of the time, Pallas kernels for 31%

profile of v13, /device:TPU:0, one launch (start us, length us, event | category | flops | bytes accessed | tf_op | source)
XLA Modules:
  0.0 129.6 jit_solution(17369356856882568646)
XLA Ops:
  0.7 2.3 %shard_map.173 = (bf16[4,8,64,128]{3,2,1,0:T(8,128)(2,1)S(1)}, f32[8,16,512]{2,1,0:T(8,128)}, bf16[128,384]{1,0:T(8,128)(2,1)S(1)}, bf16[128,384]{1,0:T(8,128)(2,1)S(1)}, bf16[128,192]{1,0:T(8,128)(2,1)S(1)}) custom-call(bf16[64,4,8,128]{3,2,1,0:T(8,128)(2,1)} %field_ref.1, bf16[96,128]{1,0:T(8,128)(2,1)} %constant.30.clone.table_ref, ...), custom_call_target="tpu_custom_call" | custom-call | flops 50331648 | bytes 1310720 | tf_op jit(solution)/shard_map/pallas_call | solution.py:633
  3.0 5.2 %all-to-all-start = ((f32[8,16,512]{2,1,0:T(8,128)}), f32[8,16,512]{2,1,0:T(8,128)S(1)}, u32[]{:S(2)}, u32[]{:S(2)}) async-start(f32[8,16,512]{2,1,0:T(8,128)} %get-tuple-element.42), calls=%async_computation | async-start | bytes 524288 | tf_op jit(solution)/shard_map/all_to_all | solution.py:754
  8.2 1.3 collective-permute-start.1
  9.5 3.0 %collective-permute-start = (bf16[8,64,128]{2,1,0:T(8,128)(2,1)S(1)}, bf16[8,64,128]{2,1,0:T(8,128)(2,1)S(1)}, u32[]{:S(2)}, u32[]{:S(2)}) collective-permute-start(bf16[8,64,128]{2,1,0:T(8,128)(2,1)S(1)} %get-tuple-element.82), channel_id=1, source_target_pairs={{0,4},{4,8},{8,12},{12,16},{16,20},{20,24},{24,28},{1,5},{5,9},{9,... | collective-permute-start | bytes 393224 | tf_op jit(solution)/shard_map/ppermute | solution.py:708
  12.6 1.5 %shard_map.175 = (bf16[576,256]{1,0:T(8,128)(2,1)S(1)}, bf16[576,256]{1,0:T(8,128)(2,1)S(1)}) custom-call(bf16[64,1728]{1,0:T(8,128)(2,1)} %taps_ref.1, bf16[64,64]{1,0:T(8,128)(2,1)} %point_ref.1), custom_call_target="tpu_custom_call" | custom-call | bytes 663552 | tf_op jit(solution)/shard_map/pallas_call | solution.py:633
  16.1 4.9 %all-to-all-start.1 = ((f32[4,32,512]{2,1,0:T(8,128)}), f32[4,32,512]{2,1,0:T(8,128)S(1)}, u32[]{:S(2)}, u32[]{:S(2)}) async-start(f32[4,32,512]{2,1,0:T(8,128)} %shard_map.174), calls=%async_computation.1 | async-start | bytes 524288 | tf_op jit(solution)/shard_map/all_to_all | solution.py:754
  21.0 3.9 %collective-permute-start.2 = (bf16[6,64,128]{2,1,0:T(8,128)(2,1)S(1)}, bf16[6,64,128]{2,1,0:T(8,128)(2,1)S(1)}, u32[]{:S(2)}, u32[]{:S(2)}) collective-permute-start(bf16[6,64,128]{2,1,0:T(8,128)(2,1)S(1)} %pad_maximum_fusion.1), channel_id=1, source_target_pairs={{0,1},{1,2},{2,3},{4,5},{5,6},{6,7},{8,9},{9,10},{10,11},{12,13},{... | collective-permute-start | bytes 294920 | tf_op jit(solution)/shard_map/ppermute | solution.py:708
  24.9 1.3 collective-permute-start.3
  26.2 4.8 %all-to-all-done.1.data_ref = f32[4,32,512]{2,1,0:T(8,128)S(1)} async-done(((f32[4,32,512]{2,1,0:T(8,128)}), f32[4,32,512]{2,1,0:T(8,128)S(1)}, u32[]{:S(2)}, u32[]{:S(2)}) %all-to-all-start.1) | async-done | bytes 262176 | tf_op jit(solution)/shard_map/all_to_all | solution.py:754
  31.0 7.9 %shard_map.176 = (bf16[4,256,128]{2,1,0:T(8,128)(2,1)S(1)}, f32[4,32,512]{2,1,0:T(8,128)S(1)}) custom-call(f32[4,32,512]{2,1,0:T(8,128)S(1)} %all-to-all-done.1.data_ref, bf16[2,2,8,32,4096]{4,3,2,1,0:T(8,128)(2,1)} %weight_ref.3, bf16[128,4096]{1,0:T(8,128)(2,1)} %constant.37.clone.table_ref.refs_2_, bf16[128,192]{1,0:T(8,128)(2,1)S(1)} %get-tuple-element.48.turn_ref), custom_call_target="tpu_custom_call" | custom-call | flops 33554432 | bytes 8388608 | tf_op jit(solution)/shard_map/pallas_call | solution.py:653
  39.0 11.9 %all_to_all.40.data_ref = f32[4,32,512]{2,1,0:T(8,128)S(1)} all-to-all(f32[4,32,512]{2,1,0:T(8,128)S(1)} %get-tuple-element.54), channel_id=1, replica_groups=mesh['gx'=8,'gy'=4] {'gy'}, dimensions={0} | all-to-all | bytes 524288 | tf_op jit(solution)/shard_map/all_to_all | solution.py:754
  51.8 3.7 %all-to-all-start.3 = ((f32[8,16,512]{2,1,0:T(8,128)}), f32[8,16,512]{2,1,0:T(8,128)S(1)}, u32[]{:S(2)}, u32[]{:S(2)}) async-start(f32[8,16,512]{2,1,0:T(8,128)} %shard_map.178), calls=%async_computation.3 | async-start | bytes 524288 | tf_op jit(solution)/shard_map/all_to_all | solution.py:754
  55.6 3.1 %shard_map.177.stencil_ref = f32[4,64,1024]{2,1,0:T(8,128)S(1)} custom-call(bf16[4,8,64,128]{3,2,1,0:T(8,128)(2,1)S(1)} %get-tuple-element.40.body_ref, bf16[8,64,128]{2,1,0:T(8,128)(2,1)} %copy-done.9, bf16[8,64,128]{2,1,0:T(8,128)(2,1)} %copy-done.8, bf16[6,64,128]{2,1,0:T(8,128)(2,1)} %copy-done.10, bf16[6,64,128]{2,1,0:T(8,128)(2,1)} %copy-done.12, ...), custom_call_target="tpu_custom_call" | custom-call | flops 905969664 | bytes 2097152 | tf_op jit(solution)/shard_map/pallas_call | solution.py:633
  58.6 3.8 %all-to-all-done.3.slab_ref = f32[8,16,512]{2,1,0:T(8,128)S(1)} async-done(((f32[8,16,512]{2,1,0:T(8,128)}), f32[8,16,512]{2,1,0:T(8,128)S(1)}, u32[]{:S(2)}, u32[]{:S(2)}) %all-to-all-start.3) | async-done | bytes 262176 | tf_op jit(solution)/shard_map/all_to_all | solution.py:754
  62.5 2.4 %shard_map.179 = (bf16[64,4,8,128]{3,2,1,0:T(8,128)(2,1)}, bf16[4,8,64,128]{3,2,1,0:T(8,128)(2,1)S(1)}, bf16[32,16,512]{2,1,0:T(8,128)(2,1)}) custom-call(f32[4,64,1024]{2,1,0:T(8,128)S(1)} %shard_map.177.stencil_ref, f32[8,16,512]{2,1,0:T(8,128)S(1)} %all-to-all-done.3.slab_ref, bf16[64,4,8,128]{3,2,1,0:T(8,128)(2,1)S(1)} %copy-done, ...), custom_call_target="tpu_custom_call" | custom-call | flops 100663296 | bytes 3145728 | tf_op jit(solution)/shard_map/pallas_call | solution.py:633
  64.9 2.6 %all-to-all-start.4 = ((bf16[32,16,512]{2,1,0:T(8,128)(2,1)}), bf16[32,16,512]{2,1,0:T(8,128)(2,1)S(1)}, u32[]{:S(2)}, u32[]{:S(2)}) async-start(bf16[32,16,512]{2,1,0:T(8,128)(2,1)} %get-tuple-element.57), calls=%async_computation.4 | async-start | bytes 1048576 | tf_op jit(solution)/shard_map/all_to_all | solution.py:754
  67.6 2.0 %collective-permute-start.4 = (bf16[8,64,128]{2,1,0:T(8,128)(2,1)S(1)}, bf16[8,64,128]{2,1,0:T(8,128)(2,1)S(1)}, u32[]{:S(2)}, u32[]{:S(2)}) collective-permute-start(bf16[8,64,128]{2,1,0:T(8,128)(2,1)S(1)} %get-tuple-element.77), channel_id=1, source_target_pairs={{0,4},{4,8},{8,12},{12,16},{16,20},{20,24},{24,28},{1,5},{5,9},{9,... | collective-permute-start | bytes 393224 | tf_op jit(solution)/shard_map/ppermute | solution.py:708
  69.6 1.3 collective-permute-start.5
  70.9 3.0 %collective-permute-done.5.xhi_ref = bf16[8,64,128]{2,1,0:T(8,128)(2,1)S(1)} collective-permute-done((bf16[8,64,128]{2,1,0:T(8,128)(2,1)S(1)}, bf16[8,64,128]{2,1,0:T(8,128)(2,1)S(1)}, u32[]{:S(2)}, u32[]{:S(2)}) %collective-permute-start.5) | collective-permute-done | bytes 131104 | tf_op jit(solution)/shard_map/ppermute | solution.py:708
  74.0 3.6 %collective-permute-start.6 = (bf16[6,64,128]{2,1,0:T(8,128)(2,1)S(1)}, bf16[6,64,128]{2,1,0:T(8,128)(2,1)S(1)}, u32[]{:S(2)}, u32[]{:S(2)}) collective-permute-start(bf16[6,64,128]{2,1,0:T(8,128)(2,1)S(1)} %pad_maximum_fusion.3), channel_id=1, source_target_pairs={{0,1},{1,2},{2,3},{4,5},{5,6},{6,7},{8,9},{9,10},{10,11},{12,13},{... | collective-permute-start | bytes 294920 | tf_op jit(solution)/shard_map/ppermute | solution.py:708
  77.6 4.0 %shard_map.180 = f32[1024,128]{1,0:T(8,128)} custom-call(bf16[4,8,64,128]{3,2,1,0:T(8,128)(2,1)S(1)} %get-tuple-element.56.grad_ref.body_ref, bf16[4,8,64,128]{3,2,1,0:T(8,128)(2,1)S(1)} %get-tuple-element.40.body_ref, bf16[8,64,128]{2,1,0:T(8,128)(2,1)} %copy-done.9, bf16[8,64,128]{2,1,0:T(8,128)(2,1)} %copy-done.8, bf16[6,64,128]{2,1,0:T(8,128)(2,1)} %copy-done.10, ...), custom_call_target="tpu_custom_call" | custom-call | flops 905969664 | bytes 2097152 | tf_op jit(solution)/shard_map/pallas_call | solution.py:633
  82.3 7.6 %all-to-all-start.5 = ((f32[8,128,128]{2,1,0:T(8,128)}), f32[8,128,128]{2,1,0:T(8,128)S(1)}, u32[]{:S(2)}, u32[]{:S(2)}) async-start(f32[8,128,128]{2,1,0:T(8,128)} %bitcast.8), calls=%async_computation.5 | async-start | bytes 1048576 | tf_op jit(solution)/shard_map/all_to_all | solution.py:754
  89.9 1.3 collective-permute-start.7
  91.2 8.0 %shard_map.181 = (f32[4,256,128]{2,1,0:T(8,128)S(1)}, bf16[4,32,512]{2,1,0:T(8,128)(2,1)S(1)}) custom-call(bf16[32,16,512]{2,1,0:T(8,128)(2,1)S(1)} %all-to-all-done.4.data_ref, bf16[2,2,8,32,4096]{4,3,2,1,0:T(8,128)(2,1)} %weight_ref.3, bf16[8,512]{1,0:T(8,128)(2,1)} %constant.38.clone.table_ref, bf16[128,192]{1,0:T(8,128)(2,1)S(1)} %get-tuple-element.48.turn_ref, ...), custom_call_target="tpu_custom_call" | custom-call | flops 33554432 | bytes 8388608 | tf_op jit(solution)/shard_map/pallas_call | solution.py:653
  100.5 4.8 %all-to-all-start.6 = ((bf16[4,64,512]{2,1,0:T(8,128)(2,1)}), bf16[4,64,512]{2,1,0:T(8,128)(2,1)S(1)}, u32[]{:S(2)}, u32[]{:S(2)}) async-start(bf16[4,64,512]{2,1,0:T(8,128)(2,1)} %pad_maximum_fusion), calls=%async_computation.6 | async-start | bytes 524288 | tf_op jit(solution)/shard_map/all_to_all | solution.py:754
  105.3 7.4 %shard_map.184.refs_3_ = f32[2,2,8,32,4096]{4,3,2,1,0:T(8,128)} custom-call(bf16[4,256,128]{2,1,0:T(8,128)(2,1)S(1)} %get-tuple-element.68.refs_0_, f32[4,256,128]{2,1,0:T(8,128)S(1)} %get-tuple-element.69.refs_1_, bf16[128,4096]{1,0:T(8,128)(2,1)} %constant.37.clone.table_ref.refs_2_), custom_call_target="tpu_custom_call" | custom-call | flops 12582912 | bytes 12582912 | tf_op jit(solution)/shard_map/pallas_call | solution.py:686
  112.7 1.9 %all-to-all-done.6.data_ref = bf16[4,64,512]{2,1,0:T(8,128)(2,1)S(1)} async-done(((bf16[4,64,512]{2,1,0:T(8,128)(2,1)}), bf16[4,64,512]{2,1,0:T(8,128)(2,1)S(1)}, u32[]{:S(2)}, u32[]{:S(2)}) %all-to-all-start.6) | async-done | bytes 262176 | tf_op jit(solution)/shard_map/all_to_all | solution.py:754
  114.7 1.0 shard_map.183
  115.6 3.8 %all-to-all-start.7 = ((bf16[8,48,512]{2,1,0:T(8,128)(2,1)}), bf16[8,48,512]{2,1,0:T(8,128)(2,1)S(1)}, u32[]{:S(2)}, u32[]{:S(2)}) async-start(bf16[8,48,512]{2,1,0:T(8,128)(2,1)} %shard_map.183), calls=%async_computation.7 | async-start | bytes 786432 | tf_op jit(solution)/shard_map/all_to_all | solution.py:754
  119.4 3.0 %shard_map.182.stencil_ref = f32[4,64,1024]{2,1,0:T(8,128)S(1)} custom-call(bf16[4,8,64,128]{3,2,1,0:T(8,128)(2,1)S(1)} %get-tuple-element.56.grad_ref.body_ref, bf16[8,64,128]{2,1,0:T(8,128)(2,1)} %copy-done.6, bf16[8,64,128]{2,1,0:T(8,128)(2,1)} %copy-done.7, bf16[6,64,128]{2,1,0:T(8,128)(2,1)} %copy-done.11, bf16[6,64,128]{2,1,0:T(8,128)(2,1)} %copy-done.13, ...), custom_call_target="tpu_custom_call" | custom-call | flops 905969664 | bytes 2097152 | tf_op jit(solution)/shard_map/pallas_call | solution.py:633
  122.5 4.3 %shard_map.186 = f32[2,2,8,32,4096]{4,3,2,1,0:T(8,128)} custom-call(bf16[4,256,128]{2,1,0:T(8,128)(2,1)S(1)} %get-tuple-element.68.refs_0_, f32[4,256,128]{2,1,0:T(8,128)S(1)} %get-tuple-element.69.refs_1_, bf16[128,4096]{1,0:T(8,128)(2,1)} %constant.37.clone.table_ref.refs_2_, f32[2,2,8,32,4096]{4,3,2,1,0:T(8,128)} %shard_map.184.refs_3_), custom_call_target="tpu_custom_call", output_to_operand_aliasing={{}: (3, {})} | custom-call | flops 4194304 | bytes 4194304 | tf_op jit(solution)/shard_map/pallas_call | solution.py:686
  127.8 1.8 %shard_map.185 = (f32[64,4,8,128]{3,2,1,0:T(8,128)}, f32[64,1728]{1,0:T(8,128)}, f32[64,64]{1,0:T(8,128)}) custom-call(f32[4,64,1024]{2,1,0:T(8,128)S(1)} %shard_map.182.stencil_ref, bf16[8,48,512]{2,1,0:T(8,128)(2,1)S(1)} %all-to-all-done.7.message_ref, bf16[96,128]{1,0:T(8,128)(2,1)S(1)} %copy-done.3), custom_call_target="tpu_custom_call" | custom-call | flops 50331648 | bytes 2621440 | tf_op jit(solution)/shard_map/pallas_call | solution.py:633
  (58 shorter events, 5.8 us)
Async XLA Ops:
  0.6 61.9 %copy-start.1 = (bf16[96,128]{1,0:T(8,128)(2,1)S(1)}, bf16[96,128]{1,0:T(8,128)(2,1)}, u32[]{:S(2)}) copy-start(bf16[96,128]{1,0:T(8,128)(2,1)} %constant.32.clone.inverse_ref) | copy-start | bytes 73732
  0.6 61.8 %copy-start.2 = (bf16[96,128]{1,0:T(8,128)(2,1)S(1)}, bf16[96,128]{1,0:T(8,128)(2,1)}, u32[]{:S(2)}) copy-start(bf16[96,128]{1,0:T(8,128)(2,1)} %constant.31.clone.forward_ref) | copy-start | bytes 73732
  0.7 61.8 %copy-start = (bf16[64,4,8,128]{3,2,1,0:T(8,128)(2,1)S(1)}, bf16[64,4,8,128]{3,2,1,0:T(8,128)(2,1)}, u32[]{:S(2)}) copy-start(bf16[64,4,8,128]{3,2,1,0:T(8,128)(2,1)} %cot_ref.1) | copy-start | bytes 1572868
  3.0 12.1 %all-to-all-start = ((f32[8,16,512]{2,1,0:T(8,128)}), f32[8,16,512]{2,1,0:T(8,128)S(1)}, u32[]{:S(2)}, u32[]{:S(2)}) async-start(f32[8,16,512]{2,1,0:T(8,128)} %get-tuple-element.42), calls=%async_computation | async-start | bytes 524288 | tf_op jit(solution)/shard_map/all_to_all | solution.py:754
  8.2 7.9 %collective-permute-start.1 = (bf16[8,64,128]{2,1,0:T(8,128)(2,1)S(1)}, bf16[8,64,128]{2,1,0:T(8,128)(2,1)S(1)}, u32[]{:S(2)}, u32[]{:S(2)}) collective-permute-start(bf16[8,64,128]{2,1,0:T(8,128)(2,1)S(1)} %get-tuple-element.81), channel_id=1, source_target_pairs={{4,0},{8,4},{12,8},{16,12},{20,16},{24,20},{28,24},{5,1},{9,5},{13... | collective-permute-start | bytes 393224 | tf_op jit(solution)/shard_map/ppermute | solution.py:708
  9.5 6.6 %collective-permute-start = (bf16[8,64,128]{2,1,0:T(8,128)(2,1)S(1)}, bf16[8,64,128]{2,1,0:T(8,128)(2,1)S(1)}, u32[]{:S(2)}, u32[]{:S(2)}) collective-permute-start(bf16[8,64,128]{2,1,0:T(8,128)(2,1)S(1)} %get-tuple-element.82), channel_id=1, source_target_pairs={{0,4},{4,8},{8,12},{12,16},{16,20},{20,24},{24,28},{1,5},{5,9},{9,... | collective-permute-start | bytes 393224 | tf_op jit(solution)/shard_map/ppermute | solution.py:708
  14.1 37.7 %copy-start.5 = (bf16[576,256]{1,0:T(8,128)(2,1)}, bf16[576,256]{1,0:T(8,128)(2,1)S(1)}, u32[]{:S(2)}) copy-start(bf16[576,256]{1,0:T(8,128)(2,1)S(1)} %get-tuple-element.52.weight_ref) | copy-start | bytes 884740
  14.1 44.5 %copy-start.4 = (bf16[576,256]{1,0:T(8,128)(2,1)}, bf16[576,256]{1,0:T(8,128)(2,1)S(1)}, u32[]{:S(2)}) copy-start(bf16[576,256]{1,0:T(8,128)(2,1)S(1)} %get-tuple-element.66.weight_ref) | copy-start | bytes 884740
  16.1 39.5 %copy-start.8 = (bf16[8,64,128]{2,1,0:T(8,128)(2,1)}, bf16[8,64,128]{2,1,0:T(8,128)(2,1)S(1)}, u32[]{:S(2)}) copy-start(bf16[8,64,128]{2,1,0:T(8,128)(2,1)S(1)} %collective-permute-done.1.xhi_ref.xhi_any) | copy-start | bytes 393220
  16.1 35.7 %copy-start.9 = (bf16[8,64,128]{2,1,0:T(8,128)(2,1)}, bf16[8,64,128]{2,1,0:T(8,128)(2,1)S(1)}, u32[]{:S(2)}) copy-start(bf16[8,64,128]{2,1,0:T(8,128)(2,1)S(1)} %collective-permute-done.xlo_ref.xlo_any) | copy-start | bytes 393220
  16.1 15.0 %all-to-all-start.1 = ((f32[4,32,512]{2,1,0:T(8,128)}), f32[4,32,512]{2,1,0:T(8,128)S(1)}, u32[]{:S(2)}, u32[]{:S(2)}) async-start(f32[4,32,512]{2,1,0:T(8,128)} %shard_map.174), calls=%async_computation.1 | async-start | bytes 524288 | tf_op jit(solution)/shard_map/all_to_all | solution.py:754
  21.0 17.9 %collective-permute-start.2 = (bf16[6,64,128]{2,1,0:T(8,128)(2,1)S(1)}, bf16[6,64,128]{2,1,0:T(8,128)(2,1)S(1)}, u32[]{:S(2)}, u32[]{:S(2)}) collective-permute-start(bf16[6,64,128]{2,1,0:T(8,128)(2,1)S(1)} %pad_maximum_fusion.1), channel_id=1, source_target_pairs={{0,1},{1,2},{2,3},{4,5},{5,6},{6,7},{8,9},{9,10},{10,11},{12,13},{... | collective-permute-start | bytes 294920 | tf_op jit(solution)/shard_map/ppermute | solution.py:708
  24.9 14.0 %collective-permute-start.3 = (bf16[6,64,128]{2,1,0:T(8,128)(2,1)S(1)}, bf16[6,64,128]{2,1,0:T(8,128)(2,1)S(1)}, u32[]{:S(2)}, u32[]{:S(2)}) collective-permute-start(bf16[6,64,128]{2,1,0:T(8,128)(2,1)S(1)} %pad_maximum_fusion.2), channel_id=1, source_target_pairs={{1,0},{2,1},{3,2},{5,4},{6,5},{7,6},{9,8},{10,9},{11,10},{13,12},{... | collective-permute-start | bytes 294920 | tf_op jit(solution)/shard_map/ppermute | solution.py:708
  38.9 12.9 %copy-start.10 = (bf16[6,64,128]{2,1,0:T(8,128)(2,1)}, bf16[6,64,128]{2,1,0:T(8,128)(2,1)S(1)}, u32[]{:S(2)}) copy-start(bf16[6,64,128]{2,1,0:T(8,128)(2,1)S(1)} %collective-permute-done.2.ylo_ref.ylo_any) | copy-start | bytes 294916
  39.0 16.6 %copy-start.12 = (bf16[6,64,128]{2,1,0:T(8,128)(2,1)}, bf16[6,64,128]{2,1,0:T(8,128)(2,1)S(1)}, u32[]{:S(2)}) copy-start(bf16[6,64,128]{2,1,0:T(8,128)(2,1)S(1)} %collective-permute-done.3.yhi_ref.yhi_any) | copy-start | bytes 294916
  51.8 10.7 %all-to-all-start.3 = ((f32[8,16,512]{2,1,0:T(8,128)}), f32[8,16,512]{2,1,0:T(8,128)S(1)}, u32[]{:S(2)}, u32[]{:S(2)}) async-start(f32[8,16,512]{2,1,0:T(8,128)} %shard_map.178), calls=%async_computation.3 | async-start | bytes 524288 | tf_op jit(solution)/shard_map/all_to_all | solution.py:754
  64.9 17.0 %all-to-all-start.4 = ((bf16[32,16,512]{2,1,0:T(8,128)(2,1)}), bf16[32,16,512]{2,1,0:T(8,128)(2,1)S(1)}, u32[]{:S(2)}, u32[]{:S(2)}) async-start(bf16[32,16,512]{2,1,0:T(8,128)(2,1)} %get-tuple-element.57), calls=%async_computation.4 | async-start | bytes 1048576 | tf_op jit(solution)/shard_map/all_to_all | solution.py:754
  67.6 3.4 %collective-permute-start.4 = (bf16[8,64,128]{2,1,0:T(8,128)(2,1)S(1)}, bf16[8,64,128]{2,1,0:T(8,128)(2,1)S(1)}, u32[]{:S(2)}, u32[]{:S(2)}) collective-permute-start(bf16[8,64,128]{2,1,0:T(8,128)(2,1)S(1)} %get-tuple-element.77), channel_id=1, source_target_pairs={{0,4},{4,8},{8,12},{12,16},{16,20},{20,24},{24,28},{1,5},{5,9},{9,... | collective-permute-start | bytes 393224 | tf_op jit(solution)/shard_map/ppermute | solution.py:708
  69.6 4.4 %collective-permute-start.5 = (bf16[8,64,128]{2,1,0:T(8,128)(2,1)S(1)}, bf16[8,64,128]{2,1,0:T(8,128)(2,1)S(1)}, u32[]{:S(2)}, u32[]{:S(2)}) collective-permute-start(bf16[8,64,128]{2,1,0:T(8,128)(2,1)S(1)} %get-tuple-element.78), channel_id=1, source_target_pairs={{4,0},{8,4},{12,8},{16,12},{20,16},{24,20},{28,24},{5,1},{9,5},{13... | collective-permute-start | bytes 393224 | tf_op jit(solution)/shard_map/ppermute | solution.py:708
  70.9 41.8 %copy-start.6 = (bf16[8,64,128]{2,1,0:T(8,128)(2,1)}, bf16[8,64,128]{2,1,0:T(8,128)(2,1)S(1)}, u32[]{:S(2)}) copy-start(bf16[8,64,128]{2,1,0:T(8,128)(2,1)S(1)} %collective-permute-done.4.xlo_ref) | copy-start | bytes 393220
  74.0 7.9 %copy-start.7 = (bf16[8,64,128]{2,1,0:T(8,128)(2,1)}, bf16[8,64,128]{2,1,0:T(8,128)(2,1)S(1)}, u32[]{:S(2)}) copy-start(bf16[8,64,128]{2,1,0:T(8,128)(2,1)S(1)} %collective-permute-done.5.xhi_ref) | copy-start | bytes 393220
  74.0 7.7 %collective-permute-start.6 = (bf16[6,64,128]{2,1,0:T(8,128)(2,1)S(1)}, bf16[6,64,128]{2,1,0:T(8,128)(2,1)S(1)}, u32[]{:S(2)}, u32[]{:S(2)}) collective-permute-start(bf16[6,64,128]{2,1,0:T(8,128)(2,1)S(1)} %pad_maximum_fusion.3), channel_id=1, source_target_pairs={{0,1},{1,2},{2,3},{4,5},{5,6},{6,7},{8,9},{9,10},{10,11},{12,13},{... | collective-permute-start | bytes 294920 | tf_op jit(solution)/shard_map/ppermute | solution.py:708
  81.7 0.6 copy-start.11
  82.3 17.4 %all-to-all-start.5 = ((f32[8,128,128]{2,1,0:T(8,128)}), f32[8,128,128]{2,1,0:T(8,128)S(1)}, u32[]{:S(2)}, u32[]{:S(2)}) async-start(f32[8,128,128]{2,1,0:T(8,128)} %bitcast.8), calls=%async_computation.5 | async-start | bytes 1048576 | tf_op jit(solution)/shard_map/all_to_all | solution.py:754
  89.9 10.5 %collective-permute-start.7 = (bf16[6,64,128]{2,1,0:T(8,128)(2,1)S(1)}, bf16[6,64,128]{2,1,0:T(8,128)(2,1)S(1)}, u32[]{:S(2)}, u32[]{:S(2)}) collective-permute-start(bf16[6,64,128]{2,1,0:T(8,128)(2,1)S(1)} %pad_maximum_fusion.4), channel_id=1, source_target_pairs={{1,0},{2,1},{3,2},{5,4},{6,5},{7,6},{9,8},{10,9},{11,10},{13,12},{... | collective-permute-start | bytes 294920 | tf_op jit(solution)/shard_map/ppermute | solution.py:708
  100.5 19.0 %copy-start.13 = (bf16[6,64,128]{2,1,0:T(8,128)(2,1)}, bf16[6,64,128]{2,1,0:T(8,128)(2,1)S(1)}, u32[]{:S(2)}) copy-start(bf16[6,64,128]{2,1,0:T(8,128)(2,1)S(1)} %collective-permute-done.7.yhi_ref) | copy-start | bytes 294916
  100.5 14.2 %all-to-all-start.6 = ((bf16[4,64,512]{2,1,0:T(8,128)(2,1)}), bf16[4,64,512]{2,1,0:T(8,128)(2,1)S(1)}, u32[]{:S(2)}, u32[]{:S(2)}) async-start(bf16[4,64,512]{2,1,0:T(8,128)(2,1)} %pad_maximum_fusion), calls=%async_computation.6 | async-start | bytes 524288 | tf_op jit(solution)/shard_map/all_to_all | solution.py:754
  115.6 12.1 %all-to-all-start.7 = ((bf16[8,48,512]{2,1,0:T(8,128)(2,1)}), bf16[8,48,512]{2,1,0:T(8,128)(2,1)S(1)}, u32[]{:S(2)}, u32[]{:S(2)}) async-start(bf16[8,48,512]{2,1,0:T(8,128)(2,1)} %shard_map.183), calls=%async_computation.7 | async-start | bytes 786432 | tf_op jit(solution)/shard_map/all_to_all | solution.py:754
  122.5 5.3 %copy-start.3 = (bf16[96,128]{1,0:T(8,128)(2,1)S(1)}, bf16[96,128]{1,0:T(8,128)(2,1)}, u32[]{:S(2)}) copy-start(bf16[96,128]{1,0:T(8,128)(2,1)} %constant.33.clone.inverse_ref) | copy-start | bytes 73732

commit v14 on v13

--- a/solution.py
+++ b/solution.py
@@ -202,6 +202,8 @@
     xhi_any,
     ylo_any,
     yhi_any,
+    slab_ref,
+    message_ref,
     out_ref,
     rim_ref,
     wide_ref,
@@ -251,6 +253,15 @@
         row = (9 + k) * c
         out_ref[row : row + c] = jnp.concatenate(last[2 * k : 2 * k + 2], axis=1)
     out_ref[14 * c :] = jnp.zeros((2 * c, 2 * c), F32)
+    devices, rows, lanes = message_ref.shape
+    skip = slab_ref.shape[1]
+    per, tiles_in = rows - skip, lanes // (2 * c)
+    for device in range(devices):
+        start = device * per * tiles_in
+        share = [out_ref[start + t * per : start + (t + 1) * per] for t in range(tiles_in)]
+        message_ref[device] = jnp.concatenate(
+            [slab_ref[device].astype(F32), jnp.concatenate(share, axis=1)], axis=0
+        ).astype(BF16)
 
 
 def gelu_kernel(
@@ -289,6 +300,7 @@
 
 def finish_kernel(
     nx,
+    shares,
     scale,
     stencil_ref,
     message_ref,
@@ -305,7 +317,7 @@
         stencil = jnp.stack([stencil_ref[x, :, y * z : (y + 1) * z] for y in range(cy)])
         out_ref[:, x] = jnp.swapaxes(spectral + stencil, 0, 1)
     skip = 2 * MZ * cx // nx
-    unpack(scale, skip, message_ref, taps_ref, point_ref, packed_ref, turned_ref)
+    unpack(scale, skip, shares, message_ref, taps_ref, point_ref, packed_ref, turned_ref)
 
 
 def x_kernel(table_ref, data_ref, out_ref):
@@ -318,7 +330,7 @@
     for owner in range(out_ref.shape[0]):
         out_ref[owner, :count] = got[owner * count : (owner + 1) * count]
     if data.shape[1] > rows:
-        extra = data[:, rows:].sum(0)
+        extra = jnp.concatenate([data[i, rows:] for i in range(data.shape[0])], axis=0)
         extra = extra.astype(out_ref.dtype)
         for owner in range(out_ref.shape[0]):
             out_ref[owner, count:] = extra
@@ -339,14 +351,17 @@
     back_ref[4 * C : 5 * C, 3 * C :] = point.T.astype(BF16)
 
 
-def unpack(scale, skip, message_ref, taps_ref, point_ref, packed_ref, turned_ref):
+def unpack(scale, skip, shares, message_ref, taps_ref, point_ref, packed_ref, turned_ref):
     devices, rows, lanes = message_ref.shape
-    per, tiles_in = rows - skip, lanes // 128
+    per, tiles_in = (rows - skip) // shares, lanes // 128
     for owner in range(devices):
-        message = message_ref[owner].astype(F32)
-        for tile in range(tiles_in):
-            row = (owner * tiles_in + tile) * per
-            packed_ref[row : row + per] = message[skip:, tile * 128 : (tile + 1) * 128]
+        message = message_ref[owner].astype(F32)[skip:]
+        for share in range(shares):
+            for tile in range(tiles_in):
+                row = ((owner * shares + share) * tiles_in + tile) * per
+                packed_ref[row : row + per] = message[
+                    share * per : (share + 1) * per, tile * 128 : (tile + 1) * 128
+                ]
     for tap in range(27):
         group, e = tap // 3, tap % 3
         if e < 2:
@@ -547,12 +562,16 @@
     def store(group, part, pair, values):
         modes_ref[group, place(part, pair), :] = jnp.concatenate([values, values], axis=1)
 
-    ny = block_ref.shape[0]
+    devices, ny = data_ref.shape[0], block_ref.shape[0]
     size = x_ref.shape[1] // 3
+    skip = size * ny // devices
+    share = data_ref[0].astype(F32)[skip:]
+    for device in range(1, devices):
+        share += data_ref[device].astype(F32)[skip:]
     blocks = []
     for owner in range(ny):
         rows = jnp.concatenate(
-            [data_ref[i].astype(F32) for i in range(owner, data_ref.shape[0], ny)], axis=0
+            [data_ref[i].astype(F32)[:skip] for i in range(owner, devices, ny)], axis=0
         ).astype(BF16)
         blocks.append(
             jnp.dot(x_ref[:, :size], rows, preferred_element_type=F32)
@@ -586,7 +605,9 @@
                 )
             )
         sum_ref[group] = jnp.concatenate(total, axis=0).T
-    y_inverse(mz, sum_ref, turn_ref, out_ref, block_ref)
+    y_inverse(mz, sum_ref, turn_ref, block_ref, block_ref)
+    for owner in range(ny):
+        out_ref[owner] = jnp.concatenate([block_ref[owner], share], axis=0).astype(BF16)
 
 
 def outer_kernel(alpha, modes_ref, back_ref, table_ref, out_ref):
@@ -644,7 +665,7 @@
     )(*args)
 
 
-def per_mode(kernel, data, weight, table, tables, modes, kind, scratch=()):
+def per_mode(kernel, data, weight, table, tables, modes, kind, scratch=(), extra=0):
     _, mz, mx, my, wide = weight.shape
     groups = mz * mx // QUAD
     rows = 2 * QUAD * MY
@@ -661,7 +682,7 @@
         out_specs=[whole(), whole()],
         out_shape=[
             jax.ShapeDtypeStruct(modes_shape, modes[1]),
-            jax.ShapeDtypeStruct(block, kind),
+            jax.ShapeDtypeStruct((block[0], block[1] + extra, block[2]), kind),
         ],
         scratch_shapes=[
             pltpu.VMEM((groups, rows, C), F32),
@@ -730,23 +751,26 @@
     )[0]
 
 
-def weight_grad(grad, turned, rim):
+def weight_grad(grad, turned, rim, slab):
     cx, cy, c, z = turned.shape
+    devices, skip, lanes = slab.shape
+    extra = 16 * c * 2 * c // (devices * lanes)
     return call(
         weight_grad_kernel,
-        [((16 * c, 2 * c), F32)],
-        (grad, turned, *map(in_hbm, rim)),
+        [((devices, skip + extra, lanes), BF16)],
+        (grad, turned, *map(in_hbm, rim), slab),
         [
+            pltpu.VMEM((16 * c, 2 * c), F32),
             pltpu.VMEM((4 * c, (cy + 2) * z), BF16),
             pltpu.VMEM((cx * 3 * c, (cy + 2) * z), BF16),
             pltpu.VMEM((9 * c, 4 * c), F32),
             *(pltpu.VMEM(halo.shape, BF16) for halo in rim),
             pltpu.SemaphoreType.DMA((len(rim),)),
         ],
-        anywhere=(2, 3, 4, 5),
         mib=32,
         flops=2 * 27 * c * c * cx * cy * z,
         moved=turned.size * 8,
+        anywhere=(2, 3, 4, 5),
     )[0]
 
 
@@ -839,27 +863,23 @@
         moved=state.size * 12,
     )
 
-    grad_taps = weight_grad(grad, turned, rim)
+    message = weight_grad(grad, turned, rim, slab)
+    extra = message.shape[1] - x_rows
     faces = x_halos(grad)
-    block = swap(slab, ("gx", "gy"))
     edges = y_halos(grad, *faces)
-    block, grad_taps, ylo, *faces = together(block, grad_taps, edges[0], *faces)
-    mine = swap(grad_taps.reshape(nx, -1, 2 * c), "gx").sum(0)
+    message, ylo, yhi = together(swap(message, ("gx", "gy")), *edges)
     back_modes, block = per_mode(
         mix_back_kernel,
-        block,
+        message,
         spectral_weight,
         gather,
         (y_turn, x_mine),
         (2 * c, F32),
         BF16,
         [pltpu.VMEM((2 * QUAD * MY, c * c), BF16)],
-    )
-    packed = jnp.concatenate(jnp.split(mine, lanes // (2 * c)), axis=1).astype(BF16)
-    extra = packed.shape[0]
-    packed = jnp.broadcast_to(packed[None], (ny, extra, lanes))
-    block, yhi = together(jnp.concatenate([block, packed], axis=1), edges[1])
-    block = x_stage(x_inv, swap(block, "gy"), nx, BF16, extra)
+        extra,
+    )
+    block = x_stage(x_inv, swap(block, "gy"), nx, BF16, ny * extra)
     shape = spectral_weight.shape
     groups = modes_in.shape[0]
     early = groups * 3 // 4
@@ -873,10 +893,10 @@
         modes_in, back_modes, spread, shape, alpha, early, groups - early, grad_modes
     )
     grad_state, grad_stencil, grad_point = call(
-        functools.partial(finish_kernel, nx, alpha),
+        functools.partial(finish_kernel, nx, ny, alpha),
         [((c, cx, cy, z), F32), ((c, 27 * c), F32), ((c, c), F32)],
         (stencil_back, message, z_back),
-        [pltpu.VMEM(grad_taps.shape, F32), pltpu.VMEM((27 * c, c), F32)],
+        [pltpu.VMEM((16 * c, 2 * c), F32), pltpu.VMEM((27 * c, c), F32)],
         flops=2 * 96 * state.size,
         moved=state.size * 10,
     )

time: 131 us -> 130 us (level)
  starting transfers between devices: 50.4 us -> 45.3 us
  waiting for transfers between devices: 15.4 us -> 19.4 us
    all_to_all x7 -> x6, starting transfers between devices: 32.6 us -> 26.5 us  [swap(): return lax.all_to_all(block, axis, split_axis=0, concat_axis=0, tiled=True)]
    ppermute x8, waiting for transfers between devices: 3.05 us -> 7.05 us  [shift(): return lax.ppermute(block, axis, pairs)]
    all_to_all x7 -> x6, waiting for transfers between devices: 12.3 us -> 12.3 us  [swap(): return lax.all_to_all(block, axis, split_axis=0, concat_axis=0, tiled=True)]
  transfers between devices with their start and end apart: 15 -> 14, of which waited for: 8 -> 8; matrix products, arithmetic and copies ran while one was open for 1% -> 1% of each run, Pallas kernels for 31% -> 22%
where the time goes in v14:
time: 130 us; the launch traced here: 128 us
  Pallas kernels  49.3 us (38%)
  starting transfers between devices  45.3 us (35%)
  waiting for transfers between devices  19.4 us (15%)
  blocking collectives  11.9 us (9%)
  local copies, waits for them, and re-layouts  1.57 us (1%)
    all_to_all x6, starting transfers between devices, swap(): return lax.all_to_all(block, axis, split_axis=0, concat_axis=0, tiled=True)  26.5 us
    pallas_call x10, Pallas kernels, call(): pl.pallas_call(kernel, out_shape=[jax.ShapeDtypeStruct(*out) for out in o...  21 us
    ppermute x8, starting transfers between devices, shift(): return lax.ppermute(block, axis, pairs)  18.8 us
    pallas_call x2, Pallas kernels, per_mode(): pl.pallas_call(functools.partial(kernel, mz), in_specs=[whole(), pl.Block...  16.5 us
    all_to_all x6, waiting for transfers between devices, swap(): return lax.all_to_all(block, axis, split_axis=0, concat_axis=0, tiled=True)  12.3 us
    all_to_all x1, blocking collectives, swap(): return lax.all_to_all(block, axis, split_axis=0, concat_axis=0, tiled=True)  11.9 us
    pallas_call x2, Pallas kernels, outer(): pl.pallas_call(kernel, grid=(count,), in_specs=[group(modes), group(back)...  11.8 us
    ppermute x8, waiting for transfers between devices, shift(): return lax.ppermute(block, axis, pairs)  7.05 us
  transfers between devices with their start and end apart: 14, of which 8 were waited for; matrix products, arithmetic and copies ran while one was open for 1% of the time, Pallas kernels for 22%

profile of v14, /device:TPU:0, one launch (start us, length us, event | category | flops | bytes accessed | tf_op | source)
XLA Modules:
  0.0 128.4 jit_solution(6846278381125061)
XLA Ops:
  0.7 2.3 %shard_map.173 = (bf16[4,8,64,128]{3,2,1,0:T(8,128)(2,1)S(1)}, f32[8,16,512]{2,1,0:T(8,128)}, bf16[128,384]{1,0:T(8,128)(2,1)S(1)}, bf16[128,384]{1,0:T(8,128)(2,1)S(1)}, bf16[128,192]{1,0:T(8,128)(2,1)S(1)}) custom-call(bf16[64,4,8,128]{3,2,1,0:T(8,128)(2,1)} %field_ref.1, bf16[96,128]{1,0:T(8,128)(2,1)} %constant.28.clone.table_ref, ...), custom_call_target="tpu_custom_call" | custom-call | flops 50331648 | bytes 1310720 | tf_op jit(solution)/shard_map/pallas_call | solution.py:654
  3.0 5.2 %all-to-all-start = ((f32[8,16,512]{2,1,0:T(8,128)}), f32[8,16,512]{2,1,0:T(8,128)S(1)}, u32[]{:S(2)}, u32[]{:S(2)}) async-start(f32[8,16,512]{2,1,0:T(8,128)} %get-tuple-element.38), calls=%async_computation | async-start | bytes 524288 | tf_op jit(solution)/shard_map/all_to_all | solution.py:778
  8.2 1.3 %collective-permute-start.1 = (bf16[8,64,128]{2,1,0:T(8,128)(2,1)S(1)}, bf16[8,64,128]{2,1,0:T(8,128)(2,1)S(1)}, u32[]{:S(2)}, u32[]{:S(2)}) collective-permute-start(bf16[8,64,128]{2,1,0:T(8,128)(2,1)S(1)} %get-tuple-element.73), channel_id=1, source_target_pairs={{4,0},{8,4},{12,8},{16,12},{20,16},{24,20},{28,24},{5,1},{9,5},{13... | collective-permute-start | bytes 393224 | tf_op jit(solution)/shard_map/ppermute | solution.py:729
  9.5 3.0 %collective-permute-start = (bf16[8,64,128]{2,1,0:T(8,128)(2,1)S(1)}, bf16[8,64,128]{2,1,0:T(8,128)(2,1)S(1)}, u32[]{:S(2)}, u32[]{:S(2)}) collective-permute-start(bf16[8,64,128]{2,1,0:T(8,128)(2,1)S(1)} %get-tuple-element.74), channel_id=1, source_target_pairs={{0,4},{4,8},{8,12},{12,16},{16,20},{20,24},{24,28},{1,5},{5,9},{9,... | collective-permute-start | bytes 393224 | tf_op jit(solution)/shard_map/ppermute | solution.py:729
  12.6 1.5 %shard_map.175 = (bf16[576,256]{1,0:T(8,128)(2,1)S(1)}, bf16[576,256]{1,0:T(8,128)(2,1)S(1)}) custom-call(bf16[64,1728]{1,0:T(8,128)(2,1)} %taps_ref.1, bf16[64,64]{1,0:T(8,128)(2,1)} %point_ref.1), custom_call_target="tpu_custom_call" | custom-call | bytes 663552 | tf_op jit(solution)/shard_map/pallas_call | solution.py:654
  16.1 4.9 %all-to-all-start.1 = ((f32[4,32,512]{2,1,0:T(8,128)}), f32[4,32,512]{2,1,0:T(8,128)S(1)}, u32[]{:S(2)}, u32[]{:S(2)}) async-start(f32[4,32,512]{2,1,0:T(8,128)} %shard_map.174), calls=%async_computation.1 | async-start | bytes 524288 | tf_op jit(solution)/shard_map/all_to_all | solution.py:778
  21.0 3.9 %collective-permute-start.2 = (bf16[6,64,128]{2,1,0:T(8,128)(2,1)S(1)}, bf16[6,64,128]{2,1,0:T(8,128)(2,1)S(1)}, u32[]{:S(2)}, u32[]{:S(2)}) collective-permute-start(bf16[6,64,128]{2,1,0:T(8,128)(2,1)S(1)} %pad_maximum_fusion), channel_id=1, source_target_pairs={{0,1},{1,2},{2,3},{4,5},{5,6},{6,7},{8,9},{9,10},{10,11},{12,13},{... | collective-permute-start | bytes 294920 | tf_op jit(solution)/shard_map/ppermute | solution.py:729
  24.9 1.3 %collective-permute-start.3 = (bf16[6,64,128]{2,1,0:T(8,128)(2,1)S(1)}, bf16[6,64,128]{2,1,0:T(8,128)(2,1)S(1)}, u32[]{:S(2)}, u32[]{:S(2)}) collective-permute-start(bf16[6,64,128]{2,1,0:T(8,128)(2,1)S(1)} %pad_maximum_fusion.1), channel_id=1, source_target_pairs={{1,0},{2,1},{3,2},{5,4},{6,5},{7,6},{9,8},{10,9},{11,10},{13,12},{... | collective-permute-start | bytes 294920 | tf_op jit(solution)/shard_map/ppermute | solution.py:729
  26.2 4.8 %all-to-all-done.1.data_ref = f32[4,32,512]{2,1,0:T(8,128)S(1)} async-done(((f32[4,32,512]{2,1,0:T(8,128)}), f32[4,32,512]{2,1,0:T(8,128)S(1)}, u32[]{:S(2)}, u32[]{:S(2)}) %all-to-all-start.1) | async-done | bytes 262176 | tf_op jit(solution)/shard_map/all_to_all | solution.py:778
  31.0 7.9 %shard_map.176 = (bf16[4,256,128]{2,1,0:T(8,128)(2,1)S(1)}, f32[4,32,512]{2,1,0:T(8,128)S(1)}) custom-call(f32[4,32,512]{2,1,0:T(8,128)S(1)} %all-to-all-done.1.data_ref, bf16[2,2,8,32,4096]{4,3,2,1,0:T(8,128)(2,1)} %weight_ref.3, bf16[128,4096]{1,0:T(8,128)(2,1)} %constant.35.clone.table_ref.refs_2_, bf16[128,192]{1,0:T(8,128)(2,1)S(1)} %get-tuple-element.44.turn_ref), custom_call_target="tpu_custom_call" | custom-call | flops 33554432 | bytes 8388608 | tf_op jit(solution)/shard_map/pallas_call | solution.py:674
  39.0 11.9 %all_to_all.35.data_ref = f32[4,32,512]{2,1,0:T(8,128)S(1)} all-to-all(f32[4,32,512]{2,1,0:T(8,128)S(1)} %get-tuple-element.50), channel_id=1, replica_groups=mesh['gx'=8,'gy'=4] {'gy'}, dimensions={0} | all-to-all | bytes 524288 | tf_op jit(solution)/shard_map/all_to_all | solution.py:778
  51.8 3.7 %all-to-all-start.3 = ((f32[8,16,512]{2,1,0:T(8,128)}), f32[8,16,512]{2,1,0:T(8,128)S(1)}, u32[]{:S(2)}, u32[]{:S(2)}) async-start(f32[8,16,512]{2,1,0:T(8,128)} %shard_map.178), calls=%async_computation.3 | async-start | bytes 524288 | tf_op jit(solution)/shard_map/all_to_all | solution.py:778
  55.6 3.1 %shard_map.177.stencil_ref = f32[4,64,1024]{2,1,0:T(8,128)S(1)} custom-call(bf16[4,8,64,128]{3,2,1,0:T(8,128)(2,1)S(1)} %get-tuple-element.36.body_ref, bf16[8,64,128]{2,1,0:T(8,128)(2,1)} %copy-done.9, bf16[8,64,128]{2,1,0:T(8,128)(2,1)} %copy-done.8, bf16[6,64,128]{2,1,0:T(8,128)(2,1)} %copy-done.11, bf16[6,64,128]{2,1,0:T(8,128)(2,1)} %copy-done.12, ...), custom_call_target="tpu_custom_call" | custom-call | flops 905969664 | bytes 2097152 | tf_op jit(solution)/shard_map/pallas_call | solution.py:654
  58.6 3.9 %all-to-all-done.3.slab_ref = f32[8,16,512]{2,1,0:T(8,128)S(1)} async-done(((f32[8,16,512]{2,1,0:T(8,128)}), f32[8,16,512]{2,1,0:T(8,128)S(1)}, u32[]{:S(2)}, u32[]{:S(2)}) %all-to-all-start.3) | async-done | bytes 262176 | tf_op jit(solution)/shard_map/all_to_all | solution.py:778
  62.5 2.2 %shard_map.179 = (bf16[64,4,8,128]{3,2,1,0:T(8,128)(2,1)}, bf16[4,8,64,128]{3,2,1,0:T(8,128)(2,1)S(1)}, bf16[32,16,512]{2,1,0:T(8,128)(2,1)S(1)}) custom-call(f32[4,64,1024]{2,1,0:T(8,128)S(1)} %shard_map.177.stencil_ref, f32[8,16,512]{2,1,0:T(8,128)S(1)} %all-to-all-done.3.slab_ref, bf16[64,4,8,128]{3,2,1,0:T(8,128)(2,1)S(1)} %copy-done, ...), custom_call_target="tpu_custom_call" | custom-call | flops 100663296 | bytes 3145728 | tf_op jit(solution)/shard_map/pallas_call | solution.py:654
  64.7 4.1 %shard_map.180 = bf16[32,24,512]{2,1,0:T(8,128)(2,1)} custom-call(bf16[4,8,64,128]{3,2,1,0:T(8,128)(2,1)S(1)} %get-tuple-element.52.grad_ref.body_ref, bf16[4,8,64,128]{3,2,1,0:T(8,128)(2,1)S(1)} %get-tuple-element.36.body_ref, bf16[8,64,128]{2,1,0:T(8,128)(2,1)} %copy-done.9, bf16[8,64,128]{2,1,0:T(8,128)(2,1)} %copy-done.8, ...), custom_call_target="tpu_custom_call" | custom-call | flops 905969664 | bytes 2097152 | tf_op jit(solution)/shard_map/pallas_call | solution.py:654
  68.9 2.6 %all-to-all-start.4 = ((bf16[32,24,512]{2,1,0:T(8,128)(2,1)}), bf16[32,24,512]{2,1,0:T(8,128)(2,1)S(1)}, u32[]{:S(2)}, u32[]{:S(2)}) async-start(bf16[32,24,512]{2,1,0:T(8,128)(2,1)} %shard_map.180), calls=%async_computation.4 | async-start | bytes 1572864 | tf_op jit(solution)/shard_map/all_to_all | solution.py:778
  71.5 1.3 %collective-permute-start.5 = (bf16[8,64,128]{2,1,0:T(8,128)(2,1)S(1)}, bf16[8,64,128]{2,1,0:T(8,128)(2,1)S(1)}, u32[]{:S(2)}, u32[]{:S(2)}) collective-permute-start(bf16[8,64,128]{2,1,0:T(8,128)(2,1)S(1)} %get-tuple-element.69), channel_id=1, source_target_pairs={{4,0},{8,4},{12,8},{16,12},{20,16},{24,20},{28,24},{5,1},{9,5},{13... | collective-permute-start | bytes 393224 | tf_op jit(solution)/shard_map/ppermute | solution.py:729
  72.8 3.0 %collective-permute-start.4 = (bf16[8,64,128]{2,1,0:T(8,128)(2,1)S(1)}, bf16[8,64,128]{2,1,0:T(8,128)(2,1)S(1)}, u32[]{:S(2)}, u32[]{:S(2)}) collective-permute-start(bf16[8,64,128]{2,1,0:T(8,128)(2,1)S(1)} %get-tuple-element.70), channel_id=1, source_target_pairs={{0,4},{4,8},{8,12},{12,16},{16,20},{20,24},{24,28},{1,5},{5,9},{9,... | collective-permute-start | bytes 393224 | tf_op jit(solution)/shard_map/ppermute | solution.py:729
  76.9 3.6 %collective-permute-start.6 = (bf16[6,64,128]{2,1,0:T(8,128)(2,1)S(1)}, bf16[6,64,128]{2,1,0:T(8,128)(2,1)S(1)}, u32[]{:S(2)}, u32[]{:S(2)}) collective-permute-start(bf16[6,64,128]{2,1,0:T(8,128)(2,1)S(1)} %pad_maximum_fusion.2), channel_id=1, source_target_pairs={{0,1},{1,2},{2,3},{4,5},{5,6},{6,7},{8,9},{9,10},{10,11},{12,13},{... | collective-permute-start | bytes 294920 | tf_op jit(solution)/shard_map/ppermute | solution.py:729
  80.5 1.3 %collective-permute-start.7 = (bf16[6,64,128]{2,1,0:T(8,128)(2,1)S(1)}, bf16[6,64,128]{2,1,0:T(8,128)(2,1)S(1)}, u32[]{:S(2)}, u32[]{:S(2)}) collective-permute-start(bf16[6,64,128]{2,1,0:T(8,128)(2,1)S(1)} %pad_maximum_fusion.3), channel_id=1, source_target_pairs={{1,0},{2,1},{3,2},{5,4},{6,5},{7,6},{9,8},{10,9},{11,10},{13,12},{... | collective-permute-start | bytes 294920 | tf_op jit(solution)/shard_map/ppermute | solution.py:729
  81.8 5.1 %collective-permute-done.6.ylo_ref = bf16[6,64,128]{2,1,0:T(8,128)(2,1)S(1)} collective-permute-done((bf16[6,64,128]{2,1,0:T(8,128)(2,1)S(1)}, bf16[6,64,128]{2,1,0:T(8,128)(2,1)S(1)}, u32[]{:S(2)}, u32[]{:S(2)}) %collective-permute-start.6) | collective-permute-done | bytes 98336 | tf_op jit(solution)/shard_map/ppermute | solution.py:729
  86.9 1.1 collective-permute-done.7.yhi_ref
  88.6 2.5 %all-to-all-done.4.data_ref = bf16[32,24,512]{2,1,0:T(8,128)(2,1)S(1)} async-done(((bf16[32,24,512]{2,1,0:T(8,128)(2,1)}), bf16[32,24,512]{2,1,0:T(8,128)(2,1)S(1)}, u32[]{:S(2)}, u32[]{:S(2)}) %all-to-all-start.4) | async-done | bytes 786464 | tf_op jit(solution)/shard_map/all_to_all | solution.py:778
  91.1 8.7 %shard_map.182 = (f32[4,256,128]{2,1,0:T(8,128)S(1)}, bf16[4,40,512]{2,1,0:T(8,128)(2,1)}) custom-call(bf16[32,24,512]{2,1,0:T(8,128)(2,1)S(1)} %all-to-all-done.4.data_ref, bf16[2,2,8,32,4096]{4,3,2,1,0:T(8,128)(2,1)} %weight_ref.3, bf16[8,512]{1,0:T(8,128)(2,1)} %constant.36.clone.table_ref, bf16[128,192]{1,0:T(8,128)(2,1)S(1)} %get-tuple-element.44.turn_ref, ...), custom_call_target="tpu_custom_call" | custom-call | flops 33554432 | bytes 8388608 | tf_op jit(solution)/shard_map/pallas_call | solution.py:674
  99.8 5.6 %all-to-all-start.5 = ((bf16[4,40,512]{2,1,0:T(8,128)(2,1)}), bf16[4,40,512]{2,1,0:T(8,128)(2,1)S(1)}, u32[]{:S(2)}, u32[]{:S(2)}) async-start(bf16[4,40,512]{2,1,0:T(8,128)(2,1)} %get-tuple-element.59), calls=%async_computation.5 | async-start | bytes 327680 | tf_op jit(solution)/shard_map/all_to_all | solution.py:778
  105.4 7.4 %shard_map.184.refs_3_ = f32[2,2,8,32,4096]{4,3,2,1,0:T(8,128)} custom-call(bf16[4,256,128]{2,1,0:T(8,128)(2,1)S(1)} %get-tuple-element.60.refs_0_, f32[4,256,128]{2,1,0:T(8,128)S(1)} %get-tuple-element.61.refs_1_, bf16[128,4096]{1,0:T(8,128)(2,1)} %constant.35.clone.table_ref.refs_2_), custom_call_target="tpu_custom_call" | custom-call | flops 12582912 | bytes 12582912 | tf_op jit(solution)/shard_map/pallas_call | solution.py:707
  112.8 1.0 shard_map.183
  113.8 4.5 %all-to-all-start.6 = ((bf16[8,48,512]{2,1,0:T(8,128)(2,1)}), bf16[8,48,512]{2,1,0:T(8,128)(2,1)S(1)}, u32[]{:S(2)}, u32[]{:S(2)}) async-start(bf16[8,48,512]{2,1,0:T(8,128)(2,1)} %shard_map.183), calls=%async_computation.6 | async-start | bytes 786432 | tf_op jit(solution)/shard_map/all_to_all | solution.py:778
  118.3 3.0 %shard_map.181.stencil_ref = f32[4,64,1024]{2,1,0:T(8,128)S(1)} custom-call(bf16[4,8,64,128]{3,2,1,0:T(8,128)(2,1)S(1)} %get-tuple-element.52.grad_ref.body_ref, bf16[8,64,128]{2,1,0:T(8,128)(2,1)} %copy-done.7, bf16[8,64,128]{2,1,0:T(8,128)(2,1)} %copy-done.6, bf16[6,64,128]{2,1,0:T(8,128)(2,1)} %copy-done.10, bf16[6,64,128]{2,1,0:T(8,128)(2,1)} %copy-done.13, ...), custom_call_target="tpu_custom_call" | custom-call | flops 905969664 | bytes 2097152 | tf_op jit(solution)/shard_map/pallas_call | solution.py:654
  121.4 4.3 %shard_map.186 = f32[2,2,8,32,4096]{4,3,2,1,0:T(8,128)} custom-call(bf16[4,256,128]{2,1,0:T(8,128)(2,1)S(1)} %get-tuple-element.60.refs_0_, f32[4,256,128]{2,1,0:T(8,128)S(1)} %get-tuple-element.61.refs_1_, bf16[128,4096]{1,0:T(8,128)(2,1)} %constant.35.clone.table_ref.refs_2_, f32[2,2,8,32,4096]{4,3,2,1,0:T(8,128)} %shard_map.184.refs_3_), custom_call_target="tpu_custom_call", output_to_operand_aliasing={{}: (3, {})} | custom-call | flops 4194304 | bytes 4194304 | tf_op jit(solution)/shard_map/pallas_call | solution.py:707
  126.6 1.8 %shard_map.185 = (f32[64,4,8,128]{3,2,1,0:T(8,128)}, f32[64,1728]{1,0:T(8,128)}, f32[64,64]{1,0:T(8,128)}) custom-call(f32[4,64,1024]{2,1,0:T(8,128)S(1)} %shard_map.181.stencil_ref, bf16[8,48,512]{2,1,0:T(8,128)(2,1)S(1)} %all-to-all-done.6.message_ref, bf16[96,128]{1,0:T(8,128)(2,1)S(1)} %copy-done.3), custom_call_target="tpu_custom_call" | custom-call | flops 50331648 | bytes 2621440 | tf_op jit(solution)/shard_map/pallas_call | solution.py:654
  (51 shorter events, 5.5 us)
Async XLA Ops:
  0.6 61.9 %copy-start.1 = (bf16[96,128]{1,0:T(8,128)(2,1)S(1)}, bf16[96,128]{1,0:T(8,128)(2,1)}, u32[]{:S(2)}) copy-start(bf16[96,128]{1,0:T(8,128)(2,1)} %constant.30.clone.inverse_ref) | copy-start | bytes 73732
  0.6 61.8 %copy-start.2 = (bf16[96,128]{1,0:T(8,128)(2,1)S(1)}, bf16[96,128]{1,0:T(8,128)(2,1)}, u32[]{:S(2)}) copy-start(bf16[96,128]{1,0:T(8,128)(2,1)} %constant.29.clone.forward_ref) | copy-start | bytes 73732
  0.7 61.8 %copy-start = (bf16[64,4,8,128]{3,2,1,0:T(8,128)(2,1)S(1)}, bf16[64,4,8,128]{3,2,1,0:T(8,128)(2,1)}, u32[]{:S(2)}) copy-start(bf16[64,4,8,128]{3,2,1,0:T(8,128)(2,1)} %cot_ref.1) | copy-start | bytes 1572868
  3.0 12.1 %all-to-all-start = ((f32[8,16,512]{2,1,0:T(8,128)}), f32[8,16,512]{2,1,0:T(8,128)S(1)}, u32[]{:S(2)}, u32[]{:S(2)}) async-start(f32[8,16,512]{2,1,0:T(8,128)} %get-tuple-element.38), calls=%async_computation | async-start | bytes 524288 | tf_op jit(solution)/shard_map/all_to_all | solution.py:778
  8.2 7.9 %collective-permute-start.1 = (bf16[8,64,128]{2,1,0:T(8,128)(2,1)S(1)}, bf16[8,64,128]{2,1,0:T(8,128)(2,1)S(1)}, u32[]{:S(2)}, u32[]{:S(2)}) collective-permute-start(bf16[8,64,128]{2,1,0:T(8,128)(2,1)S(1)} %get-tuple-element.73), channel_id=1, source_target_pairs={{4,0},{8,4},{12,8},{16,12},{20,16},{24,20},{28,24},{5,1},{9,5},{13... | collective-permute-start | bytes 393224 | tf_op jit(solution)/shard_map/ppermute | solution.py:729
  9.5 6.6 %collective-permute-start = (bf16[8,64,128]{2,1,0:T(8,128)(2,1)S(1)}, bf16[8,64,128]{2,1,0:T(8,128)(2,1)S(1)}, u32[]{:S(2)}, u32[]{:S(2)}) collective-permute-start(bf16[8,64,128]{2,1,0:T(8,128)(2,1)S(1)} %get-tuple-element.74), channel_id=1, source_target_pairs={{0,4},{4,8},{8,12},{12,16},{16,20},{20,24},{24,28},{1,5},{5,9},{9,... | collective-permute-start | bytes 393224 | tf_op jit(solution)/shard_map/ppermute | solution.py:729
  14.1 16.9 %copy-start.4 = (bf16[576,256]{1,0:T(8,128)(2,1)}, bf16[576,256]{1,0:T(8,128)(2,1)S(1)}, u32[]{:S(2)}) copy-start(bf16[576,256]{1,0:T(8,128)(2,1)S(1)} %get-tuple-element.56.weight_ref) | copy-start | bytes 884740
  14.1 37.7 %copy-start.5 = (bf16[576,256]{1,0:T(8,128)(2,1)}, bf16[576,256]{1,0:T(8,128)(2,1)S(1)}, u32[]{:S(2)}) copy-start(bf16[576,256]{1,0:T(8,128)(2,1)S(1)} %get-tuple-element.48.weight_ref) | copy-start | bytes 884740
  16.1 39.5 %copy-start.8 = (bf16[8,64,128]{2,1,0:T(8,128)(2,1)}, bf16[8,64,128]{2,1,0:T(8,128)(2,1)S(1)}, u32[]{:S(2)}) copy-start(bf16[8,64,128]{2,1,0:T(8,128)(2,1)S(1)} %collective-permute-done.1.xhi_ref.xhi_any) | copy-start | bytes 393220
  16.1 35.7 %copy-start.9 = (bf16[8,64,128]{2,1,0:T(8,128)(2,1)}, bf16[8,64,128]{2,1,0:T(8,128)(2,1)S(1)}, u32[]{:S(2)}) copy-start(bf16[8,64,128]{2,1,0:T(8,128)(2,1)S(1)} %collective-permute-done.xlo_ref.xlo_any) | copy-start | bytes 393220
  16.1 15.0 %all-to-all-start.1 = ((f32[4,32,512]{2,1,0:T(8,128)}), f32[4,32,512]{2,1,0:T(8,128)S(1)}, u32[]{:S(2)}, u32[]{:S(2)}) async-start(f32[4,32,512]{2,1,0:T(8,128)} %shard_map.174), calls=%async_computation.1 | async-start | bytes 524288 | tf_op jit(solution)/shard_map/all_to_all | solution.py:778
  21.0 17.9 %collective-permute-start.2 = (bf16[6,64,128]{2,1,0:T(8,128)(2,1)S(1)}, bf16[6,64,128]{2,1,0:T(8,128)(2,1)S(1)}, u32[]{:S(2)}, u32[]{:S(2)}) collective-permute-start(bf16[6,64,128]{2,1,0:T(8,128)(2,1)S(1)} %pad_maximum_fusion), channel_id=1, source_target_pairs={{0,1},{1,2},{2,3},{4,5},{5,6},{6,7},{8,9},{9,10},{10,11},{12,13},{... | collective-permute-start | bytes 294920 | tf_op jit(solution)/shard_map/ppermute | solution.py:729
  24.9 14.0 %collective-permute-start.3 = (bf16[6,64,128]{2,1,0:T(8,128)(2,1)S(1)}, bf16[6,64,128]{2,1,0:T(8,128)(2,1)S(1)}, u32[]{:S(2)}, u32[]{:S(2)}) collective-permute-start(bf16[6,64,128]{2,1,0:T(8,128)(2,1)S(1)} %pad_maximum_fusion.1), channel_id=1, source_target_pairs={{1,0},{2,1},{3,2},{5,4},{6,5},{7,6},{9,8},{10,9},{11,10},{13,12},{... | collective-permute-start | bytes 294920 | tf_op jit(solution)/shard_map/ppermute | solution.py:729
  38.9 12.9 %copy-start.11 = (bf16[6,64,128]{2,1,0:T(8,128)(2,1)}, bf16[6,64,128]{2,1,0:T(8,128)(2,1)S(1)}, u32[]{:S(2)}) copy-start(bf16[6,64,128]{2,1,0:T(8,128)(2,1)S(1)} %collective-permute-done.2.ylo_ref.ylo_any) | copy-start | bytes 294916
  39.0 16.6 %copy-start.12 = (bf16[6,64,128]{2,1,0:T(8,128)(2,1)}, bf16[6,64,128]{2,1,0:T(8,128)(2,1)S(1)}, u32[]{:S(2)}) copy-start(bf16[6,64,128]{2,1,0:T(8,128)(2,1)S(1)} %collective-permute-done.3.yhi_ref.yhi_any) | copy-start | bytes 294916
  51.8 10.7 %all-to-all-start.3 = ((f32[8,16,512]{2,1,0:T(8,128)}), f32[8,16,512]{2,1,0:T(8,128)S(1)}, u32[]{:S(2)}, u32[]{:S(2)}) async-start(f32[8,16,512]{2,1,0:T(8,128)} %shard_map.178), calls=%async_computation.3 | async-start | bytes 524288 | tf_op jit(solution)/shard_map/all_to_all | solution.py:778
  68.9 22.2 %all-to-all-start.4 = ((bf16[32,24,512]{2,1,0:T(8,128)(2,1)}), bf16[32,24,512]{2,1,0:T(8,128)(2,1)S(1)}, u32[]{:S(2)}, u32[]{:S(2)}) async-start(bf16[32,24,512]{2,1,0:T(8,128)(2,1)} %shard_map.180), calls=%async_computation.4 | async-start | bytes 1572864 | tf_op jit(solution)/shard_map/all_to_all | solution.py:778
  71.5 4.4 %collective-permute-start.5 = (bf16[8,64,128]{2,1,0:T(8,128)(2,1)S(1)}, bf16[8,64,128]{2,1,0:T(8,128)(2,1)S(1)}, u32[]{:S(2)}, u32[]{:S(2)}) collective-permute-start(bf16[8,64,128]{2,1,0:T(8,128)(2,1)S(1)} %get-tuple-element.69), channel_id=1, source_target_pairs={{4,0},{8,4},{12,8},{16,12},{20,16},{24,20},{28,24},{5,1},{9,5},{13... | collective-permute-start | bytes 393224 | tf_op jit(solution)/shard_map/ppermute | solution.py:729
  72.8 4.0 %collective-permute-start.4 = (bf16[8,64,128]{2,1,0:T(8,128)(2,1)S(1)}, bf16[8,64,128]{2,1,0:T(8,128)(2,1)S(1)}, u32[]{:S(2)}, u32[]{:S(2)}) collective-permute-start(bf16[8,64,128]{2,1,0:T(8,128)(2,1)S(1)} %get-tuple-element.70), channel_id=1, source_target_pairs={{0,4},{4,8},{8,12},{12,16},{16,20},{20,24},{24,28},{1,5},{5,9},{9,... | collective-permute-start | bytes 393224 | tf_op jit(solution)/shard_map/ppermute | solution.py:729
  75.9 42.4 %copy-start.6 = (bf16[8,64,128]{2,1,0:T(8,128)(2,1)}, bf16[8,64,128]{2,1,0:T(8,128)(2,1)S(1)}, u32[]{:S(2)}) copy-start(bf16[8,64,128]{2,1,0:T(8,128)(2,1)S(1)} %collective-permute-done.5.xhi_ref) | copy-start | bytes 393220
  76.8 11.1 %copy-start.7 = (bf16[8,64,128]{2,1,0:T(8,128)(2,1)}, bf16[8,64,128]{2,1,0:T(8,128)(2,1)S(1)}, u32[]{:S(2)}) copy-start(bf16[8,64,128]{2,1,0:T(8,128)(2,1)S(1)} %collective-permute-done.4.xlo_ref) | copy-start | bytes 393220
  76.9 10.0 %collective-permute-start.6 = (bf16[6,64,128]{2,1,0:T(8,128)(2,1)S(1)}, bf16[6,64,128]{2,1,0:T(8,128)(2,1)S(1)}, u32[]{:S(2)}, u32[]{:S(2)}) collective-permute-start(bf16[6,64,128]{2,1,0:T(8,128)(2,1)S(1)} %pad_maximum_fusion.2), channel_id=1, source_target_pairs={{0,1},{1,2},{2,3},{4,5},{5,6},{6,7},{8,9},{9,10},{10,11},{12,13},{... | collective-permute-start | bytes 294920 | tf_op jit(solution)/shard_map/ppermute | solution.py:729
  80.5 7.4 %collective-permute-start.7 = (bf16[6,64,128]{2,1,0:T(8,128)(2,1)S(1)}, bf16[6,64,128]{2,1,0:T(8,128)(2,1)S(1)}, u32[]{:S(2)}, u32[]{:S(2)}) collective-permute-start(bf16[6,64,128]{2,1,0:T(8,128)(2,1)S(1)} %pad_maximum_fusion.3), channel_id=1, source_target_pairs={{1,0},{2,1},{3,2},{5,4},{6,5},{7,6},{9,8},{10,9},{11,10},{13,12},{... | collective-permute-start | bytes 294920 | tf_op jit(solution)/shard_map/ppermute | solution.py:729
  86.9 31.4 %copy-start.10 = (bf16[6,64,128]{2,1,0:T(8,128)(2,1)}, bf16[6,64,128]{2,1,0:T(8,128)(2,1)S(1)}, u32[]{:S(2)}) copy-start(bf16[6,64,128]{2,1,0:T(8,128)(2,1)S(1)} %collective-permute-done.6.ylo_ref) | copy-start | bytes 294916
  87.9 0.6 copy-start.13
  99.8 13.0 %all-to-all-start.5 = ((bf16[4,40,512]{2,1,0:T(8,128)(2,1)}), bf16[4,40,512]{2,1,0:T(8,128)(2,1)S(1)}, u32[]{:S(2)}, u32[]{:S(2)}) async-start(bf16[4,40,512]{2,1,0:T(8,128)(2,1)} %get-tuple-element.59), calls=%async_computation.5 | async-start | bytes 327680 | tf_op jit(solution)/shard_map/all_to_all | solution.py:778
  113.8 12.8 %all-to-all-start.6 = ((bf16[8,48,512]{2,1,0:T(8,128)(2,1)}), bf16[8,48,512]{2,1,0:T(8,128)(2,1)S(1)}, u32[]{:S(2)}, u32[]{:S(2)}) async-start(bf16[8,48,512]{2,1,0:T(8,128)(2,1)} %shard_map.183), calls=%async_computation.6 | async-start | bytes 786432 | tf_op jit(solution)/shard_map/all_to_all | solution.py:778
  121.4 5.3 %copy-start.3 = (bf16[96,128]{1,0:T(8,128)(2,1)S(1)}, bf16[96,128]{1,0:T(8,128)(2,1)}, u32[]{:S(2)}) copy-start(bf16[96,128]{1,0:T(8,128)(2,1)} %constant.31.clone.inverse_ref) | copy-start | bytes 73732

commit v15 on v14

--- a/solution.py
+++ b/solution.py
@@ -882,7 +882,7 @@
     block = x_stage(x_inv, swap(block, "gy"), nx, BF16, ny * extra)
     shape = spectral_weight.shape
     groups = modes_in.shape[0]
-    early = groups * 3 // 4
+    early = groups // 2
     grad_modes = None
     if early:
         grad_modes = outer(modes_in, back_modes, spread, shape, alpha, 0, early)

time: 130 us -> 129 us (level)
  no operation moved by 1% of the time
where the time goes in v15:
time: 129 us; the launch traced here: 127 us
  Pallas kernels  49 us (38%)
  starting transfers between devices  44.9 us (35%)
  waiting for transfers between devices  19.1 us (15%)
  blocking collectives  11.9 us (9%)
  local copies, waits for them, and re-layouts  1.57 us (1%)
    all_to_all x6, starting transfers between devices, swap(): return lax.all_to_all(block, axis, split_axis=0, concat_axis=0, tiled=True)  26.1 us
    pallas_call x10, Pallas kernels, call(): pl.pallas_call(kernel, out_shape=[jax.ShapeDtypeStruct(*out) for out in o...  21 us
    ppermute x8, starting transfers between devices, shift(): return lax.ppermute(block, axis, pairs)  18.8 us
    pallas_call x2, Pallas kernels, per_mode(): pl.pallas_call(functools.partial(kernel, mz), in_specs=[whole(), pl.Block...  16.5 us
    all_to_all x6, waiting for transfers between devices, swap(): return lax.all_to_all(block, axis, split_axis=0, concat_axis=0, tiled=True)  12.1 us
    all_to_all x1, blocking collectives, swap(): return lax.all_to_all(block, axis, split_axis=0, concat_axis=0, tiled=True)  11.9 us
    pallas_call x2, Pallas kernels, outer(): pl.pallas_call(kernel, grid=(count,), in_specs=[group(modes), group(back)...  11.5 us
    ppermute x8, waiting for transfers between devices, shift(): return lax.ppermute(block, axis, pairs)  7.05 us
  transfers between devices with their start and end apart: 14, of which 8 were waited for; matrix products, arithmetic and copies ran while one was open for 1% of the time, Pallas kernels for 22%

profile of v15, /device:TPU:0, one launch (start us, length us, event | category | flops | bytes accessed | tf_op | source)
XLA Modules:
  0.0 127.5 jit_solution(10093180768421582142)
XLA Ops:
  0.7 2.3 %shard_map.173 = (bf16[4,8,64,128]{3,2,1,0:T(8,128)(2,1)S(1)}, f32[8,16,512]{2,1,0:T(8,128)}, bf16[128,384]{1,0:T(8,128)(2,1)S(1)}, bf16[128,384]{1,0:T(8,128)(2,1)S(1)}, bf16[128,192]{1,0:T(8,128)(2,1)S(1)}) custom-call(bf16[64,4,8,128]{3,2,1,0:T(8,128)(2,1)} %field_ref.1, bf16[96,128]{1,0:T(8,128)(2,1)} %constant.28.clone.table_ref, ...), custom_call_target="tpu_custom_call" | custom-call | flops 50331648 | bytes 1310720 | tf_op jit(solution)/shard_map/pallas_call | solution.py:654
  3.0 5.2 %all-to-all-start = ((f32[8,16,512]{2,1,0:T(8,128)}), f32[8,16,512]{2,1,0:T(8,128)S(1)}, u32[]{:S(2)}, u32[]{:S(2)}) async-start(f32[8,16,512]{2,1,0:T(8,128)} %get-tuple-element.38), calls=%async_computation | async-start | bytes 524288 | tf_op jit(solution)/shard_map/all_to_all | solution.py:778
  8.2 1.3 %collective-permute-start.1 = (bf16[8,64,128]{2,1,0:T(8,128)(2,1)S(1)}, bf16[8,64,128]{2,1,0:T(8,128)(2,1)S(1)}, u32[]{:S(2)}, u32[]{:S(2)}) collective-permute-start(bf16[8,64,128]{2,1,0:T(8,128)(2,1)S(1)} %get-tuple-element.73), channel_id=1, source_target_pairs={{4,0},{8,4},{12,8},{16,12},{20,16},{24,20},{28,24},{5,1},{9,5},{13... | collective-permute-start | bytes 393224 | tf_op jit(solution)/shard_map/ppermute | solution.py:729
  9.5 3.0 %collective-permute-start = (bf16[8,64,128]{2,1,0:T(8,128)(2,1)S(1)}, bf16[8,64,128]{2,1,0:T(8,128)(2,1)S(1)}, u32[]{:S(2)}, u32[]{:S(2)}) collective-permute-start(bf16[8,64,128]{2,1,0:T(8,128)(2,1)S(1)} %get-tuple-element.74), channel_id=1, source_target_pairs={{0,4},{4,8},{8,12},{12,16},{16,20},{20,24},{24,28},{1,5},{5,9},{9,... | collective-permute-start | bytes 393224 | tf_op jit(solution)/shard_map/ppermute | solution.py:729
  12.6 1.5 %shard_map.175 = (bf16[576,256]{1,0:T(8,128)(2,1)S(1)}, bf16[576,256]{1,0:T(8,128)(2,1)S(1)}) custom-call(bf16[64,1728]{1,0:T(8,128)(2,1)} %taps_ref.1, bf16[64,64]{1,0:T(8,128)(2,1)} %point_ref.1), custom_call_target="tpu_custom_call" | custom-call | bytes 663552 | tf_op jit(solution)/shard_map/pallas_call | solution.py:654
  16.1 4.9 %all-to-all-start.1 = ((f32[4,32,512]{2,1,0:T(8,128)}), f32[4,32,512]{2,1,0:T(8,128)S(1)}, u32[]{:S(2)}, u32[]{:S(2)}) async-start(f32[4,32,512]{2,1,0:T(8,128)} %shard_map.174), calls=%async_computation.1 | async-start | bytes 524288 | tf_op jit(solution)/shard_map/all_to_all | solution.py:778
  21.0 3.9 %collective-permute-start.2 = (bf16[6,64,128]{2,1,0:T(8,128)(2,1)S(1)}, bf16[6,64,128]{2,1,0:T(8,128)(2,1)S(1)}, u32[]{:S(2)}, u32[]{:S(2)}) collective-permute-start(bf16[6,64,128]{2,1,0:T(8,128)(2,1)S(1)} %pad_maximum_fusion), channel_id=1, source_target_pairs={{0,1},{1,2},{2,3},{4,5},{5,6},{6,7},{8,9},{9,10},{10,11},{12,13},{... | collective-permute-start | bytes 294920 | tf_op jit(solution)/shard_map/ppermute | solution.py:729
  24.9 1.3 %collective-permute-start.3 = (bf16[6,64,128]{2,1,0:T(8,128)(2,1)S(1)}, bf16[6,64,128]{2,1,0:T(8,128)(2,1)S(1)}, u32[]{:S(2)}, u32[]{:S(2)}) collective-permute-start(bf16[6,64,128]{2,1,0:T(8,128)(2,1)S(1)} %pad_maximum_fusion.1), channel_id=1, source_target_pairs={{1,0},{2,1},{3,2},{5,4},{6,5},{7,6},{9,8},{10,9},{11,10},{13,12},{... | collective-permute-start | bytes 294920 | tf_op jit(solution)/shard_map/ppermute | solution.py:729
  26.2 4.8 %all-to-all-done.1.data_ref = f32[4,32,512]{2,1,0:T(8,128)S(1)} async-done(((f32[4,32,512]{2,1,0:T(8,128)}), f32[4,32,512]{2,1,0:T(8,128)S(1)}, u32[]{:S(2)}, u32[]{:S(2)}) %all-to-all-start.1) | async-done | bytes 262176 | tf_op jit(solution)/shard_map/all_to_all | solution.py:778
  31.0 7.9 %shard_map.176 = (bf16[4,256,128]{2,1,0:T(8,128)(2,1)S(1)}, f32[4,32,512]{2,1,0:T(8,128)S(1)}) custom-call(f32[4,32,512]{2,1,0:T(8,128)S(1)} %all-to-all-done.1.data_ref, bf16[2,2,8,32,4096]{4,3,2,1,0:T(8,128)(2,1)} %weight_ref.3, bf16[128,4096]{1,0:T(8,128)(2,1)} %constant.35.clone.table_ref.refs_2_, bf16[128,192]{1,0:T(8,128)(2,1)S(1)} %get-tuple-element.44.turn_ref), custom_call_target="tpu_custom_call" | custom-call | flops 33554432 | bytes 8388608 | tf_op jit(solution)/shard_map/pallas_call | solution.py:674
  39.0 11.9 %all_to_all.35.data_ref = f32[4,32,512]{2,1,0:T(8,128)S(1)} all-to-all(f32[4,32,512]{2,1,0:T(8,128)S(1)} %get-tuple-element.50), channel_id=1, replica_groups=mesh['gx'=8,'gy'=4] {'gy'}, dimensions={0} | all-to-all | bytes 524288 | tf_op jit(solution)/shard_map/all_to_all | solution.py:778
  51.8 3.7 %all-to-all-start.3 = ((f32[8,16,512]{2,1,0:T(8,128)}), f32[8,16,512]{2,1,0:T(8,128)S(1)}, u32[]{:S(2)}, u32[]{:S(2)}) async-start(f32[8,16,512]{2,1,0:T(8,128)} %shard_map.178), calls=%async_computation.3 | async-start | bytes 524288 | tf_op jit(solution)/shard_map/all_to_all | solution.py:778
  55.6 3.1 %shard_map.177.stencil_ref = f32[4,64,1024]{2,1,0:T(8,128)S(1)} custom-call(bf16[4,8,64,128]{3,2,1,0:T(8,128)(2,1)S(1)} %get-tuple-element.36.body_ref, bf16[8,64,128]{2,1,0:T(8,128)(2,1)} %copy-done.9, bf16[8,64,128]{2,1,0:T(8,128)(2,1)} %copy-done.8, bf16[6,64,128]{2,1,0:T(8,128)(2,1)} %copy-done.11, bf16[6,64,128]{2,1,0:T(8,128)(2,1)} %copy-done.12, ...), custom_call_target="tpu_custom_call" | custom-call | flops 905969664 | bytes 2097152 | tf_op jit(solution)/shard_map/pallas_call | solution.py:654
  58.6 3.9 %all-to-all-done.3.slab_ref = f32[8,16,512]{2,1,0:T(8,128)S(1)} async-done(((f32[8,16,512]{2,1,0:T(8,128)}), f32[8,16,512]{2,1,0:T(8,128)S(1)}, u32[]{:S(2)}, u32[]{:S(2)}) %all-to-all-start.3) | async-done | bytes 262176 | tf_op jit(solution)/shard_map/all_to_all | solution.py:778
  62.5 2.2 %shard_map.179 = (bf16[64,4,8,128]{3,2,1,0:T(8,128)(2,1)}, bf16[4,8,64,128]{3,2,1,0:T(8,128)(2,1)S(1)}, bf16[32,16,512]{2,1,0:T(8,128)(2,1)S(1)}) custom-call(f32[4,64,1024]{2,1,0:T(8,128)S(1)} %shard_map.177.stencil_ref, f32[8,16,512]{2,1,0:T(8,128)S(1)} %all-to-all-done.3.slab_ref, bf16[64,4,8,128]{3,2,1,0:T(8,128)(2,1)S(1)} %copy-done, ...), custom_call_target="tpu_custom_call" | custom-call | flops 100663296 | bytes 3145728 | tf_op jit(solution)/shard_map/pallas_call | solution.py:654
  64.7 4.1 %shard_map.180 = bf16[32,24,512]{2,1,0:T(8,128)(2,1)} custom-call(bf16[4,8,64,128]{3,2,1,0:T(8,128)(2,1)S(1)} %get-tuple-element.52.grad_ref.body_ref, bf16[4,8,64,128]{3,2,1,0:T(8,128)(2,1)S(1)} %get-tuple-element.36.body_ref, bf16[8,64,128]{2,1,0:T(8,128)(2,1)} %copy-done.9, bf16[8,64,128]{2,1,0:T(8,128)(2,1)} %copy-done.8, ...), custom_call_target="tpu_custom_call" | custom-call | flops 905969664 | bytes 2097152 | tf_op jit(solution)/shard_map/pallas_call | solution.py:654
  68.9 2.6 %all-to-all-start.4 = ((bf16[32,24,512]{2,1,0:T(8,128)(2,1)}), bf16[32,24,512]{2,1,0:T(8,128)(2,1)S(1)}, u32[]{:S(2)}, u32[]{:S(2)}) async-start(bf16[32,24,512]{2,1,0:T(8,128)(2,1)} %shard_map.180), calls=%async_computation.4 | async-start | bytes 1572864 | tf_op jit(solution)/shard_map/all_to_all | solution.py:778
  71.5 1.3 %collective-permute-start.5 = (bf16[8,64,128]{2,1,0:T(8,128)(2,1)S(1)}, bf16[8,64,128]{2,1,0:T(8,128)(2,1)S(1)}, u32[]{:S(2)}, u32[]{:S(2)}) collective-permute-start(bf16[8,64,128]{2,1,0:T(8,128)(2,1)S(1)} %get-tuple-element.69), channel_id=1, source_target_pairs={{4,0},{8,4},{12,8},{16,12},{20,16},{24,20},{28,24},{5,1},{9,5},{13... | collective-permute-start | bytes 393224 | tf_op jit(solution)/shard_map/ppermute | solution.py:729
  72.8 3.0 %collective-permute-start.4 = (bf16[8,64,128]{2,1,0:T(8,128)(2,1)S(1)}, bf16[8,64,128]{2,1,0:T(8,128)(2,1)S(1)}, u32[]{:S(2)}, u32[]{:S(2)}) collective-permute-start(bf16[8,64,128]{2,1,0:T(8,128)(2,1)S(1)} %get-tuple-element.70), channel_id=1, source_target_pairs={{0,4},{4,8},{8,12},{12,16},{16,20},{20,24},{24,28},{1,5},{5,9},{9,... | collective-permute-start | bytes 393224 | tf_op jit(solution)/shard_map/ppermute | solution.py:729
  76.9 3.6 %collective-permute-start.6 = (bf16[6,64,128]{2,1,0:T(8,128)(2,1)S(1)}, bf16[6,64,128]{2,1,0:T(8,128)(2,1)S(1)}, u32[]{:S(2)}, u32[]{:S(2)}) collective-permute-start(bf16[6,64,128]{2,1,0:T(8,128)(2,1)S(1)} %pad_maximum_fusion.2), channel_id=1, source_target_pairs={{0,1},{1,2},{2,3},{4,5},{5,6},{6,7},{8,9},{9,10},{10,11},{12,13},{... | collective-permute-start | bytes 294920 | tf_op jit(solution)/shard_map/ppermute | solution.py:729
  80.5 1.3 %collective-permute-start.7 = (bf16[6,64,128]{2,1,0:T(8,128)(2,1)S(1)}, bf16[6,64,128]{2,1,0:T(8,128)(2,1)S(1)}, u32[]{:S(2)}, u32[]{:S(2)}) collective-permute-start(bf16[6,64,128]{2,1,0:T(8,128)(2,1)S(1)} %pad_maximum_fusion.3), channel_id=1, source_target_pairs={{1,0},{2,1},{3,2},{5,4},{6,5},{7,6},{9,8},{10,9},{11,10},{13,12},{... | collective-permute-start | bytes 294920 | tf_op jit(solution)/shard_map/ppermute | solution.py:729
  81.8 5.1 %collective-permute-done.6.ylo_ref = bf16[6,64,128]{2,1,0:T(8,128)(2,1)S(1)} collective-permute-done((bf16[6,64,128]{2,1,0:T(8,128)(2,1)S(1)}, bf16[6,64,128]{2,1,0:T(8,128)(2,1)S(1)}, u32[]{:S(2)}, u32[]{:S(2)}) %collective-permute-start.6) | collective-permute-done | bytes 98336 | tf_op jit(solution)/shard_map/ppermute | solution.py:729
  86.9 1.1 collective-permute-done.7.yhi_ref
  88.6 2.5 %all-to-all-done.4.data_ref = bf16[32,24,512]{2,1,0:T(8,128)(2,1)S(1)} async-done(((bf16[32,24,512]{2,1,0:T(8,128)(2,1)}), bf16[32,24,512]{2,1,0:T(8,128)(2,1)S(1)}, u32[]{:S(2)}, u32[]{:S(2)}) %all-to-all-start.4) | async-done | bytes 786464 | tf_op jit(solution)/shard_map/all_to_all | solution.py:778
  91.1 8.7 %shard_map.182 = (f32[4,256,128]{2,1,0:T(8,128)S(1)}, bf16[4,40,512]{2,1,0:T(8,128)(2,1)}) custom-call(bf16[32,24,512]{2,1,0:T(8,128)(2,1)S(1)} %all-to-all-done.4.data_ref, bf16[2,2,8,32,4096]{4,3,2,1,0:T(8,128)(2,1)} %weight_ref.3, bf16[8,512]{1,0:T(8,128)(2,1)} %constant.36.clone.table_ref, bf16[128,192]{1,0:T(8,128)(2,1)S(1)} %get-tuple-element.44.turn_ref, ...), custom_call_target="tpu_custom_call" | custom-call | flops 33554432 | bytes 8388608 | tf_op jit(solution)/shard_map/pallas_call | solution.py:674
  99.8 5.6 %all-to-all-start.5 = ((bf16[4,40,512]{2,1,0:T(8,128)(2,1)}), bf16[4,40,512]{2,1,0:T(8,128)(2,1)S(1)}, u32[]{:S(2)}, u32[]{:S(2)}) async-start(bf16[4,40,512]{2,1,0:T(8,128)(2,1)} %get-tuple-element.59), calls=%async_computation.5 | async-start | bytes 327680 | tf_op jit(solution)/shard_map/all_to_all | solution.py:778
  105.4 5.7 %shard_map.184.refs_3_ = f32[2,2,8,32,4096]{4,3,2,1,0:T(8,128)} custom-call(bf16[4,256,128]{2,1,0:T(8,128)(2,1)S(1)} %get-tuple-element.60.refs_0_, f32[4,256,128]{2,1,0:T(8,128)S(1)} %get-tuple-element.61.refs_1_, bf16[128,4096]{1,0:T(8,128)(2,1)} %constant.35.clone.table_ref.refs_2_), custom_call_target="tpu_custom_call" | custom-call | flops 8388608 | bytes 8388608 | tf_op jit(solution)/shard_map/pallas_call | solution.py:707
  111.8 1.0 shard_map.183
  112.8 4.1 %all-to-all-start.6 = ((bf16[8,48,512]{2,1,0:T(8,128)(2,1)}), bf16[8,48,512]{2,1,0:T(8,128)(2,1)S(1)}, u32[]{:S(2)}, u32[]{:S(2)}) async-start(bf16[8,48,512]{2,1,0:T(8,128)(2,1)} %shard_map.183), calls=%async_computation.6 | async-start | bytes 786432 | tf_op jit(solution)/shard_map/all_to_all | solution.py:778
  116.9 3.0 %shard_map.181.stencil_ref = f32[4,64,1024]{2,1,0:T(8,128)S(1)} custom-call(bf16[4,8,64,128]{3,2,1,0:T(8,128)(2,1)S(1)} %get-tuple-element.52.grad_ref.body_ref, bf16[8,64,128]{2,1,0:T(8,128)(2,1)} %copy-done.7, bf16[8,64,128]{2,1,0:T(8,128)(2,1)} %copy-done.6, bf16[6,64,128]{2,1,0:T(8,128)(2,1)} %copy-done.10, bf16[6,64,128]{2,1,0:T(8,128)(2,1)} %copy-done.13, ...), custom_call_target="tpu_custom_call" | custom-call | flops 905969664 | bytes 2097152 | tf_op jit(solution)/shard_map/pallas_call | solution.py:654
  119.9 5.8 %shard_map.186 = f32[2,2,8,32,4096]{4,3,2,1,0:T(8,128)} custom-call(bf16[4,256,128]{2,1,0:T(8,128)(2,1)S(1)} %get-tuple-element.60.refs_0_, f32[4,256,128]{2,1,0:T(8,128)S(1)} %get-tuple-element.61.refs_1_, bf16[128,4096]{1,0:T(8,128)(2,1)} %constant.35.clone.table_ref.refs_2_, f32[2,2,8,32,4096]{4,3,2,1,0:T(8,128)} %shard_map.184.refs_3_), custom_call_target="tpu_custom_call", output_to_operand_aliasing={{}: (3, {})} | custom-call | flops 8388608 | bytes 8388608 | tf_op jit(solution)/shard_map/pallas_call | solution.py:707
  125.7 1.8 %shard_map.185 = (f32[64,4,8,128]{3,2,1,0:T(8,128)}, f32[64,1728]{1,0:T(8,128)}, f32[64,64]{1,0:T(8,128)}) custom-call(f32[4,64,1024]{2,1,0:T(8,128)S(1)} %shard_map.181.stencil_ref, bf16[8,48,512]{2,1,0:T(8,128)(2,1)S(1)} %all-to-all-done.6.message_ref, bf16[96,128]{1,0:T(8,128)(2,1)S(1)} %copy-done.3), custom_call_target="tpu_custom_call" | custom-call | flops 50331648 | bytes 2621440 | tf_op jit(solution)/shard_map/pallas_call | solution.py:654
  (51 shorter events, 5.3 us)
Async XLA Ops:
  0.6 61.9 %copy-start.1 = (bf16[96,128]{1,0:T(8,128)(2,1)S(1)}, bf16[96,128]{1,0:T(8,128)(2,1)}, u32[]{:S(2)}) copy-start(bf16[96,128]{1,0:T(8,128)(2,1)} %constant.30.clone.inverse_ref) | copy-start | bytes 73732
  0.6 61.8 %copy-start.2 = (bf16[96,128]{1,0:T(8,128)(2,1)S(1)}, bf16[96,128]{1,0:T(8,128)(2,1)}, u32[]{:S(2)}) copy-start(bf16[96,128]{1,0:T(8,128)(2,1)} %constant.29.clone.forward_ref) | copy-start | bytes 73732
  0.7 61.8 %copy-start = (bf16[64,4,8,128]{3,2,1,0:T(8,128)(2,1)S(1)}, bf16[64,4,8,128]{3,2,1,0:T(8,128)(2,1)}, u32[]{:S(2)}) copy-start(bf16[64,4,8,128]{3,2,1,0:T(8,128)(2,1)} %cot_ref.1) | copy-start | bytes 1572868
  3.0 12.1 %all-to-all-start = ((f32[8,16,512]{2,1,0:T(8,128)}), f32[8,16,512]{2,1,0:T(8,128)S(1)}, u32[]{:S(2)}, u32[]{:S(2)}) async-start(f32[8,16,512]{2,1,0:T(8,128)} %get-tuple-element.38), calls=%async_computation | async-start | bytes 524288 | tf_op jit(solution)/shard_map/all_to_all | solution.py:778
  8.2 7.9 %collective-permute-start.1 = (bf16[8,64,128]{2,1,0:T(8,128)(2,1)S(1)}, bf16[8,64,128]{2,1,0:T(8,128)(2,1)S(1)}, u32[]{:S(2)}, u32[]{:S(2)}) collective-permute-start(bf16[8,64,128]{2,1,0:T(8,128)(2,1)S(1)} %get-tuple-element.73), channel_id=1, source_target_pairs={{4,0},{8,4},{12,8},{16,12},{20,16},{24,20},{28,24},{5,1},{9,5},{13... | collective-permute-start | bytes 393224 | tf_op jit(solution)/shard_map/ppermute | solution.py:729
  9.5 6.6 %collective-permute-start = (bf16[8,64,128]{2,1,0:T(8,128)(2,1)S(1)}, bf16[8,64,128]{2,1,0:T(8,128)(2,1)S(1)}, u32[]{:S(2)}, u32[]{:S(2)}) collective-permute-start(bf16[8,64,128]{2,1,0:T(8,128)(2,1)S(1)} %get-tuple-element.74), channel_id=1, source_target_pairs={{0,4},{4,8},{8,12},{12,16},{16,20},{20,24},{24,28},{1,5},{5,9},{9,... | collective-permute-start | bytes 393224 | tf_op jit(solution)/shard_map/ppermute | solution.py:729
  14.1 16.9 %copy-start.4 = (bf16[576,256]{1,0:T(8,128)(2,1)}, bf16[576,256]{1,0:T(8,128)(2,1)S(1)}, u32[]{:S(2)}) copy-start(bf16[576,256]{1,0:T(8,128)(2,1)S(1)} %get-tuple-element.56.weight_ref) | copy-start | bytes 884740
  14.1 37.7 %copy-start.5 = (bf16[576,256]{1,0:T(8,128)(2,1)}, bf16[576,256]{1,0:T(8,128)(2,1)S(1)}, u32[]{:S(2)}) copy-start(bf16[576,256]{1,0:T(8,128)(2,1)S(1)} %get-tuple-element.48.weight_ref) | copy-start | bytes 884740
  16.1 39.5 %copy-start.8 = (bf16[8,64,128]{2,1,0:T(8,128)(2,1)}, bf16[8,64,128]{2,1,0:T(8,128)(2,1)S(1)}, u32[]{:S(2)}) copy-start(bf16[8,64,128]{2,1,0:T(8,128)(2,1)S(1)} %collective-permute-done.1.xhi_ref.xhi_any) | copy-start | bytes 393220
  16.1 35.7 %copy-start.9 = (bf16[8,64,128]{2,1,0:T(8,128)(2,1)}, bf16[8,64,128]{2,1,0:T(8,128)(2,1)S(1)}, u32[]{:S(2)}) copy-start(bf16[8,64,128]{2,1,0:T(8,128)(2,1)S(1)} %collective-permute-done.xlo_ref.xlo_any) | copy-start | bytes 393220
  16.1 15.0 %all-to-all-start.1 = ((f32[4,32,512]{2,1,0:T(8,128)}), f32[4,32,512]{2,1,0:T(8,128)S(1)}, u32[]{:S(2)}, u32[]{:S(2)}) async-start(f32[4,32,512]{2,1,0:T(8,128)} %shard_map.174), calls=%async_computation.1 | async-start | bytes 524288 | tf_op jit(solution)/shard_map/all_to_all | solution.py:778
  21.0 17.9 %collective-permute-start.2 = (bf16[6,64,128]{2,1,0:T(8,128)(2,1)S(1)}, bf16[6,64,128]{2,1,0:T(8,128)(2,1)S(1)}, u32[]{:S(2)}, u32[]{:S(2)}) collective-permute-start(bf16[6,64,128]{2,1,0:T(8,128)(2,1)S(1)} %pad_maximum_fusion), channel_id=1, source_target_pairs={{0,1},{1,2},{2,3},{4,5},{5,6},{6,7},{8,9},{9,10},{10,11},{12,13},{... | collective-permute-start | bytes 294920 | tf_op jit(solution)/shard_map/ppermute | solution.py:729
  24.9 14.0 %collective-permute-start.3 = (bf16[6,64,128]{2,1,0:T(8,128)(2,1)S(1)}, bf16[6,64,128]{2,1,0:T(8,128)(2,1)S(1)}, u32[]{:S(2)}, u32[]{:S(2)}) collective-permute-start(bf16[6,64,128]{2,1,0:T(8,128)(2,1)S(1)} %pad_maximum_fusion.1), channel_id=1, source_target_pairs={{1,0},{2,1},{3,2},{5,4},{6,5},{7,6},{9,8},{10,9},{11,10},{13,12},{... | collective-permute-start | bytes 294920 | tf_op jit(solution)/shard_map/ppermute | solution.py:729
  38.9 12.9 %copy-start.11 = (bf16[6,64,128]{2,1,0:T(8,128)(2,1)}, bf16[6,64,128]{2,1,0:T(8,128)(2,1)S(1)}, u32[]{:S(2)}) copy-start(bf16[6,64,128]{2,1,0:T(8,128)(2,1)S(1)} %collective-permute-done.2.ylo_ref.ylo_any) | copy-start | bytes 294916
  39.0 16.6 %copy-start.12 = (bf16[6,64,128]{2,1,0:T(8,128)(2,1)}, bf16[6,64,128]{2,1,0:T(8,128)(2,1)S(1)}, u32[]{:S(2)}) copy-start(bf16[6,64,128]{2,1,0:T(8,128)(2,1)S(1)} %collective-permute-done.3.yhi_ref.yhi_any) | copy-start | bytes 294916
  51.8 10.7 %all-to-all-start.3 = ((f32[8,16,512]{2,1,0:T(8,128)}), f32[8,16,512]{2,1,0:T(8,128)S(1)}, u32[]{:S(2)}, u32[]{:S(2)}) async-start(f32[8,16,512]{2,1,0:T(8,128)} %shard_map.178), calls=%async_computation.3 | async-start | bytes 524288 | tf_op jit(solution)/shard_map/all_to_all | solution.py:778
  68.9 22.2 %all-to-all-start.4 = ((bf16[32,24,512]{2,1,0:T(8,128)(2,1)}), bf16[32,24,512]{2,1,0:T(8,128)(2,1)S(1)}, u32[]{:S(2)}, u32[]{:S(2)}) async-start(bf16[32,24,512]{2,1,0:T(8,128)(2,1)} %shard_map.180), calls=%async_computation.4 | async-start | bytes 1572864 | tf_op jit(solution)/shard_map/all_to_all | solution.py:778
  71.5 4.4 %collective-permute-start.5 = (bf16[8,64,128]{2,1,0:T(8,128)(2,1)S(1)}, bf16[8,64,128]{2,1,0:T(8,128)(2,1)S(1)}, u32[]{:S(2)}, u32[]{:S(2)}) collective-permute-start(bf16[8,64,128]{2,1,0:T(8,128)(2,1)S(1)} %get-tuple-element.69), channel_id=1, source_target_pairs={{4,0},{8,4},{12,8},{16,12},{20,16},{24,20},{28,24},{5,1},{9,5},{13... | collective-permute-start | bytes 393224 | tf_op jit(solution)/shard_map/ppermute | solution.py:729
  72.8 4.0 %collective-permute-start.4 = (bf16[8,64,128]{2,1,0:T(8,128)(2,1)S(1)}, bf16[8,64,128]{2,1,0:T(8,128)(2,1)S(1)}, u32[]{:S(2)}, u32[]{:S(2)}) collective-permute-start(bf16[8,64,128]{2,1,0:T(8,128)(2,1)S(1)} %get-tuple-element.70), channel_id=1, source_target_pairs={{0,4},{4,8},{8,12},{12,16},{16,20},{20,24},{24,28},{1,5},{5,9},{9,... | collective-permute-start | bytes 393224 | tf_op jit(solution)/shard_map/ppermute | solution.py:729
  75.9 41.0 %copy-start.6 = (bf16[8,64,128]{2,1,0:T(8,128)(2,1)}, bf16[8,64,128]{2,1,0:T(8,128)(2,1)S(1)}, u32[]{:S(2)}) copy-start(bf16[8,64,128]{2,1,0:T(8,128)(2,1)S(1)} %collective-permute-done.5.xhi_ref) | copy-start | bytes 393220
  76.8 11.1 %copy-start.7 = (bf16[8,64,128]{2,1,0:T(8,128)(2,1)}, bf16[8,64,128]{2,1,0:T(8,128)(2,1)S(1)}, u32[]{:S(2)}) copy-start(bf16[8,64,128]{2,1,0:T(8,128)(2,1)S(1)} %collective-permute-done.4.xlo_ref) | copy-start | bytes 393220
  76.9 10.0 %collective-permute-start.6 = (bf16[6,64,128]{2,1,0:T(8,128)(2,1)S(1)}, bf16[6,64,128]{2,1,0:T(8,128)(2,1)S(1)}, u32[]{:S(2)}, u32[]{:S(2)}) collective-permute-start(bf16[6,64,128]{2,1,0:T(8,128)(2,1)S(1)} %pad_maximum_fusion.2), channel_id=1, source_target_pairs={{0,1},{1,2},{2,3},{4,5},{5,6},{6,7},{8,9},{9,10},{10,11},{12,13},{... | collective-permute-start | bytes 294920 | tf_op jit(solution)/shard_map/ppermute | solution.py:729
  80.5 7.4 %collective-permute-start.7 = (bf16[6,64,128]{2,1,0:T(8,128)(2,1)S(1)}, bf16[6,64,128]{2,1,0:T(8,128)(2,1)S(1)}, u32[]{:S(2)}, u32[]{:S(2)}) collective-permute-start(bf16[6,64,128]{2,1,0:T(8,128)(2,1)S(1)} %pad_maximum_fusion.3), channel_id=1, source_target_pairs={{1,0},{2,1},{3,2},{5,4},{6,5},{7,6},{9,8},{10,9},{11,10},{13,12},{... | collective-permute-start | bytes 294920 | tf_op jit(solution)/shard_map/ppermute | solution.py:729
  86.9 30.0 %copy-start.10 = (bf16[6,64,128]{2,1,0:T(8,128)(2,1)}, bf16[6,64,128]{2,1,0:T(8,128)(2,1)S(1)}, u32[]{:S(2)}) copy-start(bf16[6,64,128]{2,1,0:T(8,128)(2,1)S(1)} %collective-permute-done.6.ylo_ref) | copy-start | bytes 294916
  87.9 0.6 copy-start.13
  99.8 12.0 %all-to-all-start.5 = ((bf16[4,40,512]{2,1,0:T(8,128)(2,1)}), bf16[4,40,512]{2,1,0:T(8,128)(2,1)S(1)}, u32[]{:S(2)}, u32[]{:S(2)}) async-start(bf16[4,40,512]{2,1,0:T(8,128)(2,1)} %get-tuple-element.59), calls=%async_computation.5 | async-start | bytes 327680 | tf_op jit(solution)/shard_map/all_to_all | solution.py:778
  112.8 12.9 %all-to-all-start.6 = ((bf16[8,48,512]{2,1,0:T(8,128)(2,1)}), bf16[8,48,512]{2,1,0:T(8,128)(2,1)S(1)}, u32[]{:S(2)}, u32[]{:S(2)}) async-start(bf16[8,48,512]{2,1,0:T(8,128)(2,1)} %shard_map.183), calls=%async_computation.6 | async-start | bytes 786432 | tf_op jit(solution)/shard_map/all_to_all | solution.py:778
  119.9 5.8 %copy-start.3 = (bf16[96,128]{1,0:T(8,128)(2,1)S(1)}, bf16[96,128]{1,0:T(8,128)(2,1)}, u32[]{:S(2)}) copy-start(bf16[96,128]{1,0:T(8,128)(2,1)} %constant.31.clone.inverse_ref) | copy-start | bytes 73732

commit v16 on v15

--- a/solution.py
+++ b/solution.py
@@ -377,7 +377,7 @@
 
 
 QUAD = 4
-SPAN = 8 * C
+SPAN = 16 * C
 
 
 def y_forward(mz, blocks, table_ref, rows_ref, store):

time: 129 us -> 129 us (level)
  no operation moved by 1% of the time
where the time goes in v16:
time: 129 us; the launch traced here: 128 us
  Pallas kernels  49.3 us (38%)
  starting transfers between devices  44.9 us (35%)
  waiting for transfers between devices  19.1 us (15%)
  blocking collectives  11.9 us (9%)
  local copies, waits for them, and re-layouts  1.57 us (1%)
    all_to_all x6, starting transfers between devices, swap(): return lax.all_to_all(block, axis, split_axis=0, concat_axis=0, tiled=True)  26.1 us
    pallas_call x10, Pallas kernels, call(): pl.pallas_call(kernel, out_shape=[jax.ShapeDtypeStruct(*out) for out in o...  21 us
    ppermute x8, starting transfers between devices, shift(): return lax.ppermute(block, axis, pairs)  18.8 us
    pallas_call x2, Pallas kernels, per_mode(): pl.pallas_call(functools.partial(kernel, mz), in_specs=[whole(), pl.Block...  16.9 us
    all_to_all x6, waiting for transfers between devices, swap(): return lax.all_to_all(block, axis, split_axis=0, concat_axis=0, tiled=True)  12.1 us
    all_to_all x1, blocking collectives, swap(): return lax.all_to_all(block, axis, split_axis=0, concat_axis=0, tiled=True)  11.9 us
    pallas_call x2, Pallas kernels, outer(): pl.pallas_call(kernel, grid=(count,), in_specs=[group(modes), group(back)...  11.5 us
    ppermute x8, waiting for transfers between devices, shift(): return lax.ppermute(block, axis, pairs)  7.05 us
  transfers between devices with their start and end apart: 14, of which 8 were waited for; matrix products, arithmetic and copies ran while one was open for 1% of the time, Pallas kernels for 22%

profile of v16, /device:TPU:0, one launch (start us, length us, event | category | flops | bytes accessed | tf_op | source)
XLA Modules:
  0.0 127.8 jit_solution(5191638392489302726)
XLA Ops:
  0.7 2.3 %shard_map.173 = (bf16[4,8,64,128]{3,2,1,0:T(8,128)(2,1)S(1)}, f32[8,16,512]{2,1,0:T(8,128)}, bf16[128,384]{1,0:T(8,128)(2,1)S(1)}, bf16[128,384]{1,0:T(8,128)(2,1)S(1)}, bf16[128,192]{1,0:T(8,128)(2,1)S(1)}) custom-call(bf16[64,4,8,128]{3,2,1,0:T(8,128)(2,1)} %field_ref.1, bf16[96,128]{1,0:T(8,128)(2,1)} %constant.28.clone.table_ref, ...), custom_call_target="tpu_custom_call" | custom-call | flops 50331648 | bytes 1310720 | tf_op jit(solution)/shard_map/pallas_call | solution.py:654
  3.0 5.2 %all-to-all-start = ((f32[8,16,512]{2,1,0:T(8,128)}), f32[8,16,512]{2,1,0:T(8,128)S(1)}, u32[]{:S(2)}, u32[]{:S(2)}) async-start(f32[8,16,512]{2,1,0:T(8,128)} %get-tuple-element.38), calls=%async_computation | async-start | bytes 524288 | tf_op jit(solution)/shard_map/all_to_all | solution.py:778
  8.2 1.3 %collective-permute-start.1 = (bf16[8,64,128]{2,1,0:T(8,128)(2,1)S(1)}, bf16[8,64,128]{2,1,0:T(8,128)(2,1)S(1)}, u32[]{:S(2)}, u32[]{:S(2)}) collective-permute-start(bf16[8,64,128]{2,1,0:T(8,128)(2,1)S(1)} %get-tuple-element.73), channel_id=1, source_target_pairs={{4,0},{8,4},{12,8},{16,12},{20,16},{24,20},{28,24},{5,1},{9,5},{13... | collective-permute-start | bytes 393224 | tf_op jit(solution)/shard_map/ppermute | solution.py:729
  9.5 3.0 %collective-permute-start = (bf16[8,64,128]{2,1,0:T(8,128)(2,1)S(1)}, bf16[8,64,128]{2,1,0:T(8,128)(2,1)S(1)}, u32[]{:S(2)}, u32[]{:S(2)}) collective-permute-start(bf16[8,64,128]{2,1,0:T(8,128)(2,1)S(1)} %get-tuple-element.74), channel_id=1, source_target_pairs={{0,4},{4,8},{8,12},{12,16},{16,20},{20,24},{24,28},{1,5},{5,9},{9,... | collective-permute-start | bytes 393224 | tf_op jit(solution)/shard_map/ppermute | solution.py:729
  12.6 1.5 %shard_map.175 = (bf16[576,256]{1,0:T(8,128)(2,1)S(1)}, bf16[576,256]{1,0:T(8,128)(2,1)S(1)}) custom-call(bf16[64,1728]{1,0:T(8,128)(2,1)} %taps_ref.1, bf16[64,64]{1,0:T(8,128)(2,1)} %point_ref.1), custom_call_target="tpu_custom_call" | custom-call | bytes 663552 | tf_op jit(solution)/shard_map/pallas_call | solution.py:654
  16.1 4.9 %all-to-all-start.1 = ((f32[4,32,512]{2,1,0:T(8,128)}), f32[4,32,512]{2,1,0:T(8,128)S(1)}, u32[]{:S(2)}, u32[]{:S(2)}) async-start(f32[4,32,512]{2,1,0:T(8,128)} %shard_map.174), calls=%async_computation.1 | async-start | bytes 524288 | tf_op jit(solution)/shard_map/all_to_all | solution.py:778
  21.0 3.9 %collective-permute-start.2 = (bf16[6,64,128]{2,1,0:T(8,128)(2,1)S(1)}, bf16[6,64,128]{2,1,0:T(8,128)(2,1)S(1)}, u32[]{:S(2)}, u32[]{:S(2)}) collective-permute-start(bf16[6,64,128]{2,1,0:T(8,128)(2,1)S(1)} %pad_maximum_fusion), channel_id=1, source_target_pairs={{0,1},{1,2},{2,3},{4,5},{5,6},{6,7},{8,9},{9,10},{10,11},{12,13},{... | collective-permute-start | bytes 294920 | tf_op jit(solution)/shard_map/ppermute | solution.py:729
  24.9 1.3 %collective-permute-start.3 = (bf16[6,64,128]{2,1,0:T(8,128)(2,1)S(1)}, bf16[6,64,128]{2,1,0:T(8,128)(2,1)S(1)}, u32[]{:S(2)}, u32[]{:S(2)}) collective-permute-start(bf16[6,64,128]{2,1,0:T(8,128)(2,1)S(1)} %pad_maximum_fusion.1), channel_id=1, source_target_pairs={{1,0},{2,1},{3,2},{5,4},{6,5},{7,6},{9,8},{10,9},{11,10},{13,12},{... | collective-permute-start | bytes 294920 | tf_op jit(solution)/shard_map/ppermute | solution.py:729
  26.2 4.8 %all-to-all-done.1.data_ref = f32[4,32,512]{2,1,0:T(8,128)S(1)} async-done(((f32[4,32,512]{2,1,0:T(8,128)}), f32[4,32,512]{2,1,0:T(8,128)S(1)}, u32[]{:S(2)}, u32[]{:S(2)}) %all-to-all-start.1) | async-done | bytes 262176 | tf_op jit(solution)/shard_map/all_to_all | solution.py:778
  31.0 8.0 %shard_map.176 = (bf16[4,256,128]{2,1,0:T(8,128)(2,1)S(1)}, f32[4,32,512]{2,1,0:T(8,128)S(1)}) custom-call(f32[4,32,512]{2,1,0:T(8,128)S(1)} %all-to-all-done.1.data_ref, bf16[2,2,8,32,4096]{4,3,2,1,0:T(8,128)(2,1)} %weight_ref.3, bf16[128,4096]{1,0:T(8,128)(2,1)} %constant.35.clone.table_ref.refs_2_, bf16[128,192]{1,0:T(8,128)(2,1)S(1)} %get-tuple-element.44.turn_ref), custom_call_target="tpu_custom_call" | custom-call | flops 33554432 | bytes 8388608 | tf_op jit(solution)/shard_map/pallas_call | solution.py:674
  39.1 11.9 %all_to_all.35.data_ref = f32[4,32,512]{2,1,0:T(8,128)S(1)} all-to-all(f32[4,32,512]{2,1,0:T(8,128)S(1)} %get-tuple-element.50), channel_id=1, replica_groups=mesh['gx'=8,'gy'=4] {'gy'}, dimensions={0} | all-to-all | bytes 524288 | tf_op jit(solution)/shard_map/all_to_all | solution.py:778
  51.9 3.7 %all-to-all-start.3 = ((f32[8,16,512]{2,1,0:T(8,128)}), f32[8,16,512]{2,1,0:T(8,128)S(1)}, u32[]{:S(2)}, u32[]{:S(2)}) async-start(f32[8,16,512]{2,1,0:T(8,128)} %shard_map.178), calls=%async_computation.3 | async-start | bytes 524288 | tf_op jit(solution)/shard_map/all_to_all | solution.py:778
  55.7 3.1 %shard_map.177.stencil_ref = f32[4,64,1024]{2,1,0:T(8,128)S(1)} custom-call(bf16[4,8,64,128]{3,2,1,0:T(8,128)(2,1)S(1)} %get-tuple-element.36.body_ref, bf16[8,64,128]{2,1,0:T(8,128)(2,1)} %copy-done.9, bf16[8,64,128]{2,1,0:T(8,128)(2,1)} %copy-done.8, bf16[6,64,128]{2,1,0:T(8,128)(2,1)} %copy-done.11, bf16[6,64,128]{2,1,0:T(8,128)(2,1)} %copy-done.12, ...), custom_call_target="tpu_custom_call" | custom-call | flops 905969664 | bytes 2097152 | tf_op jit(solution)/shard_map/pallas_call | solution.py:654
  58.7 3.9 %all-to-all-done.3.slab_ref = f32[8,16,512]{2,1,0:T(8,128)S(1)} async-done(((f32[8,16,512]{2,1,0:T(8,128)}), f32[8,16,512]{2,1,0:T(8,128)S(1)}, u32[]{:S(2)}, u32[]{:S(2)}) %all-to-all-start.3) | async-done | bytes 262176 | tf_op jit(solution)/shard_map/all_to_all | solution.py:778
  62.6 2.2 %shard_map.179 = (bf16[64,4,8,128]{3,2,1,0:T(8,128)(2,1)}, bf16[4,8,64,128]{3,2,1,0:T(8,128)(2,1)S(1)}, bf16[32,16,512]{2,1,0:T(8,128)(2,1)S(1)}) custom-call(f32[4,64,1024]{2,1,0:T(8,128)S(1)} %shard_map.177.stencil_ref, f32[8,16,512]{2,1,0:T(8,128)S(1)} %all-to-all-done.3.slab_ref, bf16[64,4,8,128]{3,2,1,0:T(8,128)(2,1)S(1)} %copy-done, ...), custom_call_target="tpu_custom_call" | custom-call | flops 100663296 | bytes 3145728 | tf_op jit(solution)/shard_map/pallas_call | solution.py:654
  64.8 4.1 %shard_map.180 = bf16[32,24,512]{2,1,0:T(8,128)(2,1)} custom-call(bf16[4,8,64,128]{3,2,1,0:T(8,128)(2,1)S(1)} %get-tuple-element.52.grad_ref.body_ref, bf16[4,8,64,128]{3,2,1,0:T(8,128)(2,1)S(1)} %get-tuple-element.36.body_ref, bf16[8,64,128]{2,1,0:T(8,128)(2,1)} %copy-done.9, bf16[8,64,128]{2,1,0:T(8,128)(2,1)} %copy-done.8, ...), custom_call_target="tpu_custom_call" | custom-call | flops 905969664 | bytes 2097152 | tf_op jit(solution)/shard_map/pallas_call | solution.py:654
  68.9 2.6 %all-to-all-start.4 = ((bf16[32,24,512]{2,1,0:T(8,128)(2,1)}), bf16[32,24,512]{2,1,0:T(8,128)(2,1)S(1)}, u32[]{:S(2)}, u32[]{:S(2)}) async-start(bf16[32,24,512]{2,1,0:T(8,128)(2,1)} %shard_map.180), calls=%async_computation.4 | async-start | bytes 1572864 | tf_op jit(solution)/shard_map/all_to_all | solution.py:778
  71.6 1.3 %collective-permute-start.5 = (bf16[8,64,128]{2,1,0:T(8,128)(2,1)S(1)}, bf16[8,64,128]{2,1,0:T(8,128)(2,1)S(1)}, u32[]{:S(2)}, u32[]{:S(2)}) collective-permute-start(bf16[8,64,128]{2,1,0:T(8,128)(2,1)S(1)} %get-tuple-element.69), channel_id=1, source_target_pairs={{4,0},{8,4},{12,8},{16,12},{20,16},{24,20},{28,24},{5,1},{9,5},{13... | collective-permute-start | bytes 393224 | tf_op jit(solution)/shard_map/ppermute | solution.py:729
  72.9 3.0 %collective-permute-start.4 = (bf16[8,64,128]{2,1,0:T(8,128)(2,1)S(1)}, bf16[8,64,128]{2,1,0:T(8,128)(2,1)S(1)}, u32[]{:S(2)}, u32[]{:S(2)}) collective-permute-start(bf16[8,64,128]{2,1,0:T(8,128)(2,1)S(1)} %get-tuple-element.70), channel_id=1, source_target_pairs={{0,4},{4,8},{8,12},{12,16},{16,20},{20,24},{24,28},{1,5},{5,9},{9,... | collective-permute-start | bytes 393224 | tf_op jit(solution)/shard_map/ppermute | solution.py:729
  77.0 3.6 %collective-permute-start.6 = (bf16[6,64,128]{2,1,0:T(8,128)(2,1)S(1)}, bf16[6,64,128]{2,1,0:T(8,128)(2,1)S(1)}, u32[]{:S(2)}, u32[]{:S(2)}) collective-permute-start(bf16[6,64,128]{2,1,0:T(8,128)(2,1)S(1)} %pad_maximum_fusion.2), channel_id=1, source_target_pairs={{0,1},{1,2},{2,3},{4,5},{5,6},{6,7},{8,9},{9,10},{10,11},{12,13},{... | collective-permute-start | bytes 294920 | tf_op jit(solution)/shard_map/ppermute | solution.py:729
  80.6 1.3 %collective-permute-start.7 = (bf16[6,64,128]{2,1,0:T(8,128)(2,1)S(1)}, bf16[6,64,128]{2,1,0:T(8,128)(2,1)S(1)}, u32[]{:S(2)}, u32[]{:S(2)}) collective-permute-start(bf16[6,64,128]{2,1,0:T(8,128)(2,1)S(1)} %pad_maximum_fusion.3), channel_id=1, source_target_pairs={{1,0},{2,1},{3,2},{5,4},{6,5},{7,6},{9,8},{10,9},{11,10},{13,12},{... | collective-permute-start | bytes 294920 | tf_op jit(solution)/shard_map/ppermute | solution.py:729
  81.9 5.1 %collective-permute-done.6.ylo_ref = bf16[6,64,128]{2,1,0:T(8,128)(2,1)S(1)} collective-permute-done((bf16[6,64,128]{2,1,0:T(8,128)(2,1)S(1)}, bf16[6,64,128]{2,1,0:T(8,128)(2,1)S(1)}, u32[]{:S(2)}, u32[]{:S(2)}) %collective-permute-start.6) | collective-permute-done | bytes 98336 | tf_op jit(solution)/shard_map/ppermute | solution.py:729
  87.0 1.1 collective-permute-done.7.yhi_ref
  88.7 2.5 %all-to-all-done.4.data_ref = bf16[32,24,512]{2,1,0:T(8,128)(2,1)S(1)} async-done(((bf16[32,24,512]{2,1,0:T(8,128)(2,1)}), bf16[32,24,512]{2,1,0:T(8,128)(2,1)S(1)}, u32[]{:S(2)}, u32[]{:S(2)}) %all-to-all-start.4) | async-done | bytes 786464 | tf_op jit(solution)/shard_map/all_to_all | solution.py:778
  91.2 8.9 %shard_map.182 = (f32[4,256,128]{2,1,0:T(8,128)S(1)}, bf16[4,40,512]{2,1,0:T(8,128)(2,1)}) custom-call(bf16[32,24,512]{2,1,0:T(8,128)(2,1)S(1)} %all-to-all-done.4.data_ref, bf16[2,2,8,32,4096]{4,3,2,1,0:T(8,128)(2,1)} %weight_ref.3, bf16[16,1024]{1,0:T(8,128)(2,1)} %constant.36.clone.table_ref, bf16[128,192]{1,0:T(8,128)(2,1)S(1)} %get-tuple-element.44.turn_ref, ...), custom_call_target="tpu_custom_call" | custom-call | flops 33554432 | bytes 8388608 | tf_op jit(solution)/shard_map/pallas_call | solution.py:674
  100.1 5.6 %all-to-all-start.5 = ((bf16[4,40,512]{2,1,0:T(8,128)(2,1)}), bf16[4,40,512]{2,1,0:T(8,128)(2,1)S(1)}, u32[]{:S(2)}, u32[]{:S(2)}) async-start(bf16[4,40,512]{2,1,0:T(8,128)(2,1)} %get-tuple-element.59), calls=%async_computation.5 | async-start | bytes 327680 | tf_op jit(solution)/shard_map/all_to_all | solution.py:778
  105.7 5.7 %shard_map.184.refs_3_ = f32[2,2,8,32,4096]{4,3,2,1,0:T(8,128)} custom-call(bf16[4,256,128]{2,1,0:T(8,128)(2,1)S(1)} %get-tuple-element.60.refs_0_, f32[4,256,128]{2,1,0:T(8,128)S(1)} %get-tuple-element.61.refs_1_, bf16[128,4096]{1,0:T(8,128)(2,1)} %constant.35.clone.table_ref.refs_2_), custom_call_target="tpu_custom_call" | custom-call | flops 8388608 | bytes 8388608 | tf_op jit(solution)/shard_map/pallas_call | solution.py:707
  112.1 1.0 shard_map.183
  113.1 4.1 %all-to-all-start.6 = ((bf16[8,48,512]{2,1,0:T(8,128)(2,1)}), bf16[8,48,512]{2,1,0:T(8,128)(2,1)S(1)}, u32[]{:S(2)}, u32[]{:S(2)}) async-start(bf16[8,48,512]{2,1,0:T(8,128)(2,1)} %shard_map.183), calls=%async_computation.6 | async-start | bytes 786432 | tf_op jit(solution)/shard_map/all_to_all | solution.py:778
  117.2 3.0 %shard_map.181.stencil_ref = f32[4,64,1024]{2,1,0:T(8,128)S(1)} custom-call(bf16[4,8,64,128]{3,2,1,0:T(8,128)(2,1)S(1)} %get-tuple-element.52.grad_ref.body_ref, bf16[8,64,128]{2,1,0:T(8,128)(2,1)} %copy-done.7, bf16[8,64,128]{2,1,0:T(8,128)(2,1)} %copy-done.6, bf16[6,64,128]{2,1,0:T(8,128)(2,1)} %copy-done.10, bf16[6,64,128]{2,1,0:T(8,128)(2,1)} %copy-done.13, ...), custom_call_target="tpu_custom_call" | custom-call | flops 905969664 | bytes 2097152 | tf_op jit(solution)/shard_map/pallas_call | solution.py:654
  120.3 5.8 %shard_map.186 = f32[2,2,8,32,4096]{4,3,2,1,0:T(8,128)} custom-call(bf16[4,256,128]{2,1,0:T(8,128)(2,1)S(1)} %get-tuple-element.60.refs_0_, f32[4,256,128]{2,1,0:T(8,128)S(1)} %get-tuple-element.61.refs_1_, bf16[128,4096]{1,0:T(8,128)(2,1)} %constant.35.clone.table_ref.refs_2_, f32[2,2,8,32,4096]{4,3,2,1,0:T(8,128)} %shard_map.184.refs_3_), custom_call_target="tpu_custom_call", output_to_operand_aliasing={{}: (3, {})} | custom-call | flops 8388608 | bytes 8388608 | tf_op jit(solution)/shard_map/pallas_call | solution.py:707
  126.1 1.8 %shard_map.185 = (f32[64,4,8,128]{3,2,1,0:T(8,128)}, f32[64,1728]{1,0:T(8,128)}, f32[64,64]{1,0:T(8,128)}) custom-call(f32[4,64,1024]{2,1,0:T(8,128)S(1)} %shard_map.181.stencil_ref, bf16[8,48,512]{2,1,0:T(8,128)(2,1)S(1)} %all-to-all-done.6.message_ref, bf16[96,128]{1,0:T(8,128)(2,1)S(1)} %copy-done.3), custom_call_target="tpu_custom_call" | custom-call | flops 50331648 | bytes 2621440 | tf_op jit(solution)/shard_map/pallas_call | solution.py:654
  (51 shorter events, 5.3 us)
Async XLA Ops:
  0.6 61.9 %copy-start.1 = (bf16[96,128]{1,0:T(8,128)(2,1)S(1)}, bf16[96,128]{1,0:T(8,128)(2,1)}, u32[]{:S(2)}) copy-start(bf16[96,128]{1,0:T(8,128)(2,1)} %constant.30.clone.inverse_ref) | copy-start | bytes 73732
  0.6 61.9 %copy-start.2 = (bf16[96,128]{1,0:T(8,128)(2,1)S(1)}, bf16[96,128]{1,0:T(8,128)(2,1)}, u32[]{:S(2)}) copy-start(bf16[96,128]{1,0:T(8,128)(2,1)} %constant.29.clone.forward_ref) | copy-start | bytes 73732
  0.7 61.9 %copy-start = (bf16[64,4,8,128]{3,2,1,0:T(8,128)(2,1)S(1)}, bf16[64,4,8,128]{3,2,1,0:T(8,128)(2,1)}, u32[]{:S(2)}) copy-start(bf16[64,4,8,128]{3,2,1,0:T(8,128)(2,1)} %cot_ref.1) | copy-start | bytes 1572868
  3.0 12.1 %all-to-all-start = ((f32[8,16,512]{2,1,0:T(8,128)}), f32[8,16,512]{2,1,0:T(8,128)S(1)}, u32[]{:S(2)}, u32[]{:S(2)}) async-start(f32[8,16,512]{2,1,0:T(8,128)} %get-tuple-element.38), calls=%async_computation | async-start | bytes 524288 | tf_op jit(solution)/shard_map/all_to_all | solution.py:778
  8.2 7.9 %collective-permute-start.1 = (bf16[8,64,128]{2,1,0:T(8,128)(2,1)S(1)}, bf16[8,64,128]{2,1,0:T(8,128)(2,1)S(1)}, u32[]{:S(2)}, u32[]{:S(2)}) collective-permute-start(bf16[8,64,128]{2,1,0:T(8,128)(2,1)S(1)} %get-tuple-element.73), channel_id=1, source_target_pairs={{4,0},{8,4},{12,8},{16,12},{20,16},{24,20},{28,24},{5,1},{9,5},{13... | collective-permute-start | bytes 393224 | tf_op jit(solution)/shard_map/ppermute | solution.py:729
  9.5 6.6 %collective-permute-start = (bf16[8,64,128]{2,1,0:T(8,128)(2,1)S(1)}, bf16[8,64,128]{2,1,0:T(8,128)(2,1)S(1)}, u32[]{:S(2)}, u32[]{:S(2)}) collective-permute-start(bf16[8,64,128]{2,1,0:T(8,128)(2,1)S(1)} %get-tuple-element.74), channel_id=1, source_target_pairs={{0,4},{4,8},{8,12},{12,16},{16,20},{20,24},{24,28},{1,5},{5,9},{9,... | collective-permute-start | bytes 393224 | tf_op jit(solution)/shard_map/ppermute | solution.py:729
  14.1 16.9 %copy-start.4 = (bf16[576,256]{1,0:T(8,128)(2,1)}, bf16[576,256]{1,0:T(8,128)(2,1)S(1)}, u32[]{:S(2)}) copy-start(bf16[576,256]{1,0:T(8,128)(2,1)S(1)} %get-tuple-element.56.weight_ref) | copy-start | bytes 884740
  14.1 37.8 %copy-start.5 = (bf16[576,256]{1,0:T(8,128)(2,1)}, bf16[576,256]{1,0:T(8,128)(2,1)S(1)}, u32[]{:S(2)}) copy-start(bf16[576,256]{1,0:T(8,128)(2,1)S(1)} %get-tuple-element.48.weight_ref) | copy-start | bytes 884740
  16.1 39.6 %copy-start.8 = (bf16[8,64,128]{2,1,0:T(8,128)(2,1)}, bf16[8,64,128]{2,1,0:T(8,128)(2,1)S(1)}, u32[]{:S(2)}) copy-start(bf16[8,64,128]{2,1,0:T(8,128)(2,1)S(1)} %collective-permute-done.1.xhi_ref.xhi_any) | copy-start | bytes 393220
  16.1 35.8 %copy-start.9 = (bf16[8,64,128]{2,1,0:T(8,128)(2,1)}, bf16[8,64,128]{2,1,0:T(8,128)(2,1)S(1)}, u32[]{:S(2)}) copy-start(bf16[8,64,128]{2,1,0:T(8,128)(2,1)S(1)} %collective-permute-done.xlo_ref.xlo_any) | copy-start | bytes 393220
  16.1 15.0 %all-to-all-start.1 = ((f32[4,32,512]{2,1,0:T(8,128)}), f32[4,32,512]{2,1,0:T(8,128)S(1)}, u32[]{:S(2)}, u32[]{:S(2)}) async-start(f32[4,32,512]{2,1,0:T(8,128)} %shard_map.174), calls=%async_computation.1 | async-start | bytes 524288 | tf_op jit(solution)/shard_map/all_to_all | solution.py:778
  21.0 18.0 %collective-permute-start.2 = (bf16[6,64,128]{2,1,0:T(8,128)(2,1)S(1)}, bf16[6,64,128]{2,1,0:T(8,128)(2,1)S(1)}, u32[]{:S(2)}, u32[]{:S(2)}) collective-permute-start(bf16[6,64,128]{2,1,0:T(8,128)(2,1)S(1)} %pad_maximum_fusion), channel_id=1, source_target_pairs={{0,1},{1,2},{2,3},{4,5},{5,6},{6,7},{8,9},{9,10},{10,11},{12,13},{... | collective-permute-start | bytes 294920 | tf_op jit(solution)/shard_map/ppermute | solution.py:729
  24.9 14.1 %collective-permute-start.3 = (bf16[6,64,128]{2,1,0:T(8,128)(2,1)S(1)}, bf16[6,64,128]{2,1,0:T(8,128)(2,1)S(1)}, u32[]{:S(2)}, u32[]{:S(2)}) collective-permute-start(bf16[6,64,128]{2,1,0:T(8,128)(2,1)S(1)} %pad_maximum_fusion.1), channel_id=1, source_target_pairs={{1,0},{2,1},{3,2},{5,4},{6,5},{7,6},{9,8},{10,9},{11,10},{13,12},{... | collective-permute-start | bytes 294920 | tf_op jit(solution)/shard_map/ppermute | solution.py:729
  39.0 12.9 %copy-start.11 = (bf16[6,64,128]{2,1,0:T(8,128)(2,1)}, bf16[6,64,128]{2,1,0:T(8,128)(2,1)S(1)}, u32[]{:S(2)}) copy-start(bf16[6,64,128]{2,1,0:T(8,128)(2,1)S(1)} %collective-permute-done.2.ylo_ref.ylo_any) | copy-start | bytes 294916
  39.1 16.6 %copy-start.12 = (bf16[6,64,128]{2,1,0:T(8,128)(2,1)}, bf16[6,64,128]{2,1,0:T(8,128)(2,1)S(1)}, u32[]{:S(2)}) copy-start(bf16[6,64,128]{2,1,0:T(8,128)(2,1)S(1)} %collective-permute-done.3.yhi_ref.yhi_any) | copy-start | bytes 294916
  51.9 10.7 %all-to-all-start.3 = ((f32[8,16,512]{2,1,0:T(8,128)}), f32[8,16,512]{2,1,0:T(8,128)S(1)}, u32[]{:S(2)}, u32[]{:S(2)}) async-start(f32[8,16,512]{2,1,0:T(8,128)} %shard_map.178), calls=%async_computation.3 | async-start | bytes 524288 | tf_op jit(solution)/shard_map/all_to_all | solution.py:778
  68.9 22.2 %all-to-all-start.4 = ((bf16[32,24,512]{2,1,0:T(8,128)(2,1)}), bf16[32,24,512]{2,1,0:T(8,128)(2,1)S(1)}, u32[]{:S(2)}, u32[]{:S(2)}) async-start(bf16[32,24,512]{2,1,0:T(8,128)(2,1)} %shard_map.180), calls=%async_computation.4 | async-start | bytes 1572864 | tf_op jit(solution)/shard_map/all_to_all | solution.py:778
  71.6 4.4 %collective-permute-start.5 = (bf16[8,64,128]{2,1,0:T(8,128)(2,1)S(1)}, bf16[8,64,128]{2,1,0:T(8,128)(2,1)S(1)}, u32[]{:S(2)}, u32[]{:S(2)}) collective-permute-start(bf16[8,64,128]{2,1,0:T(8,128)(2,1)S(1)} %get-tuple-element.69), channel_id=1, source_target_pairs={{4,0},{8,4},{12,8},{16,12},{20,16},{24,20},{28,24},{5,1},{9,5},{13... | collective-permute-start | bytes 393224 | tf_op jit(solution)/shard_map/ppermute | solution.py:729
  72.9 4.0 %collective-permute-start.4 = (bf16[8,64,128]{2,1,0:T(8,128)(2,1)S(1)}, bf16[8,64,128]{2,1,0:T(8,128)(2,1)S(1)}, u32[]{:S(2)}, u32[]{:S(2)}) collective-permute-start(bf16[8,64,128]{2,1,0:T(8,128)(2,1)S(1)} %get-tuple-element.70), channel_id=1, source_target_pairs={{0,4},{4,8},{8,12},{12,16},{16,20},{20,24},{24,28},{1,5},{5,9},{9,... | collective-permute-start | bytes 393224 | tf_op jit(solution)/shard_map/ppermute | solution.py:729
  76.0 41.2 %copy-start.6 = (bf16[8,64,128]{2,1,0:T(8,128)(2,1)}, bf16[8,64,128]{2,1,0:T(8,128)(2,1)S(1)}, u32[]{:S(2)}) copy-start(bf16[8,64,128]{2,1,0:T(8,128)(2,1)S(1)} %collective-permute-done.5.xhi_ref) | copy-start | bytes 393220
  76.9 11.1 %copy-start.7 = (bf16[8,64,128]{2,1,0:T(8,128)(2,1)}, bf16[8,64,128]{2,1,0:T(8,128)(2,1)S(1)}, u32[]{:S(2)}) copy-start(bf16[8,64,128]{2,1,0:T(8,128)(2,1)S(1)} %collective-permute-done.4.xlo_ref) | copy-start | bytes 393220
  77.0 10.0 %collective-permute-start.6 = (bf16[6,64,128]{2,1,0:T(8,128)(2,1)S(1)}, bf16[6,64,128]{2,1,0:T(8,128)(2,1)S(1)}, u32[]{:S(2)}, u32[]{:S(2)}) collective-permute-start(bf16[6,64,128]{2,1,0:T(8,128)(2,1)S(1)} %pad_maximum_fusion.2), channel_id=1, source_target_pairs={{0,1},{1,2},{2,3},{4,5},{5,6},{6,7},{8,9},{9,10},{10,11},{12,13},{... | collective-permute-start | bytes 294920 | tf_op jit(solution)/shard_map/ppermute | solution.py:729
  80.6 7.4 %collective-permute-start.7 = (bf16[6,64,128]{2,1,0:T(8,128)(2,1)S(1)}, bf16[6,64,128]{2,1,0:T(8,128)(2,1)S(1)}, u32[]{:S(2)}, u32[]{:S(2)}) collective-permute-start(bf16[6,64,128]{2,1,0:T(8,128)(2,1)S(1)} %pad_maximum_fusion.3), channel_id=1, source_target_pairs={{1,0},{2,1},{3,2},{5,4},{6,5},{7,6},{9,8},{10,9},{11,10},{13,12},{... | collective-permute-start | bytes 294920 | tf_op jit(solution)/shard_map/ppermute | solution.py:729
  86.9 30.3 %copy-start.10 = (bf16[6,64,128]{2,1,0:T(8,128)(2,1)}, bf16[6,64,128]{2,1,0:T(8,128)(2,1)S(1)}, u32[]{:S(2)}) copy-start(bf16[6,64,128]{2,1,0:T(8,128)(2,1)S(1)} %collective-permute-done.6.ylo_ref) | copy-start | bytes 294916
  88.0 0.6 copy-start.13
  100.1 12.0 %all-to-all-start.5 = ((bf16[4,40,512]{2,1,0:T(8,128)(2,1)}), bf16[4,40,512]{2,1,0:T(8,128)(2,1)S(1)}, u32[]{:S(2)}, u32[]{:S(2)}) async-start(bf16[4,40,512]{2,1,0:T(8,128)(2,1)} %get-tuple-element.59), calls=%async_computation.5 | async-start | bytes 327680 | tf_op jit(solution)/shard_map/all_to_all | solution.py:778
  113.1 12.9 %all-to-all-start.6 = ((bf16[8,48,512]{2,1,0:T(8,128)(2,1)}), bf16[8,48,512]{2,1,0:T(8,128)(2,1)S(1)}, u32[]{:S(2)}, u32[]{:S(2)}) async-start(bf16[8,48,512]{2,1,0:T(8,128)(2,1)} %shard_map.183), calls=%async_computation.6 | async-start | bytes 786432 | tf_op jit(solution)/shard_map/all_to_all | solution.py:778
  120.3 5.8 %copy-start.3 = (bf16[96,128]{1,0:T(8,128)(2,1)S(1)}, bf16[96,128]{1,0:T(8,128)(2,1)}, u32[]{:S(2)}) copy-start(bf16[96,128]{1,0:T(8,128)(2,1)} %constant.31.clone.inverse_ref) | copy-start | bytes 73732
